TPU v7x, 32 devices: a whole 2x2x4 slice. The times are simulated.
32 devices in a mesh: coarse: 4 (over z), member: 8 (over y, x, core).
Axes of the slice: x: 2, y: 2, z: 4, core: 2. Of those that a mesh axis runs over, the one named last changes fastest.
Arguments:
- samples: bfloat16 [40960, 768], P(('coarse', 'member')), may hold values from -6 to 6
- coarse_label: int32 [40960, 1], P(('coarse', 'member')), may hold values from 0 to 3; in each aligned block of 1280 rows (0 to 1279, 1280 to 2559, ...) at most 480 rows name the same one
- fine_label: int32 [40960], P(('coarse', 'member')), may hold values from 0 to 1023
- live_rows: int32 [32], P(('coarse', 'member')), may hold values from 1 to 1280, 30720 in all
- old_centroids: float32 [4, 1024, 768], P('coarse'), may hold values from -0.3 to 0.3
Outputs:
- scores: bfloat16 [40960, 1024], P(('coarse', 'member'))
- new_centroids: float32 [4, 1024, 768], P('coarse', 'member')
Inputs may be any that keep to these rules, and one draw needn't show every extreme that they name: `coarse_label`: among the rows of one device no group is named more than 480 times; some group reaches 480 on some devices. `live_rows`: the largest value equals 1280.
All inputs are finite; a program needn't handle non-finite values. No bound on the sum of `live_rows` on one device may be relied on, other than what follows from the above.
Results may differ from a plain program's by a relative error of at most 0.0085.
Values may be sent and summed in bfloat16 or wider, within the bound.
No kernel may reach another device: no remote copies, remote signals or barrier semaphores. Data moves between devices by JAX's collectives and lax.ppermute only.
A program may use at most 64 MiB of HBM per device.

v0:
```python
import jax
import jax.numpy as jnp
from jax import lax
from jax.sharding import PartitionSpec as P

CAP = 480


prior_weight = 16.0


def per_device(samples, coarse_label, fine_label, live_rows, old_centroids):
    groups = lax.axis_size("coarse")
    members = lax.axis_size("member")
    member_index = lax.axis_index("member")
    row_count = samples.shape[0]
    width = samples.shape[1]
    capacity = CAP
    centers = old_centroids.shape[1]
    share_rows = centers // members
    position = jnp.arange(row_count, dtype=jnp.int32)
    is_live = position < live_rows[0]
    group_id = coarse_label[:, 0]
    member_of = (
        (group_id[:, None] == jnp.arange(groups, dtype=jnp.int32)[None, :]) & is_live[:, None]
    ).astype(jnp.int32)
    before = jnp.cumsum(member_of, axis=0) - member_of
    slot_index = jnp.sum(before * member_of, axis=1)
    target = jnp.where(is_live, group_id * capacity + slot_index, groups * capacity)
    outgoing = (
        jnp.zeros((groups * capacity, width), samples.dtype).at[target].set(samples, mode="drop")
    )
    out_labels = (
        jnp.full((groups * capacity,), -1, jnp.int32).at[target].set(fine_label, mode="drop")
    )
    arrived, arrived_labels = (
        lax.all_to_all(
            outgoing.reshape(groups, capacity, width),
            "coarse",
            split_axis=0,
            concat_axis=0,
            tiled=True,
        ),
        lax.all_to_all(
            out_labels.reshape(groups, capacity), "coarse", split_axis=0, concat_axis=0, tiled=True
        ),
    )
    arrived = arrived.reshape(groups * capacity, width)
    arrived_labels = arrived_labels.reshape(groups * capacity)
    selector = arrived_labels[None, :] == jnp.arange(centers, dtype=jnp.int32)[:, None]
    totals = jnp.dot(selector.astype(jnp.bfloat16), arrived, preferred_element_type=jnp.float32)
    counts = jnp.sum(selector.astype(jnp.float32), axis=1)
    start = member_index * share_rows
    summed, counted = (
        lax.psum(totals.astype(jnp.bfloat16), "member").astype(jnp.float32),
        lax.psum(counts.astype(jnp.bfloat16), "member").astype(jnp.float32),
    )
    renewed = (summed + prior_weight * old_centroids[0]) / (counted[:, None] + prior_weight)
    share = lax.dynamic_slice_in_dim(renewed, start, share_rows, 0)
    centroid_bf = renewed.astype(jnp.bfloat16)
    half_norm = 0.5 * jnp.sum(jnp.square(centroid_bf.astype(jnp.float32)), axis=1)
    scored = (
        lax.dot_general(
            arrived, centroid_bf, (((1,), (1,)), ((), ())), preferred_element_type=jnp.float32
        )
        - half_norm[None, :]
    )
    returned = lax.all_to_all(
        scored.astype(jnp.bfloat16).reshape(groups, capacity, centers),
        "coarse",
        split_axis=0,
        concat_axis=0,
        tiled=True,
    )
    flattened = returned.reshape(groups * capacity, centers)
    padded = jnp.concatenate([flattened, jnp.zeros((1, centers), jnp.bfloat16)], axis=0)
    scores = padded[target]
    return (scores, share[None])


def solution(mesh):
    return jax.shard_map(
        per_device,
        mesh=mesh,
        in_specs=(
            P(("coarse", "member"), None),
            P(("coarse", "member"), None),
            P(("coarse", "member")),
            P(("coarse", "member")),
            P("coarse", None, None),
        ),
        out_specs=(P(("coarse", "member"), None), P("coarse", "member", None)),
        check_vma=False,
    )
```

profile of v0, /device:TPU:0, one launch (start us, length us, event | category | flops | bytes accessed | tf_op | source)
XLA Modules:
  0.0 288.5 jit_solution(2461157060050382578)
XLA Ops:
  7.8 0.7 reduce
  8.6 1.2 reduce-window.6
  9.7 0.2 slice_reduce_fusion
  9.9 0.2 reduce-window.9
  10.1 0.1 add_bitcast_fusion
  10.2 0.7 fusion.14
  11.0 5.4 %scatter_custom_fusion.1 = s32[1920]{0:T(1024)S(1)} fusion(s32[1280]{0:T(1024)S(1)} %get-tuple-element.3, s32[1280]{0:T(1024)} %param.7, s32[]{:T(128)} %constant.17.clone.1), kind=kCustom, calls=%fused_computation.36 | custom fusion | bytes 8192 | tf_op jit(solution)/shard_map/scatter | solution.py:34
  16.4 0.7 all_to_all.13
  17.1 6.3 %all-to-all-start.1 = ((s32[4,1,480]{2,1,0:T(1,128)}), s32[4,1,480]{2,1,0:T(1,128)S(1)}, u32[]{:S(2)}, u32[]{:S(2)}) async-start(s32[4,1,480]{2,1,0:T(1,128)} %all_to_all.13), calls=%async_computation.1 | async-start | bytes 16384 | tf_op jit(solution)/shard_map/all_to_all | solution.py:44
  23.4 10.7 %scatter_custom_fusion = bf16[1920,768]{1,0:T(8,128)(2,1)} fusion(s32[1280]{0:T(1024)S(1)} %get-tuple-element.3, bf16[1280,768]{1,0:T(8,128)(2,1)} %param.5, bf16[]{:T(256)} %constant.12.clone.1), kind=kCustom, calls=%fused_computation.12 | custom fusion | bytes 2949632 | tf_op jit(solution)/shard_map/scatter | solution.py:31
  34.1 0.0 all-to-all-done.1
  34.1 5.1 %all-to-all-start = ((bf16[4,480,768]{2,1,0:T(8,128)(2,1)}), bf16[4,480,768]{2,1,0:T(8,128)(2,1)S(1)}, u32[]{:S(2)}, u32[]{:S(2)}) async-start(bf16[4,480,768]{2,1,0:T(8,128)(2,1)} %bitcast.2), calls=%async_computation | async-start | bytes 5898240 | tf_op jit(solution)/shard_map/all_to_all | solution.py:37
  39.2 0.0 all-reduce.3.cloned.1.call-start
  39.2 0.1 eq.48
  39.3 65.8 %all-to-all-done = bf16[4,480,768]{2,1,0:T(8,128)(2,1)S(1)} async-done(((bf16[4,480,768]{2,1,0:T(8,128)(2,1)}), bf16[4,480,768]{2,1,0:T(8,128)(2,1)S(1)}, u32[]{:S(2)}, u32[]{:S(2)}) %all-to-all-start) | async-done | bytes 2949152 | tf_op jit(solution)/shard_map/all_to_all | solution.py:37
  105.1 0.0 copy-start
  105.1 4.7 %fusion.3 = bf16[1024,768]{1,0:T(8,128)(2,1)} fusion(bf16[1920,768]{1,0:T(8,128)(2,1)S(1)} %bitcast.40, s32[1920]{0:T(1024)S(1)} %eq.48), kind=kOutput, calls=%fused_computation.11 | convolution fusion | flops 3022651392 | bytes 4529664 | tf_op jit(solution)/shard_map/dot_general | solution.py:51
  109.7 0.0 copy-done
  109.7 0.0 all-reduce.3.cloned.1.call-update
  109.8 0.9 convert_reduce_fusion
  110.6 13.2 %psum.15 = bf16[1024]{0:T(1024)(128)(2,1)S(1)} all-reduce(bf16[1024]{0:T(1024)(128)(2,1)S(1)} %convert_reduce_fusion), channel_id=1, replica_groups=mesh['coarse'=4,'member'=8] {'member'}, use_global_device_ids=true, to_apply=%region_7.8 | all-reduce | flops 1024 | bytes 4096 | tf_op jit(solution)/shard_map/psum | solution.py:56
  123.9 44.2 %all-reduce.3.cloned.1.call-done = bf16[1024,768]{1,0:T(8,128)(2,1)} async-done(((bf16[1024,768]{1,0:T(8,128)(2,1)}), bf16[1024,768]{1,0:T(8,128)(2,1)}) %all-reduce.3.cloned.1.call-update) | async-done | bytes 1572880 | tf_op jit(solution)/shard_map/psum | solution.py:55
  168.1 0.0 copy-start.1
  168.1 3.2 %multiply_reduce_fusion = (f32[1024]{0:T(1024)S(1)}, f32[1024,768]{1,0:T(8,128)S(1)}) fusion(f32[1024]{0:T(1024)S(1)} %convert_add_fusion, f32[1,1024,768]{2,1,0:T(8,128)} %param.9, bf16[1024,768]{1,0:T(8,128)(2,1)} %all-reduce.3.cloned.1.call-done), kind=kLoop, calls=%fused_computation.10 | loop fusion | flops 6290432 | bytes 7872512 | tf_op jit(solution)/shard_map/reduce_sum | solution.py:61
  171.3 0.0 copy-done.1
  171.3 4.9 %subtract_convert_fusion = bf16[1920,1024]{1,0:T(8,128)(2,1)} fusion(f32[1024]{0:T(1024)S(1)} %broadcast_multiply_fusion, bf16[1920,768]{1,0:T(8,128)(2,1)S(1)} %bitcast.41, f32[1024,768]{1,0:T(8,128)S(1)} %get-tuple-element.5), kind=kOutput, calls=%fused_computation.3 | convolution fusion | flops 3024617472 | bytes 10031104 | tf_op jit(solution)/shard_map/dot_general | solution.py:63
  176.2 4.8 %all-to-all-start.2 = ((bf16[4,480,1024]{2,1,0:T(8,128)(2,1)}), bf16[4,480,1024]{2,1,0:T(8,128)(2,1)}, u32[]{:S(2)}, u32[]{:S(2)}) async-start(bf16[4,480,1024]{2,1,0:T(8,128)(2,1)} %bitcast.39), calls=%async_computation.2 | async-start | bytes 7864320 | tf_op jit(solution)/shard_map/all_to_all | solution.py:68
  181.1 0.8 dynamic-slice_bitcast_fusion
  181.9 86.1 %all-to-all-done.2 = bf16[4,480,1024]{2,1,0:T(8,128)(2,1)} async-done(((bf16[4,480,1024]{2,1,0:T(8,128)(2,1)}), bf16[4,480,1024]{2,1,0:T(8,128)(2,1)}, u32[]{:S(2)}, u32[]{:S(2)}) %all-to-all-start.2) | async-done | bytes 3932192 | tf_op jit(solution)/shard_map/all_to_all | solution.py:68
  267.9 4.4 %concatenate.3 = bf16[1921,1024]{1,0:T(8,128)(2,1)} pad(bf16[1920,1024]{1,0:T(8,128)(2,1)} %bitcast.6, bf16[]{:T(256)} %constant.12.clone.1), padding=0_1x0_0 | pad | bytes 7866370 | tf_op jit(solution)/shard_map/concatenate | solution.py:76
  272.3 9.3 %gather_fusion = bf16[1280,1024]{1,0:T(8,128)(2,1)} fusion(bf16[1921,1024]{1,0:T(8,128)(2,1)} %concatenate.3, s32[2048]{0:T(1024)S(1)} %pad_clamp_fusion), kind=kCustom, calls=%fused_computation | custom fusion | bytes 5248000 | tf_op jit(solution)/shard_map/gather | solution.py:77
  (8 shorter events, 0.1 us)
Async XLA Ops:
  17.1 17.0 %all-to-all-start.1 = ((s32[4,1,480]{2,1,0:T(1,128)}), s32[4,1,480]{2,1,0:T(1,128)S(1)}, u32[]{:S(2)}, u32[]{:S(2)}) async-start(s32[4,1,480]{2,1,0:T(1,128)} %all_to_all.13), calls=%async_computation.1 | async-start | bytes 16384 | tf_op jit(solution)/shard_map/all_to_all | solution.py:44
  34.1 71.0 %all-to-all-start = ((bf16[4,480,768]{2,1,0:T(8,128)(2,1)}), bf16[4,480,768]{2,1,0:T(8,128)(2,1)S(1)}, u32[]{:S(2)}, u32[]{:S(2)}) async-start(bf16[4,480,768]{2,1,0:T(8,128)(2,1)} %bitcast.2), calls=%async_computation | async-start | bytes 5898240 | tf_op jit(solution)/shard_map/all_to_all | solution.py:37
  39.2 128.9 %all-reduce.3.cloned.1.call-start = ((), (), s32[]{:S(2)}) async-start(), calls=%async_computation.3 | async-start | bytes 3145728 | tf_op jit(solution)/shard_map/psum | solution.py:55
  105.1 4.7 %copy-start = (bf16[4,480,768]{2,1,0:T(8,128)(2,1)}, bf16[4,480,768]{2,1,0:T(8,128)(2,1)S(1)}, u32[]{:S(2)}) copy-start(bf16[4,480,768]{2,1,0:T(8,128)(2,1)S(1)} %all-to-all-done) | copy-start | bytes 8847364
  168.1 3.3 %copy-start.1 = (bf16[4,480,768]{2,1,0:T(8,128)(2,1)S(1)}, bf16[4,480,768]{2,1,0:T(8,128)(2,1)}, u32[]{:S(2)}) copy-start(bf16[4,480,768]{2,1,0:T(8,128)(2,1)} %copy-done) | copy-start | bytes 8847364
  176.2 91.7 %all-to-all-start.2 = ((bf16[4,480,1024]{2,1,0:T(8,128)(2,1)}), bf16[4,480,1024]{2,1,0:T(8,128)(2,1)}, u32[]{:S(2)}, u32[]{:S(2)}) async-start(bf16[4,480,1024]{2,1,0:T(8,128)(2,1)} %bitcast.39), calls=%async_computation.2 | async-start | bytes 7864320 | tf_op jit(solution)/shard_map/all_to_all | solution.py:68
Sparse Core Ops, SparseCore 0:
  109.9 58.1 all-reduce.2
where the time goes:
time: 289 us; the launch traced here: 288 us
  waiting for transfers between devices  196 us (68%)
  local copies, waits for them, and re-layouts  31.6 us (11%)
  starting transfers between devices  16.2 us (6%)
  between operations  14.7 us (5%)
  blocking collectives  13.2 us (5%)
  matrix products  9.59 us (3%)
  other arithmetic  7.05 us (2%)
    all_to_all x1, waiting for transfers between devices, per_device(): lax.all_to_all(scored.astype(jnp.bfloat16).reshape(groups, capacity, cent...  86.1 us
    all_to_all x1, waiting for transfers between devices, per_device(): lax.all_to_all(outgoing.reshape(groups, capacity, width), 'coarse', split...  65.8 us
    psum x1, waiting for transfers between devices, per_device(): lax.psum(totals.astype(jnp.bfloat16), 'member').astype(jnp.float32)  44.2 us
    psum x1, blocking collectives, per_device(): lax.psum(counts.astype(jnp.bfloat16), 'member').astype(jnp.float32)  13.2 us
    scatter x1, local copies, waits for them, and re-layouts, per_device(): jnp.zeros((groups * capacity, width), samples.dtype).at[target]  10.7 us
    gather x1, local copies, waits for them, and re-layouts, per_device(): scores = padded[target]  9.32 us
    all_to_all x1, starting transfers between devices, per_device(): lax.all_to_all(out_labels.reshape(groups, capacity), 'coarse', split_axis...  6.32 us
  transfers between devices with their start and end apart: 4, of which 3 were waited for; matrix products, arithmetic and copies ran while one was open for 4% of the time, Pallas kernels for 0%

commit v1 on v0

v1 whole, which is shorter than its diff:
```python
import functools

import jax
import jax.numpy as jnp
from jax import lax
from jax.experimental import pallas as pl
from jax.experimental.pallas import tpu as pltpu
from jax.sharding import PartitionSpec as P

AXES = ("coarse", "member")
STREAMS = 2
TILE = 16
PRIOR = 16.0
PARTS = 3
F32 = jnp.float32
BF16 = jnp.bfloat16


def pad_rows(blocks):
    return max(TILE, -(-blocks // TILE) * TILE)


def orders_of(groups, members):
    inner = [(0, 1 << bit) for bit in range(1, members.bit_length() - 1)]
    outer = [((1 << (bit + 1)) - 1, 0) for bit in range(groups.bit_length() - 1)]
    dims = []
    for place in range(max(len(inner), len(outer))):
        dims += inner[place : place + 1] + outer[place : place + 1]
    count = len(dims)
    turned = {}
    for core in range(2):
        for stream in range(STREAMS):
            shift = (2 * stream + core) * count // 4
            turned[core, stream] = dims[shift:] + dims[:shift]
    return turned


def exchange(array, partner, groups, members):
    pairs = []
    for z in range(groups):
        for m in range(members):
            to_z, to_m = partner(z, m)
            pairs.append((z * members + m, to_z * members + to_m))
    return lax.ppermute(array, AXES, pairs)


def coefficients(group_rel, member_rel, dims, outer_bits):
    out = []
    for group_mask, member_mask in dims:
        if member_mask:
            out.append((member_rel >> (member_mask.bit_length() - 1)) & 1)
        else:
            top = group_mask.bit_length() - 1
            bit = (group_rel >> top) & 1
            if top + 1 < outer_bits:
                bit = bit ^ ((group_rel >> (top + 1)) & 1)
            out.append(bit)
    return out


def block_position(group_rel, member_rel, dims, outer_bits):
    place = 0
    for bit in coefficients(group_rel, member_rel, dims, outer_bits):
        place = place * 2 + (1 - bit)
    return place


def relative_of(place, dims):
    group_rel = member_rel = 0
    for at, (group_mask, member_mask) in enumerate(dims):
        if not (place >> (len(dims) - 1 - at)) & 1:
            group_rel ^= group_mask
            member_rel ^= member_mask
    return group_rel, member_rel


def sums_kernel(base, step, pos_ref, own_ref, other_ref, count_ref, out_ref):
    rows = own_ref.shape[0]
    at = pl.program_id(0)
    start = pl.multiple_of(at * step, step)
    key = lax.broadcasted_iota(jnp.int32, (step, rows), 0) + (base + start)
    first = jnp.where(pos_ref[:, :rows] == key, 1.0, 0.0).astype(BF16)
    second = jnp.where(pos_ref[:, rows:] == key, 1.0, 0.0).astype(BF16)
    total = jnp.dot(first, own_ref[...], preferred_element_type=F32)
    total += jnp.dot(second, other_ref[...], preferred_element_type=F32)
    out_ref[pl.ds(start, step), :] = total.astype(BF16)

    @pl.when(at == pl.num_programs(0) - 1)
    def _():
        tail = count_ref.shape[0]
        out_ref[pl.ds(out_ref.shape[0] - tail, tail), :] = count_ref[...]


def key_sums(pos_row, own, other, count_tile, base, keys, stream, step=1024):
    rows = own.shape[0]
    wide = own.shape[1] // STREAMS
    step = min(step, keys)
    out_rows = keys + count_tile.shape[0]
    return pl.pallas_call(
        functools.partial(sums_kernel, base, step),
        grid=(keys // step,),
        out_shape=jax.ShapeDtypeStruct((out_rows, wide), BF16),
        in_specs=[
            pl.BlockSpec((1, 2 * rows), lambda i: (0, 0)),
            pl.BlockSpec((rows, wide), lambda i: (0, stream)),
            pl.BlockSpec((rows, wide), lambda i: (0, stream)),
            pl.BlockSpec(count_tile.shape, lambda i: (0, 0)),
        ],
        out_specs=pl.BlockSpec((out_rows, wide), lambda i: (0, 0)),
        compiler_params=pltpu.CompilerParams(vmem_limit_bytes=24 << 20),
        cost_estimate=pl.CostEstimate(
            flops=2 * keys * 2 * rows * wide, bytes_accessed=(4 * rows + 2 * keys) * wide, transcendentals=0
        ),
        name="key_sums",
    )(pos_row, own, other, count_tile)


def small_call(kernel, name, outs, *args):
    whole = pl.BlockSpec(memory_space=pltpu.VMEM)
    moved = sum(a.size * a.dtype.itemsize for a in (*args, *outs))
    return pl.pallas_call(
        kernel,
        out_shape=outs,
        in_specs=[whole] * len(args),
        out_specs=[whole] * len(outs),
        compiler_params=pltpu.CompilerParams(vmem_limit_bytes=12 << 20),
        cost_estimate=pl.CostEstimate(flops=moved // 2, bytes_accessed=moved, transcendentals=0),
        name=name,
    )(*args)


def add_tail(keep_ref, got_ref, body, shift):
    kept = keep_ref[body:, :].astype(F32)
    return kept + pltpu.roll(got_ref[body:, :].astype(F32), shift, 0)


def fold_kernel(half, shift, got_ref, keep_ref, send_out, keep_out):
    tail = add_tail(keep_ref, got_ref, 2 * half, shift).astype(BF16)
    send_out[:half, :] = (got_ref[:half, :].astype(F32) + keep_ref[:half, :].astype(F32)).astype(BF16)
    keep_out[:half, :] = (
        got_ref[half : 2 * half, :].astype(F32) + keep_ref[half : 2 * half, :].astype(F32)
    ).astype(BF16)
    send_out[half:, :] = tail
    keep_out[half:, :] = tail


def seed_kernel(share, shift, got_ref, keep_ref, old_ref, send_out, near_out):
    two = 2 * share
    near = got_ref[share:two, :].astype(F32) + keep_ref[share:two, :].astype(F32) + PRIOR * old_ref[...]
    near_out[...] = near
    send_out[:share, :] = (got_ref[:share, :].astype(F32) + keep_ref[:share, :].astype(F32)).astype(BF16)
    send_out[share:two, :] = near.astype(BF16)
    send_out[two:, :] = add_tail(keep_ref, got_ref, two, shift).astype(BF16)


def centroid_kernel(share, base, digits, rows_out, got_ref, sent_ref, near_ref, fresh_out, cents_out):
    two = 2 * share
    wide = got_ref.shape[1]
    last = sent_ref.shape[0] - two - 1
    lane = lax.broadcasted_iota(jnp.int32, (share, wide), 1)
    line = lax.broadcasted_iota(jnp.int32, (share, wide), 0)
    mine = sent_ref[two:, :].astype(F32)
    theirs = got_ref[two:, :].astype(F32)
    total = (
        sent_ref[:share, :].astype(F32) + got_ref[share:two, :].astype(F32),
        near_ref[...] + got_ref[:share, :].astype(F32),
    )
    tile = jnp.zeros((rows_out, wide), F32)
    tile_row = lax.broadcasted_iota(jnp.int32, (rows_out, wide), 0)
    for block in range(2):
        row = mine[last - 1 + block : last + block, :] + theirs[last - block : last - block + 1, :]
        count = jnp.full((share, 1), PRIOR, F32)
        for digit in range(digits):
            hit = jnp.where(lane == line + digit * share, row, 0.0)
            count += jnp.sum(hit, axis=1, keepdims=True) * float(base**digit)
        fresh = total[block] / count
        rounded = fresh.astype(BF16)
        cents_out[block * share : (block + 1) * share, :] = rounded
        if block == 1:
            fresh_out[...] = fresh
        norm = 0.5 * jnp.sum(jnp.square(rounded.astype(F32)), axis=1, keepdims=True)
        spread = jnp.zeros((1, wide), F32)
        for part in range(PARTS):
            term = norm.astype(BF16).astype(F32)
            norm = norm - term
            hit = jnp.where(lane == line + part * share, term, 0.0)
            spread += jnp.sum(hit, axis=0, keepdims=True)
        tile = jnp.where(tile_row == rows_out - 2 + block, spread, tile)
    cents_out[two:, :] = tile.astype(BF16)


def join_kernel(body, shift, got_ref, held_ref, out_ref):
    out_ref[:body, :] = got_ref[:body, :]
    out_ref[body : 2 * body, :] = held_ref[:body, :]
    rows = held_ref.shape[0] - body
    moved = pltpu.roll(got_ref[body:, :].astype(F32), rows - shift, 0)
    out_ref[2 * body :, :] = (held_ref[body:, :].astype(F32) + moved).astype(BF16)


def scores_kernel(groups, share, stream, first, last, where_ref, x_ref, gid_ref, half_ref, *rest):
    pieces = 4
    piece_refs = rest[:pieces]
    rest = rest[pieces:]
    total_ref = None if first else rest[0]
    out_ref, cents, masked = rest[-3:]
    wide = x_ref.shape[1]
    keys = cents.shape[0]
    blocks = where_ref.shape[0] // pieces

    @pl.when(pl.program_id(0) == 0)
    def _():
        for piece in range(pieces):
            for block in range(blocks):
                code = where_ref[piece * blocks + block]
                group = code // (keys // share)
                member = code % (keys // share)
                cents[
                    pl.ds(pl.multiple_of(member * share, share), share),
                    pl.ds(pl.multiple_of(group * wide, 128), wide),
                ] = piece_refs[piece][block * share : (block + 1) * share, :]
        for group in range(groups):
            masked[:, group * wide : (group + 1) * wide] = jnp.where(
                gid_ref[...] == group, x_ref[...], jnp.zeros_like(x_ref)
            )

    step = out_ref.shape[1]
    start = pl.multiple_of(pl.program_id(0) * step, step)
    dots = lax.dot_general(
        masked[...], cents[pl.ds(start, step), :], (((1,), (1,)), ((), ())), preferred_element_type=F32
    )
    if not first:
        dots = dots + total_ref[...]
    if last:
        half = jnp.zeros_like(dots)
        for group in range(groups):
            half = jnp.where(gid_ref[...] == group, half_ref[group : group + 1, :], half)
        dots = dots - half
    out_ref[...] = dots.astype(out_ref.dtype)


def add_scores(samples, gid, half, pieces, where, total, groups, keys, share, stream):
    rows, width = samples.shape
    wide = width // STREAMS
    step = min(256, keys)
    first, last = stream == 0, stream == STREAMS - 1
    whole = pl.BlockSpec(memory_space=pltpu.VMEM)
    return pl.pallas_call(
        functools.partial(scores_kernel, groups, share, stream, first, last),
        grid_spec=pltpu.PrefetchScalarGridSpec(
            num_scalar_prefetch=1,
            grid=(keys // step,),
            in_specs=[
                pl.BlockSpec((rows, wide), lambda i, w: (0, stream)),
                pl.BlockSpec((rows, 1), lambda i, w: (0, 0)),
                pl.BlockSpec((groups, step), lambda i, w: (0, i)),
            ]
            + [whole] * len(pieces)
            + [pl.BlockSpec((rows, step), lambda i, w: (0, i))] * (not first),
            out_specs=pl.BlockSpec((rows, step), lambda i, w: (0, i)),
            scratch_shapes=[
                pltpu.VMEM((keys, groups * wide), BF16),
                pltpu.VMEM((rows, groups * wide), BF16),
            ],
        ),
        out_shape=jax.ShapeDtypeStruct((rows, keys), BF16 if last else F32),
        compiler_params=pltpu.CompilerParams(vmem_limit_bytes=32 << 20),
        cost_estimate=pl.CostEstimate(
            flops=2 * rows * keys * groups * wide, bytes_accessed=2 * (rows + groups * keys) * wide, transcendentals=0
        ),
        name="scores",
    )(where, samples, gid, half, *pieces, *([] if first else [total]))


def per_device(samples, coarse_label, fine_label, live_rows, old_centroids):
    groups = lax.axis_size("coarse")
    members = lax.axis_size("member")
    z = lax.axis_index("coarse")
    me = lax.axis_index("member")
    core = me & 1
    rows, width = samples.shape
    keys = old_centroids.shape[1]
    share = keys // members
    wide = width // STREAMS
    half_keys = groups * keys // 2
    blocks = half_keys // share
    outer_bits = groups.bit_length() - 1
    turned = orders_of(groups, members)
    stages = len(turned[0, 0])
    base = 256 // (groups * members // 2) + 1
    digits = 1
    while base**digits <= 2 * rows:
        digits += 1

    live = jnp.arange(rows, dtype=jnp.int32) < live_rows[0]
    label = jnp.where(live, coarse_label[:, 0] * keys + fine_label, -1)
    sibling = lambda a: exchange(a, lambda gz, m: (gz, m ^ 1), groups, members)
    other_samples = sibling(samples)
    label_all = jnp.concatenate([label, sibling(label)])

    group_of = label_all // keys
    fine = label_all % keys
    owner = fine // share
    mine = (label_all >= 0) & ((owner & 1) == core)

    def of_core(make):
        return jnp.where(core == 0, make(0), make(1))

    def pairing(stage, stream):
        def partner(gz, m):
            group_mask, member_mask = turned[m & 1, stream][stage]
            return gz ^ group_mask, m ^ member_mask

        return partner

    tail = pad_rows(blocks)
    sends, keeps = [], []
    for stream in range(STREAMS):
        place = of_core(
            lambda c: block_position(group_of ^ z, owner ^ me, turned[c, stream], outer_bits)
        )
        pos = jnp.where(mine, place * share + fine % share, -1)
        in_block = (jnp.where(mine, place, -1)[:, None] == jnp.arange(tail)[None, :]).astype(BF16)
        in_lane = ((fine % share)[:, None] == jnp.arange(share)[None, :]).astype(BF16)
        counted = lax.dot_general(
            in_block, in_lane, (((0,), (0,)), ((), ())), preferred_element_type=F32
        ).astype(jnp.int32)
        tile = [(counted // base**digit) % base for digit in range(digits)]
        tile = jnp.concatenate(tile, axis=1).astype(BF16)
        tile = jnp.pad(tile, ((0, 0), (0, wide - digits * share)))
        make = functools.partial(
            key_sums, pos[None, :], samples, other_samples, tile, keys=half_keys // 2, stream=stream
        )
        sends.append(make(base=0))
        keeps.append(make(base=half_keys // 2))

    old_share = lax.dynamic_slice(old_centroids[0], (me * share, 0), (share, width))
    bf = lambda count: jax.ShapeDtypeStruct((count * share + tail, wide), BF16)
    share_f32 = jax.ShapeDtypeStruct((share, wide), F32)
    send, keep, held, fresh, near = list(sends), list(keeps), [None] * 2, [None] * 2, [None] * 2
    count = blocks // 2
    for stage in range(stages - 1):
        for stream in range(STREAMS):
            got = exchange(send[stream], pairing(stage, stream), groups, members)
            if stage < stages - 2:
                send[stream], keep[stream] = small_call(
                    functools.partial(fold_kernel, count // 2 * share, count),
                    "fold",
                    [bf(count // 2)] * 2,
                    got,
                    keep[stream],
                )
            else:
                send[stream], near[stream] = small_call(
                    functools.partial(seed_kernel, share, count),
                    "seed",
                    [bf(2), share_f32],
                    got,
                    keep[stream],
                    old_share[:, stream * wide : (stream + 1) * wide],
                )
        count //= 2
    for stream in range(STREAMS):
        got = exchange(send[stream], pairing(stages - 1, stream), groups, members)
        fresh[stream], held[stream] = small_call(
            functools.partial(centroid_kernel, share, base, digits, tail),
            "centroid",
            [share_f32, bf(2)],
            got,
            send[stream],
            near[stream],
        )
    count = 2
    pieces = [[], []]
    for stage in reversed(range(stages - 1)):
        for stream in range(STREAMS):
            got = exchange(held[stream], pairing(stage, stream), groups, members)
            if stage:
                held[stream] = small_call(
                    functools.partial(join_kernel, count * share, count), "join", [bf(2 * count)], got, held[stream]
                )[0]
            else:
                pieces[stream] = [got, held[stream]]
        count *= 2

    half_blocks = blocks // 2
    norm_rows, where = [], []
    for stream in range(STREAMS):
        pieces[stream] += [sibling(piece) for piece in pieces[stream]]
        codes = []
        for which, piece in enumerate(pieces[stream]):
            part = which % 2
            flip = which // 2
            rows_of = piece[half_blocks * share + tail - half_blocks :].astype(F32)
            norm_rows.append(sum(rows_of[:, p * share : (p + 1) * share] for p in range(PARTS)))
            for block in range(half_blocks):
                rel = [relative_of(part * half_blocks + block, turned[c, stream]) for c in range(2)]
                holder = core ^ flip
                group_rel = jnp.where(holder == 0, rel[0][0], rel[1][0])
                member_rel = jnp.where(holder == 0, rel[0][1], rel[1][1])
                codes.append((z ^ group_rel) * members + (me ^ flip ^ member_rel))
        where.append(jnp.stack(codes).astype(jnp.int32))
    norm_rows = jnp.concatenate(norm_rows)
    where_all = jnp.concatenate(where)
    pick = (where_all[None, :] == jnp.arange(groups * members, dtype=jnp.int32)[:, None]).astype(F32)
    half_norm = jnp.dot(pick, norm_rows, precision=lax.Precision.HIGHEST).reshape(groups, keys)

    gid = jnp.where(live, coarse_label[:, 0], -1)[:, None]
    scores = None
    for stream in range(STREAMS):
        scores = add_scores(
            samples, gid, half_norm, pieces[stream], where[stream], scores, groups, keys, share, stream
        )
    return scores, jnp.concatenate(fresh, axis=1)[None]


def solution(mesh):
    return jax.shard_map(
        per_device,
        mesh=mesh,
        in_specs=(
            P(AXES, None),
            P(AXES, None),
            P(AXES),
            P(AXES),
            P("coarse", None, None),
        ),
        out_specs=(P(AXES, None), P("coarse", "member", None)),
        check_vma=False,
    )
```

time: 289 us -> 145 us (0.50)
  the two profiles are of different devices: /device:TPU:0 before, /device:TPU:11 now
where the time goes in v1:
time: 145 us; the launch traced here: 144 us
  waiting for transfers between devices  66.9 us (46%)
  Pallas kernels  44.8 us (31%)
  local copies, waits for them, and re-layouts  13.3 us (9%)
  starting transfers between devices  9.27 us (6%)
  other arithmetic  6.48 us (4%)
  between operations  1.78 us (1%)
    ppermute x20, waiting for transfers between devices, exchange(): return lax.ppermute(array, AXES, pairs)  66.9 us
    pallas_call x2, Pallas kernels, add_scores(): pl.pallas_call(functools.partial(scores_kernel, groups, share, stream, fi...  18.5 us
    pallas_call x4, Pallas kernels, key_sums(): pl.pallas_call(functools.partial(sums_kernel, base, step), grid=(keys //...  16.6 us
    unnamed x42, local copies, waits for them, and re-layouts  12.9 us
    pallas_call x12, Pallas kernels, small_call(): pl.pallas_call(kernel, out_shape=outs, in_specs=[whole] * len(args), out_...  9.63 us
    ppermute x20, starting transfers between devices, exchange(): return lax.ppermute(array, AXES, pairs)  9.27 us
  transfers between devices with their start and end apart: 20, of which 11 were waited for; matrix products, arithmetic and copies ran while one was open for 6% of the time, Pallas kernels for 15%

profile of v1, /device:TPU:11, one launch (start us, length us, event | category | flops | bytes accessed | tf_op | source)
XLA Modules:
  0.0 143.7 jit_solution(14296125002303643463)
XLA Ops:
  1.4 0.9 multiply_reduce_fusion
  2.3 0.7 add_select_fusion.14
  3.0 0.7 collective-permute-start
  3.7 0.8 collective-permute-done
  5.1 0.6 fusion.26
  6.1 1.9 %collective-permute-done.1.other_ref = bf16[1280,768]{1,0:T(8,128)(2,1)} collective-permute-done((bf16[1280,768]{1,0:T(8,128)(2,1)}, bf16[1280,768]{1,0:T(8,128)(2,1)}, u32[]{:S(2)}, u32[]{:S(2)}) %collective-permute-start.1) | collective-permute-done | bytes 1966112 | tf_op jit(solution)/shard_map/ppermute | solution.py:44
  8.0 1.5 %copy-done.17 = bf16[1280,768]{1,0:T(8,128)(2,1)S(1)} copy-done((bf16[1280,768]{1,0:T(8,128)(2,1)S(1)}, bf16[1280,768]{1,0:T(8,128)(2,1)}, u32[]{:S(2)}) %copy-start.17) | copy-done | bytes 1966104
  9.6 4.2 %key_sums.4 = bf16[1040,384]{1,0:T(8,128)(2,1)S(1)} custom-call(s32[1,2560]{1,0:T(1,128)S(1)} %fusion.16.pos_ref, bf16[1280,768]{1,0:T(8,128)(2,1)S(1)} %copy-done.17, bf16[1280,768]{1,0:T(8,128)(2,1)} %collective-permute-done.1.other_ref, bf16[16,384]{1,0:T(8,128)(2,1)S(1)} %pad_maximum_fusion.count_ref), custom_call_target="tpu_custom_call" | custom-call | flops 2013265920 | bytes 2752512 | tf_op jit(solution)/shard_map/key_sums/pallas_call | solution.py:99
  14.0 4.2 %key_sums.6 = bf16[1040,384]{1,0:T(8,128)(2,1)S(1)} custom-call(s32[1,2560]{1,0:T(1,128)S(1)} %get-tuple-element.34.pos_ref, bf16[1280,768]{1,0:T(8,128)(2,1)S(1)} %copy-done.17, bf16[1280,768]{1,0:T(8,128)(2,1)} %collective-permute-done.1.other_ref, bf16[16,384]{1,0:T(8,128)(2,1)S(1)} %pad_maximum_fusion.1.count_ref), custom_call_target="tpu_custom_call" | custom-call | flops 2013265920 | bytes 2752512 | tf_op jit(solution)/shard_map/key_sums/pallas_call | solution.py:99
  18.1 2.5 %collective-permute-start.11 = (bf16[1040,384]{1,0:T(8,128)(2,1)S(1)}, bf16[1040,384]{1,0:T(8,128)(2,1)S(1)}, u32[]{:S(2)}, u32[]{:S(2)}) collective-permute-start(bf16[1040,384]{1,0:T(8,128)(2,1)S(1)} %key_sums.6), channel_id=1, source_target_pairs={{0,4},{1,25},{2,6},{3,27},{4,0},{5,29},{6,2},{7,31},{8,12},{9,17},... | collective-permute-start | bytes 2396168 | tf_op jit(solution)/shard_map/ppermute | solution.py:44
  20.6 4.2 %key_sums.7.keep_ref = bf16[1040,384]{1,0:T(8,128)(2,1)S(1)} custom-call(s32[1,2560]{1,0:T(1,128)S(1)} %get-tuple-element.34.pos_ref, bf16[1280,768]{1,0:T(8,128)(2,1)S(1)} %copy-done.17, bf16[1280,768]{1,0:T(8,128)(2,1)} %collective-permute-done.1.other_ref, bf16[16,384]{1,0:T(8,128)(2,1)S(1)} %pad_maximum_fusion.1.count_ref), custom_call_target="tpu_custom_call" | custom-call | flops 2013265920 | bytes 2752512 | tf_op jit(solution)/shard_map/key_sums/pallas_call | solution.py:99
  24.8 4.2 %key_sums.5.keep_ref = bf16[1040,384]{1,0:T(8,128)(2,1)S(1)} custom-call(s32[1,2560]{1,0:T(1,128)S(1)} %fusion.16.pos_ref, bf16[1280,768]{1,0:T(8,128)(2,1)S(1)} %copy-done.17, bf16[1280,768]{1,0:T(8,128)(2,1)} %collective-permute-done.1.other_ref, bf16[16,384]{1,0:T(8,128)(2,1)S(1)} %pad_maximum_fusion.count_ref), custom_call_target="tpu_custom_call" | custom-call | flops 2013265920 | bytes 2752512 | tf_op jit(solution)/shard_map/key_sums/pallas_call | solution.py:99
  28.9 0.9 fold.4
  29.8 1.2 collective-permute-start.3
  31.0 18.3 %collective-permute-done.11.got_ref = bf16[1040,384]{1,0:T(8,128)(2,1)S(1)} collective-permute-done((bf16[1040,384]{1,0:T(8,128)(2,1)S(1)}, bf16[1040,384]{1,0:T(8,128)(2,1)S(1)}, u32[]{:S(2)}, u32[]{:S(2)}) %collective-permute-start.11) | collective-permute-done | bytes 798752 | tf_op jit(solution)/shard_map/ppermute | solution.py:44
  49.3 0.9 fold.6
  50.2 1.0 copy-done.4
  51.2 1.1 fold.5
  52.4 7.3 %collective-permute-done.12.got_ref = bf16[528,384]{1,0:T(8,128)(2,1)} collective-permute-done((bf16[528,384]{1,0:T(8,128)(2,1)}, bf16[528,384]{1,0:T(8,128)(2,1)}, u32[]{:S(2)}, u32[]{:S(2)}) %collective-permute-start.12) | collective-permute-done | bytes 405536 | tf_op jit(solution)/shard_map/ppermute | solution.py:44
  59.7 1.1 fold.7
  61.9 5.6 %collective-permute-done.13.got_ref = bf16[272,384]{1,0:T(8,128)(2,1)S(1)} collective-permute-done((bf16[272,384]{1,0:T(8,128)(2,1)S(1)}, bf16[272,384]{1,0:T(8,128)(2,1)S(1)}, u32[]{:S(2)}, u32[]{:S(2)}) %collective-permute-start.13) | collective-permute-done | bytes 208928 | tf_op jit(solution)/shard_map/ppermute | solution.py:44
  67.5 1.2 collective-permute-start.14
  69.0 1.7 %collective-permute-start.6 = (bf16[272,384]{1,0:T(8,128)(2,1)S(1)}, bf16[272,384]{1,0:T(8,128)(2,1)S(1)}, u32[]{:S(2)}, u32[]{:S(2)}) collective-permute-start(bf16[272,384]{1,0:T(8,128)(2,1)S(1)} %get-tuple-element.24.held_ref), channel_id=1, source_target_pairs={{0,4},{1,25},{2,6},{3,27},{4,0},{5,29},{6,2},{7,31},{8,12},{9,17},... | collective-permute-start | bytes 626696 | tf_op jit(solution)/shard_map/ppermute | solution.py:44
  70.7 2.0 %collective-permute-done.14.got_ref = bf16[272,384]{1,0:T(8,128)(2,1)S(1)} collective-permute-done((bf16[272,384]{1,0:T(8,128)(2,1)S(1)}, bf16[272,384]{1,0:T(8,128)(2,1)S(1)}, u32[]{:S(2)}, u32[]{:S(2)}) %collective-permute-start.14) | collective-permute-done | bytes 208928 | tf_op jit(solution)/shard_map/ppermute | solution.py:44
  73.1 3.5 %collective-permute-done.6.got_ref = bf16[272,384]{1,0:T(8,128)(2,1)S(1)} collective-permute-done((bf16[272,384]{1,0:T(8,128)(2,1)S(1)}, bf16[272,384]{1,0:T(8,128)(2,1)S(1)}, u32[]{:S(2)}, u32[]{:S(2)}) %collective-permute-start.6) | collective-permute-done | bytes 208928 | tf_op jit(solution)/shard_map/ppermute | solution.py:44
  76.9 4.7 %collective-permute-done.15.got_ref = bf16[272,384]{1,0:T(8,128)(2,1)S(1)} collective-permute-done((bf16[272,384]{1,0:T(8,128)(2,1)S(1)}, bf16[272,384]{1,0:T(8,128)(2,1)S(1)}, u32[]{:S(2)}, u32[]{:S(2)}) %collective-permute-start.15) | collective-permute-done | bytes 208928 | tf_op jit(solution)/shard_map/ppermute | solution.py:44
  81.6 0.8 join.6.held_ref
  82.7 1.8 %copy.9 = s32[1280,1]{1,0:T(8,128)} copy(s32[1280,1]{0,1:T(1,128)} %param.6) | data formatting | bytes 10240 | tf_op args[1]
  84.5 2.0 %join.5.rest_1_ = bf16[1040,384]{1,0:T(8,128)(2,1)} custom-call(bf16[528,384]{1,0:T(8,128)(2,1)} %collective-permute-done.7.got_ref, bf16[528,384]{1,0:T(8,128)(2,1)S(1)} %join.4.held_ref), custom_call_target="tpu_custom_call" | custom-call | flops 804864 | bytes 1609728 | tf_op jit(solution)/shard_map/join/pallas_call | solution.py:121
  86.5 7.3 %collective-permute-done.16.got_ref = bf16[528,384]{1,0:T(8,128)(2,1)} collective-permute-done((bf16[528,384]{1,0:T(8,128)(2,1)}, bf16[528,384]{1,0:T(8,128)(2,1)}, u32[]{:S(2)}, u32[]{:S(2)}) %collective-permute-start.16) | collective-permute-done | bytes 405536 | tf_op jit(solution)/shard_map/ppermute | solution.py:44
  93.9 2.1 %join.7.rest_1_ = bf16[1040,384]{1,0:T(8,128)(2,1)} custom-call(bf16[528,384]{1,0:T(8,128)(2,1)} %collective-permute-done.16.got_ref, bf16[528,384]{1,0:T(8,128)(2,1)} %join.6.held_ref), custom_call_target="tpu_custom_call" | custom-call | flops 804864 | bytes 1609728 | tf_op jit(solution)/shard_map/join/pallas_call | solution.py:121
  96.0 0.9 fusion.6.gid_ref
  97.3 0.8 maximum_bitcast_fusion
  98.5 0.7 slice_convert_fusion.6
  99.2 0.7 slice_convert_fusion.2
  99.9 15.1 %collective-permute-done.17.rest_0_ = bf16[1040,384]{1,0:T(8,128)(2,1)} collective-permute-done((bf16[1040,384]{1,0:T(8,128)(2,1)}, bf16[1040,384]{1,0:T(8,128)(2,1)}, u32[]{:S(2)}, u32[]{:S(2)}) %collective-permute-start.17) | collective-permute-done | bytes 798752 | tf_op jit(solution)/shard_map/ppermute | solution.py:44
  115.0 0.7 slice_convert_fusion.7
  115.7 0.7 slice_convert_fusion.3
  116.4 0.9 copy-done.11
  117.4 0.9 copy-done.9
  118.3 0.9 copy-done.13
  119.2 0.9 copy-done.15
  120.3 1.1 copy-done.1
  121.4 1.1 copy-done.12
  122.5 1.1 copy-done.14
  123.6 1.5 %copy-done.18 = bf16[1280,768]{1,0:T(8,128)(2,1)S(1)} copy-done((bf16[1280,768]{1,0:T(8,128)(2,1)S(1)}, bf16[1280,768]{1,0:T(8,128)(2,1)}, u32[]{:S(2)}) %copy-start.18) | copy-done | bytes 1966104
  125.2 8.4 %scores.2.rest_4_ = f32[1280,1024]{1,0:T(8,128)S(1)} custom-call(s32[32]{0:T(128)S(1)} %stack.167.where_ref, bf16[1280,768]{1,0:T(8,128)(2,1)S(1)} %copy-done.18, s32[1280,1]{1,0:T(8,128)S(1)} %copy-done.1, f32[4,1024]{1,0:T(4,128)S(1)} %reshape.750.half_ref, bf16[1040,384]{1,0:T(8,128)(2,1)} %collective-permute-done.8.rest_0_, ...), custom_call_target="tpu_custom_call" | custom-call | flops 4026531840 | bytes 4128768 | tf_op jit(solution)/shard_map/scores/pallas_call | solution.py:247
  133.7 10.1 %scores.3 = bf16[1280,1024]{1,0:T(8,128)(2,1)} custom-call(s32[32]{0:T(128)S(1)} %stack.166.where_ref, bf16[1280,768]{1,0:T(8,128)(2,1)S(1)} %copy-done.18, s32[1280,1]{1,0:T(8,128)S(1)} %copy-done.2, f32[4,1024]{1,0:T(4,128)S(1)} %reshape.750.half_ref, bf16[1040,384]{1,0:T(8,128)(2,1)} %collective-permute-done.17.rest_0_, bf16[1040,384]{1,0:T(8,128)(2,1)} %join.7.rest_1_, ...), custom_call_target="tpu_custom_call" | custom-call | flops 4026531840 | bytes 4128768 | tf_op jit(solution)/shard_map/scores/pallas_call | solution.py:247
  (87 shorter events, 5.0 us)
Async XLA Ops:
  0.6 49.5 %copy-start = (f32[1,1024,768]{2,1,0:T(8,128)S(1)}, f32[1,1024,768]{2,1,0:T(8,128)}, u32[]{:S(2)}) copy-start(f32[1,1024,768]{2,1,0:T(8,128)} %param.9) | copy-start | bytes 9437188
  3.0 1.5 %collective-permute-start = (s32[1280]{0:T(1024)S(1)}, s32[1280]{0:T(1024)S(1)}, u32[]{:S(2)}, u32[]{:S(2)}) collective-permute-start(s32[1280]{0:T(1024)S(1)} %add_select_fusion.14), channel_id=1, source_target_pairs={{0,1},{1,0},{2,3},{3,2},{4,5},{5,4},{6,7},{7,6},{8,9},{9,8},{10,11... | collective-permute-start | bytes 15368 | tf_op jit(solution)/shard_map/ppermute | solution.py:44
  3.7 4.3 %collective-permute-start.1 = (bf16[1280,768]{1,0:T(8,128)(2,1)}, bf16[1280,768]{1,0:T(8,128)(2,1)}, u32[]{:S(2)}, u32[]{:S(2)}) collective-permute-start(bf16[1280,768]{1,0:T(8,128)(2,1)} %x_ref.3), channel_id=1, source_target_pairs={{0,1},{1,0},{2,3},{3,2},{4,5},{5,4},{6,7},{7,6},{8,9},{9,8},{10,11... | collective-permute-start | bytes 5898248 | tf_op jit(solution)/shard_map/ppermute | solution.py:44
  8.0 1.5 %copy-start.17 = (bf16[1280,768]{1,0:T(8,128)(2,1)S(1)}, bf16[1280,768]{1,0:T(8,128)(2,1)}, u32[]{:S(2)}) copy-start(bf16[1280,768]{1,0:T(8,128)(2,1)} %x_ref.3) | copy-start | bytes 5898244
  13.7 15.2 %collective-permute-start.2 = (bf16[1040,384]{1,0:T(8,128)(2,1)S(1)}, bf16[1040,384]{1,0:T(8,128)(2,1)S(1)}, u32[]{:S(2)}, u32[]{:S(2)}) collective-permute-start(bf16[1040,384]{1,0:T(8,128)(2,1)S(1)} %key_sums.4), channel_id=1, source_target_pairs={{0,2},{1,9},{2,0},{3,11},{4,6},{5,13},{6,4},{7,15},{8,10},{9,1},{1... | collective-permute-start | bytes 2396168 | tf_op jit(solution)/shard_map/ppermute | solution.py:44
  18.1 31.2 %collective-permute-start.11 = (bf16[1040,384]{1,0:T(8,128)(2,1)S(1)}, bf16[1040,384]{1,0:T(8,128)(2,1)S(1)}, u32[]{:S(2)}, u32[]{:S(2)}) collective-permute-start(bf16[1040,384]{1,0:T(8,128)(2,1)S(1)} %key_sums.6), channel_id=1, source_target_pairs={{0,4},{1,25},{2,6},{3,27},{4,0},{5,29},{6,2},{7,31},{8,12},{9,17},... | collective-permute-start | bytes 2396168 | tf_op jit(solution)/shard_map/ppermute | solution.py:44
  29.8 20.4 %copy-start.3 = (bf16[528,384]{1,0:T(8,128)(2,1)}, bf16[528,384]{1,0:T(8,128)(2,1)S(1)}, u32[]{:S(2)}) copy-start(bf16[528,384]{1,0:T(8,128)(2,1)S(1)} %get-tuple-element.19.keep_ref) | copy-start | bytes 1216516
  29.8 20.4 %collective-permute-start.3 = (bf16[528,384]{1,0:T(8,128)(2,1)}, bf16[528,384]{1,0:T(8,128)(2,1)}, u32[]{:S(2)}, u32[]{:S(2)}) collective-permute-start(bf16[528,384]{1,0:T(8,128)(2,1)} %get-tuple-element.18), channel_id=1, source_target_pairs={{0,8},{1,5},{2,10},{3,7},{4,12},{5,1},{6,14},{7,3},{8,0},{9,13},{1... | collective-permute-start | bytes 1216520 | tf_op jit(solution)/shard_map/ppermute | solution.py:44
  50.2 9.5 %collective-permute-start.12 = (bf16[528,384]{1,0:T(8,128)(2,1)}, bf16[528,384]{1,0:T(8,128)(2,1)}, u32[]{:S(2)}, u32[]{:S(2)}) collective-permute-start(bf16[528,384]{1,0:T(8,128)(2,1)} %get-tuple-element.25), channel_id=1, source_target_pairs={{0,24},{1,3},{2,26},{3,1},{4,28},{5,7},{6,30},{7,5},{8,16},{9,11},... | collective-permute-start | bytes 1216520 | tf_op jit(solution)/shard_map/ppermute | solution.py:44
  50.2 1.0 copy-start.4
  52.3 9.0 %collective-permute-start.4 = (bf16[272,384]{1,0:T(8,128)(2,1)S(1)}, bf16[272,384]{1,0:T(8,128)(2,1)S(1)}, u32[]{:S(2)}, u32[]{:S(2)}) collective-permute-start(bf16[272,384]{1,0:T(8,128)(2,1)S(1)} %get-tuple-element.20), channel_id=1, source_target_pairs={{0,4},{1,25},{2,6},{3,27},{4,0},{5,29},{6,2},{7,31},{8,12},{9,17},... | collective-permute-start | bytes 626696 | tf_op jit(solution)/shard_map/ppermute | solution.py:44
  60.8 6.7 %collective-permute-start.13 = (bf16[272,384]{1,0:T(8,128)(2,1)S(1)}, bf16[272,384]{1,0:T(8,128)(2,1)S(1)}, u32[]{:S(2)}, u32[]{:S(2)}) collective-permute-start(bf16[272,384]{1,0:T(8,128)(2,1)S(1)} %get-tuple-element.27), channel_id=1, source_target_pairs={{0,2},{1,9},{2,0},{3,11},{4,6},{5,13},{6,4},{7,15},{8,10},{9,1},{1... | collective-permute-start | bytes 626696 | tf_op jit(solution)/shard_map/ppermute | solution.py:44
  61.4 7.3 %collective-permute-start.5 = (bf16[272,384]{1,0:T(8,128)(2,1)S(1)}, bf16[272,384]{1,0:T(8,128)(2,1)S(1)}, u32[]{:S(2)}, u32[]{:S(2)}) collective-permute-start(bf16[272,384]{1,0:T(8,128)(2,1)S(1)} %get-tuple-element.22.sent_ref), channel_id=1, source_target_pairs={{0,24},{1,3},{2,26},{3,1},{4,28},{5,7},{6,30},{7,5},{8,16},{9,11},... | collective-permute-start | bytes 626696 | tf_op jit(solution)/shard_map/ppermute | solution.py:44
  67.5 5.1 %collective-permute-start.14 = (bf16[272,384]{1,0:T(8,128)(2,1)S(1)}, bf16[272,384]{1,0:T(8,128)(2,1)S(1)}, u32[]{:S(2)}, u32[]{:S(2)}) collective-permute-start(bf16[272,384]{1,0:T(8,128)(2,1)S(1)} %get-tuple-element.29.sent_ref), channel_id=1, source_target_pairs={{0,8},{1,5},{2,10},{3,7},{4,12},{5,1},{6,14},{7,3},{8,0},{9,13},{1... | collective-permute-start | bytes 626696 | tf_op jit(solution)/shard_map/ppermute | solution.py:44
  69.0 13.3 %copy-start.5 = (f32[128,384]{1,0:T(8,128)}, f32[128,384]{1,0:T(8,128)S(1)}, u32[]{:S(2)}) copy-start(f32[128,384]{1,0:T(8,128)S(1)} %get-tuple-element.32) | copy-start | bytes 589828
  69.0 7.5 %collective-permute-start.6 = (bf16[272,384]{1,0:T(8,128)(2,1)S(1)}, bf16[272,384]{1,0:T(8,128)(2,1)S(1)}, u32[]{:S(2)}, u32[]{:S(2)}) collective-permute-start(bf16[272,384]{1,0:T(8,128)(2,1)S(1)} %get-tuple-element.24.held_ref), channel_id=1, source_target_pairs={{0,4},{1,25},{2,6},{3,27},{4,0},{5,29},{6,2},{7,31},{8,12},{9,17},... | collective-permute-start | bytes 626696 | tf_op jit(solution)/shard_map/ppermute | solution.py:44
  73.0 3.6 %copy-start.7 = (f32[128,384]{1,0:T(8,128)}, f32[128,384]{1,0:T(8,128)S(1)}, u32[]{:S(2)}) copy-start(f32[128,384]{1,0:T(8,128)S(1)} %get-tuple-element.33) | copy-start | bytes 589828
  73.0 8.6 %collective-permute-start.15 = (bf16[272,384]{1,0:T(8,128)(2,1)S(1)}, bf16[272,384]{1,0:T(8,128)(2,1)S(1)}, u32[]{:S(2)}, u32[]{:S(2)}) collective-permute-start(bf16[272,384]{1,0:T(8,128)(2,1)S(1)} %get-tuple-element.31.held_ref), channel_id=1, source_target_pairs={{0,2},{1,9},{2,0},{3,11},{4,6},{5,13},{6,4},{7,15},{8,10},{9,1},{1... | collective-permute-start | bytes 626696 | tf_op jit(solution)/shard_map/ppermute | solution.py:44
  76.6 7.9 %collective-permute-start.7 = (bf16[528,384]{1,0:T(8,128)(2,1)S(1)}, bf16[528,384]{1,0:T(8,128)(2,1)}, u32[]{:S(2)}, u32[]{:S(2)}) collective-permute-start(bf16[528,384]{1,0:T(8,128)(2,1)S(1)} %join.4.held_ref), channel_id=1, source_target_pairs={{0,8},{1,5},{2,10},{3,7},{4,12},{5,1},{6,14},{7,3},{8,0},{9,13},{1... | collective-permute-start | bytes 1216520 | tf_op jit(solution)/shard_map/ppermute | solution.py:44
  82.4 11.5 %collective-permute-start.16 = (bf16[528,384]{1,0:T(8,128)(2,1)}, bf16[528,384]{1,0:T(8,128)(2,1)}, u32[]{:S(2)}, u32[]{:S(2)}) collective-permute-start(bf16[528,384]{1,0:T(8,128)(2,1)} %join.6.held_ref), channel_id=1, source_target_pairs={{0,24},{1,3},{2,26},{3,1},{4,28},{5,7},{6,30},{7,5},{8,16},{9,11},... | collective-permute-start | bytes 1216520 | tf_op jit(solution)/shard_map/ppermute | solution.py:44
  84.5 11.5 %copy-start.19 = (s32[1280,1]{1,0:T(8,128)S(1)}, s32[1280,1]{1,0:T(8,128)}, u32[]{:S(2)}) copy-start(s32[1280,1]{1,0:T(8,128)} %copy.9) | copy-start | bytes 15364
  86.5 10.8 %copy-start.6 = (f32[128,384]{1,0:T(8,128)S(1)}, f32[128,384]{1,0:T(8,128)}, u32[]{:S(2)}) copy-start(f32[128,384]{1,0:T(8,128)} %copy-done.5) | copy-start | bytes 589828
  86.5 10.8 %copy-start.8 = (f32[128,384]{1,0:T(8,128)S(1)}, f32[128,384]{1,0:T(8,128)}, u32[]{:S(2)}) copy-start(f32[128,384]{1,0:T(8,128)} %copy-done.7) | copy-start | bytes 589828
  86.5 13.4 %collective-permute-start.8 = (bf16[1040,384]{1,0:T(8,128)(2,1)}, bf16[1040,384]{1,0:T(8,128)(2,1)}, u32[]{:S(2)}, u32[]{:S(2)}) collective-permute-start(bf16[1040,384]{1,0:T(8,128)(2,1)} %join.5.rest_1_), channel_id=1, source_target_pairs={{0,2},{1,9},{2,0},{3,11},{4,6},{5,13},{6,4},{7,15},{8,10},{9,1},{1... | collective-permute-start | bytes 2396168 | tf_op jit(solution)/shard_map/ppermute | solution.py:44
  95.9 19.1 %collective-permute-start.17 = (bf16[1040,384]{1,0:T(8,128)(2,1)}, bf16[1040,384]{1,0:T(8,128)(2,1)}, u32[]{:S(2)}, u32[]{:S(2)}) collective-permute-start(bf16[1040,384]{1,0:T(8,128)(2,1)} %join.7.rest_1_), channel_id=1, source_target_pairs={{0,4},{1,25},{2,6},{3,27},{4,0},{5,29},{6,2},{7,31},{8,12},{9,17},... | collective-permute-start | bytes 2396168 | tf_op jit(solution)/shard_map/ppermute | solution.py:44
  98.0 18.4 %collective-permute-start.10 = (bf16[1040,384]{1,0:T(8,128)(2,1)}, bf16[1040,384]{1,0:T(8,128)(2,1)S(1)}, u32[]{:S(2)}, u32[]{:S(2)}) collective-permute-start(bf16[1040,384]{1,0:T(8,128)(2,1)} %join.5.rest_1_), channel_id=1, source_target_pairs={{0,1},{1,0},{2,3},{3,2},{4,5},{5,4},{6,7},{7,6},{8,9},{9,8},{10,11... | collective-permute-start | bytes 2396168 | tf_op jit(solution)/shard_map/ppermute | solution.py:44
  98.0 19.3 %collective-permute-start.19 = (bf16[1040,384]{1,0:T(8,128)(2,1)}, bf16[1040,384]{1,0:T(8,128)(2,1)S(1)}, u32[]{:S(2)}, u32[]{:S(2)}) collective-permute-start(bf16[1040,384]{1,0:T(8,128)(2,1)} %join.7.rest_1_), channel_id=1, source_target_pairs={{0,1},{1,0},{2,3},{3,2},{4,5},{5,4},{6,7},{7,6},{8,9},{9,8},{10,11... | collective-permute-start | bytes 2396168 | tf_op jit(solution)/shard_map/ppermute | solution.py:44
  99.9 18.3 %collective-permute-start.9 = (bf16[1040,384]{1,0:T(8,128)(2,1)}, bf16[1040,384]{1,0:T(8,128)(2,1)S(1)}, u32[]{:S(2)}, u32[]{:S(2)}) collective-permute-start(bf16[1040,384]{1,0:T(8,128)(2,1)} %collective-permute-done.8.rest_0_), channel_id=1, source_target_pairs={{0,1},{1,0},{2,3},{3,2},{4,5},{5,4},{6,7},{7,6},{8,9},{9,8},{10,11... | collective-permute-start | bytes 2396168 | tf_op jit(solution)/shard_map/ppermute | solution.py:44
  115.0 4.2 %collective-permute-start.18 = (bf16[1040,384]{1,0:T(8,128)(2,1)}, bf16[1040,384]{1,0:T(8,128)(2,1)S(1)}, u32[]{:S(2)}, u32[]{:S(2)}) collective-permute-start(bf16[1040,384]{1,0:T(8,128)(2,1)} %collective-permute-done.17.rest_0_), channel_id=1, source_target_pairs={{0,1},{1,0},{2,3},{3,2},{4,5},{5,4},{6,7},{7,6},{8,9},{9,8},{10,11... | collective-permute-start | bytes 2396168 | tf_op jit(solution)/shard_map/ppermute | solution.py:44
  116.4 0.9 copy-start.11
  117.4 0.9 copy-start.9
  118.3 0.9 copy-start.13
  119.2 0.9 copy-start.15
  120.3 1.1 copy-start.1
  121.4 1.1 copy-start.12
  122.5 1.1 copy-start.14
  123.6 1.5 %copy-start.18 = (bf16[1280,768]{1,0:T(8,128)(2,1)S(1)}, bf16[1280,768]{1,0:T(8,128)(2,1)}, u32[]{:S(2)}) copy-start(bf16[1280,768]{1,0:T(8,128)(2,1)} %x_ref.3) | copy-start | bytes 5898244
  125.2 8.5 %copy-start.2 = (s32[1280,1]{1,0:T(8,128)S(1)}, s32[1280,1]{1,0:T(8,128)}, u32[]{:S(2)}) copy-start(s32[1280,1]{1,0:T(8,128)} %fusion.6.gid_ref) | copy-start | bytes 15364
  125.2 8.5 %copy-start.10 = (bf16[1040,384]{1,0:T(8,128)(2,1)S(1)}, bf16[1040,384]{1,0:T(8,128)(2,1)}, u32[]{:S(2)}) copy-start(bf16[1040,384]{1,0:T(8,128)(2,1)} %copy-done.9) | copy-start | bytes 2396164
  125.2 8.5 %copy-start.16 = (bf16[1040,384]{1,0:T(8,128)(2,1)S(1)}, bf16[1040,384]{1,0:T(8,128)(2,1)}, u32[]{:S(2)}) copy-start(bf16[1040,384]{1,0:T(8,128)(2,1)} %copy-done.15) | copy-start | bytes 2396164

commit v2 on v1

v2 whole, which is shorter than its diff:
```python
import functools

import jax
import jax.numpy as jnp
from jax import lax
from jax.experimental import pallas as pl
from jax.experimental.pallas import tpu as pltpu
from jax.sharding import PartitionSpec as P

AXES = ("coarse", "member")
TILE = 16
PRIOR = 16.0
PARTS = 2
F32 = jnp.float32
BF16 = jnp.bfloat16


def pad_rows(blocks):
    return max(TILE, -(-blocks // TILE) * TILE)


def streams_of(width):
    wide = width * 2 // 3
    return ((0, wide), (wide, width - wide))


def orders_of(groups, members):
    inner = [(0, 1 << bit) for bit in range(1, members.bit_length() - 1)]
    outer = [((1 << (bit + 1)) - 1, 0) for bit in range(groups.bit_length() - 1)]
    found = {}
    for core in range(2):
        cut = core * len(inner) // 2
        turned = inner[cut:] + inner[:cut]
        found[core, 0] = turned + outer
        found[core, 1] = outer[:1] + turned + outer[1:]
    return found


def exchange(array, partner, groups, members):
    pairs = []
    for z in range(groups):
        for m in range(members):
            to_z, to_m = partner(z, m)
            pairs.append((z * members + m, to_z * members + to_m))
    return lax.ppermute(array, AXES, pairs)


def coefficients(group_rel, member_rel, dims, outer_bits):
    out = []
    for group_mask, member_mask in dims:
        if member_mask:
            out.append((member_rel >> (member_mask.bit_length() - 1)) & 1)
        else:
            top = group_mask.bit_length() - 1
            bit = (group_rel >> top) & 1
            if top + 1 < outer_bits:
                bit = bit ^ ((group_rel >> (top + 1)) & 1)
            out.append(bit)
    return out


def block_position(group_rel, member_rel, dims, outer_bits):
    place = 0
    for bit in coefficients(group_rel, member_rel, dims, outer_bits):
        place = place * 2 + (1 - bit)
    return place


def relative_of(place, dims):
    group_rel = member_rel = 0
    for at, (group_mask, member_mask) in enumerate(dims):
        if not (place >> (len(dims) - 1 - at)) & 1:
            group_rel ^= group_mask
            member_rel ^= member_mask
    return group_rel, member_rel


def sums_kernel(base, pos_ref, own_ref, other_ref, *rest):
    out_ref = rest[-1]
    rows = own_ref.shape[0]
    keys = out_ref.shape[0] - (rest[0].shape[0] if len(rest) > 1 else 0)
    key = lax.broadcasted_iota(jnp.int32, (keys, rows), 0) + base
    first = jnp.where(pos_ref[:, :rows] == key, 1.0, 0.0).astype(BF16)
    second = jnp.where(pos_ref[:, rows:] == key, 1.0, 0.0).astype(BF16)
    total = jnp.dot(first, own_ref[...], preferred_element_type=F32)
    total += jnp.dot(second, other_ref[...], preferred_element_type=F32)
    out_ref[:keys, :] = total.astype(BF16)
    if len(rest) > 1:
        out_ref[keys:, :] = rest[0][...]


def key_sums(pos_row, own, other, count_tile, base, keys, start, wide):
    rows = own.shape[0]
    extra = [] if count_tile is None else [count_tile]
    out_rows = keys + sum(e.shape[0] for e in extra)
    return pl.pallas_call(
        functools.partial(sums_kernel, base),
        grid=(1,),
        out_shape=jax.ShapeDtypeStruct((out_rows, wide), BF16),
        in_specs=[
            pl.BlockSpec((1, 2 * rows), lambda i: (0, 0)),
            pl.BlockSpec((rows, wide), lambda i: (0, start // wide)),
            pl.BlockSpec((rows, wide), lambda i: (0, start // wide)),
        ]
        + [pl.BlockSpec(e.shape, lambda i: (0, 0)) for e in extra],
        out_specs=pl.BlockSpec((out_rows, wide), lambda i: (0, 0)),
        compiler_params=pltpu.CompilerParams(vmem_limit_bytes=24 << 20),
        cost_estimate=pl.CostEstimate(
            flops=2 * keys * 2 * rows * wide, bytes_accessed=(4 * rows + 2 * keys) * wide, transcendentals=0
        ),
        name="key_sums",
    )(pos_row, own, other, *extra)


def small_call(kernel, name, outs, *args):
    whole = pl.BlockSpec(memory_space=pltpu.VMEM)
    moved = sum(a.size * a.dtype.itemsize for a in (*args, *outs))
    return pl.pallas_call(
        kernel,
        out_shape=outs,
        in_specs=[whole] * len(args),
        out_specs=[whole] * len(outs),
        compiler_params=pltpu.CompilerParams(vmem_limit_bytes=12 << 20),
        cost_estimate=pl.CostEstimate(flops=moved // 2, bytes_accessed=moved, transcendentals=0),
        name=name,
    )(*args)


def add_pair(got_ref, keep_ref, start, stop):
    return got_ref[start:stop, :].astype(F32) + keep_ref[start:stop, :].astype(F32)


def add_tail(got_ref, keep_ref, body, shift):
    kept = keep_ref[body:, :].astype(F32)
    return (kept + pltpu.roll(got_ref[body:, :].astype(F32), shift, 0)).astype(BF16)


def fold_kernel(half, shift, got_ref, keep_ref, send_out, keep_out):
    send_out[:half, :] = add_pair(got_ref, keep_ref, 0, half).astype(BF16)
    keep_out[:half, :] = add_pair(got_ref, keep_ref, half, 2 * half).astype(BF16)
    if got_ref.shape[0] > 2 * half:
        tail = add_tail(got_ref, keep_ref, 2 * half, shift)
        send_out[half:, :] = tail
        keep_out[half:, :] = tail


def seed_kernel(share, shift, got_ref, keep_ref, old_ref, send_out, near_out):
    two = 2 * share
    near = add_pair(got_ref, keep_ref, share, two) + PRIOR * old_ref[...]
    near_out[...] = near
    send_out[:share, :] = add_pair(got_ref, keep_ref, 0, share).astype(BF16)
    send_out[share:two, :] = near.astype(BF16)
    if got_ref.shape[0] > two:
        send_out[two:, :] = add_tail(got_ref, keep_ref, two, shift)


def summed(share, block, got_ref, sent_ref, near_ref):
    if block == 0:
        return sent_ref[:share, :].astype(F32) + got_ref[share : 2 * share, :].astype(F32)
    return near_ref[...] + got_ref[:share, :].astype(F32)


def square_sums(rounded):
    return jnp.sum(jnp.square(rounded.astype(F32)), axis=1, keepdims=True)


def first_kernel(share, base, digits, got_ref, sent_ref, near_ref, fresh_out, cents_out, scale_out, norm_out):
    two = 2 * share
    wide = got_ref.shape[1]
    last = sent_ref.shape[0] - two - 1
    lane = lax.broadcasted_iota(jnp.int32, (share, wide), 1)
    line = lax.broadcasted_iota(jnp.int32, (share, wide), 0)
    mine = sent_ref[two:, :].astype(F32)
    theirs = got_ref[two:, :].astype(F32)
    for block in range(2):
        row = mine[last - 1 + block : last + block, :] + theirs[last - block : last - block + 1, :]
        count = jnp.full((share, 1), PRIOR, F32)
        for digit in range(digits):
            hit = jnp.where(lane == line + digit * share, row, 0.0)
            count += jnp.sum(hit, axis=1, keepdims=True) * float(base**digit)
        scale_out[block * share : (block + 1) * share, :] = count
        fresh = summed(share, block, got_ref, sent_ref, near_ref) / count
        rounded = fresh.astype(BF16)
        cents_out[block * share : (block + 1) * share, :] = rounded
        norm_out[block * share : (block + 1) * share, :] = square_sums(rounded)
        if block == 1:
            fresh_out[...] = fresh


def last_kernel(share, tail, got_ref, sent_ref, near_ref, scale_ref, norm_ref, fresh_out, cents_out):
    two = 2 * share
    wide = got_ref.shape[1]
    lane = lax.broadcasted_iota(jnp.int32, (share, wide), 1)
    line = lax.broadcasted_iota(jnp.int32, (share, wide), 0)
    tile = jnp.zeros((tail, wide), F32)
    tile_row = lax.broadcasted_iota(jnp.int32, (tail, wide), 0)
    for block in range(2):
        part = slice(block * share, (block + 1) * share)
        fresh = summed(share, block, got_ref, sent_ref, near_ref) / scale_ref[part, :]
        rounded = fresh.astype(BF16)
        cents_out[part, :] = rounded
        if block == 1:
            fresh_out[...] = fresh
        norm = 0.5 * (norm_ref[part, :] + square_sums(rounded))
        spread = jnp.zeros((1, wide), F32)
        for term_at in range(PARTS):
            term = norm.astype(BF16).astype(F32)
            norm = norm - term
            hit = jnp.where(lane == line + term_at * share, term, 0.0)
            spread += jnp.sum(hit, axis=0, keepdims=True)
        tile = jnp.where(tile_row == tail - 2 + block, spread, tile)
    cents_out[two:, :] = tile.astype(BF16)


def join_kernel(body, shift, got_ref, held_ref, out_ref):
    out_ref[:body, :] = got_ref[:body, :]
    out_ref[body : 2 * body, :] = held_ref[:body, :]
    if held_ref.shape[0] > body:
        rows = held_ref.shape[0] - body
        moved = pltpu.roll(got_ref[body:, :].astype(F32), rows - shift, 0)
        out_ref[2 * body :, :] = (held_ref[body:, :].astype(F32) + moved).astype(BF16)


def scores_kernel(groups, share, last, where_ref, x_ref, gid_ref, *rest):
    pieces = 4
    piece_refs, rest = rest[:pieces], rest[pieces:]
    if last:
        total_ref, half_ref, out_ref, cents, masked, half = rest
    else:
        out_ref, cents, masked = rest
    wide = x_ref.shape[1]
    keys = cents.shape[0]
    members = keys // share
    blocks = where_ref.shape[0] // pieces
    lanes = 128

    @pl.when(pl.program_id(0) == 0)
    def _():
        if last and share < lanes:
            half[...] = half_ref[...]
        for piece in range(pieces):
            ref = piece_refs[piece]
            for block in range(blocks):
                code = where_ref[piece * blocks + block]
                group = code // members
                member = code % members
                cents[
                    pl.ds(pl.multiple_of(member * share, share), share),
                    pl.ds(pl.multiple_of(group * wide, lanes), wide),
                ] = ref[block * share : (block + 1) * share, :]
            if last and share >= lanes:
                tail = ref[blocks * share :, :].astype(F32)
                for block in range(blocks):
                    code = where_ref[piece * blocks + block]
                    at = tail.shape[0] - blocks + block
                    row = sum(tail[at : at + 1, p * share : (p + 1) * share] for p in range(PARTS))
                    for cut in range(share // lanes):
                        half[pl.ds(code * (share // lanes) + cut, 1), :] = row[:, cut * lanes : (cut + 1) * lanes]
        for group in range(groups):
            masked[:, group * wide : (group + 1) * wide] = jnp.where(
                gid_ref[...] == group, x_ref[...], jnp.zeros_like(x_ref)
            )

    step = out_ref.shape[1]
    at = pl.program_id(0)
    start = pl.multiple_of(at * step, step)
    dots = lax.dot_general(
        masked[...], cents[pl.ds(start, step), :], (((1,), (1,)), ((), ())), preferred_element_type=F32
    )
    if not last:
        out_ref[...] = dots
        return
    gid = gid_ref[...]
    for cut in range(step // lanes):
        columns = slice(cut * lanes, (cut + 1) * lanes)
        offset = jnp.zeros((out_ref.shape[0], lanes), F32)
        for group in range(groups):
            row = half[pl.ds(group * (keys // lanes) + at * (step // lanes) + cut, 1), :]
            offset = jnp.where(gid == group, row, offset)
        out_ref[:, columns] = (dots[:, columns] + total_ref[:, columns] - offset).astype(BF16)


def add_scores(samples, gid, pieces, where, total, half, groups, keys, share, start, wide):
    rows = samples.shape[0]
    step = min(256, keys)
    last = total is not None
    whole = pl.BlockSpec(memory_space=pltpu.VMEM)
    return pl.pallas_call(
        functools.partial(scores_kernel, groups, share, last),
        grid_spec=pltpu.PrefetchScalarGridSpec(
            num_scalar_prefetch=1,
            grid=(keys // step,),
            in_specs=[
                pl.BlockSpec((rows, wide), lambda i, w: (0, start // wide)),
                pl.BlockSpec((rows, 1), lambda i, w: (0, 0)),
            ]
            + [whole] * len(pieces)
            + [pl.BlockSpec((rows, step), lambda i, w: (0, i)), whole] * last,
            out_specs=pl.BlockSpec((rows, step), lambda i, w: (0, i)),
            scratch_shapes=[
                pltpu.VMEM((keys, groups * wide), BF16),
                pltpu.VMEM((rows, groups * wide), BF16),
            ]
            + [pltpu.VMEM((groups * keys // 128, 128), F32)] * last,
        ),
        out_shape=jax.ShapeDtypeStruct((rows, keys), BF16 if last else F32),
        compiler_params=pltpu.CompilerParams(vmem_limit_bytes=26 << 20),
        cost_estimate=pl.CostEstimate(
            flops=2 * rows * keys * groups * wide, bytes_accessed=2 * (rows + groups * keys) * wide, transcendentals=0
        ),
        name="scores",
    )(where, samples, gid, *pieces, *([total, half] if last else []))


def per_device(samples, coarse_label, fine_label, live_rows, old_centroids):
    groups = lax.axis_size("coarse")
    members = lax.axis_size("member")
    z = lax.axis_index("coarse")
    me = lax.axis_index("member")
    core = me & 1
    rows, width = samples.shape
    keys = old_centroids.shape[1]
    share = keys // members
    columns = streams_of(width)
    streams = range(len(columns))
    half_keys = groups * keys // 2
    blocks = half_keys // share
    outer_bits = groups.bit_length() - 1
    turned = orders_of(groups, members)
    stages = len(turned[0, 0])
    base = 256 // (groups * members // 2) + 1
    digits = 1
    while base**digits <= 2 * rows:
        digits += 1

    live = jnp.arange(rows, dtype=jnp.int32) < live_rows[0]
    label = jnp.where(live, coarse_label[:, 0] * keys + fine_label, -1)
    sibling = lambda a: exchange(a, lambda gz, m: (gz, m ^ 1), groups, members)
    other_samples = sibling(samples)
    label_all = jnp.concatenate([label, sibling(label)])

    group_of = label_all // keys
    fine = label_all % keys
    owner = fine // share
    mine = (label_all >= 0) & ((owner & 1) == core)

    def of_core(make):
        return jnp.where(core == 0, make(0), make(1))

    def pairing(stage, stream):
        def partner(gz, m):
            group_mask, member_mask = turned[m & 1, stream][stage]
            return gz ^ group_mask, m ^ member_mask

        return partner

    tail = pad_rows(blocks)
    sends, keeps = [], []
    for stream, (start, wide) in enumerate(columns):
        place = of_core(
            lambda c: block_position(group_of ^ z, owner ^ me, turned[c, stream], outer_bits)
        )
        pos = jnp.where(mine, place * share + fine % share, -1)
        tile = None
        if stream == 0:
            in_block = (jnp.where(mine, place, -1)[:, None] == jnp.arange(tail)[None, :]).astype(BF16)
            in_lane = ((fine % share)[:, None] == jnp.arange(share)[None, :]).astype(BF16)
            counted = lax.dot_general(
                in_block, in_lane, (((0,), (0,)), ((), ())), preferred_element_type=F32
            ).astype(jnp.int32)
            tile = [(counted // base**digit) % base for digit in range(digits)]
            tile = jnp.concatenate(tile, axis=1).astype(BF16)
            tile = jnp.pad(tile, ((0, 0), (0, wide - digits * share)))
        make = functools.partial(
            key_sums, pos[None, :], samples, other_samples, tile, keys=half_keys // 2, start=start, wide=wide
        )
        sends.append(make(base=0))
        keeps.append(make(base=half_keys // 2))

    old_share = lax.dynamic_slice(old_centroids[0], (me * share, 0), (share, width))

    def bf(count, stream, tailed):
        rows_out = count * share + (tail if stream == tailed else 0)
        return jax.ShapeDtypeStruct((rows_out, columns[stream][1]), BF16)

    share_f32 = [jax.ShapeDtypeStruct((share, wide), F32) for _, wide in columns]
    send, keep, held, fresh, near = list(sends), list(keeps), [None] * 2, [None] * 2, [None] * 2
    count = blocks // 2
    for stage in range(stages - 1):
        for stream, (start, wide) in enumerate(columns):
            got = exchange(send[stream], pairing(stage, stream), groups, members)
            if stage < stages - 2:
                send[stream], keep[stream] = small_call(
                    functools.partial(fold_kernel, count // 2 * share, count),
                    "fold",
                    [bf(count // 2, stream, 0)] * 2,
                    got,
                    keep[stream],
                )
            else:
                send[stream], near[stream] = small_call(
                    functools.partial(seed_kernel, share, count),
                    "seed",
                    [bf(2, stream, 0), share_f32[stream]],
                    got,
                    keep[stream],
                    old_share[:, start : start + wide],
                )
        count //= 2
    column = jax.ShapeDtypeStruct((2 * share, 1), F32)
    for stream in streams:
        got = exchange(send[stream], pairing(stages - 1, stream), groups, members)
        if stream == 0:
            fresh[0], held[0], scale, norm = small_call(
                functools.partial(first_kernel, share, base, digits),
                "first_centroids",
                [share_f32[0], bf(2, 0, 1), column, column],
                got,
                send[0],
                near[0],
            )
        else:
            fresh[1], held[1] = small_call(
                functools.partial(last_kernel, share, tail),
                "last_centroids",
                [share_f32[1], bf(2, 1, 1)],
                got,
                send[1],
                near[1],
                scale,
                norm,
            )
    count = 2
    pieces = [[], []]
    for stage in reversed(range(stages - 1)):
        for stream in streams:
            got = exchange(held[stream], pairing(stage, stream), groups, members)
            if stage:
                held[stream] = small_call(
                    functools.partial(join_kernel, count * share, count),
                    "join",
                    [bf(2 * count, stream, 1)],
                    got,
                    held[stream],
                )[0]
            else:
                pieces[stream] = [got, held[stream]]
        count *= 2

    half_blocks = blocks // 2
    where = []
    for stream in streams:
        pieces[stream] += [sibling(piece) for piece in pieces[stream]]
        codes = []
        for which in range(len(pieces[stream])):
            part = which % 2
            flip = which // 2
            for block in range(half_blocks):
                rel = [relative_of(part * half_blocks + block, turned[c, stream]) for c in range(2)]
                holder = core ^ flip
                group_rel = jnp.where(holder == 0, rel[0][0], rel[1][0])
                member_rel = jnp.where(holder == 0, rel[0][1], rel[1][1])
                codes.append((z ^ group_rel) * members + (me ^ flip ^ member_rel))
        where.append(jnp.stack(codes).astype(jnp.int32))
    half = jnp.zeros((groups * keys // 128, 128), F32)
    if share < 128:
        norm_rows = []
        for piece in pieces[1]:
            rows_of = piece[half_blocks * share + tail - half_blocks :].astype(F32)
            norm_rows.append(sum(rows_of[:, p * share : (p + 1) * share] for p in range(PARTS)))
        pick = (where[1][None, :] == jnp.arange(groups * members, dtype=jnp.int32)[:, None]).astype(F32)
        half = jnp.dot(pick, jnp.concatenate(norm_rows), precision=lax.Precision.HIGHEST).reshape(half.shape)

    gid = jnp.where(live, coarse_label[:, 0], -1)[:, None]
    scores = None
    for stream, (start, wide) in enumerate(columns):
        scores = add_scores(
            samples, gid, pieces[stream], where[stream], scores, half, groups, keys, share, start, wide
        )
    return scores, jnp.concatenate(fresh, axis=1)[None]


def solution(mesh):
    return jax.shard_map(
        per_device,
        mesh=mesh,
        in_specs=(
            P(AXES, None),
            P(AXES, None),
            P(AXES),
            P(AXES),
            P("coarse", None, None),
        ),
        out_specs=(P(AXES, None), P("coarse", "member", None)),
        check_vma=False,
    )
```

time: 145 us -> 151 us (1.041)
  the two profiles are of different devices: /device:TPU:11 before, /device:TPU:0 now
where the time goes in v2:
time: 151 us; the launch traced here: 150 us
  waiting for transfers between devices  71.5 us (47%)
  Pallas kernels  38.1 us (25%)
  starting transfers between devices  31.7 us (21%)
  other arithmetic  3.88 us (3%)
  local copies, waits for them, and re-layouts  2.97 us (2%)
  between operations  1.77 us (1%)
    ppermute x20, waiting for transfers between devices, exchange(): return lax.ppermute(array, AXES, pairs)  71.5 us
    ppermute x20, starting transfers between devices, exchange(): return lax.ppermute(array, AXES, pairs)  31.7 us
    pallas_call x2, Pallas kernels, add_scores(): pl.pallas_call(functools.partial(scores_kernel, groups, share, last), gri...  19.5 us
    pallas_call x4, Pallas kernels, key_sums(): pl.pallas_call(functools.partial(sums_kernel, base), grid=(1,), out_shape...  13.8 us
    pallas_call x12, Pallas kernels, small_call(): pl.pallas_call(kernel, out_shape=outs, in_specs=[whole] * len(args), out_...  4.8 us
  transfers between devices with their start and end apart: 20, of which 14 were waited for; matrix products, arithmetic and copies ran while one was open for 4% of the time, Pallas kernels for 15%

profile of v2, /device:TPU:0, one launch (start us, length us, event | category | flops | bytes accessed | tf_op | source)
XLA Modules:
  0.0 150.5 jit_solution(5976764219863653820)
XLA Ops:
  0.6 0.5 collective-permute-start.1
  2.1 0.7 multiply_reduce_fusion
  2.8 0.7 add_select_fusion.9
  3.5 1.3 collective-permute-done
  4.8 0.6 fusion.21
  5.7 1.5 %copy-done.1 = bf16[1280,768]{1,0:T(8,128)(2,1)S(1)} copy-done((bf16[1280,768]{1,0:T(8,128)(2,1)S(1)}, bf16[1280,768]{1,0:T(8,128)(2,1)}, u32[]{:S(2)}) %copy-start.1) | copy-done | bytes 1966104
  7.2 4.3 %key_sums.6 = bf16[1040,512]{1,0:T(8,128)(2,1)S(1)} custom-call(s32[1,2560]{1,0:T(1,128)S(1)} %get-tuple-element.38.pos_ref, bf16[1280,768]{1,0:T(8,128)(2,1)S(1)} %copy-done.1, bf16[1280,768]{1,0:T(8,128)(2,1)} %collective-permute-done.1.other_ref, bf16[16,512]{1,0:T(8,128)(2,1)S(1)} %fusion.9.rest_0_), custom_call_target="tpu_custom_call" | custom-call | flops 2684354560 | bytes 3670016 | tf_op jit(solution)/shard_map/key_sums/pallas_call | solution.py:96
  11.5 2.9 %collective-permute-start.6 = (bf16[1040,512]{1,0:T(8,128)(2,1)S(1)}, bf16[1040,512]{1,0:T(8,128)(2,1)S(1)}, u32[]{:S(2)}, u32[]{:S(2)}) collective-permute-start(bf16[1040,512]{1,0:T(8,128)(2,1)S(1)} %key_sums.6), channel_id=1, source_target_pairs={{0,2},{1,5},{2,0},{3,7},{4,6},{5,1},{6,4},{7,3},{8,10},{9,13},{10,... | collective-permute-start | bytes 3194888 | tf_op jit(solution)/shard_map/ppermute | solution.py:45
  14.4 4.3 %key_sums.7.keep_ref = bf16[1040,512]{1,0:T(8,128)(2,1)S(1)} custom-call(s32[1,2560]{1,0:T(1,128)S(1)} %get-tuple-element.38.pos_ref, bf16[1280,768]{1,0:T(8,128)(2,1)S(1)} %copy-done.1, bf16[1280,768]{1,0:T(8,128)(2,1)} %collective-permute-done.1.other_ref, bf16[16,512]{1,0:T(8,128)(2,1)S(1)} %fusion.9.rest_0_), custom_call_target="tpu_custom_call" | custom-call | flops 2684354560 | bytes 3670016 | tf_op jit(solution)/shard_map/key_sums/pallas_call | solution.py:96
  18.7 8.7 %collective-permute-done.6.got_ref = bf16[1040,512]{1,0:T(8,128)(2,1)S(1)} collective-permute-done((bf16[1040,512]{1,0:T(8,128)(2,1)S(1)}, bf16[1040,512]{1,0:T(8,128)(2,1)S(1)}, u32[]{:S(2)}, u32[]{:S(2)}) %collective-permute-start.6) | collective-permute-done | bytes 1064992 | tf_op jit(solution)/shard_map/ppermute | solution.py:45
  27.6 2.1 %collective-permute-start.7 = (bf16[528,512]{1,0:T(8,128)(2,1)S(1)}, bf16[528,512]{1,0:T(8,128)(2,1)S(1)}, u32[]{:S(2)}, u32[]{:S(2)}) collective-permute-start(bf16[528,512]{1,0:T(8,128)(2,1)S(1)} %get-tuple-element.26), channel_id=1, source_target_pairs={{0,4},{1,3},{2,6},{3,1},{4,0},{5,7},{6,2},{7,5},{8,12},{9,11},{10,... | collective-permute-start | bytes 1622024 | tf_op jit(solution)/shard_map/ppermute | solution.py:45
  29.7 7.3 %collective-permute-done.7.got_ref = bf16[528,512]{1,0:T(8,128)(2,1)S(1)} collective-permute-done((bf16[528,512]{1,0:T(8,128)(2,1)S(1)}, bf16[528,512]{1,0:T(8,128)(2,1)S(1)}, u32[]{:S(2)}, u32[]{:S(2)}) %collective-permute-start.7) | collective-permute-done | bytes 540704 | tf_op jit(solution)/shard_map/ppermute | solution.py:45
  37.0 0.8 fold.7
  37.8 2.1 %collective-permute-start.8 = (bf16[272,512]{1,0:T(8,128)(2,1)}, bf16[272,512]{1,0:T(8,128)(2,1)}, u32[]{:S(2)}, u32[]{:S(2)}) collective-permute-start(bf16[272,512]{1,0:T(8,128)(2,1)} %get-tuple-element.28), channel_id=1, source_target_pairs={{0,8},{1,9},{2,10},{3,11},{4,12},{5,13},{6,14},{7,15},{8,0},{9,1},... | collective-permute-start | bytes 835592 | tf_op jit(solution)/shard_map/ppermute | solution.py:45
  40.0 5.5 %collective-permute-done.8.got_ref = bf16[272,512]{1,0:T(8,128)(2,1)} collective-permute-done((bf16[272,512]{1,0:T(8,128)(2,1)}, bf16[272,512]{1,0:T(8,128)(2,1)}, u32[]{:S(2)}, u32[]{:S(2)}) %collective-permute-start.8) | collective-permute-done | bytes 278560 | tf_op jit(solution)/shard_map/ppermute | solution.py:45
  45.5 1.0 seed.3
  46.5 3.8 %collective-permute-start.9 = (bf16[272,512]{1,0:T(8,128)(2,1)S(1)}, bf16[272,512]{1,0:T(8,128)(2,1)S(1)}, u32[]{:S(2)}, u32[]{:S(2)}) collective-permute-start(bf16[272,512]{1,0:T(8,128)(2,1)S(1)} %get-tuple-element.30.sent_ref), channel_id=1, source_target_pairs={{0,24},{1,25},{2,26},{3,27},{4,28},{5,29},{6,30},{7,31},{8,16},{9,... | collective-permute-start | bytes 835592 | tf_op jit(solution)/shard_map/ppermute | solution.py:45
  50.3 4.6 %collective-permute-done.9.got_ref = bf16[272,512]{1,0:T(8,128)(2,1)S(1)} collective-permute-done((bf16[272,512]{1,0:T(8,128)(2,1)S(1)}, bf16[272,512]{1,0:T(8,128)(2,1)S(1)}, u32[]{:S(2)}, u32[]{:S(2)}) %collective-permute-start.9) | collective-permute-done | bytes 278560 | tf_op jit(solution)/shard_map/ppermute | solution.py:45
  55.3 5.4 %collective-permute-start.15 = (bf16[256,512]{1,0:T(8,128)(2,1)S(1)}, bf16[256,512]{1,0:T(8,128)(2,1)S(1)}, u32[]{:S(2)}, u32[]{:S(2)}) collective-permute-start(bf16[256,512]{1,0:T(8,128)(2,1)S(1)} %get-tuple-element.35.held_ref), channel_id=1, source_target_pairs={{0,8},{1,9},{2,10},{3,11},{4,12},{5,13},{6,14},{7,15},{8,0},{9,1},... | collective-permute-start | bytes 786440 | tf_op jit(solution)/shard_map/ppermute | solution.py:45
  60.7 5.5 %collective-permute-done.15.got_ref = bf16[256,512]{1,0:T(8,128)(2,1)S(1)} collective-permute-done((bf16[256,512]{1,0:T(8,128)(2,1)S(1)}, bf16[256,512]{1,0:T(8,128)(2,1)S(1)}, u32[]{:S(2)}, u32[]{:S(2)}) %collective-permute-start.15) | collective-permute-done | bytes 262176 | tf_op jit(solution)/shard_map/ppermute | solution.py:45
  66.3 1.6 %collective-permute-start.16 = (bf16[512,512]{1,0:T(8,128)(2,1)S(1)}, bf16[512,512]{1,0:T(8,128)(2,1)S(1)}, u32[]{:S(2)}, u32[]{:S(2)}) collective-permute-start(bf16[512,512]{1,0:T(8,128)(2,1)S(1)} %join.6.held_ref), channel_id=1, source_target_pairs={{0,4},{1,3},{2,6},{3,1},{4,0},{5,7},{6,2},{7,5},{8,12},{9,11},{10,... | collective-permute-start | bytes 1572872 | tf_op jit(solution)/shard_map/ppermute | solution.py:45
  68.0 2.6 %key_sums.4 = bf16[1024,256]{1,0:T(8,128)(2,1)S(1)} custom-call(s32[1,2560]{1,0:T(1,128)S(1)} %fusion.16.pos_ref, bf16[1280,768]{1,0:T(8,128)(2,1)S(1)} %copy-done.2, bf16[1280,768]{1,0:T(8,128)(2,1)} %collective-permute-done.1.other_ref), custom_call_target="tpu_custom_call" | custom-call | flops 1342177280 | bytes 1835008 | tf_op jit(solution)/shard_map/key_sums/pallas_call | solution.py:96
  70.6 1.8 %collective-permute-start.2 = (bf16[1024,256]{1,0:T(8,128)(2,1)S(1)}, bf16[1024,256]{1,0:T(8,128)(2,1)S(1)}, u32[]{:S(2)}, u32[]{:S(2)}) collective-permute-start(bf16[1024,256]{1,0:T(8,128)(2,1)S(1)} %key_sums.4), channel_id=1, source_target_pairs={{0,8},{1,9},{2,10},{3,11},{4,12},{5,13},{6,14},{7,15},{8,0},{9,1},... | collective-permute-start | bytes 1572872 | tf_op jit(solution)/shard_map/ppermute | solution.py:45
  72.4 3.1 %collective-permute-done.16.got_ref = bf16[512,512]{1,0:T(8,128)(2,1)S(1)} collective-permute-done((bf16[512,512]{1,0:T(8,128)(2,1)S(1)}, bf16[512,512]{1,0:T(8,128)(2,1)S(1)}, u32[]{:S(2)}, u32[]{:S(2)}) %collective-permute-start.16) | collective-permute-done | bytes 524320 | tf_op jit(solution)/shard_map/ppermute | solution.py:45
  75.5 1.0 join.7.rest_1_
  76.6 1.5 %collective-permute-start.17 = (bf16[1024,512]{1,0:T(8,128)(2,1)}, bf16[1024,512]{1,0:T(8,128)(2,1)}, u32[]{:S(2)}, u32[]{:S(2)}) collective-permute-start(bf16[1024,512]{1,0:T(8,128)(2,1)} %join.7.rest_1_), channel_id=1, source_target_pairs={{0,2},{1,5},{2,0},{3,7},{4,6},{5,1},{6,4},{7,3},{8,10},{9,13},{10,... | collective-permute-start | bytes 3145736 | tf_op jit(solution)/shard_map/ppermute | solution.py:45
  78.1 2.6 %key_sums.5.keep_ref = bf16[1024,256]{1,0:T(8,128)(2,1)S(1)} custom-call(s32[1,2560]{1,0:T(1,128)S(1)} %fusion.16.pos_ref, bf16[1280,768]{1,0:T(8,128)(2,1)S(1)} %copy-done.2, bf16[1280,768]{1,0:T(8,128)(2,1)} %collective-permute-done.1.other_ref), custom_call_target="tpu_custom_call" | custom-call | flops 1342177280 | bytes 1835008 | tf_op jit(solution)/shard_map/key_sums/pallas_call | solution.py:96
  80.7 2.0 %collective-permute-done.2.got_ref = bf16[1024,256]{1,0:T(8,128)(2,1)S(1)} collective-permute-done((bf16[1024,256]{1,0:T(8,128)(2,1)S(1)}, bf16[1024,256]{1,0:T(8,128)(2,1)S(1)}, u32[]{:S(2)}, u32[]{:S(2)}) %collective-permute-start.2) | collective-permute-done | bytes 524320 | tf_op jit(solution)/shard_map/ppermute | solution.py:45
  82.8 0.5 collective-permute-start.3
  83.3 11.4 %collective-permute-done.3.got_ref = bf16[512,256]{1,0:T(8,128)(2,1)S(1)} collective-permute-done((bf16[512,256]{1,0:T(8,128)(2,1)S(1)}, bf16[512,256]{1,0:T(8,128)(2,1)S(1)}, u32[]{:S(2)}, u32[]{:S(2)}) %collective-permute-start.3) | collective-permute-done | bytes 262176 | tf_op jit(solution)/shard_map/ppermute | solution.py:45
  94.8 1.6 %collective-permute-start.4 = (bf16[256,256]{1,0:T(8,128)(2,1)S(1)}, bf16[256,256]{1,0:T(8,128)(2,1)S(1)}, u32[]{:S(2)}, u32[]{:S(2)}) collective-permute-start(bf16[256,256]{1,0:T(8,128)(2,1)S(1)} %get-tuple-element.22), channel_id=1, source_target_pairs={{0,4},{1,3},{2,6},{3,1},{4,0},{5,7},{6,2},{7,5},{8,12},{9,11},{10,... | collective-permute-start | bytes 393224 | tf_op jit(solution)/shard_map/ppermute | solution.py:45
  96.4 3.4 %collective-permute-done.4.got_ref = bf16[256,256]{1,0:T(8,128)(2,1)S(1)} collective-permute-done((bf16[256,256]{1,0:T(8,128)(2,1)S(1)}, bf16[256,256]{1,0:T(8,128)(2,1)S(1)}, u32[]{:S(2)}, u32[]{:S(2)}) %collective-permute-start.4) | collective-permute-done | bytes 131104 | tf_op jit(solution)/shard_map/ppermute | solution.py:45
  99.9 2.5 %collective-permute-start.5 = (bf16[256,256]{1,0:T(8,128)(2,1)S(1)}, bf16[256,256]{1,0:T(8,128)(2,1)S(1)}, u32[]{:S(2)}, u32[]{:S(2)}) collective-permute-start(bf16[256,256]{1,0:T(8,128)(2,1)S(1)} %get-tuple-element.24.sent_ref), channel_id=1, source_target_pairs={{0,24},{1,25},{2,26},{3,27},{4,28},{5,29},{6,30},{7,31},{8,16},{9,... | collective-permute-start | bytes 393224 | tf_op jit(solution)/shard_map/ppermute | solution.py:45
  102.5 4.4 %collective-permute-done.5.got_ref = bf16[256,256]{1,0:T(8,128)(2,1)S(1)} collective-permute-done((bf16[256,256]{1,0:T(8,128)(2,1)S(1)}, bf16[256,256]{1,0:T(8,128)(2,1)S(1)}, u32[]{:S(2)}, u32[]{:S(2)}) %collective-permute-start.5) | collective-permute-done | bytes 131104 | tf_op jit(solution)/shard_map/ppermute | solution.py:45
  106.9 0.3 last_centroids.1
  107.1 1.6 %collective-permute-start.10 = (bf16[272,256]{1,0:T(8,128)(2,1)S(1)}, bf16[272,256]{1,0:T(8,128)(2,1)S(1)}, u32[]{:S(2)}, u32[]{:S(2)}) collective-permute-start(bf16[272,256]{1,0:T(8,128)(2,1)S(1)} %get-tuple-element.34.held_ref), channel_id=1, source_target_pairs={{0,4},{1,3},{2,6},{3,1},{4,0},{5,7},{6,2},{7,5},{8,12},{9,11},{10,... | collective-permute-start | bytes 417800 | tf_op jit(solution)/shard_map/ppermute | solution.py:45
  108.7 0.5 collective-permute-start.18
  109.2 3.4 %collective-permute-done.10.got_ref = bf16[272,256]{1,0:T(8,128)(2,1)S(1)} collective-permute-done((bf16[272,256]{1,0:T(8,128)(2,1)S(1)}, bf16[272,256]{1,0:T(8,128)(2,1)S(1)}, u32[]{:S(2)}, u32[]{:S(2)}) %collective-permute-start.10) | collective-permute-done | bytes 139296 | tf_op jit(solution)/shard_map/ppermute | solution.py:45
  112.7 1.6 %collective-permute-start.11 = (bf16[528,256]{1,0:T(8,128)(2,1)S(1)}, bf16[528,256]{1,0:T(8,128)(2,1)S(1)}, u32[]{:S(2)}, u32[]{:S(2)}) collective-permute-start(bf16[528,256]{1,0:T(8,128)(2,1)S(1)} %join.4.held_ref), channel_id=1, source_target_pairs={{0,2},{1,5},{2,0},{3,7},{4,6},{5,1},{6,4},{7,3},{8,10},{9,13},{10,... | collective-permute-start | bytes 811016 | tf_op jit(solution)/shard_map/ppermute | solution.py:45
  114.2 5.0 %collective-permute-done.11.got_ref = bf16[528,256]{1,0:T(8,128)(2,1)S(1)} collective-permute-done((bf16[528,256]{1,0:T(8,128)(2,1)S(1)}, bf16[528,256]{1,0:T(8,128)(2,1)S(1)}, u32[]{:S(2)}, u32[]{:S(2)}) %collective-permute-start.11) | collective-permute-done | bytes 270368 | tf_op jit(solution)/shard_map/ppermute | solution.py:45
  119.2 0.8 join.5.rest_1_
  120.0 1.5 %collective-permute-start.12 = (bf16[1040,256]{1,0:T(8,128)(2,1)}, bf16[1040,256]{1,0:T(8,128)(2,1)}, u32[]{:S(2)}, u32[]{:S(2)}) collective-permute-start(bf16[1040,256]{1,0:T(8,128)(2,1)} %join.5.rest_1_), channel_id=1, source_target_pairs={{0,8},{1,9},{2,10},{3,11},{4,12},{5,13},{6,14},{7,15},{8,0},{9,1},... | collective-permute-start | bytes 1597448 | tf_op jit(solution)/shard_map/ppermute | solution.py:45
  121.5 1.1 copy.8
  122.9 1.3 fusion.3.gid_ref
  124.3 5.9 %collective-permute-done.12.rest_0_ = bf16[1040,256]{1,0:T(8,128)(2,1)} collective-permute-done((bf16[1040,256]{1,0:T(8,128)(2,1)}, bf16[1040,256]{1,0:T(8,128)(2,1)}, u32[]{:S(2)}, u32[]{:S(2)}) %collective-permute-start.12) | collective-permute-done | bytes 532512 | tf_op jit(solution)/shard_map/ppermute | solution.py:45
  130.2 0.8 maximum_bitcast_fusion
  130.9 10.7 %scores.2.rest_4_ = f32[1280,1024]{1,0:T(8,128)S(1)} custom-call(s32[32]{0:T(128)S(1)} %stack.167.where_ref, bf16[1280,768]{1,0:T(8,128)(2,1)S(1)} %copy-done.3, s32[1280,1]{1,0:T(8,128)S(1)} %fusion.3.gid_ref, bf16[1024,512]{1,0:T(8,128)(2,1)} %collective-permute-done.17.rest_0_, bf16[1024,512]{1,0:T(8,128)(2,1)} %join.7.rest_1_, ...), custom_call_target="tpu_custom_call" | custom-call | flops 5368709120 | bytes 5505024 | tf_op jit(solution)/shard_map/scores/pallas_call | solution.py:288
  141.7 8.7 %scores.3 = bf16[1280,1024]{1,0:T(8,128)(2,1)} custom-call(s32[32]{0:T(128)S(1)} %stack.166.where_ref, bf16[1280,768]{1,0:T(8,128)(2,1)S(1)} %copy-done.3, s32[1280,1]{1,0:T(8,128)S(1)} %fusion.3.gid_ref, bf16[1040,256]{1,0:T(8,128)(2,1)} %collective-permute-done.12.rest_0_, bf16[1040,256]{1,0:T(8,128)(2,1)} %join.5.rest_1_, ...), custom_call_target="tpu_custom_call" | custom-call | flops 2684354560 | bytes 2752512 | tf_op jit(solution)/shard_map/scores/pallas_call | solution.py:288
  (38 shorter events, 1.6 us)
Async XLA Ops:
  0.6 39.3 %copy-start = (f32[1,1024,768]{2,1,0:T(8,128)S(1)}, f32[1,1024,768]{2,1,0:T(8,128)}, u32[]{:S(2)}) copy-start(f32[1,1024,768]{2,1,0:T(8,128)} %param.9) | copy-start | bytes 9437188
  0.6 5.0 %collective-permute-start.1 = (bf16[1280,768]{1,0:T(8,128)(2,1)}, bf16[1280,768]{1,0:T(8,128)(2,1)}, u32[]{:S(2)}, u32[]{:S(2)}) collective-permute-start(bf16[1280,768]{1,0:T(8,128)(2,1)} %x_ref.3), channel_id=1, source_target_pairs={{0,1},{1,0},{2,3},{3,2},{4,5},{5,4},{6,7},{7,6},{8,9},{9,8},{10,11... | collective-permute-start | bytes 5898248 | tf_op jit(solution)/shard_map/ppermute | solution.py:45
  3.5 1.3 collective-permute-start
  5.7 1.5 %copy-start.1 = (bf16[1280,768]{1,0:T(8,128)(2,1)S(1)}, bf16[1280,768]{1,0:T(8,128)(2,1)}, u32[]{:S(2)}) copy-start(bf16[1280,768]{1,0:T(8,128)(2,1)} %x_ref.3) | copy-start | bytes 5898244
  11.5 15.9 %collective-permute-start.6 = (bf16[1040,512]{1,0:T(8,128)(2,1)S(1)}, bf16[1040,512]{1,0:T(8,128)(2,1)S(1)}, u32[]{:S(2)}, u32[]{:S(2)}) collective-permute-start(bf16[1040,512]{1,0:T(8,128)(2,1)S(1)} %key_sums.6), channel_id=1, source_target_pairs={{0,2},{1,5},{2,0},{3,7},{4,6},{5,1},{6,4},{7,3},{8,10},{9,13},{10,... | collective-permute-start | bytes 3194888 | tf_op jit(solution)/shard_map/ppermute | solution.py:45
  27.6 9.4 %collective-permute-start.7 = (bf16[528,512]{1,0:T(8,128)(2,1)S(1)}, bf16[528,512]{1,0:T(8,128)(2,1)S(1)}, u32[]{:S(2)}, u32[]{:S(2)}) collective-permute-start(bf16[528,512]{1,0:T(8,128)(2,1)S(1)} %get-tuple-element.26), channel_id=1, source_target_pairs={{0,4},{1,3},{2,6},{3,1},{4,0},{5,7},{6,2},{7,5},{8,12},{9,11},{10,... | collective-permute-start | bytes 1622024 | tf_op jit(solution)/shard_map/ppermute | solution.py:45
  37.8 7.6 %collective-permute-start.8 = (bf16[272,512]{1,0:T(8,128)(2,1)}, bf16[272,512]{1,0:T(8,128)(2,1)}, u32[]{:S(2)}, u32[]{:S(2)}) collective-permute-start(bf16[272,512]{1,0:T(8,128)(2,1)} %get-tuple-element.28), channel_id=1, source_target_pairs={{0,8},{1,9},{2,10},{3,11},{4,12},{5,13},{6,14},{7,15},{8,0},{9,1},... | collective-permute-start | bytes 835592 | tf_op jit(solution)/shard_map/ppermute | solution.py:45
  39.9 28.1 %copy-start.2 = (bf16[1280,768]{1,0:T(8,128)(2,1)S(1)}, bf16[1280,768]{1,0:T(8,128)(2,1)}, u32[]{:S(2)}) copy-start(bf16[1280,768]{1,0:T(8,128)(2,1)} %x_ref.3) | copy-start | bytes 5898244
  46.5 8.5 %collective-permute-start.9 = (bf16[272,512]{1,0:T(8,128)(2,1)S(1)}, bf16[272,512]{1,0:T(8,128)(2,1)S(1)}, u32[]{:S(2)}, u32[]{:S(2)}) collective-permute-start(bf16[272,512]{1,0:T(8,128)(2,1)S(1)} %get-tuple-element.30.sent_ref), channel_id=1, source_target_pairs={{0,24},{1,25},{2,26},{3,27},{4,28},{5,29},{6,30},{7,31},{8,16},{9,... | collective-permute-start | bytes 835592 | tf_op jit(solution)/shard_map/ppermute | solution.py:45
  55.3 11.0 %collective-permute-start.15 = (bf16[256,512]{1,0:T(8,128)(2,1)S(1)}, bf16[256,512]{1,0:T(8,128)(2,1)S(1)}, u32[]{:S(2)}, u32[]{:S(2)}) collective-permute-start(bf16[256,512]{1,0:T(8,128)(2,1)S(1)} %get-tuple-element.35.held_ref), channel_id=1, source_target_pairs={{0,8},{1,9},{2,10},{3,11},{4,12},{5,13},{6,14},{7,15},{8,0},{9,1},... | collective-permute-start | bytes 786440 | tf_op jit(solution)/shard_map/ppermute | solution.py:45
  66.3 9.2 %collective-permute-start.16 = (bf16[512,512]{1,0:T(8,128)(2,1)S(1)}, bf16[512,512]{1,0:T(8,128)(2,1)S(1)}, u32[]{:S(2)}, u32[]{:S(2)}) collective-permute-start(bf16[512,512]{1,0:T(8,128)(2,1)S(1)} %join.6.held_ref), channel_id=1, source_target_pairs={{0,4},{1,3},{2,6},{3,1},{4,0},{5,7},{6,2},{7,5},{8,12},{9,11},{10,... | collective-permute-start | bytes 1572872 | tf_op jit(solution)/shard_map/ppermute | solution.py:45
  70.6 12.0 %collective-permute-start.2 = (bf16[1024,256]{1,0:T(8,128)(2,1)S(1)}, bf16[1024,256]{1,0:T(8,128)(2,1)S(1)}, u32[]{:S(2)}, u32[]{:S(2)}) collective-permute-start(bf16[1024,256]{1,0:T(8,128)(2,1)S(1)} %key_sums.4), channel_id=1, source_target_pairs={{0,8},{1,9},{2,10},{3,11},{4,12},{5,13},{6,14},{7,15},{8,0},{9,1},... | collective-permute-start | bytes 1572872 | tf_op jit(solution)/shard_map/ppermute | solution.py:45
  76.6 32.2 %collective-permute-start.17 = (bf16[1024,512]{1,0:T(8,128)(2,1)}, bf16[1024,512]{1,0:T(8,128)(2,1)}, u32[]{:S(2)}, u32[]{:S(2)}) collective-permute-start(bf16[1024,512]{1,0:T(8,128)(2,1)} %join.7.rest_1_), channel_id=1, source_target_pairs={{0,2},{1,5},{2,0},{3,7},{4,6},{5,1},{6,4},{7,3},{8,10},{9,13},{10,... | collective-permute-start | bytes 3145736 | tf_op jit(solution)/shard_map/ppermute | solution.py:45
  82.8 38.7 %copy-start.4 = (s32[1280,1]{0,1:T(1,128)S(1)}, s32[1280,1]{0,1:T(1,128)}, u32[]{:S(2)}) copy-start(s32[1280,1]{0,1:T(1,128)} %param.6) | copy-start | bytes 15364
  82.8 12.0 %collective-permute-start.3 = (bf16[512,256]{1,0:T(8,128)(2,1)S(1)}, bf16[512,256]{1,0:T(8,128)(2,1)S(1)}, u32[]{:S(2)}, u32[]{:S(2)}) collective-permute-start(bf16[512,256]{1,0:T(8,128)(2,1)S(1)} %get-tuple-element.20), channel_id=1, source_target_pairs={{0,2},{1,5},{2,0},{3,7},{4,6},{5,1},{6,4},{7,3},{8,10},{9,13},{10,... | collective-permute-start | bytes 786440 | tf_op jit(solution)/shard_map/ppermute | solution.py:45
  94.8 5.0 %collective-permute-start.4 = (bf16[256,256]{1,0:T(8,128)(2,1)S(1)}, bf16[256,256]{1,0:T(8,128)(2,1)S(1)}, u32[]{:S(2)}, u32[]{:S(2)}) collective-permute-start(bf16[256,256]{1,0:T(8,128)(2,1)S(1)} %get-tuple-element.22), channel_id=1, source_target_pairs={{0,4},{1,3},{2,6},{3,1},{4,0},{5,7},{6,2},{7,5},{8,12},{9,11},{10,... | collective-permute-start | bytes 393224 | tf_op jit(solution)/shard_map/ppermute | solution.py:45
  99.9 6.9 %collective-permute-start.5 = (bf16[256,256]{1,0:T(8,128)(2,1)S(1)}, bf16[256,256]{1,0:T(8,128)(2,1)S(1)}, u32[]{:S(2)}, u32[]{:S(2)}) collective-permute-start(bf16[256,256]{1,0:T(8,128)(2,1)S(1)} %get-tuple-element.24.sent_ref), channel_id=1, source_target_pairs={{0,24},{1,25},{2,26},{3,27},{4,28},{5,29},{6,30},{7,31},{8,16},{9,... | collective-permute-start | bytes 393224 | tf_op jit(solution)/shard_map/ppermute | solution.py:45
  107.1 5.5 %collective-permute-start.10 = (bf16[272,256]{1,0:T(8,128)(2,1)S(1)}, bf16[272,256]{1,0:T(8,128)(2,1)S(1)}, u32[]{:S(2)}, u32[]{:S(2)}) collective-permute-start(bf16[272,256]{1,0:T(8,128)(2,1)S(1)} %get-tuple-element.34.held_ref), channel_id=1, source_target_pairs={{0,4},{1,3},{2,6},{3,1},{4,0},{5,7},{6,2},{7,5},{8,12},{9,11},{10,... | collective-permute-start | bytes 417800 | tf_op jit(solution)/shard_map/ppermute | solution.py:45
  108.7 22.2 %collective-permute-start.19 = (bf16[1024,512]{1,0:T(8,128)(2,1)}, bf16[1024,512]{1,0:T(8,128)(2,1)}, u32[]{:S(2)}, u32[]{:S(2)}) collective-permute-start(bf16[1024,512]{1,0:T(8,128)(2,1)} %join.7.rest_1_), channel_id=1, source_target_pairs={{0,1},{1,0},{2,3},{3,2},{4,5},{5,4},{6,7},{7,6},{8,9},{9,8},{10,11... | collective-permute-start | bytes 3145736 | tf_op jit(solution)/shard_map/ppermute | solution.py:45
  108.7 22.2 %collective-permute-start.18 = (bf16[1024,512]{1,0:T(8,128)(2,1)}, bf16[1024,512]{1,0:T(8,128)(2,1)}, u32[]{:S(2)}, u32[]{:S(2)}) collective-permute-start(bf16[1024,512]{1,0:T(8,128)(2,1)} %collective-permute-done.17.rest_0_), channel_id=1, source_target_pairs={{0,1},{1,0},{2,3},{3,2},{4,5},{5,4},{6,7},{7,6},{8,9},{9,8},{10,11... | collective-permute-start | bytes 3145736 | tf_op jit(solution)/shard_map/ppermute | solution.py:45
  112.7 6.5 %collective-permute-start.11 = (bf16[528,256]{1,0:T(8,128)(2,1)S(1)}, bf16[528,256]{1,0:T(8,128)(2,1)S(1)}, u32[]{:S(2)}, u32[]{:S(2)}) collective-permute-start(bf16[528,256]{1,0:T(8,128)(2,1)S(1)} %join.4.held_ref), channel_id=1, source_target_pairs={{0,2},{1,5},{2,0},{3,7},{4,6},{5,1},{6,4},{7,3},{8,10},{9,13},{10,... | collective-permute-start | bytes 811016 | tf_op jit(solution)/shard_map/ppermute | solution.py:45
  120.0 10.1 %collective-permute-start.12 = (bf16[1040,256]{1,0:T(8,128)(2,1)}, bf16[1040,256]{1,0:T(8,128)(2,1)}, u32[]{:S(2)}, u32[]{:S(2)}) collective-permute-start(bf16[1040,256]{1,0:T(8,128)(2,1)} %join.5.rest_1_), channel_id=1, source_target_pairs={{0,8},{1,9},{2,10},{3,11},{4,12},{5,13},{6,14},{7,15},{8,0},{9,1},... | collective-permute-start | bytes 1597448 | tf_op jit(solution)/shard_map/ppermute | solution.py:45
  122.9 8.1 %copy-start.3 = (bf16[1280,768]{1,0:T(8,128)(2,1)S(1)}, bf16[1280,768]{1,0:T(8,128)(2,1)}, u32[]{:S(2)}) copy-start(bf16[1280,768]{1,0:T(8,128)(2,1)} %x_ref.3) | copy-start | bytes 5898244
  124.2 17.5 %collective-permute-start.14 = (bf16[1040,256]{1,0:T(8,128)(2,1)}, bf16[1040,256]{1,0:T(8,128)(2,1)S(1)}, u32[]{:S(2)}, u32[]{:S(2)}) collective-permute-start(bf16[1040,256]{1,0:T(8,128)(2,1)} %join.5.rest_1_), channel_id=1, source_target_pairs={{0,1},{1,0},{2,3},{3,2},{4,5},{5,4},{6,7},{7,6},{8,9},{9,8},{10,11... | collective-permute-start | bytes 1597448 | tf_op jit(solution)/shard_map/ppermute | solution.py:45
  130.2 11.5 %collective-permute-start.13 = (bf16[1040,256]{1,0:T(8,128)(2,1)}, bf16[1040,256]{1,0:T(8,128)(2,1)S(1)}, u32[]{:S(2)}, u32[]{:S(2)}) collective-permute-start(bf16[1040,256]{1,0:T(8,128)(2,1)} %collective-permute-done.12.rest_0_), channel_id=1, source_target_pairs={{0,1},{1,0},{2,3},{3,2},{4,5},{5,4},{6,7},{7,6},{8,9},{9,8},{10,11... | collective-permute-start | bytes 1597448 | tf_op jit(solution)/shard_map/ppermute | solution.py:45

commit v3 on v2

--- a/solution.py
+++ b/solution.py
@@ -75,6 +75,18 @@
     return group_rel, member_rel
 
 
+def token_shape():
+    return jax.ShapeDtypeStruct((8, 128), F32)
+
+
+def hand_on(kernel, inputs):
+    def run(*refs):
+        kernel(*refs[:inputs], *refs[inputs + 1 : -1])
+        refs[-1][...] = refs[inputs][...]
+
+    return run
+
+
 def sums_kernel(base, pos_ref, own_ref, other_ref, *rest):
     out_ref = rest[-1]
     rows = own_ref.shape[0]
@@ -89,41 +101,43 @@
         out_ref[keys:, :] = rest[0][...]
 
 
-def key_sums(pos_row, own, other, count_tile, base, keys, start, wide):
+def key_sums(token, pos_row, own, other, count_tile, base, keys, start, wide):
     rows = own.shape[0]
     extra = [] if count_tile is None else [count_tile]
     out_rows = keys + sum(e.shape[0] for e in extra)
+    whole = lambda shape: pl.BlockSpec(shape, lambda i: (0, 0))
     return pl.pallas_call(
-        functools.partial(sums_kernel, base),
+        hand_on(functools.partial(sums_kernel, base), 3 + len(extra)),
         grid=(1,),
-        out_shape=jax.ShapeDtypeStruct((out_rows, wide), BF16),
+        out_shape=[jax.ShapeDtypeStruct((out_rows, wide), BF16), token_shape()],
         in_specs=[
-            pl.BlockSpec((1, 2 * rows), lambda i: (0, 0)),
+            whole((1, 2 * rows)),
             pl.BlockSpec((rows, wide), lambda i: (0, start // wide)),
             pl.BlockSpec((rows, wide), lambda i: (0, start // wide)),
         ]
-        + [pl.BlockSpec(e.shape, lambda i: (0, 0)) for e in extra],
-        out_specs=pl.BlockSpec((out_rows, wide), lambda i: (0, 0)),
+        + [whole(e.shape) for e in extra]
+        + [whole(token.shape)],
+        out_specs=[whole((out_rows, wide)), whole(token.shape)],
         compiler_params=pltpu.CompilerParams(vmem_limit_bytes=24 << 20),
         cost_estimate=pl.CostEstimate(
             flops=2 * keys * 2 * rows * wide, bytes_accessed=(4 * rows + 2 * keys) * wide, transcendentals=0
         ),
         name="key_sums",
-    )(pos_row, own, other, *extra)
-
-
-def small_call(kernel, name, outs, *args):
+    )(pos_row, own, other, *extra, token)
+
+
+def small_call(kernel, name, outs, token, *args):
     whole = pl.BlockSpec(memory_space=pltpu.VMEM)
     moved = sum(a.size * a.dtype.itemsize for a in (*args, *outs))
     return pl.pallas_call(
-        kernel,
-        out_shape=outs,
-        in_specs=[whole] * len(args),
-        out_specs=[whole] * len(outs),
+        hand_on(kernel, len(args)),
+        out_shape=[*outs, token_shape()],
+        in_specs=[whole] * (len(args) + 1),
+        out_specs=[whole] * (len(outs) + 1),
         compiler_params=pltpu.CompilerParams(vmem_limit_bytes=12 << 20),
         cost_estimate=pl.CostEstimate(flops=moved // 2, bytes_accessed=moved, transcendentals=0),
         name=name,
-    )(*args)
+    )(*args, token)
 
 
 def add_pair(got_ref, keep_ref, start, stop):
@@ -221,95 +235,148 @@
         out_ref[2 * body :, :] = (held_ref[body:, :].astype(F32) + moved).astype(BF16)
 
 
-def scores_kernel(groups, share, last, where_ref, x_ref, gid_ref, *rest):
-    pieces = 4
-    piece_refs, rest = rest[:pieces], rest[pieces:]
-    if last:
-        total_ref, half_ref, out_ref, cents, masked, half = rest
-    else:
-        out_ref, cents, masked = rest
-    wide = x_ref.shape[1]
-    keys = cents.shape[0]
-    members = keys // share
-    blocks = where_ref.shape[0] // pieces
-    lanes = 128
+def mask_kernel(groups, columns, gid_ref, x_ref, *outs):
+    gid = gid_ref[...]
+    for (start, wide), out in zip(columns, outs):
+        x = x_ref[:, start : start + wide]
+        for group in range(groups):
+            out[:, group * wide : (group + 1) * wide] = jnp.where(gid == group, x, jnp.zeros_like(x))
+    pick = outs[-1]
+    lane = lax.broadcasted_iota(jnp.int32, pick.shape, 1)
+    hit = (lane % groups == gid) & (lane < PARTS * groups)
+    pick[...] = jnp.where(hit, -1.0, 0.0).astype(BF16)
+
+
+def product(a, b):
+    return lax.dot_general(a, b, (((1,), (1,)), ((), ())), preferred_element_type=F32)
+
+
+def part_kernel(groups, share, group_ref, masked_ref, own_ref, other_ref, *rest):
+    out_ref, cents = rest[-2:]
+    wide = own_ref.shape[1]
+    blocks = own_ref.shape[0] // share
 
     @pl.when(pl.program_id(0) == 0)
     def _():
-        if last and share < lanes:
-            half[...] = half_ref[...]
-        for piece in range(pieces):
-            ref = piece_refs[piece]
+        for piece, ref in enumerate((own_ref, other_ref)):
             for block in range(blocks):
-                code = where_ref[piece * blocks + block]
+                group = group_ref[piece * blocks + block]
+                slot = (piece * blocks + block) // groups
+                cents[
+                    slot * share : (slot + 1) * share, pl.ds(pl.multiple_of(group * wide, 128), wide)
+                ] = ref[block * share : (block + 1) * share, :]
+
+    step = out_ref.shape[1]
+    start = pl.multiple_of(pl.program_id(0) * step, step)
+    out_ref[...] = product(masked_ref[...], cents[pl.ds(start, step), :])
+
+
+def part_scores(token, masked, group_of, pieces, before, groups, keys, share):
+    rows = masked.shape[0]
+    wide = pieces[0].shape[1]
+    half = pieces[0].shape[0] * len(pieces) // groups
+    step = min(256, half)
+    steps = half // step
+    at = 0 if before is None else steps
+    whole = pl.BlockSpec(memory_space=pltpu.VMEM)
+    extra = [] if before is None else [before]
+
+    def kernel(group_ref, *refs):
+        count = 3 + len(extra)
+        part_kernel(groups, share, group_ref, *refs[:3], refs[count + 1], refs[-1])
+        refs[count + 2][...] = refs[count][...]
+
+    return pl.pallas_call(
+        kernel,
+        grid_spec=pltpu.PrefetchScalarGridSpec(
+            num_scalar_prefetch=1,
+            grid=(steps,),
+            in_specs=[whole] * 3 + [pl.BlockSpec(memory_space=pl.ANY)] * len(extra) + [whole],
+            out_specs=[pl.BlockSpec((rows, step), lambda i, w: (0, i + at)), whole],
+            scratch_shapes=[pltpu.VMEM((half, groups * wide), BF16)],
+        ),
+        out_shape=[jax.ShapeDtypeStruct((rows, keys), F32), token_shape()],
+        input_output_aliases={} if before is None else {4: 0},
+        compiler_params=pltpu.CompilerParams(vmem_limit_bytes=16 << 20),
+        cost_estimate=pl.CostEstimate(
+            flops=2 * rows * half * groups * wide,
+            bytes_accessed=2 * (rows + half) * groups * wide + 4 * rows * half,
+            transcendentals=0,
+        ),
+        name="part_scores",
+    )(group_of, masked, *pieces, *extra, token)
+
+
+def final_kernel(groups, share, code_ref, slot_ref, masked_ref, pick_ref, half_ref, *rest):
+    pieces = 4
+    piece_refs, total_refs = rest[:pieces], rest[pieces : pieces + 2]
+    out_ref, cents, half = rest[-3:]
+    keys = cents.shape[0]
+    wide = cents.shape[1] // groups
+    members = keys // share
+    blocks = code_ref.shape[0] // pieces
+    lanes = 128
+
+    @pl.when(pl.program_id(0) == 0)
+    def _():
+        half[...] = half_ref[...]
+        for piece, ref in enumerate(piece_refs):
+            for block in range(blocks):
+                code = code_ref[piece * blocks + block]
                 group = code // members
-                member = code % members
-                cents[
-                    pl.ds(pl.multiple_of(member * share, share), share),
-                    pl.ds(pl.multiple_of(group * wide, lanes), wide),
-                ] = ref[block * share : (block + 1) * share, :]
-            if last and share >= lanes:
-                tail = ref[blocks * share :, :].astype(F32)
-                for block in range(blocks):
-                    code = where_ref[piece * blocks + block]
+                row_at = pl.multiple_of((code % members) * share, share)
+                cents[pl.ds(row_at, share), pl.ds(pl.multiple_of(group * wide, lanes), wide)] = ref[
+                    block * share : (block + 1) * share, :
+                ]
+                if share >= lanes:
+                    tail = ref[blocks * share :, :].astype(F32)
                     at = tail.shape[0] - blocks + block
-                    row = sum(tail[at : at + 1, p * share : (p + 1) * share] for p in range(PARTS))
-                    for cut in range(share // lanes):
-                        half[pl.ds(code * (share // lanes) + cut, 1), :] = row[:, cut * lanes : (cut + 1) * lanes]
-        for group in range(groups):
-            masked[:, group * wide : (group + 1) * wide] = jnp.where(
-                gid_ref[...] == group, x_ref[...], jnp.zeros_like(x_ref)
-            )
+                    lines = pl.ds(pl.multiple_of(row_at, lanes), share)
+                    line = lax.broadcasted_iota(jnp.int32, (half.shape[0], share), 0)
+                    filled = half[:, lines]
+                    for term in range(PARTS):
+                        row = tail[at : at + 1, term * share : (term + 1) * share]
+                        filled = jnp.where(line == group + term * groups, row, filled)
+                    half[:, lines] = filled
 
     step = out_ref.shape[1]
-    at = pl.program_id(0)
-    start = pl.multiple_of(at * step, step)
-    dots = lax.dot_general(
-        masked[...], cents[pl.ds(start, step), :], (((1,), (1,)), ((), ())), preferred_element_type=F32
-    )
-    if not last:
-        out_ref[...] = dots
-        return
-    gid = gid_ref[...]
-    for cut in range(step // lanes):
-        columns = slice(cut * lanes, (cut + 1) * lanes)
-        offset = jnp.zeros((out_ref.shape[0], lanes), F32)
-        for group in range(groups):
-            row = half[pl.ds(group * (keys // lanes) + at * (step // lanes) + cut, 1), :]
-            offset = jnp.where(gid == group, row, offset)
-        out_ref[:, columns] = (dots[:, columns] + total_ref[:, columns] - offset).astype(BF16)
-
-
-def add_scores(samples, gid, pieces, where, total, half, groups, keys, share, start, wide):
-    rows = samples.shape[0]
+    start = pl.multiple_of(pl.program_id(0) * step, step)
+    dots = product(masked_ref[...], cents[pl.ds(start, step), :])
+    offsets = half[:, pl.ds(start, step)].astype(BF16)
+    dots += jnp.dot(pick_ref[...], offsets, preferred_element_type=F32)
+    cut = step // 2
+    out_ref[:, :cut] = (dots[:, :cut] + total_refs[0][...]).astype(BF16)
+    out_ref[:, cut:] = (dots[:, cut:] + total_refs[1][...]).astype(BF16)
+
+
+def final_scores(masked, pick, codes, slots, pieces, total, half, groups, keys, share):
+    rows = masked.shape[0]
+    wide = pieces[0].shape[1]
     step = min(256, keys)
-    last = total is not None
+    cut = step // 2
     whole = pl.BlockSpec(memory_space=pltpu.VMEM)
     return pl.pallas_call(
-        functools.partial(scores_kernel, groups, share, last),
+        functools.partial(final_kernel, groups, share),
         grid_spec=pltpu.PrefetchScalarGridSpec(
-            num_scalar_prefetch=1,
+            num_scalar_prefetch=2,
             grid=(keys // step,),
-            in_specs=[
-                pl.BlockSpec((rows, wide), lambda i, w: (0, start // wide)),
-                pl.BlockSpec((rows, 1), lambda i, w: (0, 0)),
-            ]
-            + [whole] * len(pieces)
-            + [pl.BlockSpec((rows, step), lambda i, w: (0, i)), whole] * last,
-            out_specs=pl.BlockSpec((rows, step), lambda i, w: (0, i)),
-            scratch_shapes=[
-                pltpu.VMEM((keys, groups * wide), BF16),
-                pltpu.VMEM((rows, groups * wide), BF16),
-            ]
-            + [pltpu.VMEM((groups * keys // 128, 128), F32)] * last,
+            in_specs=[whole] * (3 + len(pieces))
+            + [
+                pl.BlockSpec((rows, cut), lambda i, c, s: (0, s[2 * i])),
+                pl.BlockSpec((rows, cut), lambda i, c, s: (0, s[2 * i + 1])),
+            ],
+            out_specs=pl.BlockSpec((rows, step), lambda i, c, s: (0, i)),
+            scratch_shapes=[pltpu.VMEM((keys, groups * wide), BF16), pltpu.VMEM(half.shape, F32)],
         ),
-        out_shape=jax.ShapeDtypeStruct((rows, keys), BF16 if last else F32),
-        compiler_params=pltpu.CompilerParams(vmem_limit_bytes=26 << 20),
+        out_shape=jax.ShapeDtypeStruct((rows, keys), BF16),
+        compiler_params=pltpu.CompilerParams(vmem_limit_bytes=16 << 20),
         cost_estimate=pl.CostEstimate(
-            flops=2 * rows * keys * groups * wide, bytes_accessed=2 * (rows + groups * keys) * wide, transcendentals=0
+            flops=2 * rows * keys * groups * wide,
+            bytes_accessed=2 * (rows + keys) * groups * wide + 6 * rows * keys,
+            transcendentals=0,
         ),
-        name="scores",
-    )(where, samples, gid, *pieces, *([total, half] if last else []))
+        name="final_scores",
+    )(codes, slots, masked, pick, half, *pieces, total, total)
 
 
 def per_device(samples, coarse_label, fine_label, live_rows, old_centroids):
@@ -355,12 +422,13 @@
         return partner
 
     tail = pad_rows(blocks)
-    sends, keeps = [], []
+    token = jnp.zeros((8, 128), F32)
+    rows_of, tiles = [], []
     for stream, (start, wide) in enumerate(columns):
         place = of_core(
             lambda c: block_position(group_of ^ z, owner ^ me, turned[c, stream], outer_bits)
         )
-        pos = jnp.where(mine, place * share + fine % share, -1)
+        rows_of.append(jnp.where(mine, place * share + fine % share, -1)[None, :])
         tile = None
         if stream == 0:
             in_block = (jnp.where(mine, place, -1)[:, None] == jnp.arange(tail)[None, :]).astype(BF16)
@@ -371,11 +439,26 @@
             tile = [(counted // base**digit) % base for digit in range(digits)]
             tile = jnp.concatenate(tile, axis=1).astype(BF16)
             tile = jnp.pad(tile, ((0, 0), (0, wide - digits * share)))
-        make = functools.partial(
-            key_sums, pos[None, :], samples, other_samples, tile, keys=half_keys // 2, start=start, wide=wide
-        )
-        sends.append(make(base=0))
-        keeps.append(make(base=half_keys // 2))
+        tiles.append(tile)
+
+    half_keys //= 2
+    send, keep = [None] * 2, [None] * 2
+    for part, found in enumerate((send, keep)):
+        for stream, (start, wide) in enumerate(columns):
+            found[stream], token = key_sums(
+                token, rows_of[stream], samples, other_samples, tiles[stream], part * half_keys, half_keys, start, wide
+            )
+
+    gid = jnp.where(live, coarse_label[:, 0], -1)[:, None]
+    *masked, pick, token = small_call(
+        functools.partial(mask_kernel, groups, columns),
+        "mask",
+        [jax.ShapeDtypeStruct((rows, groups * wide), BF16) for _, wide in columns]
+        + [jax.ShapeDtypeStruct((rows, TILE), BF16)],
+        token,
+        gid,
+        samples,
+    )
 
     old_share = lax.dynamic_slice(old_centroids[0], (me * share, 0), (share, width))
 
@@ -384,24 +467,26 @@
         return jax.ShapeDtypeStruct((rows_out, columns[stream][1]), BF16)
 
     share_f32 = [jax.ShapeDtypeStruct((share, wide), F32) for _, wide in columns]
-    send, keep, held, fresh, near = list(sends), list(keeps), [None] * 2, [None] * 2, [None] * 2
+    held, fresh, near = [None] * 2, [None] * 2, [None] * 2
     count = blocks // 2
     for stage in range(stages - 1):
         for stream, (start, wide) in enumerate(columns):
             got = exchange(send[stream], pairing(stage, stream), groups, members)
             if stage < stages - 2:
-                send[stream], keep[stream] = small_call(
+                send[stream], keep[stream], token = small_call(
                     functools.partial(fold_kernel, count // 2 * share, count),
                     "fold",
                     [bf(count // 2, stream, 0)] * 2,
+                    token,
                     got,
                     keep[stream],
                 )
             else:
-                send[stream], near[stream] = small_call(
+                send[stream], near[stream], token = small_call(
                     functools.partial(seed_kernel, share, count),
                     "seed",
                     [bf(2, stream, 0), share_f32[stream]],
+                    token,
                     got,
                     keep[stream],
                     old_share[:, start : start + wide],
@@ -411,19 +496,21 @@
     for stream in streams:
         got = exchange(send[stream], pairing(stages - 1, stream), groups, members)
         if stream == 0:
-            fresh[0], held[0], scale, norm = small_call(
+            fresh[0], held[0], scale, norm, token = small_call(
                 functools.partial(first_kernel, share, base, digits),
                 "first_centroids",
                 [share_f32[0], bf(2, 0, 1), column, column],
+                token,
                 got,
                 send[0],
                 near[0],
             )
         else:
-            fresh[1], held[1] = small_call(
+            fresh[1], held[1], token = small_call(
                 functools.partial(last_kernel, share, tail),
                 "last_centroids",
                 [share_f32[1], bf(2, 1, 1)],
+                token,
                 got,
                 send[1],
                 near[1],
@@ -431,52 +518,70 @@
                 norm,
             )
     count = 2
-    pieces = [[], []]
+    arrived = [None] * 2
     for stage in reversed(range(stages - 1)):
         for stream in streams:
             got = exchange(held[stream], pairing(stage, stream), groups, members)
             if stage:
-                held[stream] = small_call(
+                held[stream], token = small_call(
                     functools.partial(join_kernel, count * share, count),
                     "join",
                     [bf(2 * count, stream, 1)],
+                    token,
                     got,
                     held[stream],
-                )[0]
+                )
             else:
-                pieces[stream] = [got, held[stream]]
+                arrived[stream] = got
         count *= 2
 
     half_blocks = blocks // 2
-    where = []
-    for stream in streams:
-        pieces[stream] += [sibling(piece) for piece in pieces[stream]]
+
+    def codes_of(stream, part, flip):
         codes = []
-        for which in range(len(pieces[stream])):
-            part = which % 2
-            flip = which // 2
-            for block in range(half_blocks):
-                rel = [relative_of(part * half_blocks + block, turned[c, stream]) for c in range(2)]
-                holder = core ^ flip
-                group_rel = jnp.where(holder == 0, rel[0][0], rel[1][0])
-                member_rel = jnp.where(holder == 0, rel[0][1], rel[1][1])
-                codes.append((z ^ group_rel) * members + (me ^ flip ^ member_rel))
-        where.append(jnp.stack(codes).astype(jnp.int32))
-    half = jnp.zeros((groups * keys // 128, 128), F32)
+        for block in range(half_blocks):
+            rel = [relative_of(part * half_blocks + block, turned[c, stream]) for c in range(2)]
+            holder = core ^ flip
+            group_rel = jnp.where(holder == 0, rel[0][0], rel[1][0])
+            member_rel = jnp.where(holder == 0, rel[0][1], rel[1][1])
+            codes.append((z ^ group_rel) * members + (me ^ flip ^ member_rel))
+        return jnp.stack(codes).astype(jnp.int32)
+
+    total = None
+    for part, piece in ((1, held[0]), (0, arrived[0])):
+        group_codes = jnp.concatenate([codes_of(0, part, flip) for flip in range(2)]) // members
+        total, token = part_scores(
+            token, masked[0], group_codes, [piece, sibling(piece)], total, groups, keys, share
+        )
+
+    every = jnp.arange(members, dtype=jnp.int32)
+    flip_of = (every ^ me) & 1
+    spot = jnp.where(
+        (core ^ flip_of) == 0,
+        *(block_position(jnp.zeros_like(every), every ^ me, turned[c, 0], outer_bits) // groups for c in range(2)),
+    )
+    quarter = half_blocks // groups
+    slots = jnp.where(spot >= quarter, spot - quarter, spot + 2 * quarter) + flip_of * quarter
+    flat = [piece for got in (arrived[1], held[1]) for piece in (got, sibling(got))]
+    codes = jnp.concatenate([codes_of(1, part, flip) for part in range(2) for flip in range(2)])
+    half = jnp.zeros((TILE, keys), F32)
     if share < 128:
         norm_rows = []
-        for piece in pieces[1]:
-            rows_of = piece[half_blocks * share + tail - half_blocks :].astype(F32)
-            norm_rows.append(sum(rows_of[:, p * share : (p + 1) * share] for p in range(PARTS)))
-        pick = (where[1][None, :] == jnp.arange(groups * members, dtype=jnp.int32)[:, None]).astype(F32)
-        half = jnp.dot(pick, jnp.concatenate(norm_rows), precision=lax.Precision.HIGHEST).reshape(half.shape)
-
-    gid = jnp.where(live, coarse_label[:, 0], -1)[:, None]
-    scores = None
-    for stream, (start, wide) in enumerate(columns):
-        scores = add_scores(
-            samples, gid, pieces[stream], where[stream], scores, half, groups, keys, share, start, wide
-        )
+        for piece in flat:
+            norm_rows.append(piece[half_blocks * share + tail - half_blocks :].astype(F32))
+        norm_rows = jnp.concatenate(norm_rows)
+        spread = (codes[None, :] == jnp.arange(groups * members, dtype=jnp.int32)[:, None]).astype(F32)
+        for term in range(PARTS):
+            found = jnp.dot(
+                spread, norm_rows[:, term * share : (term + 1) * share], precision=lax.Precision.HIGHEST
+            )
+            half = half.at[term * groups : (term + 1) * groups].set(found.reshape(groups, keys))
+        lane = jnp.arange(keys, dtype=jnp.int32)
+        source = jnp.repeat(slots, share) * share + lane % share
+        move = (lane[:, None] == source[None, :]).astype(F32)
+        total = jnp.dot(total, move, precision=lax.Precision.HIGHEST)
+        slots = jnp.arange(keys // 128, dtype=jnp.int32)
+    scores = final_scores(masked[1], pick, codes, slots, flat, total, half, groups, keys, share)
     return scores, jnp.concatenate(fresh, axis=1)[None]
 
 

time: 151 us -> 155 us (1.026)
  local copies, waits for them, and re-layouts: 2.97 us -> 14 us
  starting transfers between devices: 31.7 us -> 23.7 us
  waiting for transfers between devices: 71.5 us -> 67.5 us
  Pallas kernels: 38.1 us -> 41.2 us
  other arithmetic: 3.88 us -> 5.79 us
    unnamed x12 -> x30, local copies, waits for them, and re-layouts: 2.67 us -> 13.6 us
    ppermute x20, starting transfers between devices: 31.7 us -> 23.7 us  [exchange(): return lax.ppermute(array, AXES, pairs)]
    ppermute x20, waiting for transfers between devices: 71.5 us -> 67.5 us  [exchange(): return lax.ppermute(array, AXES, pairs)]
    pallas_call x18 -> x20, Pallas kernels: 38.1 us -> 41.2 us  [the longest x4 14 us: key_sums(): pl.pallas_call(hand_on(functools.partial(sums_kernel, base), 3 + len(extr...]
  transfers between devices with their start and end apart: 20 -> 20, of which waited for: 14 -> 9; matrix products, arithmetic and copies ran while one was open for 4% -> 4% of each run, Pallas kernels for 15% -> 17%
where the time goes in v3:
time: 155 us; the launch traced here: 154 us
  waiting for transfers between devices  67.5 us (44%)
  Pallas kernels  41.2 us (27%)
  starting transfers between devices  23.7 us (15%)
  local copies, waits for them, and re-layouts  14 us (9%)
  other arithmetic  5.79 us (4%)
  between operations  1.74 us (1%)
    ppermute x20, waiting for transfers between devices, exchange(): return lax.ppermute(array, AXES, pairs)  67.5 us
    ppermute x20, starting transfers between devices, exchange(): return lax.ppermute(array, AXES, pairs)  23.7 us
    pallas_call x4, Pallas kernels, key_sums(): pl.pallas_call(hand_on(functools.partial(sums_kernel, base), 3 + len(extr...  14 us
    unnamed x30, local copies, waits for them, and re-layouts  13.6 us
    pallas_call x2, Pallas kernels, part_scores(): pl.pallas_call(kernel, grid_spec=pltpu.PrefetchScalarGridSpec(num_scalar_...  12 us
    pallas_call x13, Pallas kernels, small_call(): pl.pallas_call(hand_on(kernel, len(args)), out_shape=[*outs, token_shape(...  8.46 us
    pallas_call x1, Pallas kernels, final_scores(): pl.pallas_call(functools.partial(final_kernel, groups, share), grid_spec=...  6.69 us
  transfers between devices with their start and end apart: 20, of which 9 were waited for; matrix products, arithmetic and copies ran while one was open for 4% of the time, Pallas kernels for 17%

profile of v3, /device:TPU:0, one launch (start us, length us, event | category | flops | bytes accessed | tf_op | source)
XLA Modules:
  0.0 154.4 jit_solution(5859221267073898350)
XLA Ops:
  1.4 0.9 multiply_reduce_fusion
  2.3 0.7 add_select_fusion.9
  3.5 1.8 %copy.9 = s32[1280,1]{1,0:T(8,128)} copy(s32[1280,1]{0,1:T(1,128)} %param.6) | data formatting | bytes 10240 | tf_op args[1]
  5.3 2.0 %fusion.3.refs_0_ = s32[1280,1]{1,0:T(8,128)} fusion(s32[1280,1]{1,0:T(8,128)} %copy.9, s32[]{:T(128)} %bitcast.37), kind=kLoop, calls=%fused_computation.5 | loop fusion | flops 2560 | bytes 10244 | tf_op jit(solution)/shard_map/jit(_where)/select_n | solution.py:452
  8.2 1.5 copy-done.6
  9.8 4.4 %key_sums.4 = (bf16[1040,512]{1,0:T(8,128)(2,1)S(1)}, f32[8,128]{1,0:T(8,128)S(1)}) custom-call(s32[1,2560]{1,0:T(1,128)S(1)} %get-tuple-element.100.refs_0_, bf16[1280,768]{1,0:T(8,128)(2,1)S(1)} %copy-done.6, bf16[1280,768]{1,0:T(8,128)(2,1)} %collective-permute-done.1.refs_2_, bf16[16,512]{1,0:T(8,128)(2,1)S(1)} %fusion.9.refs_3_, ...), custom_call_target="tpu_custom_call" | custom-call | flops 2684354560 | bytes 3670016 | tf_op jit(solution)/shard_map/key_sums/pallas_call | solution.py:109
  14.2 3.0 %collective-permute-start.3 = (bf16[1040,512]{1,0:T(8,128)(2,1)S(1)}, bf16[1040,512]{1,0:T(8,128)(2,1)S(1)}, u32[]{:S(2)}, u32[]{:S(2)}) collective-permute-start(bf16[1040,512]{1,0:T(8,128)(2,1)S(1)} %get-tuple-element.59), channel_id=1, source_target_pairs={{0,2},{1,5},{2,0},{3,7},{4,6},{5,1},{6,4},{7,3},{8,10},{9,13},{10,... | collective-permute-start | bytes 3194888 | tf_op jit(solution)/shard_map/ppermute | solution.py:45
  17.3 2.6 %key_sums.5 = (bf16[1024,256]{1,0:T(8,128)(2,1)S(1)}, f32[8,128]{1,0:T(8,128)S(1)}) custom-call(s32[1,2560]{1,0:T(1,128)S(1)} %fusion.16.refs_0_, bf16[1280,768]{1,0:T(8,128)(2,1)S(1)} %copy-done.7, bf16[1280,768]{1,0:T(8,128)(2,1)} %collective-permute-done.1.refs_2_, f32[8,128]{1,0:T(8,128)S(1)} %get-tuple-element.51.refs_3_), custom_call_target="tpu_custom_call" | custom-call | flops 1342177280 | bytes 1835008 | tf_op jit(solution)/shard_map/key_sums/pallas_call | solution.py:109
  19.9 4.3 %key_sums.6 = (bf16[1040,512]{1,0:T(8,128)(2,1)S(1)}, f32[8,128]{1,0:T(8,128)S(1)}) custom-call(s32[1,2560]{1,0:T(1,128)S(1)} %get-tuple-element.100.refs_0_, bf16[1280,768]{1,0:T(8,128)(2,1)S(1)} %copy-done.7, bf16[1280,768]{1,0:T(8,128)(2,1)} %collective-permute-done.1.refs_2_, bf16[16,512]{1,0:T(8,128)(2,1)S(1)} %fusion.9.refs_3_, ...), custom_call_target="tpu_custom_call" | custom-call | flops 2684354560 | bytes 3670016 | tf_op jit(solution)/shard_map/key_sums/pallas_call | solution.py:109
  24.2 2.7 %key_sums.7 = (bf16[1024,256]{1,0:T(8,128)(2,1)S(1)}, f32[8,128]{1,0:T(8,128)S(1)}) custom-call(s32[1,2560]{1,0:T(1,128)S(1)} %fusion.16.refs_0_, bf16[1280,768]{1,0:T(8,128)(2,1)S(1)} %copy-done.7, bf16[1280,768]{1,0:T(8,128)(2,1)} %collective-permute-done.1.refs_2_, f32[8,128]{1,0:T(8,128)S(1)} %get-tuple-element.53.refs_3_), custom_call_target="tpu_custom_call" | custom-call | flops 1342177280 | bytes 1835008 | tf_op jit(solution)/shard_map/key_sums/pallas_call | solution.py:109
  26.9 1.1 mask.1
  28.1 2.3 %copy-done.1 = bf16[1280,2048]{1,0:T(8,128)(2,1)} copy-done((bf16[1280,2048]{1,0:T(8,128)(2,1)}, bf16[1280,2048]{1,0:T(8,128)(2,1)S(1)}, u32[]{:S(2)}) %copy-start.1) | copy-done | bytes 5242904
  30.4 1.5 copy-done.3
  32.1 1.6 %collective-permute-start.5 = (bf16[528,512]{1,0:T(8,128)(2,1)S(1)}, bf16[528,512]{1,0:T(8,128)(2,1)S(1)}, u32[]{:S(2)}, u32[]{:S(2)}) collective-permute-start(bf16[528,512]{1,0:T(8,128)(2,1)S(1)} %get-tuple-element.65), channel_id=1, source_target_pairs={{0,4},{1,3},{2,6},{3,1},{4,0},{5,7},{6,2},{7,5},{8,12},{9,11},{10,... | collective-permute-start | bytes 1622024 | tf_op jit(solution)/shard_map/ppermute | solution.py:45
  33.7 1.6 %collective-permute-start.2 = (bf16[1024,256]{1,0:T(8,128)(2,1)S(1)}, bf16[1024,256]{1,0:T(8,128)(2,1)S(1)}, u32[]{:S(2)}, u32[]{:S(2)}) collective-permute-start(bf16[1024,256]{1,0:T(8,128)(2,1)S(1)} %get-tuple-element.57), channel_id=1, source_target_pairs={{0,8},{1,9},{2,10},{3,11},{4,12},{5,13},{6,14},{7,15},{8,0},{9,1},... | collective-permute-start | bytes 1572872 | tf_op jit(solution)/shard_map/ppermute | solution.py:45
  35.3 11.7 %collective-permute-done.2.refs_0_ = bf16[1024,256]{1,0:T(8,128)(2,1)S(1)} collective-permute-done((bf16[1024,256]{1,0:T(8,128)(2,1)S(1)}, bf16[1024,256]{1,0:T(8,128)(2,1)S(1)}, u32[]{:S(2)}, u32[]{:S(2)}) %collective-permute-start.2) | collective-permute-done | bytes 524320 | tf_op jit(solution)/shard_map/ppermute | solution.py:45
  47.0 0.8 fold.5
  47.8 0.7 copy-done.11
  48.5 0.8 fold.6
  49.2 0.7 copy-done.8
  49.9 1.6 %collective-permute-start.7 = (bf16[272,512]{1,0:T(8,128)(2,1)}, bf16[272,512]{1,0:T(8,128)(2,1)}, u32[]{:S(2)}, u32[]{:S(2)}) collective-permute-start(bf16[272,512]{1,0:T(8,128)(2,1)} %get-tuple-element.71), channel_id=1, source_target_pairs={{0,8},{1,9},{2,10},{3,11},{4,12},{5,13},{6,14},{7,15},{8,0},{9,1},... | collective-permute-start | bytes 835592 | tf_op jit(solution)/shard_map/ppermute | solution.py:45
  52.1 6.1 %collective-permute-done.4.refs_0_ = bf16[512,256]{1,0:T(8,128)(2,1)} collective-permute-done((bf16[512,256]{1,0:T(8,128)(2,1)}, bf16[512,256]{1,0:T(8,128)(2,1)}, u32[]{:S(2)}, u32[]{:S(2)}) %collective-permute-start.4) | collective-permute-done | bytes 262176 | tf_op jit(solution)/shard_map/ppermute | solution.py:45
  58.2 0.9 copy-done.12
  59.2 1.0 fold.7
  60.2 0.9 copy-done.9
  61.1 1.0 seed.2
  62.2 2.5 %collective-permute-start.9 = (bf16[272,512]{1,0:T(8,128)(2,1)S(1)}, bf16[272,512]{1,0:T(8,128)(2,1)S(1)}, u32[]{:S(2)}, u32[]{:S(2)}) collective-permute-start(bf16[272,512]{1,0:T(8,128)(2,1)S(1)} %get-tuple-element.77.refs_1_), channel_id=1, source_target_pairs={{0,24},{1,25},{2,26},{3,27},{4,28},{5,29},{6,30},{7,31},{8,16},{9,... | collective-permute-start | bytes 835592 | tf_op jit(solution)/shard_map/ppermute | solution.py:45
  65.3 4.4 %collective-permute-done.6.refs_0_ = bf16[256,256]{1,0:T(8,128)(2,1)S(1)} collective-permute-done((bf16[256,256]{1,0:T(8,128)(2,1)S(1)}, bf16[256,256]{1,0:T(8,128)(2,1)S(1)}, u32[]{:S(2)}, u32[]{:S(2)}) %collective-permute-start.6) | collective-permute-done | bytes 131104 | tf_op jit(solution)/shard_map/ppermute | solution.py:45
  69.8 1.0 collective-permute-done.9.refs_0_
  71.0 4.9 %collective-permute-start.11 = (bf16[256,512]{1,0:T(8,128)(2,1)S(1)}, bf16[256,512]{1,0:T(8,128)(2,1)S(1)}, u32[]{:S(2)}, u32[]{:S(2)}) collective-permute-start(bf16[256,512]{1,0:T(8,128)(2,1)S(1)} %get-tuple-element.84.refs_1_), channel_id=1, source_target_pairs={{0,8},{1,9},{2,10},{3,11},{4,12},{5,13},{6,14},{7,15},{8,0},{9,1},... | collective-permute-start | bytes 786440 | tf_op jit(solution)/shard_map/ppermute | solution.py:45
  75.9 2.6 %collective-permute-start.8 = (bf16[256,256]{1,0:T(8,128)(2,1)S(1)}, bf16[256,256]{1,0:T(8,128)(2,1)S(1)}, u32[]{:S(2)}, u32[]{:S(2)}) collective-permute-start(bf16[256,256]{1,0:T(8,128)(2,1)S(1)} %get-tuple-element.75.refs_1_), channel_id=1, source_target_pairs={{0,24},{1,25},{2,26},{3,27},{4,28},{5,29},{6,30},{7,31},{8,16},{9,... | collective-permute-start | bytes 393224 | tf_op jit(solution)/shard_map/ppermute | solution.py:45
  78.6 8.2 %collective-permute-done.8.refs_0_ = bf16[256,256]{1,0:T(8,128)(2,1)S(1)} collective-permute-done((bf16[256,256]{1,0:T(8,128)(2,1)S(1)}, bf16[256,256]{1,0:T(8,128)(2,1)S(1)}, u32[]{:S(2)}, u32[]{:S(2)}) %collective-permute-start.8) | collective-permute-done | bytes 131104 | tf_op jit(solution)/shard_map/ppermute | solution.py:45
  87.0 0.7 copy-done.13
  87.8 0.6 collective-permute-start.13
  88.3 1.5 collective-permute-start.10
  89.8 8.6 %collective-permute-done.10.refs_0_ = bf16[272,256]{1,0:T(8,128)(2,1)S(1)} collective-permute-done((bf16[272,256]{1,0:T(8,128)(2,1)S(1)}, bf16[272,256]{1,0:T(8,128)(2,1)S(1)}, u32[]{:S(2)}, u32[]{:S(2)}) %collective-permute-start.10) | collective-permute-done | bytes 139296 | tf_op jit(solution)/shard_map/ppermute | solution.py:45
  98.5 0.7 join.5
  99.2 1.0 join.6
  100.8 1.5 collective-permute-start.12
  102.3 13.1 %collective-permute-done.17.refs_1_ = bf16[1024,512]{1,0:T(8,128)(2,1)} collective-permute-done((bf16[1024,512]{1,0:T(8,128)(2,1)}, bf16[1024,512]{1,0:T(8,128)(2,1)}, u32[]{:S(2)}, u32[]{:S(2)}) %collective-permute-start.17) | collective-permute-done | bytes 1048608 | tf_op jit(solution)/shard_map/ppermute | solution.py:45
  115.7 2.6 %collective-permute-done.12.refs_0_ = bf16[528,256]{1,0:T(8,128)(2,1)} collective-permute-done((bf16[528,256]{1,0:T(8,128)(2,1)}, bf16[528,256]{1,0:T(8,128)(2,1)}, u32[]{:S(2)}, u32[]{:S(2)}) %collective-permute-start.12) | collective-permute-done | bytes 270368 | tf_op jit(solution)/shard_map/ppermute | solution.py:45
  118.3 1.1 join.7
  119.6 11.8 %collective-permute-done.14.rest_0_ = bf16[1040,256]{1,0:T(8,128)(2,1)S(1)} collective-permute-done((bf16[1040,256]{1,0:T(8,128)(2,1)S(1)}, bf16[1040,256]{1,0:T(8,128)(2,1)S(1)}, u32[]{:S(2)}, u32[]{:S(2)}) %collective-permute-start.14) | collective-permute-done | bytes 532512 | tf_op jit(solution)/shard_map/ppermute | solution.py:45
  131.4 1.8 %maximum_bitcast_fusion = f32[1,128,768]{2,1,0:T(8,128)} fusion(f32[128,256]{1,0:T(8,128)} %copy-done.13, f32[128,512]{1,0:T(8,128)} %copy-done.10), kind=kLoop, calls=%fused_computation.6 | loop fusion | flops 98304 | bytes 786432 | tf_op jit(solution)/shard_map/broadcast_in_dim | solution.py:585
  133.2 2.5 %copy-done.2 = bf16[1280,2048]{1,0:T(8,128)(2,1)S(1)} copy-done((bf16[1280,2048]{1,0:T(8,128)(2,1)S(1)}, bf16[1280,2048]{1,0:T(8,128)(2,1)}, u32[]{:S(2)}) %copy-start.2) | copy-done | bytes 5242904
  135.7 5.6 %part_scores.2 = (f32[1280,1024]{1,0:T(8,128)S(1)}, f32[8,128]{1,0:T(8,128)S(1)}) custom-call(s32[16]{0:T(128)S(1)} %and_select_fusion.4.group_ref, bf16[1280,2048]{1,0:T(8,128)(2,1)S(1)} %copy-done.2, bf16[1024,512]{1,0:T(8,128)(2,1)} %get-tuple-element.93.refs_1_, bf16[1024,512]{1,0:T(8,128)(2,1)} %collective-permute-done.19.refs_2_, ...), custom_call_target="tpu_custom_call" | custom-call | flops 2684354560 | bytes 9961472 | tf_op jit(solution)/shard_map/part_scores/pallas_call | solution.py:289
  141.3 6.4 %part_scores.3 = (f32[1280,1024]{1,0:T(8,128)S(1)}, f32[8,128]{1,0:T(8,128)}) custom-call(s32[16]{0:T(128)S(1)} %and_select_fusion.5.group_ref, bf16[1280,2048]{1,0:T(8,128)(2,1)S(1)} %copy-done.2, bf16[1024,512]{1,0:T(8,128)(2,1)} %collective-permute-done.17.refs_1_, ...), custom_call_target="tpu_custom_call", output_to_operand_aliasing={{0}: (4, {})} | custom-call | flops 2684354560 | bytes 9961472 | tf_op jit(solution)/shard_map/part_scores/pallas_call | solution.py:289
  147.8 6.7 %final_scores.1 = bf16[1280,1024]{1,0:T(8,128)(2,1)} custom-call(s32[32]{0:T(128)S(1)} %concatenate.113.code_ref, s32[8]{0:T(128)S(1)} %fusion.27.slot_ref, bf16[1280,1024]{1,0:T(8,128)(2,1)S(1)} %copy-done.4, bf16[1280,16]{1,0:T(8,128)(2,1)S(1)} %get-tuple-element.56.pick_ref, f32[16,1024]{1,0:T(8,128)S(1)} %broadcast_in_dim.30.half_ref, ...), custom_call_target="tpu_custom_call" | custom-call | flops 2684354560 | bytes 12582912 | tf_op jit(solution)/shard_map/final_scores/pallas_call | solution.py:358
  (63 shorter events, 4.5 us)
Async XLA Ops:
  0.6 51.4 %copy-start = (f32[1,1024,768]{2,1,0:T(8,128)S(1)}, f32[1,1024,768]{2,1,0:T(8,128)}, u32[]{:S(2)}) copy-start(f32[1,1024,768]{2,1,0:T(8,128)} %param.9) | copy-start | bytes 9437188
  3.0 4.3 %collective-permute-start = (s32[1280]{0:T(1024)S(1)}, s32[1280]{0:T(1024)S(1)}, u32[]{:S(2)}, u32[]{:S(2)}) collective-permute-start(s32[1280]{0:T(1024)S(1)} %add_select_fusion.9), channel_id=1, source_target_pairs={{0,1},{1,0},{2,3},{3,2},{4,5},{5,4},{6,7},{7,6},{8,9},{9,8},{10,11... | collective-permute-start | bytes 15368 | tf_op jit(solution)/shard_map/ppermute | solution.py:45
  3.5 4.7 %collective-permute-start.1 = (bf16[1280,768]{1,0:T(8,128)(2,1)}, bf16[1280,768]{1,0:T(8,128)(2,1)}, u32[]{:S(2)}, u32[]{:S(2)}) collective-permute-start(bf16[1280,768]{1,0:T(8,128)(2,1)} %refs_1_.9), channel_id=1, source_target_pairs={{0,1},{1,0},{2,3},{3,2},{4,5},{5,4},{6,7},{7,6},{8,9},{9,8},{10,11... | collective-permute-start | bytes 5898248 | tf_op jit(solution)/shard_map/ppermute | solution.py:45
  8.2 1.5 %copy-start.6 = (bf16[1280,768]{1,0:T(8,128)(2,1)S(1)}, bf16[1280,768]{1,0:T(8,128)(2,1)}, u32[]{:S(2)}) copy-start(bf16[1280,768]{1,0:T(8,128)(2,1)} %refs_1_.9) | copy-start | bytes 5898244
  9.8 7.5 %copy-start.7 = (bf16[1280,768]{1,0:T(8,128)(2,1)S(1)}, bf16[1280,768]{1,0:T(8,128)(2,1)}, u32[]{:S(2)}) copy-start(bf16[1280,768]{1,0:T(8,128)(2,1)} %refs_1_.9) | copy-start | bytes 5898244
  14.2 17.7 %collective-permute-start.3 = (bf16[1040,512]{1,0:T(8,128)(2,1)S(1)}, bf16[1040,512]{1,0:T(8,128)(2,1)S(1)}, u32[]{:S(2)}, u32[]{:S(2)}) collective-permute-start(bf16[1040,512]{1,0:T(8,128)(2,1)S(1)} %get-tuple-element.59), channel_id=1, source_target_pairs={{0,2},{1,5},{2,0},{3,7},{4,6},{5,1},{6,4},{7,3},{8,10},{9,13},{10,... | collective-permute-start | bytes 3194888 | tf_op jit(solution)/shard_map/ppermute | solution.py:45
  24.2 2.7 %copy-start.5 = (s32[1280,1]{1,0:T(8,128)S(1)}, s32[1280,1]{1,0:T(8,128)}, u32[]{:S(2)}) copy-start(s32[1280,1]{1,0:T(8,128)} %fusion.3.refs_0_) | copy-start | bytes 15364
  28.0 2.3 %copy-start.1 = (bf16[1280,2048]{1,0:T(8,128)(2,1)}, bf16[1280,2048]{1,0:T(8,128)(2,1)S(1)}, u32[]{:S(2)}) copy-start(bf16[1280,2048]{1,0:T(8,128)(2,1)S(1)} %get-tuple-element.92.refs_0_) | copy-start | bytes 15728644
  30.4 1.5 copy-start.3
  32.1 16.3 %collective-permute-start.5 = (bf16[528,512]{1,0:T(8,128)(2,1)S(1)}, bf16[528,512]{1,0:T(8,128)(2,1)S(1)}, u32[]{:S(2)}, u32[]{:S(2)}) collective-permute-start(bf16[528,512]{1,0:T(8,128)(2,1)S(1)} %get-tuple-element.65), channel_id=1, source_target_pairs={{0,4},{1,3},{2,6},{3,1},{4,0},{5,7},{6,2},{7,5},{8,12},{9,11},{10,... | collective-permute-start | bytes 1622024 | tf_op jit(solution)/shard_map/ppermute | solution.py:45
  33.7 13.3 %collective-permute-start.2 = (bf16[1024,256]{1,0:T(8,128)(2,1)S(1)}, bf16[1024,256]{1,0:T(8,128)(2,1)S(1)}, u32[]{:S(2)}, u32[]{:S(2)}) collective-permute-start(bf16[1024,256]{1,0:T(8,128)(2,1)S(1)} %get-tuple-element.57), channel_id=1, source_target_pairs={{0,8},{1,9},{2,10},{3,11},{4,12},{5,13},{6,14},{7,15},{8,0},{9,1},... | collective-permute-start | bytes 1572872 | tf_op jit(solution)/shard_map/ppermute | solution.py:45
  47.8 0.7 copy-start.11
  49.2 0.7 copy-start.8
  49.9 10.2 %collective-permute-start.7 = (bf16[272,512]{1,0:T(8,128)(2,1)}, bf16[272,512]{1,0:T(8,128)(2,1)}, u32[]{:S(2)}, u32[]{:S(2)}) collective-permute-start(bf16[272,512]{1,0:T(8,128)(2,1)} %get-tuple-element.71), channel_id=1, source_target_pairs={{0,8},{1,9},{2,10},{3,11},{4,12},{5,13},{6,14},{7,15},{8,0},{9,1},... | collective-permute-start | bytes 835592 | tf_op jit(solution)/shard_map/ppermute | solution.py:45
  51.5 6.7 %collective-permute-start.4 = (bf16[512,256]{1,0:T(8,128)(2,1)}, bf16[512,256]{1,0:T(8,128)(2,1)}, u32[]{:S(2)}, u32[]{:S(2)}) collective-permute-start(bf16[512,256]{1,0:T(8,128)(2,1)} %get-tuple-element.63), channel_id=1, source_target_pairs={{0,2},{1,5},{2,0},{3,7},{4,6},{5,1},{6,4},{7,3},{8,10},{9,13},{10,... | collective-permute-start | bytes 786440 | tf_op jit(solution)/shard_map/ppermute | solution.py:45
  58.2 1.0 copy-start.12
  60.2 1.0 copy-start.9
  62.2 8.5 %collective-permute-start.9 = (bf16[272,512]{1,0:T(8,128)(2,1)S(1)}, bf16[272,512]{1,0:T(8,128)(2,1)S(1)}, u32[]{:S(2)}, u32[]{:S(2)}) collective-permute-start(bf16[272,512]{1,0:T(8,128)(2,1)S(1)} %get-tuple-element.77.refs_1_), channel_id=1, source_target_pairs={{0,24},{1,25},{2,26},{3,27},{4,28},{5,29},{6,30},{7,31},{8,16},{9,... | collective-permute-start | bytes 835592 | tf_op jit(solution)/shard_map/ppermute | solution.py:45
  64.7 5.0 %collective-permute-start.6 = (bf16[256,256]{1,0:T(8,128)(2,1)S(1)}, bf16[256,256]{1,0:T(8,128)(2,1)S(1)}, u32[]{:S(2)}, u32[]{:S(2)}) collective-permute-start(bf16[256,256]{1,0:T(8,128)(2,1)S(1)} %get-tuple-element.69), channel_id=1, source_target_pairs={{0,4},{1,3},{2,6},{3,1},{4,0},{5,7},{6,2},{7,5},{8,12},{9,11},{10,... | collective-permute-start | bytes 393224 | tf_op jit(solution)/shard_map/ppermute | solution.py:45
  71.0 16.7 %copy-start.10 = (f32[128,512]{1,0:T(8,128)}, f32[128,512]{1,0:T(8,128)S(1)}, u32[]{:S(2)}) copy-start(f32[128,512]{1,0:T(8,128)S(1)} %get-tuple-element.98) | copy-start | bytes 786436
  71.0 16.7 %collective-permute-start.11 = (bf16[256,512]{1,0:T(8,128)(2,1)S(1)}, bf16[256,512]{1,0:T(8,128)(2,1)S(1)}, u32[]{:S(2)}, u32[]{:S(2)}) collective-permute-start(bf16[256,512]{1,0:T(8,128)(2,1)S(1)} %get-tuple-element.84.refs_1_), channel_id=1, source_target_pairs={{0,8},{1,9},{2,10},{3,11},{4,12},{5,13},{6,14},{7,15},{8,0},{9,1},... | collective-permute-start | bytes 786440 | tf_op jit(solution)/shard_map/ppermute | solution.py:45
  75.9 10.8 %collective-permute-start.8 = (bf16[256,256]{1,0:T(8,128)(2,1)S(1)}, bf16[256,256]{1,0:T(8,128)(2,1)S(1)}, u32[]{:S(2)}, u32[]{:S(2)}) collective-permute-start(bf16[256,256]{1,0:T(8,128)(2,1)S(1)} %get-tuple-element.75.refs_1_), channel_id=1, source_target_pairs={{0,24},{1,25},{2,26},{3,27},{4,28},{5,29},{6,30},{7,31},{8,16},{9,... | collective-permute-start | bytes 393224 | tf_op jit(solution)/shard_map/ppermute | solution.py:45
  87.0 0.7 copy-start.13
  87.8 11.5 %collective-permute-start.13 = (bf16[512,512]{1,0:T(8,128)(2,1)S(1)}, bf16[512,512]{1,0:T(8,128)(2,1)S(1)}, u32[]{:S(2)}, u32[]{:S(2)}) collective-permute-start(bf16[512,512]{1,0:T(8,128)(2,1)S(1)} %get-tuple-element.88.refs_1_), channel_id=1, source_target_pairs={{0,4},{1,3},{2,6},{3,1},{4,0},{5,7},{6,2},{7,5},{8,12},{9,11},{10,... | collective-permute-start | bytes 1572872 | tf_op jit(solution)/shard_map/ppermute | solution.py:45
  88.3 10.2 %collective-permute-start.10 = (bf16[272,256]{1,0:T(8,128)(2,1)S(1)}, bf16[272,256]{1,0:T(8,128)(2,1)S(1)}, u32[]{:S(2)}, u32[]{:S(2)}) collective-permute-start(bf16[272,256]{1,0:T(8,128)(2,1)S(1)} %get-tuple-element.83.refs_1_), channel_id=1, source_target_pairs={{0,4},{1,3},{2,6},{3,1},{4,0},{5,7},{6,2},{7,5},{8,12},{9,11},{10,... | collective-permute-start | bytes 417800 | tf_op jit(solution)/shard_map/ppermute | solution.py:45
  100.3 15.1 %collective-permute-start.17 = (bf16[1024,512]{1,0:T(8,128)(2,1)}, bf16[1024,512]{1,0:T(8,128)(2,1)}, u32[]{:S(2)}, u32[]{:S(2)}) collective-permute-start(bf16[1024,512]{1,0:T(8,128)(2,1)} %get-tuple-element.93.refs_1_), channel_id=1, source_target_pairs={{0,2},{1,5},{2,0},{3,7},{4,6},{5,1},{6,4},{7,3},{8,10},{9,13},{10,... | collective-permute-start | bytes 3145736 | tf_op jit(solution)/shard_map/ppermute | solution.py:45
  100.8 32.4 %collective-permute-start.19 = (bf16[1024,512]{1,0:T(8,128)(2,1)}, bf16[1024,512]{1,0:T(8,128)(2,1)}, u32[]{:S(2)}, u32[]{:S(2)}) collective-permute-start(bf16[1024,512]{1,0:T(8,128)(2,1)} %get-tuple-element.93.refs_1_), channel_id=1, source_target_pairs={{0,1},{1,0},{2,3},{3,2},{4,5},{5,4},{6,7},{7,6},{8,9},{9,8},{10,11... | collective-permute-start | bytes 3145736 | tf_op jit(solution)/shard_map/ppermute | solution.py:45
  100.8 17.5 %collective-permute-start.12 = (bf16[528,256]{1,0:T(8,128)(2,1)}, bf16[528,256]{1,0:T(8,128)(2,1)}, u32[]{:S(2)}, u32[]{:S(2)}) collective-permute-start(bf16[528,256]{1,0:T(8,128)(2,1)} %get-tuple-element.87.refs_1_), channel_id=1, source_target_pairs={{0,2},{1,5},{2,0},{3,7},{4,6},{5,1},{6,4},{7,3},{8,10},{9,13},{10,... | collective-permute-start | bytes 811016 | tf_op jit(solution)/shard_map/ppermute | solution.py:45
  115.4 25.9 %collective-permute-start.18 = (bf16[1024,512]{1,0:T(8,128)(2,1)}, bf16[1024,512]{1,0:T(8,128)(2,1)}, u32[]{:S(2)}, u32[]{:S(2)}) collective-permute-start(bf16[1024,512]{1,0:T(8,128)(2,1)} %collective-permute-done.17.refs_1_), channel_id=1, source_target_pairs={{0,1},{1,0},{2,3},{3,2},{4,5},{5,4},{6,7},{7,6},{8,9},{9,8},{10,11... | collective-permute-start | bytes 3145736 | tf_op jit(solution)/shard_map/ppermute | solution.py:45
  119.4 12.0 %collective-permute-start.14 = (bf16[1040,256]{1,0:T(8,128)(2,1)S(1)}, bf16[1040,256]{1,0:T(8,128)(2,1)S(1)}, u32[]{:S(2)}, u32[]{:S(2)}) collective-permute-start(bf16[1040,256]{1,0:T(8,128)(2,1)S(1)} %get-tuple-element.91.rest_2_), channel_id=1, source_target_pairs={{0,8},{1,9},{2,10},{3,11},{4,12},{5,13},{6,14},{7,15},{8,0},{9,1},... | collective-permute-start | bytes 1597448 | tf_op jit(solution)/shard_map/ppermute | solution.py:45
  119.5 28.2 %collective-permute-start.16 = (bf16[1040,256]{1,0:T(8,128)(2,1)S(1)}, bf16[1040,256]{1,0:T(8,128)(2,1)S(1)}, u32[]{:S(2)}, u32[]{:S(2)}) collective-permute-start(bf16[1040,256]{1,0:T(8,128)(2,1)S(1)} %get-tuple-element.91.rest_2_), channel_id=1, source_target_pairs={{0,1},{1,0},{2,3},{3,2},{4,5},{5,4},{6,7},{7,6},{8,9},{9,8},{10,11... | collective-permute-start | bytes 1597448 | tf_op jit(solution)/shard_map/ppermute | solution.py:45
  131.4 16.4 %collective-permute-start.15 = (bf16[1040,256]{1,0:T(8,128)(2,1)S(1)}, bf16[1040,256]{1,0:T(8,128)(2,1)S(1)}, u32[]{:S(2)}, u32[]{:S(2)}) collective-permute-start(bf16[1040,256]{1,0:T(8,128)(2,1)S(1)} %collective-permute-done.14.rest_0_), channel_id=1, source_target_pairs={{0,1},{1,0},{2,3},{3,2},{4,5},{5,4},{6,7},{7,6},{8,9},{9,8},{10,11... | collective-permute-start | bytes 1597448 | tf_op jit(solution)/shard_map/ppermute | solution.py:45
  133.2 2.5 %copy-start.2 = (bf16[1280,2048]{1,0:T(8,128)(2,1)S(1)}, bf16[1280,2048]{1,0:T(8,128)(2,1)}, u32[]{:S(2)}) copy-start(bf16[1280,2048]{1,0:T(8,128)(2,1)} %copy-done.1) | copy-start | bytes 15728644
  141.3 6.5 %copy-start.4 = (bf16[1280,1024]{1,0:T(8,128)(2,1)S(1)}, bf16[1280,1024]{1,0:T(8,128)(2,1)}, u32[]{:S(2)}) copy-start(bf16[1280,1024]{1,0:T(8,128)(2,1)} %copy-done.3) | copy-start | bytes 7864324

commit v4 on v3

--- a/solution.py
+++ b/solution.py
@@ -20,19 +20,20 @@
 
 
 def streams_of(width):
-    wide = width * 2 // 3
-    return ((0, wide), (wide, width - wide))
+    wide = width // 2
+    return ((0, wide), (wide, wide))
 
 
 def orders_of(groups, members):
     inner = [(0, 1 << bit) for bit in range(1, members.bit_length() - 1)]
     outer = [((1 << (bit + 1)) - 1, 0) for bit in range(groups.bit_length() - 1)]
+    cut = len(inner) // 2
+    other = inner[cut:] + inner[:cut]
     found = {}
-    for core in range(2):
-        cut = core * len(inner) // 2
-        turned = inner[cut:] + inner[:cut]
-        found[core, 0] = turned + outer
-        found[core, 1] = outer[:1] + turned + outer[1:]
+    found[0, 0] = inner + outer
+    found[1, 0] = other[:cut] + outer[:1] + other[cut:] + outer[1:]
+    found[0, 1] = outer[:1] + inner + outer[1:]
+    found[1, 1] = inner + outer
     return found
 
 
@@ -118,7 +119,7 @@
         + [whole(e.shape) for e in extra]
         + [whole(token.shape)],
         out_specs=[whole((out_rows, wide)), whole(token.shape)],
-        compiler_params=pltpu.CompilerParams(vmem_limit_bytes=24 << 20),
+        compiler_params=pltpu.CompilerParams(vmem_limit_bytes=16 << 20),
         cost_estimate=pl.CostEstimate(
             flops=2 * keys * 2 * rows * wide, bytes_accessed=(4 * rows + 2 * keys) * wide, transcendentals=0
         ),
@@ -235,6 +236,10 @@
         out_ref[2 * body :, :] = (held_ref[body:, :].astype(F32) + moved).astype(BF16)
 
 
+def pass_kernel(in_ref, out_ref):
+    out_ref[...] = in_ref[...]
+
+
 def mask_kernel(groups, columns, gid_ref, x_ref, *outs):
     gid = gid_ref[...]
     for (start, wide), out in zip(columns, outs):
@@ -251,7 +256,7 @@
     return lax.dot_general(a, b, (((1,), (1,)), ((), ())), preferred_element_type=F32)
 
 
-def part_kernel(groups, share, group_ref, masked_ref, own_ref, other_ref, *rest):
+def part_kernel(groups, share, code_ref, masked_ref, own_ref, other_ref, *rest):
     out_ref, cents = rest[-2:]
     wide = own_ref.shape[1]
     blocks = own_ref.shape[0] // share
@@ -260,18 +265,16 @@
     def _():
         for piece, ref in enumerate((own_ref, other_ref)):
             for block in range(blocks):
-                group = group_ref[piece * blocks + block]
-                slot = (piece * blocks + block) // groups
-                cents[
-                    slot * share : (slot + 1) * share, pl.ds(pl.multiple_of(group * wide, 128), wide)
-                ] = ref[block * share : (block + 1) * share, :]
+                code = code_ref[piece * blocks + block]
+                slot = pl.multiple_of(code // groups * share, share)
+                cents[pl.ds(slot, share), pl.ds(pl.multiple_of(code % groups * wide, 128), wide)] = ref[block * share : (block + 1) * share, :]
 
     step = out_ref.shape[1]
     start = pl.multiple_of(pl.program_id(0) * step, step)
     out_ref[...] = product(masked_ref[...], cents[pl.ds(start, step), :])
 
 
-def part_scores(token, masked, group_of, pieces, before, groups, keys, share):
+def part_scores(token, masked, codes, pieces, before, groups, keys, share):
     rows = masked.shape[0]
     wide = pieces[0].shape[1]
     half = pieces[0].shape[0] * len(pieces) // groups
@@ -281,9 +284,9 @@
     whole = pl.BlockSpec(memory_space=pltpu.VMEM)
     extra = [] if before is None else [before]
 
-    def kernel(group_ref, *refs):
+    def kernel(code_ref, *refs):
         count = 3 + len(extra)
-        part_kernel(groups, share, group_ref, *refs[:3], refs[count + 1], refs[-1])
+        part_kernel(groups, share, code_ref, *refs[:3], refs[count + 1], refs[-1])
         refs[count + 2][...] = refs[count][...]
 
     return pl.pallas_call(
@@ -298,13 +301,9 @@
         out_shape=[jax.ShapeDtypeStruct((rows, keys), F32), token_shape()],
         input_output_aliases={} if before is None else {4: 0},
         compiler_params=pltpu.CompilerParams(vmem_limit_bytes=16 << 20),
-        cost_estimate=pl.CostEstimate(
-            flops=2 * rows * half * groups * wide,
-            bytes_accessed=2 * (rows + half) * groups * wide + 4 * rows * half,
-            transcendentals=0,
-        ),
+        cost_estimate=pl.CostEstimate(flops=1, bytes_accessed=1, transcendentals=0),
         name="part_scores",
-    )(group_of, masked, *pieces, *extra, token)
+    )(codes, masked, *pieces, *extra, token)
 
 
 def final_kernel(groups, share, code_ref, slot_ref, masked_ref, pick_ref, half_ref, *rest):
@@ -370,11 +369,7 @@
         ),
         out_shape=jax.ShapeDtypeStruct((rows, keys), BF16),
         compiler_params=pltpu.CompilerParams(vmem_limit_bytes=16 << 20),
-        cost_estimate=pl.CostEstimate(
-            flops=2 * rows * keys * groups * wide,
-            bytes_accessed=2 * (rows + keys) * groups * wide + 6 * rows * keys,
-            transcendentals=0,
-        ),
+        cost_estimate=pl.CostEstimate(flops=1, bytes_accessed=1, transcendentals=0),
         name="final_scores",
     )(codes, slots, masked, pick, half, *pieces, total, total)
 
@@ -422,7 +417,7 @@
         return partner
 
     tail = pad_rows(blocks)
-    token = jnp.zeros((8, 128), F32)
+    token = start_token = jnp.zeros((8, 128), F32)
     rows_of, tiles = [], []
     for stream, (start, wide) in enumerate(columns):
         place = of_core(
@@ -449,17 +444,8 @@
                 token, rows_of[stream], samples, other_samples, tiles[stream], part * half_keys, half_keys, start, wide
             )
 
-    gid = jnp.where(live, coarse_label[:, 0], -1)[:, None]
-    *masked, pick, token = small_call(
-        functools.partial(mask_kernel, groups, columns),
-        "mask",
-        [jax.ShapeDtypeStruct((rows, groups * wide), BF16) for _, wide in columns]
-        + [jax.ShapeDtypeStruct((rows, TILE), BF16)],
-        token,
-        gid,
-        samples,
-    )
-
+    tokens = [start_token] * 2
+    pick_token = lambda stream: tokens[1 - stream]
     old_share = lax.dynamic_slice(old_centroids[0], (me * share, 0), (share, width))
 
     def bf(count, stream, tailed):
@@ -473,20 +459,20 @@
         for stream, (start, wide) in enumerate(columns):
             got = exchange(send[stream], pairing(stage, stream), groups, members)
             if stage < stages - 2:
-                send[stream], keep[stream], token = small_call(
+                send[stream], keep[stream], tokens[stream] = small_call(
                     functools.partial(fold_kernel, count // 2 * share, count),
                     "fold",
                     [bf(count // 2, stream, 0)] * 2,
-                    token,
+                    pick_token(stream),
                     got,
                     keep[stream],
                 )
             else:
-                send[stream], near[stream], token = small_call(
+                send[stream], near[stream], tokens[stream] = small_call(
                     functools.partial(seed_kernel, share, count),
                     "seed",
                     [bf(2, stream, 0), share_f32[stream]],
-                    token,
+                    pick_token(stream),
                     got,
                     keep[stream],
                     old_share[:, start : start + wide],
@@ -496,21 +482,21 @@
     for stream in streams:
         got = exchange(send[stream], pairing(stages - 1, stream), groups, members)
         if stream == 0:
-            fresh[0], held[0], scale, norm, token = small_call(
+            fresh[0], held[0], scale, norm, tokens[stream] = small_call(
                 functools.partial(first_kernel, share, base, digits),
                 "first_centroids",
                 [share_f32[0], bf(2, 0, 1), column, column],
-                token,
+                pick_token(stream),
                 got,
                 send[0],
                 near[0],
             )
         else:
-            fresh[1], held[1], token = small_call(
+            fresh[1], held[1], tokens[stream] = small_call(
                 functools.partial(last_kernel, share, tail),
                 "last_centroids",
                 [share_f32[1], bf(2, 1, 1)],
-                token,
+                pick_token(stream),
                 got,
                 send[1],
                 near[1],
@@ -523,11 +509,11 @@
         for stream in streams:
             got = exchange(held[stream], pairing(stage, stream), groups, members)
             if stage:
-                held[stream], token = small_call(
+                held[stream], tokens[stream] = small_call(
                     functools.partial(join_kernel, count * share, count),
                     "join",
                     [bf(2 * count, stream, 1)],
-                    token,
+                    pick_token(stream),
                     got,
                     held[stream],
                 )
@@ -547,22 +533,45 @@
             codes.append((z ^ group_rel) * members + (me ^ flip ^ member_rel))
         return jnp.stack(codes).astype(jnp.int32)
 
+    gid = jnp.where(live, coarse_label[:, 0], -1)[:, None]
+    *masked, pick, token = small_call(
+        functools.partial(mask_kernel, groups, columns),
+        "mask",
+        [jax.ShapeDtypeStruct((rows, groups * wide), BF16) for _, wide in columns]
+        + [jax.ShapeDtypeStruct((rows, TILE), BF16)],
+        token,
+        gid,
+        samples,
+    )
+
+    quarter = half_blocks // groups
+    inner_of = [[dim for dim in turned[c, 0] if dim[1]] for c in range(2)]
     total = None
     for part, piece in ((1, held[0]), (0, arrived[0])):
-        group_codes = jnp.concatenate([codes_of(0, part, flip) for flip in range(2)]) // members
+        part_codes = []
+        for flip in range(2):
+            for block in range(half_blocks):
+                code = []
+                for c in range(2):
+                    group_rel, member_rel = relative_of(part * half_blocks + block, turned[c, 0])
+                    spot = block_position(0, member_rel, inner_of[c], outer_bits) % quarter
+                    code.append((spot + flip * quarter) * groups + (z ^ group_rel))
+                part_codes.append(jnp.where(core ^ flip == 0, *code))
         total, token = part_scores(
-            token, masked[0], group_codes, [piece, sibling(piece)], total, groups, keys, share
+            token, masked[0], jnp.stack(part_codes).astype(jnp.int32), [piece, sibling(piece)], total, groups, keys, share
         )
 
+    last, token = small_call(
+        pass_kernel, "pass", [jax.ShapeDtypeStruct(arrived[1].shape, BF16)], token, arrived[1]
+    )
     every = jnp.arange(members, dtype=jnp.int32)
     flip_of = (every ^ me) & 1
     spot = jnp.where(
         (core ^ flip_of) == 0,
-        *(block_position(jnp.zeros_like(every), every ^ me, turned[c, 0], outer_bits) // groups for c in range(2)),
+        *(block_position(0, every ^ me, inner_of[c], outer_bits) for c in range(2)),
     )
-    quarter = half_blocks // groups
     slots = jnp.where(spot >= quarter, spot - quarter, spot + 2 * quarter) + flip_of * quarter
-    flat = [piece for got in (arrived[1], held[1]) for piece in (got, sibling(got))]
+    flat = [piece for got in (last, held[1]) for piece in (got, sibling(got))]
     codes = jnp.concatenate([codes_of(1, part, flip) for part in range(2) for flip in range(2)])
     half = jnp.zeros((TILE, keys), F32)
     if share < 128:

time: 155 us -> 138 us (0.89)
  waiting for transfers between devices: 67.5 us -> 42.9 us
  Pallas kernels: 41.2 us -> 46.1 us
  local copies, waits for them, and re-layouts: 14 us -> 17 us
    ppermute x20, waiting for transfers between devices: 67.5 us -> 42.9 us  [exchange(): return lax.ppermute(array, AXES, pairs)]
    unnamed x30 -> x32, local copies, waits for them, and re-layouts: 13.6 us -> 16.8 us
    pallas_call x1, Pallas kernels: 6.69 us -> 9.71 us  [final_scores(): pl.pallas_call(functools.partial(final_kernel, groups, share), grid_spec=...]
    pallas_call x4, Pallas kernels: 14 us -> 16.8 us  [key_sums(): pl.pallas_call(hand_on(functools.partial(sums_kernel, base), 3 + len(extr...]
    pallas_call x2, Pallas kernels: 12 us -> 9.49 us  [part_scores(): pl.pallas_call(kernel, grid_spec=pltpu.PrefetchScalarGridSpec(num_scalar_...]
    pallas_call x13 -> x14, Pallas kernels: 8.46 us -> 10.1 us  [small_call(): pl.pallas_call(hand_on(kernel, len(args)), out_shape=[*outs, token_shape(...]
  transfers between devices with their start and end apart: 20 -> 20, of which waited for: 9 -> 9; matrix products, arithmetic and copies ran while one was open for 4% -> 5% of each run, Pallas kernels for 17% -> 23%
where the time goes in v4:
time: 138 us
  Pallas kernels  46.1 us (33%)
  waiting for transfers between devices  42.9 us (31%)
  starting transfers between devices  24.3 us (18%)
  local copies, waits for them, and re-layouts  17 us (12%)
  other arithmetic  4.78 us (3%)
  between operations  1.85 us (1%)
    ppermute x20, waiting for transfers between devices, exchange(): return lax.ppermute(array, AXES, pairs)  42.9 us
    ppermute x20, starting transfers between devices, exchange(): return lax.ppermute(array, AXES, pairs)  24.3 us
    pallas_call x4, Pallas kernels, key_sums(): pl.pallas_call(hand_on(functools.partial(sums_kernel, base), 3 + len(extr...  16.8 us
    unnamed x32, local copies, waits for them, and re-layouts  16.8 us
    pallas_call x14, Pallas kernels, small_call(): pl.pallas_call(hand_on(kernel, len(args)), out_shape=[*outs, token_shape(...  10.1 us
    pallas_call x1, Pallas kernels, final_scores(): pl.pallas_call(functools.partial(final_kernel, groups, share), grid_spec=...  9.71 us
    pallas_call x2, Pallas kernels, part_scores(): pl.pallas_call(kernel, grid_spec=pltpu.PrefetchScalarGridSpec(num_scalar_...  9.49 us
  transfers between devices with their start and end apart: 20, of which 9 were waited for; matrix products, arithmetic and copies ran while one was open for 5% of the time, Pallas kernels for 23%

profile of v4, /device:TPU:0, one launch (start us, length us, event | category | flops | bytes accessed | tf_op | source)
XLA Modules:
  0.0 137.5 jit_solution(3432330549279627136)
XLA Ops:
  2.1 0.7 multiply_reduce_fusion
  2.8 0.7 add_select_fusion.9
  3.5 1.3 collective-permute-done
  5.7 1.5 %copy-done.5 = bf16[1280,768]{1,0:T(8,128)(2,1)S(1)} copy-done((bf16[1280,768]{1,0:T(8,128)(2,1)S(1)}, bf16[1280,768]{1,0:T(8,128)(2,1)}, u32[]{:S(2)}) %copy-start.5) | copy-done | bytes 1966104
  7.2 4.3 %key_sums.4 = (bf16[1040,384]{1,0:T(8,128)(2,1)S(1)}, f32[8,128]{1,0:T(8,128)S(1)}) custom-call(s32[1,2560]{1,0:T(1,128)S(1)} %get-tuple-element.102.refs_0_, bf16[1280,768]{1,0:T(8,128)(2,1)S(1)} %copy-done.5, bf16[1280,768]{1,0:T(8,128)(2,1)} %collective-permute-done.1.refs_2_, bf16[16,384]{1,0:T(8,128)(2,1)S(1)} %pad_maximum_fusion.refs_3_, ...), custom_call_target="tpu_custom_call" | custom-call | flops 2013265920 | bytes 2752512 | tf_op jit(solution)/shard_map/key_sums/pallas_call | solution.py:110
  11.5 2.9 %collective-permute-start.3 = (bf16[1040,384]{1,0:T(8,128)(2,1)S(1)}, bf16[1040,384]{1,0:T(8,128)(2,1)S(1)}, u32[]{:S(2)}, u32[]{:S(2)}) collective-permute-start(bf16[1040,384]{1,0:T(8,128)(2,1)S(1)} %get-tuple-element.60), channel_id=1, source_target_pairs={{0,2},{1,5},{2,0},{3,7},{4,6},{5,1},{6,4},{7,3},{8,10},{9,13},{10,... | collective-permute-start | bytes 2396168 | tf_op jit(solution)/shard_map/ppermute | solution.py:46
  14.6 4.2 %key_sums.5 = (bf16[1024,384]{1,0:T(8,128)(2,1)S(1)}, f32[8,128]{1,0:T(8,128)S(1)}) custom-call(s32[1,2560]{1,0:T(1,128)S(1)} %fusion.11.refs_0_, bf16[1280,768]{1,0:T(8,128)(2,1)S(1)} %copy-done.6, bf16[1280,768]{1,0:T(8,128)(2,1)} %collective-permute-done.1.refs_2_, f32[8,128]{1,0:T(8,128)S(1)} %get-tuple-element.52.refs_3_), custom_call_target="tpu_custom_call" | custom-call | flops 2013265920 | bytes 2752512 | tf_op jit(solution)/shard_map/key_sums/pallas_call | solution.py:110
  18.7 1.6 %collective-permute-start.2 = (bf16[1024,384]{1,0:T(8,128)(2,1)S(1)}, bf16[1024,384]{1,0:T(8,128)(2,1)S(1)}, u32[]{:S(2)}, u32[]{:S(2)}) collective-permute-start(bf16[1024,384]{1,0:T(8,128)(2,1)S(1)} %get-tuple-element.58), channel_id=1, source_target_pairs={{0,8},{1,3},{2,10},{3,1},{4,12},{5,7},{6,14},{7,5},{8,0},{9,11},{1... | collective-permute-start | bytes 2359304 | tf_op jit(solution)/shard_map/ppermute | solution.py:46
  20.4 4.2 %key_sums.6 = (bf16[1040,384]{1,0:T(8,128)(2,1)S(1)}, f32[8,128]{1,0:T(8,128)S(1)}) custom-call(s32[1,2560]{1,0:T(1,128)S(1)} %get-tuple-element.102.refs_0_, bf16[1280,768]{1,0:T(8,128)(2,1)S(1)} %copy-done.6, bf16[1280,768]{1,0:T(8,128)(2,1)} %collective-permute-done.1.refs_2_, bf16[16,384]{1,0:T(8,128)(2,1)S(1)} %pad_maximum_fusion.refs_3_, ...), custom_call_target="tpu_custom_call" | custom-call | flops 2013265920 | bytes 2752512 | tf_op jit(solution)/shard_map/key_sums/pallas_call | solution.py:110
  24.5 3.3 %collective-permute-done.3.refs_0_ = bf16[1040,384]{1,0:T(8,128)(2,1)S(1)} collective-permute-done((bf16[1040,384]{1,0:T(8,128)(2,1)S(1)}, bf16[1040,384]{1,0:T(8,128)(2,1)S(1)}, u32[]{:S(2)}, u32[]{:S(2)}) %collective-permute-start.3) | collective-permute-done | bytes 798752 | tf_op jit(solution)/shard_map/ppermute | solution.py:46
  27.8 0.9 fold.4
  28.7 3.7 %collective-permute-start.5 = (bf16[528,384]{1,0:T(8,128)(2,1)}, bf16[528,384]{1,0:T(8,128)(2,1)}, u32[]{:S(2)}, u32[]{:S(2)}) collective-permute-start(bf16[528,384]{1,0:T(8,128)(2,1)} %get-tuple-element.65), channel_id=1, source_target_pairs={{0,4},{1,9},{2,6},{3,11},{4,0},{5,13},{6,2},{7,15},{8,12},{9,1},{1... | collective-permute-start | bytes 1216520 | tf_op jit(solution)/shard_map/ppermute | solution.py:46
  32.4 4.2 %key_sums.7 = (bf16[1024,384]{1,0:T(8,128)(2,1)S(1)}, f32[8,128]{1,0:T(8,128)S(1)}) custom-call(s32[1,2560]{1,0:T(1,128)S(1)} %fusion.11.refs_0_, bf16[1280,768]{1,0:T(8,128)(2,1)S(1)} %copy-done.6, bf16[1280,768]{1,0:T(8,128)(2,1)} %collective-permute-done.1.refs_2_, f32[8,128]{1,0:T(8,128)S(1)} %get-tuple-element.54.refs_3_), custom_call_target="tpu_custom_call" | custom-call | flops 2013265920 | bytes 2752512 | tf_op jit(solution)/shard_map/key_sums/pallas_call | solution.py:110
  36.6 0.9 fold.5
  37.4 0.8 copy-done.8
  38.8 1.3 collective-permute-start.4
  40.1 0.7 copy-done.13
  40.8 1.1 fold.6
  41.9 1.6 %collective-permute-start.7 = (bf16[272,384]{1,0:T(8,128)(2,1)S(1)}, bf16[272,384]{1,0:T(8,128)(2,1)S(1)}, u32[]{:S(2)}, u32[]{:S(2)}) collective-permute-start(bf16[272,384]{1,0:T(8,128)(2,1)S(1)} %get-tuple-element.71), channel_id=1, source_target_pairs={{0,8},{1,3},{2,10},{3,1},{4,12},{5,7},{6,14},{7,5},{8,0},{9,11},{1... | collective-permute-start | bytes 626696 | tf_op jit(solution)/shard_map/ppermute | solution.py:46
  43.6 4.5 %collective-permute-done.4.refs_0_ = bf16[512,384]{1,0:T(8,128)(2,1)} collective-permute-done((bf16[512,384]{1,0:T(8,128)(2,1)}, bf16[512,384]{1,0:T(8,128)(2,1)}, u32[]{:S(2)}, u32[]{:S(2)}) %collective-permute-start.4) | collective-permute-done | bytes 393248 | tf_op jit(solution)/shard_map/ppermute | solution.py:46
  48.1 1.0 copy-done.9
  49.1 1.1 fold.7
  50.3 3.7 %collective-permute-start.9 = (bf16[272,384]{1,0:T(8,128)(2,1)S(1)}, bf16[272,384]{1,0:T(8,128)(2,1)S(1)}, u32[]{:S(2)}, u32[]{:S(2)}) collective-permute-start(bf16[272,384]{1,0:T(8,128)(2,1)S(1)} %get-tuple-element.77.refs_1_), channel_id=1, source_target_pairs={{0,24},{1,25},{2,26},{3,27},{4,28},{5,29},{6,30},{7,31},{8,16},{9,... | collective-permute-start | bytes 626696 | tf_op jit(solution)/shard_map/ppermute | solution.py:46
  54.5 5.2 %collective-permute-done.6.refs_0_ = bf16[256,384]{1,0:T(8,128)(2,1)S(1)} collective-permute-done((bf16[256,384]{1,0:T(8,128)(2,1)S(1)}, bf16[256,384]{1,0:T(8,128)(2,1)S(1)}, u32[]{:S(2)}, u32[]{:S(2)}) %collective-permute-start.6) | collective-permute-done | bytes 196640 | tf_op jit(solution)/shard_map/ppermute | solution.py:46
  60.3 0.7 copy-done.10
  61.0 3.0 %collective-permute-start.11 = (bf16[256,384]{1,0:T(8,128)(2,1)S(1)}, bf16[256,384]{1,0:T(8,128)(2,1)S(1)}, u32[]{:S(2)}, u32[]{:S(2)}) collective-permute-start(bf16[256,384]{1,0:T(8,128)(2,1)S(1)} %get-tuple-element.84.refs_1_), channel_id=1, source_target_pairs={{0,8},{1,3},{2,10},{3,1},{4,12},{5,7},{6,14},{7,5},{8,0},{9,11},{1... | collective-permute-start | bytes 589832 | tf_op jit(solution)/shard_map/ppermute | solution.py:46
  63.9 3.5 %collective-permute-done.8.refs_0_ = bf16[256,384]{1,0:T(8,128)(2,1)S(1)} collective-permute-done((bf16[256,384]{1,0:T(8,128)(2,1)S(1)}, bf16[256,384]{1,0:T(8,128)(2,1)S(1)}, u32[]{:S(2)}, u32[]{:S(2)}) %collective-permute-start.8) | collective-permute-done | bytes 196640 | tf_op jit(solution)/shard_map/ppermute | solution.py:46
  67.8 1.8 %collective-permute-done.11.refs_0_ = bf16[256,384]{1,0:T(8,128)(2,1)S(1)} collective-permute-done((bf16[256,384]{1,0:T(8,128)(2,1)S(1)}, bf16[256,384]{1,0:T(8,128)(2,1)S(1)}, u32[]{:S(2)}, u32[]{:S(2)}) %collective-permute-start.11) | collective-permute-done | bytes 196640 | tf_op jit(solution)/shard_map/ppermute | solution.py:46
  69.7 2.0 %collective-permute-start.10 = (bf16[272,384]{1,0:T(8,128)(2,1)S(1)}, bf16[272,384]{1,0:T(8,128)(2,1)S(1)}, u32[]{:S(2)}, u32[]{:S(2)}) collective-permute-start(bf16[272,384]{1,0:T(8,128)(2,1)S(1)} %get-tuple-element.83.refs_1_), channel_id=1, source_target_pairs={{0,4},{1,9},{2,6},{3,11},{4,0},{5,13},{6,2},{7,15},{8,12},{9,1},{1... | collective-permute-start | bytes 626696 | tf_op jit(solution)/shard_map/ppermute | solution.py:46
  71.7 8.0 %collective-permute-done.10.refs_0_ = bf16[272,384]{1,0:T(8,128)(2,1)S(1)} collective-permute-done((bf16[272,384]{1,0:T(8,128)(2,1)S(1)}, bf16[272,384]{1,0:T(8,128)(2,1)S(1)}, u32[]{:S(2)}, u32[]{:S(2)}) %collective-permute-start.10) | collective-permute-done | bytes 208928 | tf_op jit(solution)/shard_map/ppermute | solution.py:46
  79.7 0.9 join.6
  80.7 1.3 collective-permute-start.15
  81.9 0.8 collective-permute-start.12
  82.7 15.1 %collective-permute-done.12.refs_0_ = bf16[528,384]{1,0:T(8,128)(2,1)S(1)} collective-permute-done((bf16[528,384]{1,0:T(8,128)(2,1)S(1)}, bf16[528,384]{1,0:T(8,128)(2,1)S(1)}, u32[]{:S(2)}, u32[]{:S(2)}) %collective-permute-start.12) | collective-permute-done | bytes 405536 | tf_op jit(solution)/shard_map/ppermute | solution.py:46
  97.8 1.0 join.7
  99.3 1.1 copy.9
  100.5 1.2 fusion.3.refs_0_
  101.7 1.5 %copy-done.7 = bf16[1280,768]{1,0:T(8,128)(2,1)S(1)} copy-done((bf16[1280,768]{1,0:T(8,128)(2,1)S(1)}, bf16[1280,768]{1,0:T(8,128)(2,1)}, u32[]{:S(2)}) %copy-start.7) | copy-done | bytes 1966104
  103.2 1.3 mask.1
  104.6 1.9 %copy-done.3 = bf16[1280,1536]{1,0:T(8,128)(2,1)} copy-done((bf16[1280,1536]{1,0:T(8,128)(2,1)}, bf16[1280,1536]{1,0:T(8,128)(2,1)S(1)}, u32[]{:S(2)}) %copy-start.3) | copy-done | bytes 3932184
  106.6 4.7 %part_scores.2 = (f32[1280,1024]{1,0:T(8,128)S(1)}, f32[8,128]{1,0:T(8,128)S(1)}) custom-call(s32[16]{0:T(128)S(1)} %stack.212.code_ref, bf16[1280,1536]{1,0:T(8,128)(2,1)S(1)} %get-tuple-element.92.refs_0_, bf16[1024,384]{1,0:T(8,128)(2,1)} %get-tuple-element.93.refs_1_, bf16[1024,384]{1,0:T(8,128)(2,1)} %collective-permute-done.17.refs_2_, ...), custom_call_target="tpu_custom_call" | custom-call | flops 1 | bytes 1 | tf_op jit(solution)/shard_map/part_scores/pallas_call | solution.py:292
  111.3 4.7 %part_scores.3 = (f32[1280,1024]{1,0:T(8,128)S(1)}, f32[8,128]{1,0:T(8,128)S(1)}) custom-call(s32[16]{0:T(128)S(1)} %stack.212.code_ref, bf16[1280,1536]{1,0:T(8,128)(2,1)S(1)} %get-tuple-element.92.refs_0_, bf16[1024,384]{1,0:T(8,128)(2,1)} %collective-permute-done.15.refs_1_, ...), custom_call_target="tpu_custom_call", output_to_operand_aliasing={{0}: (4, {})} | custom-call | flops 1 | bytes 1 | tf_op jit(solution)/shard_map/part_scores/pallas_call | solution.py:292
  116.1 2.3 %copy-done.1 = f32[1280,1024]{1,0:T(8,128)} copy-done((f32[1280,1024]{1,0:T(8,128)}, f32[1280,1024]{1,0:T(8,128)S(1)}, u32[]{:S(2)}) %copy-start.1) | copy-done | bytes 5242904
  118.4 2.1 %pass.1 = (bf16[1040,384]{1,0:T(8,128)(2,1)}, f32[8,128]{1,0:T(8,128)}) custom-call(bf16[1040,384]{1,0:T(8,128)(2,1)} %collective-permute-done.14.refs_0_, f32[8,128]{1,0:T(8,128)S(1)} %get-tuple-element.97.refs_1_), custom_call_target="tpu_custom_call" | custom-call | flops 798720 | bytes 1597440 | tf_op jit(solution)/shard_map/pass/pallas_call | solution.py:133
  121.1 1.8 %maximum_bitcast_fusion = f32[1,128,768]{2,1,0:T(8,128)} fusion(f32[128,384]{1,0:T(8,128)} %copy-done.11, f32[128,384]{1,0:T(8,128)} %copy-done.10), kind=kLoop, calls=%fused_computation.6 | loop fusion | flops 98304 | bytes 786432 | tf_op jit(solution)/shard_map/broadcast_in_dim | solution.py:594
  123.2 2.5 %copy-done.2 = f32[1280,1024]{1,0:T(8,128)S(1)} copy-done((f32[1280,1024]{1,0:T(8,128)S(1)}, f32[1280,1024]{1,0:T(8,128)}, u32[]{:S(2)}) %copy-start.2) | copy-done | bytes 5242904
  125.7 2.1 %copy-done.4 = bf16[1280,1536]{1,0:T(8,128)(2,1)S(1)} copy-done((bf16[1280,1536]{1,0:T(8,128)(2,1)S(1)}, bf16[1280,1536]{1,0:T(8,128)(2,1)}, u32[]{:S(2)}) %copy-start.4) | copy-done | bytes 3932184
  127.8 9.7 %final_scores.1 = bf16[1280,1024]{1,0:T(8,128)(2,1)} custom-call(s32[32]{0:T(128)S(1)} %concatenate.107.code_ref, s32[8]{0:T(128)S(1)} %fusion.22.slot_ref, bf16[1280,1536]{1,0:T(8,128)(2,1)S(1)} %copy-done.4, bf16[1280,16]{1,0:T(8,128)(2,1)S(1)} %get-tuple-element.57.pick_ref, f32[16,1024]{1,0:T(8,128)S(1)} %broadcast_in_dim.30.half_ref, ...), custom_call_target="tpu_custom_call" | custom-call | flops 1 | bytes 1 | tf_op jit(solution)/shard_map/final_scores/pallas_call | solution.py:357
  (62 shorter events, 5.5 us)
Async XLA Ops:
  0.6 39.4 %copy-start = (f32[1,1024,768]{2,1,0:T(8,128)S(1)}, f32[1,1024,768]{2,1,0:T(8,128)}, u32[]{:S(2)}) copy-start(f32[1,1024,768]{2,1,0:T(8,128)} %param.9) | copy-start | bytes 9437188
  0.6 5.0 %collective-permute-start.1 = (bf16[1280,768]{1,0:T(8,128)(2,1)}, bf16[1280,768]{1,0:T(8,128)(2,1)}, u32[]{:S(2)}, u32[]{:S(2)}) collective-permute-start(bf16[1280,768]{1,0:T(8,128)(2,1)} %refs_1_.9), channel_id=1, source_target_pairs={{0,1},{1,0},{2,3},{3,2},{4,5},{5,4},{6,7},{7,6},{8,9},{9,8},{10,11... | collective-permute-start | bytes 5898248 | tf_op jit(solution)/shard_map/ppermute | solution.py:46
  3.5 1.3 collective-permute-start
  5.7 1.5 %copy-start.5 = (bf16[1280,768]{1,0:T(8,128)(2,1)S(1)}, bf16[1280,768]{1,0:T(8,128)(2,1)}, u32[]{:S(2)}) copy-start(bf16[1280,768]{1,0:T(8,128)(2,1)} %refs_1_.9) | copy-start | bytes 5898244
  7.2 7.3 %copy-start.6 = (bf16[1280,768]{1,0:T(8,128)(2,1)S(1)}, bf16[1280,768]{1,0:T(8,128)(2,1)}, u32[]{:S(2)}) copy-start(bf16[1280,768]{1,0:T(8,128)(2,1)} %refs_1_.9) | copy-start | bytes 5898244
  11.5 16.3 %collective-permute-start.3 = (bf16[1040,384]{1,0:T(8,128)(2,1)S(1)}, bf16[1040,384]{1,0:T(8,128)(2,1)S(1)}, u32[]{:S(2)}, u32[]{:S(2)}) collective-permute-start(bf16[1040,384]{1,0:T(8,128)(2,1)S(1)} %get-tuple-element.60), channel_id=1, source_target_pairs={{0,2},{1,5},{2,0},{3,7},{4,6},{5,1},{6,4},{7,3},{8,10},{9,13},{10,... | collective-permute-start | bytes 2396168 | tf_op jit(solution)/shard_map/ppermute | solution.py:46
  18.7 17.8 %collective-permute-start.2 = (bf16[1024,384]{1,0:T(8,128)(2,1)S(1)}, bf16[1024,384]{1,0:T(8,128)(2,1)S(1)}, u32[]{:S(2)}, u32[]{:S(2)}) collective-permute-start(bf16[1024,384]{1,0:T(8,128)(2,1)S(1)} %get-tuple-element.58), channel_id=1, source_target_pairs={{0,8},{1,3},{2,10},{3,1},{4,12},{5,7},{6,14},{7,5},{8,0},{9,11},{1... | collective-permute-start | bytes 2359304 | tf_op jit(solution)/shard_map/ppermute | solution.py:46
  28.7 11.4 %collective-permute-start.5 = (bf16[528,384]{1,0:T(8,128)(2,1)}, bf16[528,384]{1,0:T(8,128)(2,1)}, u32[]{:S(2)}, u32[]{:S(2)}) collective-permute-start(bf16[528,384]{1,0:T(8,128)(2,1)} %get-tuple-element.65), channel_id=1, source_target_pairs={{0,4},{1,9},{2,6},{3,11},{4,0},{5,13},{6,2},{7,15},{8,12},{9,1},{1... | collective-permute-start | bytes 1216520 | tf_op jit(solution)/shard_map/ppermute | solution.py:46
  37.4 0.8 copy-start.8
  38.2 0.6 copy-start.12
  38.8 9.3 %collective-permute-start.4 = (bf16[512,384]{1,0:T(8,128)(2,1)}, bf16[512,384]{1,0:T(8,128)(2,1)}, u32[]{:S(2)}, u32[]{:S(2)}) collective-permute-start(bf16[512,384]{1,0:T(8,128)(2,1)} %get-tuple-element.63), channel_id=1, source_target_pairs={{0,2},{1,5},{2,0},{3,7},{4,6},{5,1},{6,4},{7,3},{8,10},{9,13},{10,... | collective-permute-start | bytes 1179656 | tf_op jit(solution)/shard_map/ppermute | solution.py:46
  40.1 0.7 copy-start.13
  41.9 8.3 %collective-permute-start.7 = (bf16[272,384]{1,0:T(8,128)(2,1)S(1)}, bf16[272,384]{1,0:T(8,128)(2,1)S(1)}, u32[]{:S(2)}, u32[]{:S(2)}) collective-permute-start(bf16[272,384]{1,0:T(8,128)(2,1)S(1)} %get-tuple-element.71), channel_id=1, source_target_pairs={{0,8},{1,3},{2,10},{3,1},{4,12},{5,7},{6,14},{7,5},{8,0},{9,11},{1... | collective-permute-start | bytes 626696 | tf_op jit(solution)/shard_map/ppermute | solution.py:46
  43.5 55.8 %copy-start.14 = (s32[1280,1]{0,1:T(1,128)S(1)}, s32[1280,1]{0,1:T(1,128)}, u32[]{:S(2)}) copy-start(s32[1280,1]{0,1:T(1,128)} %param.6) | copy-start | bytes 15364
  48.1 1.0 copy-start.9
  50.3 9.7 %collective-permute-start.9 = (bf16[272,384]{1,0:T(8,128)(2,1)S(1)}, bf16[272,384]{1,0:T(8,128)(2,1)S(1)}, u32[]{:S(2)}, u32[]{:S(2)}) collective-permute-start(bf16[272,384]{1,0:T(8,128)(2,1)S(1)} %get-tuple-element.77.refs_1_), channel_id=1, source_target_pairs={{0,24},{1,25},{2,26},{3,27},{4,28},{5,29},{6,30},{7,31},{8,16},{9,... | collective-permute-start | bytes 626696 | tf_op jit(solution)/shard_map/ppermute | solution.py:46
  54.0 5.7 %collective-permute-start.6 = (bf16[256,384]{1,0:T(8,128)(2,1)S(1)}, bf16[256,384]{1,0:T(8,128)(2,1)S(1)}, u32[]{:S(2)}, u32[]{:S(2)}) collective-permute-start(bf16[256,384]{1,0:T(8,128)(2,1)S(1)} %get-tuple-element.69), channel_id=1, source_target_pairs={{0,4},{1,9},{2,6},{3,11},{4,0},{5,13},{6,2},{7,15},{8,12},{9,1},{1... | collective-permute-start | bytes 589832 | tf_op jit(solution)/shard_map/ppermute | solution.py:46
  59.7 7.7 %collective-permute-start.8 = (bf16[256,384]{1,0:T(8,128)(2,1)S(1)}, bf16[256,384]{1,0:T(8,128)(2,1)S(1)}, u32[]{:S(2)}, u32[]{:S(2)}) collective-permute-start(bf16[256,384]{1,0:T(8,128)(2,1)S(1)} %get-tuple-element.75.refs_1_), channel_id=1, source_target_pairs={{0,24},{1,25},{2,26},{3,27},{4,28},{5,29},{6,30},{7,31},{8,16},{9,... | collective-permute-start | bytes 589832 | tf_op jit(solution)/shard_map/ppermute | solution.py:46
  60.3 0.7 copy-start.10
  61.0 8.6 %collective-permute-start.11 = (bf16[256,384]{1,0:T(8,128)(2,1)S(1)}, bf16[256,384]{1,0:T(8,128)(2,1)S(1)}, u32[]{:S(2)}, u32[]{:S(2)}) collective-permute-start(bf16[256,384]{1,0:T(8,128)(2,1)S(1)} %get-tuple-element.84.refs_1_), channel_id=1, source_target_pairs={{0,8},{1,3},{2,10},{3,1},{4,12},{5,7},{6,14},{7,5},{8,0},{9,11},{1... | collective-permute-start | bytes 589832 | tf_op jit(solution)/shard_map/ppermute | solution.py:46
  67.8 1.8 %copy-start.11 = (f32[128,384]{1,0:T(8,128)}, f32[128,384]{1,0:T(8,128)S(1)}, u32[]{:S(2)}) copy-start(f32[128,384]{1,0:T(8,128)S(1)} %get-tuple-element.101) | copy-start | bytes 589828
  69.6 10.1 %collective-permute-start.13 = (bf16[512,384]{1,0:T(8,128)(2,1)S(1)}, bf16[512,384]{1,0:T(8,128)(2,1)S(1)}, u32[]{:S(2)}, u32[]{:S(2)}) collective-permute-start(bf16[512,384]{1,0:T(8,128)(2,1)S(1)} %get-tuple-element.88.refs_1_), channel_id=1, source_target_pairs={{0,4},{1,9},{2,6},{3,11},{4,0},{5,13},{6,2},{7,15},{8,12},{9,1},{1... | collective-permute-start | bytes 1179656 | tf_op jit(solution)/shard_map/ppermute | solution.py:46
  69.7 10.0 %collective-permute-start.10 = (bf16[272,384]{1,0:T(8,128)(2,1)S(1)}, bf16[272,384]{1,0:T(8,128)(2,1)S(1)}, u32[]{:S(2)}, u32[]{:S(2)}) collective-permute-start(bf16[272,384]{1,0:T(8,128)(2,1)S(1)} %get-tuple-element.83.refs_1_), channel_id=1, source_target_pairs={{0,4},{1,9},{2,6},{3,11},{4,0},{5,13},{6,2},{7,15},{8,12},{9,1},{1... | collective-permute-start | bytes 626696 | tf_op jit(solution)/shard_map/ppermute | solution.py:46
  80.7 18.1 %collective-permute-start.15 = (bf16[1024,384]{1,0:T(8,128)(2,1)}, bf16[1024,384]{1,0:T(8,128)(2,1)}, u32[]{:S(2)}, u32[]{:S(2)}) collective-permute-start(bf16[1024,384]{1,0:T(8,128)(2,1)} %get-tuple-element.93.refs_1_), channel_id=1, source_target_pairs={{0,2},{1,5},{2,0},{3,7},{4,6},{5,1},{6,4},{7,3},{8,10},{9,13},{10,... | collective-permute-start | bytes 2359304 | tf_op jit(solution)/shard_map/ppermute | solution.py:46
  81.9 15.8 %collective-permute-start.12 = (bf16[528,384]{1,0:T(8,128)(2,1)S(1)}, bf16[528,384]{1,0:T(8,128)(2,1)S(1)}, u32[]{:S(2)}, u32[]{:S(2)}) collective-permute-start(bf16[528,384]{1,0:T(8,128)(2,1)S(1)} %get-tuple-element.87.refs_1_), channel_id=1, source_target_pairs={{0,2},{1,5},{2,0},{3,7},{4,6},{5,1},{6,4},{7,3},{8,10},{9,13},{10,... | collective-permute-start | bytes 1216520 | tf_op jit(solution)/shard_map/ppermute | solution.py:46
  98.8 19.6 %collective-permute-start.14 = (bf16[1040,384]{1,0:T(8,128)(2,1)}, bf16[1040,384]{1,0:T(8,128)(2,1)}, u32[]{:S(2)}, u32[]{:S(2)}) collective-permute-start(bf16[1040,384]{1,0:T(8,128)(2,1)} %get-tuple-element.91.rest_2_), channel_id=1, source_target_pairs={{0,8},{1,3},{2,10},{3,1},{4,12},{5,7},{6,14},{7,5},{8,0},{9,11},{1... | collective-permute-start | bytes 2396168 | tf_op jit(solution)/shard_map/ppermute | solution.py:46
  98.8 7.8 %collective-permute-start.17 = (bf16[1024,384]{1,0:T(8,128)(2,1)}, bf16[1024,384]{1,0:T(8,128)(2,1)}, u32[]{:S(2)}, u32[]{:S(2)}) collective-permute-start(bf16[1024,384]{1,0:T(8,128)(2,1)} %get-tuple-element.93.refs_1_), channel_id=1, source_target_pairs={{0,1},{1,0},{2,3},{3,2},{4,5},{5,4},{6,7},{7,6},{8,9},{9,8},{10,11... | collective-permute-start | bytes 2359304 | tf_op jit(solution)/shard_map/ppermute | solution.py:46
  98.8 12.5 %collective-permute-start.16 = (bf16[1024,384]{1,0:T(8,128)(2,1)}, bf16[1024,384]{1,0:T(8,128)(2,1)}, u32[]{:S(2)}, u32[]{:S(2)}) collective-permute-start(bf16[1024,384]{1,0:T(8,128)(2,1)} %collective-permute-done.15.refs_1_), channel_id=1, source_target_pairs={{0,1},{1,0},{2,3},{3,2},{4,5},{5,4},{6,7},{7,6},{8,9},{9,8},{10,11... | collective-permute-start | bytes 2359304 | tf_op jit(solution)/shard_map/ppermute | solution.py:46
  101.6 1.5 %copy-start.7 = (bf16[1280,768]{1,0:T(8,128)(2,1)S(1)}, bf16[1280,768]{1,0:T(8,128)(2,1)}, u32[]{:S(2)}) copy-start(bf16[1280,768]{1,0:T(8,128)(2,1)} %refs_1_.9) | copy-start | bytes 5898244
  104.5 1.9 %copy-start.3 = (bf16[1280,1536]{1,0:T(8,128)(2,1)}, bf16[1280,1536]{1,0:T(8,128)(2,1)S(1)}, u32[]{:S(2)}) copy-start(bf16[1280,1536]{1,0:T(8,128)(2,1)S(1)} %get-tuple-element.56.masked_ref) | copy-start | bytes 11796484
  106.5 16.4 %collective-permute-start.19 = (bf16[1040,384]{1,0:T(8,128)(2,1)}, bf16[1040,384]{1,0:T(8,128)(2,1)}, u32[]{:S(2)}, u32[]{:S(2)}) collective-permute-start(bf16[1040,384]{1,0:T(8,128)(2,1)} %get-tuple-element.91.rest_2_), channel_id=1, source_target_pairs={{0,1},{1,0},{2,3},{3,2},{4,5},{5,4},{6,7},{7,6},{8,9},{9,8},{10,11... | collective-permute-start | bytes 2396168 | tf_op jit(solution)/shard_map/ppermute | solution.py:46
  116.1 2.3 %copy-start.1 = (f32[1280,1024]{1,0:T(8,128)}, f32[1280,1024]{1,0:T(8,128)S(1)}, u32[]{:S(2)}) copy-start(f32[1280,1024]{1,0:T(8,128)S(1)} %get-tuple-element.99.rest_4_.rest_5_) | copy-start | bytes 15728644
  120.5 2.7 %collective-permute-start.18 = (bf16[1040,384]{1,0:T(8,128)(2,1)}, bf16[1040,384]{1,0:T(8,128)(2,1)}, u32[]{:S(2)}, u32[]{:S(2)}) collective-permute-start(bf16[1040,384]{1,0:T(8,128)(2,1)} %get-tuple-element.98.rest_0_), channel_id=1, source_target_pairs={{0,1},{1,0},{2,3},{3,2},{4,5},{5,4},{6,7},{7,6},{8,9},{9,8},{10,11... | collective-permute-start | bytes 2396168 | tf_op jit(solution)/shard_map/ppermute | solution.py:46
  123.2 2.5 %copy-start.2 = (f32[1280,1024]{1,0:T(8,128)S(1)}, f32[1280,1024]{1,0:T(8,128)}, u32[]{:S(2)}) copy-start(f32[1280,1024]{1,0:T(8,128)} %copy-done.1) | copy-start | bytes 15728644
  125.7 2.1 %copy-start.4 = (bf16[1280,1536]{1,0:T(8,128)(2,1)S(1)}, bf16[1280,1536]{1,0:T(8,128)(2,1)}, u32[]{:S(2)}) copy-start(bf16[1280,1536]{1,0:T(8,128)(2,1)} %copy-done.3) | copy-start | bytes 11796484

commit v5 on v4

--- a/solution.py
+++ b/solution.py
@@ -127,15 +127,15 @@
     )(pos_row, own, other, *extra, token)
 
 
-def small_call(kernel, name, outs, token, *args):
+def small_call(kernel, name, outs, token, *args, scalars=0, limit=4):
     whole = pl.BlockSpec(memory_space=pltpu.VMEM)
     moved = sum(a.size * a.dtype.itemsize for a in (*args, *outs))
     return pl.pallas_call(
         hand_on(kernel, len(args)),
         out_shape=[*outs, token_shape()],
-        in_specs=[whole] * (len(args) + 1),
-        out_specs=[whole] * (len(outs) + 1),
-        compiler_params=pltpu.CompilerParams(vmem_limit_bytes=12 << 20),
+        in_specs=[pl.BlockSpec(memory_space=pltpu.SMEM)] * scalars + [whole] * (len(args) + 1 - scalars),
+        out_specs=[whole if limit < 16 else pl.BlockSpec()] * len(outs) + [whole],
+        compiler_params=pltpu.CompilerParams(vmem_limit_bytes=limit << 20),
         cost_estimate=pl.CostEstimate(flops=moved // 2, bytes_accessed=moved, transcendentals=0),
         name=name,
     )(*args, token)
@@ -202,7 +202,7 @@
             fresh_out[...] = fresh
 
 
-def last_kernel(share, tail, got_ref, sent_ref, near_ref, scale_ref, norm_ref, fresh_out, cents_out):
+def last_kernel(share, tail, got_ref, sent_ref, near_ref, scale_ref, norm_ref, first_ref, fresh_out, cents_out):
     two = 2 * share
     wide = got_ref.shape[1]
     lane = lax.broadcasted_iota(jnp.int32, (share, wide), 1)
@@ -215,7 +215,9 @@
         rounded = fresh.astype(BF16)
         cents_out[part, :] = rounded
         if block == 1:
-            fresh_out[...] = fresh
+            before = first_ref.shape[1]
+            fresh_out[:, :before] = first_ref[...]
+            fresh_out[:, before:] = fresh
         norm = 0.5 * (norm_ref[part, :] + square_sums(rounded))
         spread = jnp.zeros((1, wide), F32)
         for term_at in range(PARTS):
@@ -236,20 +238,32 @@
         out_ref[2 * body :, :] = (held_ref[body:, :].astype(F32) + moved).astype(BF16)
 
 
-def pass_kernel(in_ref, out_ref):
-    out_ref[...] = in_ref[...]
-
-
-def mask_kernel(groups, columns, gid_ref, x_ref, *outs):
-    gid = gid_ref[...]
-    for (start, wide), out in zip(columns, outs):
-        x = x_ref[:, start : start + wide]
-        for group in range(groups):
-            out[:, group * wide : (group + 1) * wide] = jnp.where(gid == group, x, jnp.zeros_like(x))
-    pick = outs[-1]
-    lane = lax.broadcasted_iota(jnp.int32, pick.shape, 1)
-    hit = (lane % groups == gid) & (lane < PARTS * groups)
-    pick[...] = jnp.where(hit, -1.0, 0.0).astype(BF16)
+def behind(array, token):
+    def kernel(in_ref, token_ref, out_ref):
+        del in_ref, token_ref, out_ref
+
+    return pl.pallas_call(
+        kernel,
+        out_shape=jax.ShapeDtypeStruct(array.shape, array.dtype),
+        in_specs=[pl.BlockSpec(memory_space=pl.ANY)] * 2,
+        out_specs=pl.BlockSpec(memory_space=pl.ANY),
+        input_output_aliases={0: 0},
+        compiler_params=pltpu.CompilerParams(vmem_limit_bytes=1 << 20),
+        cost_estimate=pl.CostEstimate(flops=1, bytes_accessed=1, transcendentals=0),
+        name="behind",
+    )(array, token)
+
+
+def mask_kernel(groups, start, wide, live_ref, label_ref, x_ref, out_ref, *pick_out):
+    row = lax.broadcasted_iota(jnp.int32, label_ref.shape, 0)
+    gid = jnp.where(row < live_ref[0], label_ref[...], -1)
+    x = x_ref[:, start : start + wide]
+    for group in range(groups):
+        out_ref[:, group * wide : (group + 1) * wide] = jnp.where(gid == group, x, jnp.zeros_like(x))
+    for pick_ref in pick_out:
+        lane = lax.broadcasted_iota(jnp.int32, pick_ref.shape, 1)
+        hit = (lane % groups == gid) & (lane < PARTS * groups)
+        pick_ref[...] = jnp.where(hit, -1.0, 0.0).astype(BF16)
 
 
 def product(a, b):
@@ -300,7 +314,7 @@
         ),
         out_shape=[jax.ShapeDtypeStruct((rows, keys), F32), token_shape()],
         input_output_aliases={} if before is None else {4: 0},
-        compiler_params=pltpu.CompilerParams(vmem_limit_bytes=16 << 20),
+        compiler_params=pltpu.CompilerParams(vmem_limit_bytes=46 << 20),
         cost_estimate=pl.CostEstimate(flops=1, bytes_accessed=1, transcendentals=0),
         name="part_scores",
     )(codes, masked, *pieces, *extra, token)
@@ -309,7 +323,8 @@
 def final_kernel(groups, share, code_ref, slot_ref, masked_ref, pick_ref, half_ref, *rest):
     pieces = 4
     piece_refs, total_refs = rest[:pieces], rest[pieces : pieces + 2]
-    out_ref, cents, half = rest[-3:]
+    out_ref, cents, half, rows_of, sem = rest[-5:]
+    load = pltpu.make_async_copy(masked_ref, rows_of, sem)
     keys = cents.shape[0]
     wide = cents.shape[1] // groups
     members = keys // share
@@ -318,6 +333,7 @@
 
     @pl.when(pl.program_id(0) == 0)
     def _():
+        load.start()
         half[...] = half_ref[...]
         for piece, ref in enumerate(piece_refs):
             for block in range(blocks):
@@ -337,10 +353,11 @@
                         row = tail[at : at + 1, term * share : (term + 1) * share]
                         filled = jnp.where(line == group + term * groups, row, filled)
                     half[:, lines] = filled
+        load.wait()
 
     step = out_ref.shape[1]
     start = pl.multiple_of(pl.program_id(0) * step, step)
-    dots = product(masked_ref[...], cents[pl.ds(start, step), :])
+    dots = product(rows_of[...], cents[pl.ds(start, step), :])
     offsets = half[:, pl.ds(start, step)].astype(BF16)
     dots += jnp.dot(pick_ref[...], offsets, preferred_element_type=F32)
     cut = step // 2
@@ -359,16 +376,22 @@
         grid_spec=pltpu.PrefetchScalarGridSpec(
             num_scalar_prefetch=2,
             grid=(keys // step,),
-            in_specs=[whole] * (3 + len(pieces))
+            in_specs=[pl.BlockSpec(memory_space=pl.ANY)]
+            + [whole] * (2 + len(pieces))
             + [
                 pl.BlockSpec((rows, cut), lambda i, c, s: (0, s[2 * i])),
                 pl.BlockSpec((rows, cut), lambda i, c, s: (0, s[2 * i + 1])),
             ],
             out_specs=pl.BlockSpec((rows, step), lambda i, c, s: (0, i)),
-            scratch_shapes=[pltpu.VMEM((keys, groups * wide), BF16), pltpu.VMEM(half.shape, F32)],
+            scratch_shapes=[
+                pltpu.VMEM((keys, groups * wide), BF16),
+                pltpu.VMEM(half.shape, F32),
+                pltpu.VMEM(masked.shape, BF16),
+                pltpu.SemaphoreType.DMA,
+            ],
         ),
         out_shape=jax.ShapeDtypeStruct((rows, keys), BF16),
-        compiler_params=pltpu.CompilerParams(vmem_limit_bytes=16 << 20),
+        compiler_params=pltpu.CompilerParams(vmem_limit_bytes=50 << 20),
         cost_estimate=pl.CostEstimate(flops=1, bytes_accessed=1, transcendentals=0),
         name="final_scores",
     )(codes, slots, masked, pick, half, *pieces, total, total)
@@ -495,14 +518,45 @@
             fresh[1], held[1], tokens[stream] = small_call(
                 functools.partial(last_kernel, share, tail),
                 "last_centroids",
-                [share_f32[1], bf(2, 1, 1)],
+                [jax.ShapeDtypeStruct((share, width), F32), bf(2, 1, 1)],
                 pick_token(stream),
                 got,
                 send[1],
                 near[1],
                 scale,
                 norm,
+                fresh[0],
             )
+    half_blocks = blocks // 2
+    quarter = half_blocks // groups
+    inner_of = [[dim for dim in turned[c, 0] if dim[1]] for c in range(2)]
+
+    def mask_rows(token, stream, more):
+        start, wide = columns[stream]
+        return small_call(
+            functools.partial(mask_kernel, groups, start, wide),
+            "mask",
+            [jax.ShapeDtypeStruct((rows, groups * wide), BF16), *more],
+            token,
+            live_rows,
+            coarse_label,
+            samples,
+            scalars=1,
+            limit=52 if stream else 4,
+        )
+
+    def part_codes(part):
+        codes = []
+        for flip in range(2):
+            for block in range(half_blocks):
+                code = []
+                for c in range(2):
+                    group_rel, member_rel = relative_of(part * half_blocks + block, turned[c, 0])
+                    spot = block_position(0, member_rel, inner_of[c], outer_bits) % quarter
+                    code.append((spot + flip * quarter) * groups + (z ^ group_rel))
+                codes.append(jnp.where(core ^ flip == 0, *code))
+        return jnp.stack(codes).astype(jnp.int32)
+
     count = 2
     arrived = [None] * 2
     for stage in reversed(range(stages - 1)):
@@ -519,9 +573,12 @@
                 )
             else:
                 arrived[stream] = got
+            if (stage, stream) == (1, 0):
+                masked, tokens[0] = mask_rows(tokens[0], 0, [])
+                total, tokens[0] = part_scores(
+                    tokens[0], masked, part_codes(1), [held[0], sibling(held[0])], None, groups, keys, share
+                )
         count *= 2
-
-    half_blocks = blocks // 2
 
     def codes_of(stream, part, flip):
         codes = []
@@ -533,37 +590,11 @@
             codes.append((z ^ group_rel) * members + (me ^ flip ^ member_rel))
         return jnp.stack(codes).astype(jnp.int32)
 
-    gid = jnp.where(live, coarse_label[:, 0], -1)[:, None]
-    *masked, pick, token = small_call(
-        functools.partial(mask_kernel, groups, columns),
-        "mask",
-        [jax.ShapeDtypeStruct((rows, groups * wide), BF16) for _, wide in columns]
-        + [jax.ShapeDtypeStruct((rows, TILE), BF16)],
-        token,
-        gid,
-        samples,
+    total, token = part_scores(
+        tokens[1], masked, part_codes(0), [arrived[0], sibling(arrived[0])], total, groups, keys, share
     )
-
-    quarter = half_blocks // groups
-    inner_of = [[dim for dim in turned[c, 0] if dim[1]] for c in range(2)]
-    total = None
-    for part, piece in ((1, held[0]), (0, arrived[0])):
-        part_codes = []
-        for flip in range(2):
-            for block in range(half_blocks):
-                code = []
-                for c in range(2):
-                    group_rel, member_rel = relative_of(part * half_blocks + block, turned[c, 0])
-                    spot = block_position(0, member_rel, inner_of[c], outer_bits) % quarter
-                    code.append((spot + flip * quarter) * groups + (z ^ group_rel))
-                part_codes.append(jnp.where(core ^ flip == 0, *code))
-        total, token = part_scores(
-            token, masked[0], jnp.stack(part_codes).astype(jnp.int32), [piece, sibling(piece)], total, groups, keys, share
-        )
-
-    last, token = small_call(
-        pass_kernel, "pass", [jax.ShapeDtypeStruct(arrived[1].shape, BF16)], token, arrived[1]
-    )
+    masked, pick, token = mask_rows(token, 1, [jax.ShapeDtypeStruct((rows, TILE), BF16)])
+    last = behind(arrived[1], token)
     every = jnp.arange(members, dtype=jnp.int32)
     flip_of = (every ^ me) & 1
     spot = jnp.where(
@@ -590,8 +621,8 @@
         move = (lane[:, None] == source[None, :]).astype(F32)
         total = jnp.dot(total, move, precision=lax.Precision.HIGHEST)
         slots = jnp.arange(keys // 128, dtype=jnp.int32)
-    scores = final_scores(masked[1], pick, codes, slots, flat, total, half, groups, keys, share)
-    return scores, jnp.concatenate(fresh, axis=1)[None]
+    scores = final_scores(masked, pick, codes, slots, flat, total, half, groups, keys, share)
+    return scores, fresh[1][None]
 
 
 def solution(mesh):

time: 138 us -> 129 us (0.935)
  local copies, waits for them, and re-layouts: 17 us -> 9.29 us
  Pallas kernels: 46.1 us -> 53.6 us
  waiting for transfers between devices: 42.9 us -> 37.7 us
  other arithmetic: 4.78 us -> 1.99 us
    unnamed x32 -> x22, local copies, waits for them, and re-layouts: 16.8 us -> 9.02 us
    ppermute x20, waiting for transfers between devices: 42.9 us -> 37.7 us  [exchange(): return lax.ppermute(array, AXES, pairs)]
    pallas_call x14, Pallas kernels: 10.1 us -> 13.6 us  [small_call(): pl.pallas_call(hand_on(kernel, len(args)), out_shape=[*outs, token_shape(...]
    pallas_call x1, Pallas kernels: 9.71 us -> 11.6 us  [final_scores(): pl.pallas_call(functools.partial(final_kernel, groups, share), grid_spec=...]
    broadcast_in_dim x1 -> x0, other arithmetic: 1.79 us -> none  [per_device(): return (scores, jnp.concatenate(fresh, axis=1)[None])]
    pallas_call x2, Pallas kernels: 9.49 us -> 11.1 us  [part_scores(): pl.pallas_call(kernel, grid_spec=pltpu.PrefetchScalarGridSpec(num_scalar_...]
  transfers between devices with their start and end apart: 20 -> 20, of which waited for: 9 -> 10; matrix products, arithmetic and copies ran while one was open for 5% -> 2% of each run, Pallas kernels for 23% -> 29%
where the time goes in v5:
time: 129 us; the launch traced here: 128 us
  Pallas kernels  53.6 us (42%)
  waiting for transfers between devices  37.7 us (29%)
  starting transfers between devices  23.6 us (18%)
  local copies, waits for them, and re-layouts  9.29 us (7%)
  other arithmetic  1.99 us (2%)
  between operations  1.77 us (1%)
    ppermute x20, waiting for transfers between devices, exchange(): return lax.ppermute(array, AXES, pairs)  37.7 us
    ppermute x20, starting transfers between devices, exchange(): return lax.ppermute(array, AXES, pairs)  23.6 us
    pallas_call x4, Pallas kernels, key_sums(): pl.pallas_call(hand_on(functools.partial(sums_kernel, base), 3 + len(extr...  17.3 us
    pallas_call x14, Pallas kernels, small_call(): pl.pallas_call(hand_on(kernel, len(args)), out_shape=[*outs, token_shape(...  13.6 us
    pallas_call x1, Pallas kernels, final_scores(): pl.pallas_call(functools.partial(final_kernel, groups, share), grid_spec=...  11.6 us
    pallas_call x2, Pallas kernels, part_scores(): pl.pallas_call(kernel, grid_spec=pltpu.PrefetchScalarGridSpec(num_scalar_...  11.1 us
    unnamed x22, local copies, waits for them, and re-layouts  9.02 us
  transfers between devices with their start and end apart: 20, of which 10 were waited for; matrix products, arithmetic and copies ran while one was open for 2% of the time, Pallas kernels for 29%

profile of v5, /device:TPU:0, one launch (start us, length us, event | category | flops | bytes accessed | tf_op | source)
XLA Modules:
  0.0 128.5 jit_solution(10054950748833741335)
XLA Ops:
  1.4 0.9 multiply_reduce_fusion
  2.3 0.7 add_select_fusion.9
  3.5 0.8 collective-permute-done
  4.3 0.6 fusion.15
  5.3 2.5 %collective-permute-done.1.refs_2_ = bf16[1280,768]{1,0:T(8,128)(2,1)} collective-permute-done((bf16[1280,768]{1,0:T(8,128)(2,1)}, bf16[1280,768]{1,0:T(8,128)(2,1)}, u32[]{:S(2)}, u32[]{:S(2)}) %collective-permute-start.1) | collective-permute-done | bytes 1966112 | tf_op jit(solution)/shard_map/ppermute | solution.py:46
  7.8 1.5 %copy-done.1 = bf16[1280,768]{1,0:T(8,128)(2,1)S(1)} copy-done((bf16[1280,768]{1,0:T(8,128)(2,1)S(1)}, bf16[1280,768]{1,0:T(8,128)(2,1)}, u32[]{:S(2)}) %copy-start.1) | copy-done | bytes 1966104
  9.3 4.3 %key_sums.4 = (bf16[1040,384]{1,0:T(8,128)(2,1)S(1)}, f32[8,128]{1,0:T(8,128)S(1)}) custom-call(s32[1,2560]{1,0:T(1,128)S(1)} %fusion.10.refs_0_, bf16[1280,768]{1,0:T(8,128)(2,1)S(1)} %copy-done.1, bf16[1280,768]{1,0:T(8,128)(2,1)} %collective-permute-done.1.refs_2_, bf16[16,384]{1,0:T(8,128)(2,1)S(1)} %pad_maximum_fusion.refs_3_, ...), custom_call_target="tpu_custom_call" | custom-call | flops 2013265920 | bytes 2752512 | tf_op jit(solution)/shard_map/key_sums/pallas_call | solution.py:110
  13.6 2.7 %collective-permute-start.2 = (bf16[1040,384]{1,0:T(8,128)(2,1)S(1)}, bf16[1040,384]{1,0:T(8,128)(2,1)S(1)}, u32[]{:S(2)}, u32[]{:S(2)}) collective-permute-start(bf16[1040,384]{1,0:T(8,128)(2,1)S(1)} %get-tuple-element.52), channel_id=1, source_target_pairs={{0,2},{1,5},{2,0},{3,7},{4,6},{5,1},{6,4},{7,3},{8,10},{9,13},{10,... | collective-permute-start | bytes 2396168 | tf_op jit(solution)/shard_map/ppermute | solution.py:46
  16.3 4.2 %key_sums.5 = (bf16[1024,384]{1,0:T(8,128)(2,1)S(1)}, f32[8,128]{1,0:T(8,128)S(1)}) custom-call(s32[1,2560]{1,0:T(1,128)S(1)} %get-tuple-element.102.refs_0_, bf16[1280,768]{1,0:T(8,128)(2,1)S(1)} %copy-done.2, bf16[1280,768]{1,0:T(8,128)(2,1)} %collective-permute-done.1.refs_2_, f32[8,128]{1,0:T(8,128)S(1)} %get-tuple-element.53.refs_3_), custom_call_target="tpu_custom_call" | custom-call | flops 2013265920 | bytes 2752512 | tf_op jit(solution)/shard_map/key_sums/pallas_call | solution.py:110
  20.5 1.6 %collective-permute-start.4 = (bf16[1024,384]{1,0:T(8,128)(2,1)S(1)}, bf16[1024,384]{1,0:T(8,128)(2,1)S(1)}, u32[]{:S(2)}, u32[]{:S(2)}) collective-permute-start(bf16[1024,384]{1,0:T(8,128)(2,1)S(1)} %get-tuple-element.58), channel_id=1, source_target_pairs={{0,8},{1,3},{2,10},{3,1},{4,12},{5,7},{6,14},{7,5},{8,0},{9,11},{1... | collective-permute-start | bytes 2359304 | tf_op jit(solution)/shard_map/ppermute | solution.py:46
  22.1 4.2 %key_sums.6 = (bf16[1040,384]{1,0:T(8,128)(2,1)S(1)}, f32[8,128]{1,0:T(8,128)S(1)}) custom-call(s32[1,2560]{1,0:T(1,128)S(1)} %fusion.10.refs_0_, bf16[1280,768]{1,0:T(8,128)(2,1)S(1)} %copy-done.2, bf16[1280,768]{1,0:T(8,128)(2,1)} %collective-permute-done.1.refs_2_, bf16[16,384]{1,0:T(8,128)(2,1)S(1)} %pad_maximum_fusion.refs_3_, ...), custom_call_target="tpu_custom_call" | custom-call | flops 2013265920 | bytes 2752512 | tf_op jit(solution)/shard_map/key_sums/pallas_call | solution.py:110
  26.3 3.3 %collective-permute-done.2.refs_0_ = bf16[1040,384]{1,0:T(8,128)(2,1)S(1)} collective-permute-done((bf16[1040,384]{1,0:T(8,128)(2,1)S(1)}, bf16[1040,384]{1,0:T(8,128)(2,1)S(1)}, u32[]{:S(2)}, u32[]{:S(2)}) %collective-permute-start.2) | collective-permute-done | bytes 798752 | tf_op jit(solution)/shard_map/ppermute | solution.py:46
  29.6 0.8 fold.4
  30.4 3.7 %collective-permute-start.3 = (bf16[528,384]{1,0:T(8,128)(2,1)}, bf16[528,384]{1,0:T(8,128)(2,1)}, u32[]{:S(2)}, u32[]{:S(2)}) collective-permute-start(bf16[528,384]{1,0:T(8,128)(2,1)} %get-tuple-element.56), channel_id=1, source_target_pairs={{0,4},{1,9},{2,6},{3,11},{4,0},{5,13},{6,2},{7,15},{8,12},{9,1},{1... | collective-permute-start | bytes 1216520 | tf_op jit(solution)/shard_map/ppermute | solution.py:46
  34.1 4.7 %key_sums.7 = (bf16[1024,384]{1,0:T(8,128)(2,1)S(1)}, f32[8,128]{1,0:T(8,128)}) custom-call(s32[1,2560]{1,0:T(1,128)S(1)} %get-tuple-element.102.refs_0_, bf16[1280,768]{1,0:T(8,128)(2,1)S(1)} %copy-done.2, bf16[1280,768]{1,0:T(8,128)(2,1)} %collective-permute-done.1.refs_2_, f32[8,128]{1,0:T(8,128)S(1)} %get-tuple-element.59.refs_3_), custom_call_target="tpu_custom_call" | custom-call | flops 2013265920 | bytes 2752512 | tf_op jit(solution)/shard_map/key_sums/pallas_call | solution.py:110
  38.8 0.9 fold.5
  39.7 0.8 copy-done.6
  40.4 1.3 collective-permute-start.6
  41.8 1.1 fold.6
  42.9 1.6 %collective-permute-start.5 = (bf16[272,384]{1,0:T(8,128)(2,1)S(1)}, bf16[272,384]{1,0:T(8,128)(2,1)S(1)}, u32[]{:S(2)}, u32[]{:S(2)}) collective-permute-start(bf16[272,384]{1,0:T(8,128)(2,1)S(1)} %get-tuple-element.63), channel_id=1, source_target_pairs={{0,8},{1,3},{2,10},{3,1},{4,12},{5,7},{6,14},{7,5},{8,0},{9,11},{1... | collective-permute-start | bytes 626696 | tf_op jit(solution)/shard_map/ppermute | solution.py:46
  44.5 4.0 %collective-permute-done.6.refs_0_ = bf16[512,384]{1,0:T(8,128)(2,1)} collective-permute-done((bf16[512,384]{1,0:T(8,128)(2,1)}, bf16[512,384]{1,0:T(8,128)(2,1)}, u32[]{:S(2)}, u32[]{:S(2)}) %collective-permute-start.6) | collective-permute-done | bytes 393248 | tf_op jit(solution)/shard_map/ppermute | solution.py:46
  48.5 1.0 copy-done.7
  49.5 1.1 fold.7
  50.7 3.6 %collective-permute-start.7 = (bf16[272,384]{1,0:T(8,128)(2,1)S(1)}, bf16[272,384]{1,0:T(8,128)(2,1)S(1)}, u32[]{:S(2)}, u32[]{:S(2)}) collective-permute-start(bf16[272,384]{1,0:T(8,128)(2,1)S(1)} %get-tuple-element.69.refs_1_), channel_id=1, source_target_pairs={{0,24},{1,25},{2,26},{3,27},{4,28},{5,29},{6,30},{7,31},{8,16},{9,... | collective-permute-start | bytes 626696 | tf_op jit(solution)/shard_map/ppermute | solution.py:46
  54.8 5.1 %collective-permute-done.8.refs_0_ = bf16[256,384]{1,0:T(8,128)(2,1)S(1)} collective-permute-done((bf16[256,384]{1,0:T(8,128)(2,1)S(1)}, bf16[256,384]{1,0:T(8,128)(2,1)S(1)}, u32[]{:S(2)}, u32[]{:S(2)}) %collective-permute-start.8) | collective-permute-done | bytes 196640 | tf_op jit(solution)/shard_map/ppermute | solution.py:46
  60.9 1.1 collective-permute-start.9
  62.0 5.7 %collective-permute-done.10.refs_0_ = bf16[256,384]{1,0:T(8,128)(2,1)S(1)} collective-permute-done((bf16[256,384]{1,0:T(8,128)(2,1)S(1)}, bf16[256,384]{1,0:T(8,128)(2,1)S(1)}, u32[]{:S(2)}, u32[]{:S(2)}) %collective-permute-start.10) | collective-permute-done | bytes 196640 | tf_op jit(solution)/shard_map/ppermute | solution.py:46
  67.7 1.0 last_centroids.1
  68.7 1.4 %collective-permute-start.11 = (bf16[512,384]{1,0:T(8,128)(2,1)S(1)}, bf16[512,384]{1,0:T(8,128)(2,1)S(1)}, u32[]{:S(2)}, u32[]{:S(2)}) collective-permute-start(bf16[512,384]{1,0:T(8,128)(2,1)S(1)} %get-tuple-element.83.refs_1_), channel_id=1, source_target_pairs={{0,4},{1,9},{2,6},{3,11},{4,0},{5,13},{6,2},{7,15},{8,12},{9,1},{1... | collective-permute-start | bytes 1179656 | tf_op jit(solution)/shard_map/ppermute | solution.py:46
  70.1 0.7 collective-permute-start.12
  70.8 8.0 %collective-permute-done.12.refs_0_ = bf16[272,384]{1,0:T(8,128)(2,1)S(1)} collective-permute-done((bf16[272,384]{1,0:T(8,128)(2,1)S(1)}, bf16[272,384]{1,0:T(8,128)(2,1)S(1)}, u32[]{:S(2)}, u32[]{:S(2)}) %collective-permute-start.12) | collective-permute-done | bytes 208928 | tf_op jit(solution)/shard_map/ppermute | solution.py:46
  78.9 0.9 join.6
  79.8 0.6 copy-done.8
  80.4 1.5 %collective-permute-start.13 = (bf16[1024,384]{1,0:T(8,128)(2,1)}, bf16[1024,384]{1,0:T(8,128)(2,1)}, u32[]{:S(2)}, u32[]{:S(2)}) collective-permute-start(bf16[1024,384]{1,0:T(8,128)(2,1)} %get-tuple-element.89.refs_1_), channel_id=1, source_target_pairs={{0,2},{1,5},{2,0},{3,7},{4,6},{5,1},{6,4},{7,3},{8,10},{9,13},{10,... | collective-permute-start | bytes 2359304 | tf_op jit(solution)/shard_map/ppermute | solution.py:46
  82.5 1.8 %copy.12.refs_1_ = s32[1280,1]{1,0:T(8,128)} copy(s32[1280,1]{0,1:T(1,128)} %param.6) | data formatting | bytes 10240 | tf_op args[1]
  84.4 1.5 %copy-done.3 = bf16[1280,768]{1,0:T(8,128)(2,1)S(1)} copy-done((bf16[1280,768]{1,0:T(8,128)(2,1)S(1)}, bf16[1280,768]{1,0:T(8,128)(2,1)}, u32[]{:S(2)}) %copy-start.3) | copy-done | bytes 1966104
  85.9 1.1 copy-done.4
  87.0 0.7 copy-done.9
  87.7 0.8 mask.2
  88.5 5.7 %part_scores.2 = (f32[1280,1024]{1,0:T(8,128)}, f32[8,128]{1,0:T(8,128)S(1)}) custom-call(s32[16]{0:T(128)S(1)} %stack.212.code_ref, bf16[1280,1536]{1,0:T(8,128)(2,1)S(1)} %get-tuple-element.88.refs_0_, bf16[1024,384]{1,0:T(8,128)(2,1)} %get-tuple-element.89.refs_1_, bf16[1024,384]{1,0:T(8,128)(2,1)} %collective-permute-done.15.refs_2_, ...), custom_call_target="tpu_custom_call" | custom-call | flops 1 | bytes 1 | tf_op jit(solution)/shard_map/part_scores/pallas_call | solution.py:306
  94.2 2.9 %collective-permute-done.16.refs_0_ = bf16[528,384]{1,0:T(8,128)(2,1)} collective-permute-done((bf16[528,384]{1,0:T(8,128)(2,1)S(1)}, bf16[528,384]{1,0:T(8,128)(2,1)}, u32[]{:S(2)}, u32[]{:S(2)}) %collective-permute-start.16) | collective-permute-done | bytes 405536 | tf_op jit(solution)/shard_map/ppermute | solution.py:46
  97.1 2.0 %join.7 = (bf16[1040,384]{1,0:T(8,128)(2,1)}, f32[8,128]{1,0:T(8,128)S(1)}) custom-call(bf16[528,384]{1,0:T(8,128)(2,1)} %collective-permute-done.16.refs_0_, bf16[528,384]{1,0:T(8,128)(2,1)S(1)} %get-tuple-element.92.refs_1_, f32[8,128]{1,0:T(8,128)S(1)} %get-tuple-element.93.refs_2_), custom_call_target="tpu_custom_call" | custom-call | flops 804864 | bytes 1609728 | tf_op jit(solution)/shard_map/join/pallas_call | solution.py:133
  99.1 1.8 %collective-permute-start.17 = (bf16[1040,384]{1,0:T(8,128)(2,1)}, bf16[1040,384]{1,0:T(8,128)(2,1)}, u32[]{:S(2)}, u32[]{:S(2)}) collective-permute-start(bf16[1040,384]{1,0:T(8,128)(2,1)} %get-tuple-element.98.rest_2_), channel_id=1, source_target_pairs={{0,8},{1,3},{2,10},{3,1},{4,12},{5,7},{6,14},{7,5},{8,0},{9,11},{1... | collective-permute-start | bytes 2396168 | tf_op jit(solution)/shard_map/ppermute | solution.py:46
  101.3 3.1 %collective-permute-done.14.refs_2_ = bf16[1024,384]{1,0:T(8,128)(2,1)S(1)} collective-permute-done((bf16[1024,384]{1,0:T(8,128)(2,1)}, bf16[1024,384]{1,0:T(8,128)(2,1)S(1)}, u32[]{:S(2)}, u32[]{:S(2)}) %collective-permute-start.14) | collective-permute-done | bytes 786464 | tf_op jit(solution)/shard_map/ppermute | solution.py:46
  104.4 5.4 %part_scores.3 = (f32[1280,1024]{1,0:T(8,128)}, f32[8,128]{1,0:T(8,128)S(1)}) custom-call(s32[16]{0:T(128)S(1)} %stack.212.code_ref, bf16[1280,1536]{1,0:T(8,128)(2,1)S(1)} %get-tuple-element.88.refs_0_, bf16[1024,384]{1,0:T(8,128)(2,1)} %collective-permute-done.13.refs_1_, ...), custom_call_target="tpu_custom_call", output_to_operand_aliasing={{0}: (4, {})} | custom-call | flops 1 | bytes 1 | tf_op jit(solution)/shard_map/part_scores/pallas_call | solution.py:306
  109.8 4.3 %mask.3 = (bf16[1280,1536]{1,0:T(8,128)(2,1)}, bf16[1280,16]{1,0:T(8,128)(2,1)S(1)}, f32[8,128]{1,0:T(8,128)S(1)}) custom-call(s32[1]{0:T(128)} %copy.16.refs_0_, s32[1280,1]{1,0:T(8,128)S(1)} %copy-done.5, bf16[1280,768]{1,0:T(8,128)(2,1)} %refs_2_.3, f32[8,128]{1,0:T(8,128)S(1)} %get-tuple-element.95.refs_3_), custom_call_target="tpu_custom_call" | custom-call | flops 2972162 | bytes 5944324 | tf_op jit(solution)/shard_map/mask/pallas_call | solution.py:133
  114.4 2.4 %collective-permute-done.18.rest_1_ = bf16[1040,384]{1,0:T(8,128)(2,1)} collective-permute-done((bf16[1040,384]{1,0:T(8,128)(2,1)}, bf16[1040,384]{1,0:T(8,128)(2,1)}, u32[]{:S(2)}, u32[]{:S(2)}) %collective-permute-start.18) | collective-permute-done | bytes 798752 | tf_op jit(solution)/shard_map/ppermute | solution.py:46
  116.8 11.6 %final_scores.1 = bf16[1280,1024]{1,0:T(8,128)(2,1)} custom-call(s32[32]{0:T(128)S(1)} %concatenate.104.code_ref, s32[8]{0:T(128)S(1)} %fusion.21.slot_ref, bf16[1280,1536]{1,0:T(8,128)(2,1)} %get-tuple-element.96.masked_ref, bf16[1280,16]{1,0:T(8,128)(2,1)S(1)} %get-tuple-element.97.pick_ref, f32[16,1024]{1,0:T(8,128)S(1)} %broadcast_in_dim.25.half_ref, ...), custom_call_target="tpu_custom_call" | custom-call | flops 1 | bytes 1 | tf_op jit(solution)/shard_map/final_scores/pallas_call | solution.py:374
  (51 shorter events, 4.1 us)
Async XLA Ops:
  0.6 41.1 %copy-start = (f32[1,1024,768]{2,1,0:T(8,128)S(1)}, f32[1,1024,768]{2,1,0:T(8,128)}, u32[]{:S(2)}) copy-start(f32[1,1024,768]{2,1,0:T(8,128)} %param.9) | copy-start | bytes 9437188
  3.0 1.3 collective-permute-start
  3.5 4.3 %collective-permute-start.1 = (bf16[1280,768]{1,0:T(8,128)(2,1)}, bf16[1280,768]{1,0:T(8,128)(2,1)}, u32[]{:S(2)}, u32[]{:S(2)}) collective-permute-start(bf16[1280,768]{1,0:T(8,128)(2,1)} %refs_2_.3), channel_id=1, source_target_pairs={{0,1},{1,0},{2,3},{3,2},{4,5},{5,4},{6,7},{7,6},{8,9},{9,8},{10,11... | collective-permute-start | bytes 5898248 | tf_op jit(solution)/shard_map/ppermute | solution.py:46
  7.8 1.5 %copy-start.1 = (bf16[1280,768]{1,0:T(8,128)(2,1)S(1)}, bf16[1280,768]{1,0:T(8,128)(2,1)}, u32[]{:S(2)}) copy-start(bf16[1280,768]{1,0:T(8,128)(2,1)} %refs_2_.3) | copy-start | bytes 5898244
  9.3 7.0 %copy-start.2 = (bf16[1280,768]{1,0:T(8,128)(2,1)S(1)}, bf16[1280,768]{1,0:T(8,128)(2,1)}, u32[]{:S(2)}) copy-start(bf16[1280,768]{1,0:T(8,128)(2,1)} %refs_2_.3) | copy-start | bytes 5898244
  13.6 15.9 %collective-permute-start.2 = (bf16[1040,384]{1,0:T(8,128)(2,1)S(1)}, bf16[1040,384]{1,0:T(8,128)(2,1)S(1)}, u32[]{:S(2)}, u32[]{:S(2)}) collective-permute-start(bf16[1040,384]{1,0:T(8,128)(2,1)S(1)} %get-tuple-element.52), channel_id=1, source_target_pairs={{0,2},{1,5},{2,0},{3,7},{4,6},{5,1},{6,4},{7,3},{8,10},{9,13},{10,... | collective-permute-start | bytes 2396168 | tf_op jit(solution)/shard_map/ppermute | solution.py:46
  20.5 18.3 %collective-permute-start.4 = (bf16[1024,384]{1,0:T(8,128)(2,1)S(1)}, bf16[1024,384]{1,0:T(8,128)(2,1)S(1)}, u32[]{:S(2)}, u32[]{:S(2)}) collective-permute-start(bf16[1024,384]{1,0:T(8,128)(2,1)S(1)} %get-tuple-element.58), channel_id=1, source_target_pairs={{0,8},{1,3},{2,10},{3,1},{4,12},{5,7},{6,14},{7,5},{8,0},{9,11},{1... | collective-permute-start | bytes 2359304 | tf_op jit(solution)/shard_map/ppermute | solution.py:46
  30.4 11.3 %collective-permute-start.3 = (bf16[528,384]{1,0:T(8,128)(2,1)}, bf16[528,384]{1,0:T(8,128)(2,1)}, u32[]{:S(2)}, u32[]{:S(2)}) collective-permute-start(bf16[528,384]{1,0:T(8,128)(2,1)} %get-tuple-element.56), channel_id=1, source_target_pairs={{0,4},{1,9},{2,6},{3,11},{4,0},{5,13},{6,2},{7,15},{8,12},{9,1},{1... | collective-permute-start | bytes 1216520 | tf_op jit(solution)/shard_map/ppermute | solution.py:46
  39.7 0.8 copy-start.6
  40.4 8.1 %collective-permute-start.6 = (bf16[512,384]{1,0:T(8,128)(2,1)}, bf16[512,384]{1,0:T(8,128)(2,1)}, u32[]{:S(2)}, u32[]{:S(2)}) collective-permute-start(bf16[512,384]{1,0:T(8,128)(2,1)} %get-tuple-element.65), channel_id=1, source_target_pairs={{0,2},{1,5},{2,0},{3,7},{4,6},{5,1},{6,4},{7,3},{8,10},{9,13},{10,... | collective-permute-start | bytes 1179656 | tf_op jit(solution)/shard_map/ppermute | solution.py:46
  42.9 7.8 %collective-permute-start.5 = (bf16[272,384]{1,0:T(8,128)(2,1)S(1)}, bf16[272,384]{1,0:T(8,128)(2,1)S(1)}, u32[]{:S(2)}, u32[]{:S(2)}) collective-permute-start(bf16[272,384]{1,0:T(8,128)(2,1)S(1)} %get-tuple-element.63), channel_id=1, source_target_pairs={{0,8},{1,3},{2,10},{3,1},{4,12},{5,7},{6,14},{7,5},{8,0},{9,11},{1... | collective-permute-start | bytes 626696 | tf_op jit(solution)/shard_map/ppermute | solution.py:46
  48.5 1.0 copy-start.7
  50.7 9.7 %collective-permute-start.7 = (bf16[272,384]{1,0:T(8,128)(2,1)S(1)}, bf16[272,384]{1,0:T(8,128)(2,1)S(1)}, u32[]{:S(2)}, u32[]{:S(2)}) collective-permute-start(bf16[272,384]{1,0:T(8,128)(2,1)S(1)} %get-tuple-element.69.refs_1_), channel_id=1, source_target_pairs={{0,24},{1,25},{2,26},{3,27},{4,28},{5,29},{6,30},{7,31},{8,16},{9,... | collective-permute-start | bytes 626696 | tf_op jit(solution)/shard_map/ppermute | solution.py:46
  54.3 5.7 %collective-permute-start.8 = (bf16[256,384]{1,0:T(8,128)(2,1)S(1)}, bf16[256,384]{1,0:T(8,128)(2,1)S(1)}, u32[]{:S(2)}, u32[]{:S(2)}) collective-permute-start(bf16[256,384]{1,0:T(8,128)(2,1)S(1)} %get-tuple-element.71), channel_id=1, source_target_pairs={{0,4},{1,9},{2,6},{3,11},{4,0},{5,13},{6,2},{7,15},{8,12},{9,1},{1... | collective-permute-start | bytes 589832 | tf_op jit(solution)/shard_map/ppermute | solution.py:46
  60.0 7.7 %collective-permute-start.10 = (bf16[256,384]{1,0:T(8,128)(2,1)S(1)}, bf16[256,384]{1,0:T(8,128)(2,1)S(1)}, u32[]{:S(2)}, u32[]{:S(2)}) collective-permute-start(bf16[256,384]{1,0:T(8,128)(2,1)S(1)} %get-tuple-element.76.refs_1_), channel_id=1, source_target_pairs={{0,24},{1,25},{2,26},{3,27},{4,28},{5,29},{6,30},{7,31},{8,16},{9,... | collective-permute-start | bytes 589832 | tf_op jit(solution)/shard_map/ppermute | solution.py:46
  60.9 7.8 %collective-permute-start.9 = (bf16[256,384]{1,0:T(8,128)(2,1)S(1)}, bf16[256,384]{1,0:T(8,128)(2,1)S(1)}, u32[]{:S(2)}, u32[]{:S(2)}) collective-permute-start(bf16[256,384]{1,0:T(8,128)(2,1)S(1)} %get-tuple-element.75.refs_1_), channel_id=1, source_target_pairs={{0,8},{1,3},{2,10},{3,1},{4,12},{5,7},{6,14},{7,5},{8,0},{9,11},{1... | collective-permute-start | bytes 589832 | tf_op jit(solution)/shard_map/ppermute | solution.py:46
  68.7 10.1 %collective-permute-start.11 = (bf16[512,384]{1,0:T(8,128)(2,1)S(1)}, bf16[512,384]{1,0:T(8,128)(2,1)S(1)}, u32[]{:S(2)}, u32[]{:S(2)}) collective-permute-start(bf16[512,384]{1,0:T(8,128)(2,1)S(1)} %get-tuple-element.83.refs_1_), channel_id=1, source_target_pairs={{0,4},{1,9},{2,6},{3,11},{4,0},{5,13},{6,2},{7,15},{8,12},{9,1},{1... | collective-permute-start | bytes 1179656 | tf_op jit(solution)/shard_map/ppermute | solution.py:46
  70.1 8.7 %collective-permute-start.12 = (bf16[272,384]{1,0:T(8,128)(2,1)S(1)}, bf16[272,384]{1,0:T(8,128)(2,1)S(1)}, u32[]{:S(2)}, u32[]{:S(2)}) collective-permute-start(bf16[272,384]{1,0:T(8,128)(2,1)S(1)} %get-tuple-element.84.refs_1_), channel_id=1, source_target_pairs={{0,4},{1,9},{2,6},{3,11},{4,0},{5,13},{6,2},{7,15},{8,12},{9,1},{1... | collective-permute-start | bytes 626696 | tf_op jit(solution)/shard_map/ppermute | solution.py:46
  79.8 0.6 copy-start.8
  80.4 8.1 %collective-permute-start.15 = (bf16[1024,384]{1,0:T(8,128)(2,1)}, bf16[1024,384]{1,0:T(8,128)(2,1)}, u32[]{:S(2)}, u32[]{:S(2)}) collective-permute-start(bf16[1024,384]{1,0:T(8,128)(2,1)} %get-tuple-element.89.refs_1_), channel_id=1, source_target_pairs={{0,1},{1,0},{2,3},{3,2},{4,5},{5,4},{6,7},{7,6},{8,9},{9,8},{10,11... | collective-permute-start | bytes 2359304 | tf_op jit(solution)/shard_map/ppermute | solution.py:46
  80.4 20.4 %collective-permute-start.13 = (bf16[1024,384]{1,0:T(8,128)(2,1)}, bf16[1024,384]{1,0:T(8,128)(2,1)}, u32[]{:S(2)}, u32[]{:S(2)}) collective-permute-start(bf16[1024,384]{1,0:T(8,128)(2,1)} %get-tuple-element.89.refs_1_), channel_id=1, source_target_pairs={{0,2},{1,5},{2,0},{3,7},{4,6},{5,1},{6,4},{7,3},{8,10},{9,13},{10,... | collective-permute-start | bytes 2359304 | tf_op jit(solution)/shard_map/ppermute | solution.py:46
  81.9 15.2 %collective-permute-start.16 = (bf16[528,384]{1,0:T(8,128)(2,1)S(1)}, bf16[528,384]{1,0:T(8,128)(2,1)}, u32[]{:S(2)}, u32[]{:S(2)}) collective-permute-start(bf16[528,384]{1,0:T(8,128)(2,1)S(1)} %get-tuple-element.92.refs_1_), channel_id=1, source_target_pairs={{0,2},{1,5},{2,0},{3,7},{4,6},{5,1},{6,4},{7,3},{8,10},{9,13},{10,... | collective-permute-start | bytes 1216520 | tf_op jit(solution)/shard_map/ppermute | solution.py:46
  84.3 1.6 %copy-start.3 = (bf16[1280,768]{1,0:T(8,128)(2,1)S(1)}, bf16[1280,768]{1,0:T(8,128)(2,1)}, u32[]{:S(2)}) copy-start(bf16[1280,768]{1,0:T(8,128)(2,1)} %refs_2_.3) | copy-start | bytes 5898244
  85.9 1.1 copy-start.4
  87.0 0.7 copy-start.9
  99.1 15.1 %collective-permute-start.17 = (bf16[1040,384]{1,0:T(8,128)(2,1)}, bf16[1040,384]{1,0:T(8,128)(2,1)}, u32[]{:S(2)}, u32[]{:S(2)}) collective-permute-start(bf16[1040,384]{1,0:T(8,128)(2,1)} %get-tuple-element.98.rest_2_), channel_id=1, source_target_pairs={{0,8},{1,3},{2,10},{3,1},{4,12},{5,7},{6,14},{7,5},{8,0},{9,11},{1... | collective-permute-start | bytes 2396168 | tf_op jit(solution)/shard_map/ppermute | solution.py:46
  100.8 3.6 %collective-permute-start.14 = (bf16[1024,384]{1,0:T(8,128)(2,1)}, bf16[1024,384]{1,0:T(8,128)(2,1)S(1)}, u32[]{:S(2)}, u32[]{:S(2)}) collective-permute-start(bf16[1024,384]{1,0:T(8,128)(2,1)} %collective-permute-done.13.refs_1_), channel_id=1, source_target_pairs={{0,1},{1,0},{2,3},{3,2},{4,5},{5,4},{6,7},{7,6},{8,9},{9,8},{10,11... | collective-permute-start | bytes 2359304 | tf_op jit(solution)/shard_map/ppermute | solution.py:46
  100.8 13.6 %collective-permute-start.19 = (bf16[1040,384]{1,0:T(8,128)(2,1)}, bf16[1040,384]{1,0:T(8,128)(2,1)}, u32[]{:S(2)}, u32[]{:S(2)}) collective-permute-start(bf16[1040,384]{1,0:T(8,128)(2,1)} %get-tuple-element.98.rest_2_), channel_id=1, source_target_pairs={{0,1},{1,0},{2,3},{3,2},{4,5},{5,4},{6,7},{7,6},{8,9},{9,8},{10,11... | collective-permute-start | bytes 2396168 | tf_op jit(solution)/shard_map/ppermute | solution.py:46
  104.4 5.4 %copy-start.5 = (s32[1280,1]{1,0:T(8,128)S(1)}, s32[1280,1]{1,0:T(8,128)}, u32[]{:S(2)}) copy-start(s32[1280,1]{1,0:T(8,128)} %copy.12.refs_1_) | copy-start | bytes 15364
  114.1 2.6 %collective-permute-start.18 = (bf16[1040,384]{1,0:T(8,128)(2,1)}, bf16[1040,384]{1,0:T(8,128)(2,1)}, u32[]{:S(2)}, u32[]{:S(2)}) collective-permute-start(bf16[1040,384]{1,0:T(8,128)(2,1)} %behind.1.rest_0_), channel_id=1, source_target_pairs={{0,1},{1,0},{2,3},{3,2},{4,5},{5,4},{6,7},{7,6},{8,9},{9,8},{10,11... | collective-permute-start | bytes 2396168 | tf_op jit(solution)/shard_map/ppermute | solution.py:46

commit v6 on v5

--- a/solution.py
+++ b/solution.py
@@ -32,8 +32,8 @@
     found = {}
     found[0, 0] = inner + outer
     found[1, 0] = other[:cut] + outer[:1] + other[cut:] + outer[1:]
-    found[0, 1] = outer[:1] + inner + outer[1:]
-    found[1, 1] = inner + outer
+    found[0, 1] = found[1, 0]
+    found[1, 1] = inner[:cut] + outer[:1] + inner[cut:] + outer[1:]
     return found
 
 
@@ -254,16 +254,17 @@
     )(array, token)
 
 
-def mask_kernel(groups, start, wide, live_ref, label_ref, x_ref, out_ref, *pick_out):
+def mask_kernel(groups, columns, live_ref, label_ref, x_ref, *outs):
     row = lax.broadcasted_iota(jnp.int32, label_ref.shape, 0)
     gid = jnp.where(row < live_ref[0], label_ref[...], -1)
-    x = x_ref[:, start : start + wide]
-    for group in range(groups):
-        out_ref[:, group * wide : (group + 1) * wide] = jnp.where(gid == group, x, jnp.zeros_like(x))
-    for pick_ref in pick_out:
-        lane = lax.broadcasted_iota(jnp.int32, pick_ref.shape, 1)
-        hit = (lane % groups == gid) & (lane < PARTS * groups)
-        pick_ref[...] = jnp.where(hit, -1.0, 0.0).astype(BF16)
+    for (start, wide), out_ref in zip(columns, outs):
+        x = x_ref[:, start : start + wide]
+        for group in range(groups):
+            out_ref[:, group * wide : (group + 1) * wide] = jnp.where(gid == group, x, jnp.zeros_like(x))
+    pick_ref = outs[len(columns)]
+    lane = lax.broadcasted_iota(jnp.int32, pick_ref.shape, 1)
+    hit = (lane % groups == gid) & (lane < PARTS * groups)
+    pick_ref[...] = jnp.where(hit, -1.0, 0.0).astype(BF16)
 
 
 def product(a, b):
@@ -271,21 +272,24 @@
 
 
 def part_kernel(groups, share, code_ref, masked_ref, own_ref, other_ref, *rest):
-    out_ref, cents = rest[-2:]
+    out_ref, cents, rows_of, sem = rest
+    load = pltpu.make_async_copy(masked_ref, rows_of, sem)
     wide = own_ref.shape[1]
     blocks = own_ref.shape[0] // share
 
     @pl.when(pl.program_id(0) == 0)
     def _():
+        load.start()
         for piece, ref in enumerate((own_ref, other_ref)):
             for block in range(blocks):
                 code = code_ref[piece * blocks + block]
                 slot = pl.multiple_of(code // groups * share, share)
                 cents[pl.ds(slot, share), pl.ds(pl.multiple_of(code % groups * wide, 128), wide)] = ref[block * share : (block + 1) * share, :]
+        load.wait()
 
     step = out_ref.shape[1]
     start = pl.multiple_of(pl.program_id(0) * step, step)
-    out_ref[...] = product(masked_ref[...], cents[pl.ds(start, step), :])
+    out_ref[...] = product(rows_of[...], cents[pl.ds(start, step), :])
 
 
 def part_scores(token, masked, codes, pieces, before, groups, keys, share):
@@ -297,10 +301,11 @@
     at = 0 if before is None else steps
     whole = pl.BlockSpec(memory_space=pltpu.VMEM)
     extra = [] if before is None else [before]
+    anywhere = pl.BlockSpec(memory_space=pl.ANY)
 
     def kernel(code_ref, *refs):
         count = 3 + len(extra)
-        part_kernel(groups, share, code_ref, *refs[:3], refs[count + 1], refs[-1])
+        part_kernel(groups, share, code_ref, *refs[:3], refs[count + 1], *refs[-3:])
         refs[count + 2][...] = refs[count][...]
 
     return pl.pallas_call(
@@ -308,13 +313,17 @@
         grid_spec=pltpu.PrefetchScalarGridSpec(
             num_scalar_prefetch=1,
             grid=(steps,),
-            in_specs=[whole] * 3 + [pl.BlockSpec(memory_space=pl.ANY)] * len(extra) + [whole],
+            in_specs=[anywhere] + [whole] * 2 + [anywhere] * len(extra) + [whole],
             out_specs=[pl.BlockSpec((rows, step), lambda i, w: (0, i + at)), whole],
-            scratch_shapes=[pltpu.VMEM((half, groups * wide), BF16)],
+            scratch_shapes=[
+                pltpu.VMEM((half, groups * wide), BF16),
+                pltpu.VMEM(masked.shape, BF16),
+                pltpu.SemaphoreType.DMA,
+            ],
         ),
         out_shape=[jax.ShapeDtypeStruct((rows, keys), F32), token_shape()],
         input_output_aliases={} if before is None else {4: 0},
-        compiler_params=pltpu.CompilerParams(vmem_limit_bytes=46 << 20),
+        compiler_params=pltpu.CompilerParams(vmem_limit_bytes=51 << 20),
         cost_estimate=pl.CostEstimate(flops=1, bytes_accessed=1, transcendentals=0),
         name="part_scores",
     )(codes, masked, *pieces, *extra, token)
@@ -468,7 +477,11 @@
             )
 
     tokens = [start_token] * 2
-    pick_token = lambda stream: tokens[1 - stream]
+    own_turn = (2, 3, 4)
+
+    def step_token(step, stream):
+        return tokens[stream if stream == 0 and step in own_turn else 1 - stream]
+
     old_share = lax.dynamic_slice(old_centroids[0], (me * share, 0), (share, width))
 
     def bf(count, stream, tailed):
@@ -486,7 +499,7 @@
                     functools.partial(fold_kernel, count // 2 * share, count),
                     "fold",
                     [bf(count // 2, stream, 0)] * 2,
-                    pick_token(stream),
+                    step_token(stage, stream),
                     got,
                     keep[stream],
                 )
@@ -495,7 +508,7 @@
                     functools.partial(seed_kernel, share, count),
                     "seed",
                     [bf(2, stream, 0), share_f32[stream]],
-                    pick_token(stream),
+                    step_token(stage, stream),
                     got,
                     keep[stream],
                     old_share[:, start : start + wide],
@@ -509,7 +522,7 @@
                 functools.partial(first_kernel, share, base, digits),
                 "first_centroids",
                 [share_f32[0], bf(2, 0, 1), column, column],
-                pick_token(stream),
+                step_token(stages - 1, stream),
                 got,
                 send[0],
                 near[0],
@@ -519,7 +532,7 @@
                 functools.partial(last_kernel, share, tail),
                 "last_centroids",
                 [jax.ShapeDtypeStruct((share, width), F32), bf(2, 1, 1)],
-                pick_token(stream),
+                step_token(stages - 1, stream),
                 got,
                 send[1],
                 near[1],
@@ -530,20 +543,6 @@
     half_blocks = blocks // 2
     quarter = half_blocks // groups
     inner_of = [[dim for dim in turned[c, 0] if dim[1]] for c in range(2)]
-
-    def mask_rows(token, stream, more):
-        start, wide = columns[stream]
-        return small_call(
-            functools.partial(mask_kernel, groups, start, wide),
-            "mask",
-            [jax.ShapeDtypeStruct((rows, groups * wide), BF16), *more],
-            token,
-            live_rows,
-            coarse_label,
-            samples,
-            scalars=1,
-            limit=52 if stream else 4,
-        )
 
     def part_codes(part):
         codes = []
@@ -567,16 +566,28 @@
                     functools.partial(join_kernel, count * share, count),
                     "join",
                     [bf(2 * count, stream, 1)],
-                    pick_token(stream),
+                    step_token(2 * stages - 2 - stage, stream),
                     got,
                     held[stream],
                 )
             else:
                 arrived[stream] = got
+            if (stage, stream) == (stages - 2, 0):
+                *masked, pick, tokens[0] = small_call(
+                    functools.partial(mask_kernel, groups, columns),
+                    "mask",
+                    [jax.ShapeDtypeStruct((rows, groups * wide), BF16) for _, wide in columns]
+                    + [jax.ShapeDtypeStruct((rows, TILE), BF16)],
+                    tokens[0],
+                    live_rows,
+                    coarse_label,
+                    samples,
+                    scalars=1,
+                    limit=48,
+                )
             if (stage, stream) == (1, 0):
-                masked, tokens[0] = mask_rows(tokens[0], 0, [])
                 total, tokens[0] = part_scores(
-                    tokens[0], masked, part_codes(1), [held[0], sibling(held[0])], None, groups, keys, share
+                    tokens[0], masked[0], part_codes(1), [held[0], sibling(held[0])], None, groups, keys, share
                 )
         count *= 2
 
@@ -591,9 +602,8 @@
         return jnp.stack(codes).astype(jnp.int32)
 
     total, token = part_scores(
-        tokens[1], masked, part_codes(0), [arrived[0], sibling(arrived[0])], total, groups, keys, share
+        tokens[1], masked[0], part_codes(0), [arrived[0], sibling(arrived[0])], total, groups, keys, share
     )
-    masked, pick, token = mask_rows(token, 1, [jax.ShapeDtypeStruct((rows, TILE), BF16)])
     last = behind(arrived[1], token)
     every = jnp.arange(members, dtype=jnp.int32)
     flip_of = (every ^ me) & 1
@@ -621,7 +631,7 @@
         move = (lane[:, None] == source[None, :]).astype(F32)
         total = jnp.dot(total, move, precision=lax.Precision.HIGHEST)
         slots = jnp.arange(keys // 128, dtype=jnp.int32)
-    scores = final_scores(masked, pick, codes, slots, flat, total, half, groups, keys, share)
+    scores = final_scores(masked[1], pick, codes, slots, flat, total, half, groups, keys, share)
     return scores, fresh[1][None]
 
 

time: 129 us -> 135 us (1.047)
  waiting for transfers between devices: 37.7 us -> 27.3 us
  Pallas kernels: 53.6 us -> 61.2 us
  starting transfers between devices: 23.6 us -> 29.5 us
  local copies, waits for them, and re-layouts: 9.29 us -> 11.5 us
    ppermute x20, waiting for transfers between devices: 37.7 us -> 27.3 us  [exchange(): return lax.ppermute(array, AXES, pairs)]
    ppermute x20, starting transfers between devices: 23.6 us -> 29.5 us  [exchange(): return lax.ppermute(array, AXES, pairs)]
    pallas_call x2, Pallas kernels: 11.1 us -> 15.3 us  [part_scores(): pl.pallas_call(kernel, grid_spec=pltpu.PrefetchScalarGridSpec(num_scalar_...]
    pallas_call x14 -> x13, Pallas kernels: 13.6 us -> 16.2 us  [small_call(): pl.pallas_call(hand_on(kernel, len(args)), out_shape=[*outs, token_shape(...]
    unnamed x22 -> x34, local copies, waits for them, and re-layouts: 9.02 us -> 11.2 us
  transfers between devices with their start and end apart: 20 -> 20, of which waited for: 10 -> 11; matrix products, arithmetic and copies ran while one was open for 2% -> 2% of each run, Pallas kernels for 29% -> 32%
where the time goes in v6:
time: 135 us; the launch traced here: 134 us
  Pallas kernels  61.2 us (45%)
  starting transfers between devices  29.5 us (22%)
  waiting for transfers between devices  27.3 us (20%)
  local copies, waits for them, and re-layouts  11.5 us (9%)
  other arithmetic  1.99 us (1%)
  between operations  1.86 us (1%)
    ppermute x20, starting transfers between devices, exchange(): return lax.ppermute(array, AXES, pairs)  29.5 us
    ppermute x20, waiting for transfers between devices, exchange(): return lax.ppermute(array, AXES, pairs)  27.3 us
    pallas_call x4, Pallas kernels, key_sums(): pl.pallas_call(hand_on(functools.partial(sums_kernel, base), 3 + len(extr...  18.2 us
    pallas_call x13, Pallas kernels, small_call(): pl.pallas_call(hand_on(kernel, len(args)), out_shape=[*outs, token_shape(...  16.2 us
    pallas_call x2, Pallas kernels, part_scores(): pl.pallas_call(kernel, grid_spec=pltpu.PrefetchScalarGridSpec(num_scalar_...  15.3 us
    pallas_call x1, Pallas kernels, final_scores(): pl.pallas_call(functools.partial(final_kernel, groups, share), grid_spec=...  11.6 us
    unnamed x34, local copies, waits for them, and re-layouts  11.2 us
  transfers between devices with their start and end apart: 20, of which 11 were waited for; matrix products, arithmetic and copies ran while one was open for 2% of the time, Pallas kernels for 32%

profile of v6, /device:TPU:0, one launch (start us, length us, event | category | flops | bytes accessed | tf_op | source)
XLA Modules:
  0.0 133.9 jit_solution(12694769416528146018)
XLA Ops:
  1.4 0.9 multiply_reduce_fusion
  2.3 0.7 add_select_fusion.9
  3.5 0.8 collective-permute-done
  5.3 2.5 %collective-permute-done.1.refs_2_ = bf16[1280,768]{1,0:T(8,128)(2,1)} collective-permute-done((bf16[1280,768]{1,0:T(8,128)(2,1)}, bf16[1280,768]{1,0:T(8,128)(2,1)}, u32[]{:S(2)}, u32[]{:S(2)}) %collective-permute-start.1) | collective-permute-done | bytes 1966112 | tf_op jit(solution)/shard_map/ppermute | solution.py:46
  7.8 1.5 %copy-done.2 = bf16[1280,768]{1,0:T(8,128)(2,1)S(1)} copy-done((bf16[1280,768]{1,0:T(8,128)(2,1)S(1)}, bf16[1280,768]{1,0:T(8,128)(2,1)}, u32[]{:S(2)}) %copy-start.2) | copy-done | bytes 1966104
  9.3 4.3 %key_sums.4 = (bf16[1040,384]{1,0:T(8,128)(2,1)S(1)}, f32[8,128]{1,0:T(8,128)S(1)}) custom-call(s32[1,2560]{1,0:T(1,128)S(1)} %fusion.10.refs_0_, bf16[1280,768]{1,0:T(8,128)(2,1)S(1)} %copy-done.2, bf16[1280,768]{1,0:T(8,128)(2,1)} %collective-permute-done.1.refs_2_, bf16[16,384]{1,0:T(8,128)(2,1)S(1)} %pad_maximum_fusion.refs_3_, ...), custom_call_target="tpu_custom_call" | custom-call | flops 2013265920 | bytes 2752512 | tf_op jit(solution)/shard_map/key_sums/pallas_call | solution.py:110
  13.6 2.7 %collective-permute-start.2 = (bf16[1040,384]{1,0:T(8,128)(2,1)S(1)}, bf16[1040,384]{1,0:T(8,128)(2,1)S(1)}, u32[]{:S(2)}, u32[]{:S(2)}) collective-permute-start(bf16[1040,384]{1,0:T(8,128)(2,1)S(1)} %get-tuple-element.48), channel_id=1, source_target_pairs={{0,2},{1,5},{2,0},{3,7},{4,6},{5,1},{6,4},{7,3},{8,10},{9,13},{10,... | collective-permute-start | bytes 2396168 | tf_op jit(solution)/shard_map/ppermute | solution.py:46
  16.3 5.0 %key_sums.5 = (bf16[1024,384]{1,0:T(8,128)(2,1)}, f32[8,128]{1,0:T(8,128)S(1)}) custom-call(s32[1,2560]{1,0:T(1,128)S(1)} %get-tuple-element.94.refs_0_, bf16[1280,768]{1,0:T(8,128)(2,1)S(1)} %copy-done.3, bf16[1280,768]{1,0:T(8,128)(2,1)} %collective-permute-done.1.refs_2_, f32[8,128]{1,0:T(8,128)S(1)} %get-tuple-element.49.refs_3_), custom_call_target="tpu_custom_call" | custom-call | flops 2013265920 | bytes 2752512 | tf_op jit(solution)/shard_map/key_sums/pallas_call | solution.py:110
  21.4 1.5 %collective-permute-start.4 = (bf16[1024,384]{1,0:T(8,128)(2,1)}, bf16[1024,384]{1,0:T(8,128)(2,1)}, u32[]{:S(2)}, u32[]{:S(2)}) collective-permute-start(bf16[1024,384]{1,0:T(8,128)(2,1)} %get-tuple-element.54), channel_id=1, source_target_pairs={{0,4},{1,3},{2,6},{3,1},{4,0},{5,7},{6,2},{7,5},{8,12},{9,11},{10,... | collective-permute-start | bytes 2359304 | tf_op jit(solution)/shard_map/ppermute | solution.py:46
  22.9 4.2 %key_sums.6 = (bf16[1040,384]{1,0:T(8,128)(2,1)S(1)}, f32[8,128]{1,0:T(8,128)S(1)}) custom-call(s32[1,2560]{1,0:T(1,128)S(1)} %fusion.10.refs_0_, bf16[1280,768]{1,0:T(8,128)(2,1)S(1)} %copy-done.3, bf16[1280,768]{1,0:T(8,128)(2,1)} %collective-permute-done.1.refs_2_, bf16[16,384]{1,0:T(8,128)(2,1)S(1)} %pad_maximum_fusion.refs_3_, ...), custom_call_target="tpu_custom_call" | custom-call | flops 2013265920 | bytes 2752512 | tf_op jit(solution)/shard_map/key_sums/pallas_call | solution.py:110
  27.1 1.5 %collective-permute-done.2.refs_0_ = bf16[1040,384]{1,0:T(8,128)(2,1)S(1)} collective-permute-done((bf16[1040,384]{1,0:T(8,128)(2,1)S(1)}, bf16[1040,384]{1,0:T(8,128)(2,1)S(1)}, u32[]{:S(2)}, u32[]{:S(2)}) %collective-permute-start.2) | collective-permute-done | bytes 798752 | tf_op jit(solution)/shard_map/ppermute | solution.py:46
  28.5 0.9 fold.4
  29.4 3.7 %collective-permute-start.3 = (bf16[528,384]{1,0:T(8,128)(2,1)}, bf16[528,384]{1,0:T(8,128)(2,1)}, u32[]{:S(2)}, u32[]{:S(2)}) collective-permute-start(bf16[528,384]{1,0:T(8,128)(2,1)} %get-tuple-element.52), channel_id=1, source_target_pairs={{0,4},{1,9},{2,6},{3,11},{4,0},{5,13},{6,2},{7,15},{8,12},{9,1},{1... | collective-permute-start | bytes 1216520 | tf_op jit(solution)/shard_map/ppermute | solution.py:46
  33.2 1.5 %copy-done.4 = bf16[1280,768]{1,0:T(8,128)(2,1)S(1)} copy-done((bf16[1280,768]{1,0:T(8,128)(2,1)S(1)}, bf16[1280,768]{1,0:T(8,128)(2,1)}, u32[]{:S(2)}) %copy-start.4) | copy-done | bytes 1966104
  34.7 0.7 copy-done.11
  36.1 4.7 %key_sums.7 = (bf16[1024,384]{1,0:T(8,128)(2,1)S(1)}, f32[8,128]{1,0:T(8,128)}) custom-call(s32[1,2560]{1,0:T(1,128)S(1)} %copy-done.11, bf16[1280,768]{1,0:T(8,128)(2,1)S(1)} %copy-done.4, bf16[1280,768]{1,0:T(8,128)(2,1)} %collective-permute-done.1.refs_2_, f32[8,128]{1,0:T(8,128)S(1)} %copy-done.15), custom_call_target="tpu_custom_call" | custom-call | flops 2013265920 | bytes 2752512 | tf_op jit(solution)/shard_map/key_sums/pallas_call | solution.py:110
  40.8 1.3 fold.5
  42.1 1.4 %collective-permute-start.8 = (bf16[512,384]{1,0:T(8,128)(2,1)S(1)}, bf16[512,384]{1,0:T(8,128)(2,1)S(1)}, u32[]{:S(2)}, u32[]{:S(2)}) collective-permute-start(bf16[512,384]{1,0:T(8,128)(2,1)S(1)} %get-tuple-element.70), channel_id=1, source_target_pairs={{0,8},{1,9},{2,10},{3,11},{4,12},{5,13},{6,14},{7,15},{8,0},{9,1},... | collective-permute-start | bytes 1179656 | tf_op jit(solution)/shard_map/ppermute | solution.py:46
  43.5 1.1 fold.6
  44.6 0.7 collective-permute-start.5
  45.4 8.0 %collective-permute-done.5.refs_0_ = bf16[272,384]{1,0:T(8,128)(2,1)S(1)} collective-permute-done((bf16[272,384]{1,0:T(8,128)(2,1)S(1)}, bf16[272,384]{1,0:T(8,128)(2,1)S(1)}, u32[]{:S(2)}, u32[]{:S(2)}) %collective-permute-start.5) | collective-permute-done | bytes 208928 | tf_op jit(solution)/shard_map/ppermute | solution.py:46
  53.4 4.5 %collective-permute-start.6 = (bf16[272,384]{1,0:T(8,128)(2,1)S(1)}, bf16[272,384]{1,0:T(8,128)(2,1)S(1)}, u32[]{:S(2)}, u32[]{:S(2)}) collective-permute-start(bf16[272,384]{1,0:T(8,128)(2,1)S(1)} %get-tuple-element.62.refs_1_), channel_id=1, source_target_pairs={{0,24},{1,25},{2,26},{3,27},{4,28},{5,29},{6,30},{7,31},{8,16},{9,... | collective-permute-start | bytes 626696 | tf_op jit(solution)/shard_map/ppermute | solution.py:46
  59.2 3.0 %collective-permute-done.6.refs_0_ = bf16[272,384]{1,0:T(8,128)(2,1)S(1)} collective-permute-done((bf16[272,384]{1,0:T(8,128)(2,1)S(1)}, bf16[272,384]{1,0:T(8,128)(2,1)S(1)}, u32[]{:S(2)}, u32[]{:S(2)}) %collective-permute-start.6) | collective-permute-done | bytes 208928 | tf_op jit(solution)/shard_map/ppermute | solution.py:46
  62.5 5.2 %collective-permute-start.7 = (bf16[256,384]{1,0:T(8,128)(2,1)S(1)}, bf16[256,384]{1,0:T(8,128)(2,1)S(1)}, u32[]{:S(2)}, u32[]{:S(2)}) collective-permute-start(bf16[256,384]{1,0:T(8,128)(2,1)S(1)} %get-tuple-element.65.refs_1_), channel_id=1, source_target_pairs={{0,8},{1,3},{2,10},{3,1},{4,12},{5,7},{6,14},{7,5},{8,0},{9,11},{1... | collective-permute-start | bytes 589832 | tf_op jit(solution)/shard_map/ppermute | solution.py:46
  67.7 0.8 seed.3
  68.5 1.9 %collective-permute-start.10 = (bf16[256,384]{1,0:T(8,128)(2,1)S(1)}, bf16[256,384]{1,0:T(8,128)(2,1)S(1)}, u32[]{:S(2)}, u32[]{:S(2)}) collective-permute-start(bf16[256,384]{1,0:T(8,128)(2,1)S(1)} %get-tuple-element.74.refs_1_), channel_id=1, source_target_pairs={{0,24},{1,25},{2,26},{3,27},{4,28},{5,29},{6,30},{7,31},{8,16},{9,... | collective-permute-start | bytes 589832 | tf_op jit(solution)/shard_map/ppermute | solution.py:46
  70.3 1.0 collective-permute-done.7.refs_0_
  71.3 0.8 join.4
  72.1 1.5 %collective-permute-start.13 = (bf16[512,384]{1,0:T(8,128)(2,1)}, bf16[512,384]{1,0:T(8,128)(2,1)}, u32[]{:S(2)}, u32[]{:S(2)}) collective-permute-start(bf16[512,384]{1,0:T(8,128)(2,1)} %get-tuple-element.83.refs_1_), channel_id=1, source_target_pairs={{0,4},{1,9},{2,6},{3,11},{4,0},{5,13},{6,2},{7,15},{8,12},{9,1},{1... | collective-permute-start | bytes 1179656 | tf_op jit(solution)/shard_map/ppermute | solution.py:46
  73.6 2.3 %collective-permute-done.10.refs_0_ = bf16[256,384]{1,0:T(8,128)(2,1)S(1)} collective-permute-done((bf16[256,384]{1,0:T(8,128)(2,1)S(1)}, bf16[256,384]{1,0:T(8,128)(2,1)S(1)}, u32[]{:S(2)}, u32[]{:S(2)}) %collective-permute-start.10) | collective-permute-done | bytes 196640 | tf_op jit(solution)/shard_map/ppermute | solution.py:46
  75.9 1.0 last_centroids.1
  76.9 2.3 %collective-permute-start.11 = (bf16[272,384]{1,0:T(8,128)(2,1)S(1)}, bf16[272,384]{1,0:T(8,128)(2,1)}, u32[]{:S(2)}, u32[]{:S(2)}) collective-permute-start(bf16[272,384]{1,0:T(8,128)(2,1)S(1)} %get-tuple-element.79.refs_1_), channel_id=1, source_target_pairs={{0,2},{1,5},{2,0},{3,7},{4,6},{5,1},{6,4},{7,3},{8,10},{9,13},{10,... | collective-permute-start | bytes 626696 | tf_op jit(solution)/shard_map/ppermute | solution.py:46
  79.3 1.8 %copy.10.refs_1_ = s32[1280,1]{1,0:T(8,128)} copy(s32[1280,1]{0,1:T(1,128)} %param.6) | data formatting | bytes 10240 | tf_op args[1]
  81.0 1.1 copy-done.1
  82.1 1.5 %copy-done.5 = bf16[1280,768]{1,0:T(8,128)(2,1)S(1)} copy-done((bf16[1280,768]{1,0:T(8,128)(2,1)S(1)}, bf16[1280,768]{1,0:T(8,128)(2,1)}, u32[]{:S(2)}) %copy-start.5) | copy-done | bytes 1966104
  83.7 4.3 %mask.1 = (bf16[1280,1536]{1,0:T(8,128)(2,1)}, bf16[1280,1536]{1,0:T(8,128)(2,1)}, bf16[1280,16]{1,0:T(8,128)(2,1)S(1)}, f32[8,128]{1,0:T(8,128)S(1)}) custom-call(s32[1]{0:T(128)} %copy.14.refs_0_, s32[1280,1]{1,0:T(8,128)S(1)} %copy-done.1, bf16[1280,768]{1,0:T(8,128)(2,1)S(1)} %copy-done.5, f32[8,128]{1,0:T(8,128)S(1)} %get-tuple-element.67.refs_3_), custom_call_target="tpu_custom_call" | custom-call | flops 4938242 | bytes 9876484 | tf_op jit(solution)/shard_map/mask/pallas_call | solution.py:133
  88.0 1.0 copy-done.9
  89.0 1.0 join.5
  90.0 2.1 %join.6 = (bf16[1024,384]{1,0:T(8,128)(2,1)}, f32[8,128]{1,0:T(8,128)S(1)}) custom-call(bf16[512,384]{1,0:T(8,128)(2,1)} %collective-permute-done.13.refs_0_, bf16[512,384]{1,0:T(8,128)(2,1)} %get-tuple-element.83.refs_1_, f32[8,128]{1,0:T(8,128)S(1)} %get-tuple-element.84.refs_2_), custom_call_target="tpu_custom_call" | custom-call | flops 786432 | bytes 1572864 | tf_op jit(solution)/shard_map/join/pallas_call | solution.py:133
  92.9 2.4 %collective-permute-done.14.refs_2_ = bf16[1024,384]{1,0:T(8,128)(2,1)} collective-permute-done((bf16[1024,384]{1,0:T(8,128)(2,1)}, bf16[1024,384]{1,0:T(8,128)(2,1)}, u32[]{:S(2)}, u32[]{:S(2)}) %collective-permute-start.14) | collective-permute-done | bytes 786464 | tf_op jit(solution)/shard_map/ppermute | solution.py:46
  95.3 0.7 copy-done.13
  96.0 7.8 %part_scores.2 = (f32[1280,1024]{1,0:T(8,128)}, f32[8,128]{1,0:T(8,128)S(1)}) custom-call(s32[16]{0:T(128)S(1)} %stack.212.code_ref, bf16[1280,1536]{1,0:T(8,128)(2,1)} %get-tuple-element.82.refs_0_, bf16[1024,384]{1,0:T(8,128)(2,1)} %get-tuple-element.85.refs_1_, bf16[1024,384]{1,0:T(8,128)(2,1)} %collective-permute-done.14.refs_2_, f32[8,128]{1,0:T(8,128)S(1)} %copy-done.13), custom_call_target="tpu_custom_call" | custom-call | flops 1 | bytes 1 | tf_op jit(solution)/shard_map/part_scores/pallas_call | solution.py:311
  104.2 2.0 %join.7 = (bf16[1040,384]{1,0:T(8,128)(2,1)}, f32[8,128]{1,0:T(8,128)S(1)}) custom-call(bf16[528,384]{1,0:T(8,128)(2,1)} %collective-permute-done.12.refs_0_, bf16[528,384]{1,0:T(8,128)(2,1)S(1)} %get-tuple-element.81.refs_1_, f32[8,128]{1,0:T(8,128)S(1)} %get-tuple-element.87.refs_2_), custom_call_target="tpu_custom_call" | custom-call | flops 804864 | bytes 1609728 | tf_op jit(solution)/shard_map/join/pallas_call | solution.py:133
  106.2 2.1 %collective-permute-start.15 = (bf16[1040,384]{1,0:T(8,128)(2,1)}, bf16[1040,384]{1,0:T(8,128)(2,1)}, u32[]{:S(2)}, u32[]{:S(2)}) collective-permute-start(bf16[1040,384]{1,0:T(8,128)(2,1)} %get-tuple-element.88.rest_2_), channel_id=1, source_target_pairs={{0,4},{1,3},{2,6},{3,1},{4,0},{5,7},{6,2},{7,5},{8,12},{9,11},{10,... | collective-permute-start | bytes 2396168 | tf_op jit(solution)/shard_map/ppermute | solution.py:46
  108.8 3.1 %collective-permute-done.17.refs_2_ = bf16[1024,384]{1,0:T(8,128)(2,1)S(1)} collective-permute-done((bf16[1024,384]{1,0:T(8,128)(2,1)}, bf16[1024,384]{1,0:T(8,128)(2,1)S(1)}, u32[]{:S(2)}, u32[]{:S(2)}) %collective-permute-start.17) | collective-permute-done | bytes 786464 | tf_op jit(solution)/shard_map/ppermute | solution.py:46
  111.9 7.6 %part_scores.3 = (f32[1280,1024]{1,0:T(8,128)}, f32[8,128]{1,0:T(8,128)S(1)}) custom-call(s32[16]{0:T(128)S(1)} %stack.212.code_ref, bf16[1280,1536]{1,0:T(8,128)(2,1)} %get-tuple-element.82.refs_0_, bf16[1024,384]{1,0:T(8,128)(2,1)} %collective-permute-done.16.refs_1_, ...), custom_call_target="tpu_custom_call", output_to_operand_aliasing={{0}: (4, {})} | custom-call | flops 1 | bytes 1 | tf_op jit(solution)/shard_map/part_scores/pallas_call | solution.py:311
  119.8 2.4 %collective-permute-done.18.rest_1_ = bf16[1040,384]{1,0:T(8,128)(2,1)} collective-permute-done((bf16[1040,384]{1,0:T(8,128)(2,1)}, bf16[1040,384]{1,0:T(8,128)(2,1)}, u32[]{:S(2)}, u32[]{:S(2)}) %collective-permute-start.18) | collective-permute-done | bytes 798752 | tf_op jit(solution)/shard_map/ppermute | solution.py:46
  122.2 11.6 %final_scores.1 = bf16[1280,1024]{1,0:T(8,128)(2,1)} custom-call(s32[32]{0:T(128)S(1)} %concatenate.104.code_ref, s32[8]{0:T(128)S(1)} %fusion.21.slot_ref, bf16[1280,1536]{1,0:T(8,128)(2,1)} %get-tuple-element.68.masked_ref, bf16[1280,16]{1,0:T(8,128)(2,1)S(1)} %copy-done.7, f32[16,1024]{1,0:T(8,128)S(1)} %broadcast_in_dim.25.half_ref, ...), custom_call_target="tpu_custom_call" | custom-call | flops 1 | bytes 1 | tf_op jit(solution)/shard_map/final_scores/pallas_call | solution.py:383
  (62 shorter events, 5.9 us)
Async XLA Ops:
  0.6 32.5 %copy-start = (f32[1,1024,768]{2,1,0:T(8,128)S(1)}, f32[1,1024,768]{2,1,0:T(8,128)}, u32[]{:S(2)}) copy-start(f32[1,1024,768]{2,1,0:T(8,128)} %param.9) | copy-start | bytes 9437188
  3.0 1.3 collective-permute-start
  3.5 4.3 %collective-permute-start.1 = (bf16[1280,768]{1,0:T(8,128)(2,1)}, bf16[1280,768]{1,0:T(8,128)(2,1)}, u32[]{:S(2)}, u32[]{:S(2)}) collective-permute-start(bf16[1280,768]{1,0:T(8,128)(2,1)} %refs_2_.1), channel_id=1, source_target_pairs={{0,1},{1,0},{2,3},{3,2},{4,5},{5,4},{6,7},{7,6},{8,9},{9,8},{10,11... | collective-permute-start | bytes 5898248 | tf_op jit(solution)/shard_map/ppermute | solution.py:46
  5.2 11.1 %copy-start.10 = (s32[1,2560]{1,0:T(1,128)}, s32[1,2560]{1,0:T(1,128)S(1)}, u32[]{:S(2)}) copy-start(s32[1,2560]{1,0:T(1,128)S(1)} %get-tuple-element.94.refs_0_) | copy-start | bytes 30724
  7.8 1.5 %copy-start.2 = (bf16[1280,768]{1,0:T(8,128)(2,1)S(1)}, bf16[1280,768]{1,0:T(8,128)(2,1)}, u32[]{:S(2)}) copy-start(bf16[1280,768]{1,0:T(8,128)(2,1)} %refs_2_.1) | copy-start | bytes 5898244
  9.3 7.0 %copy-start.3 = (bf16[1280,768]{1,0:T(8,128)(2,1)S(1)}, bf16[1280,768]{1,0:T(8,128)(2,1)}, u32[]{:S(2)}) copy-start(bf16[1280,768]{1,0:T(8,128)(2,1)} %refs_2_.1) | copy-start | bytes 5898244
  13.6 14.9 %collective-permute-start.2 = (bf16[1040,384]{1,0:T(8,128)(2,1)S(1)}, bf16[1040,384]{1,0:T(8,128)(2,1)S(1)}, u32[]{:S(2)}, u32[]{:S(2)}) collective-permute-start(bf16[1040,384]{1,0:T(8,128)(2,1)S(1)} %get-tuple-element.48), channel_id=1, source_target_pairs={{0,2},{1,5},{2,0},{3,7},{4,6},{5,1},{6,4},{7,3},{8,10},{9,13},{10,... | collective-permute-start | bytes 2396168 | tf_op jit(solution)/shard_map/ppermute | solution.py:46
  21.4 19.4 %collective-permute-start.4 = (bf16[1024,384]{1,0:T(8,128)(2,1)}, bf16[1024,384]{1,0:T(8,128)(2,1)}, u32[]{:S(2)}, u32[]{:S(2)}) collective-permute-start(bf16[1024,384]{1,0:T(8,128)(2,1)} %get-tuple-element.54), channel_id=1, source_target_pairs={{0,4},{1,3},{2,6},{3,1},{4,0},{5,7},{6,2},{7,5},{8,12},{9,11},{10,... | collective-permute-start | bytes 2359304 | tf_op jit(solution)/shard_map/ppermute | solution.py:46
  27.0 2.3 %copy-start.14 = (f32[8,128]{1,0:T(8,128)}, f32[8,128]{1,0:T(8,128)S(1)}, u32[]{:S(2)}) copy-start(f32[8,128]{1,0:T(8,128)S(1)} %get-tuple-element.55.refs_3_) | copy-start | bytes 12292
  29.4 14.1 %collective-permute-start.3 = (bf16[528,384]{1,0:T(8,128)(2,1)}, bf16[528,384]{1,0:T(8,128)(2,1)}, u32[]{:S(2)}, u32[]{:S(2)}) collective-permute-start(bf16[528,384]{1,0:T(8,128)(2,1)} %get-tuple-element.52), channel_id=1, source_target_pairs={{0,4},{1,9},{2,6},{3,11},{4,0},{5,13},{6,2},{7,15},{8,12},{9,1},{1... | collective-permute-start | bytes 1216520 | tf_op jit(solution)/shard_map/ppermute | solution.py:46
  33.2 1.5 %copy-start.4 = (bf16[1280,768]{1,0:T(8,128)(2,1)S(1)}, bf16[1280,768]{1,0:T(8,128)(2,1)}, u32[]{:S(2)}) copy-start(bf16[1280,768]{1,0:T(8,128)(2,1)} %refs_2_.1) | copy-start | bytes 5898244
  34.7 0.7 copy-start.11
  35.4 0.7 copy-start.15
  42.1 15.9 %collective-permute-start.8 = (bf16[512,384]{1,0:T(8,128)(2,1)S(1)}, bf16[512,384]{1,0:T(8,128)(2,1)S(1)}, u32[]{:S(2)}, u32[]{:S(2)}) collective-permute-start(bf16[512,384]{1,0:T(8,128)(2,1)S(1)} %get-tuple-element.70), channel_id=1, source_target_pairs={{0,8},{1,9},{2,10},{3,11},{4,12},{5,13},{6,14},{7,15},{8,0},{9,1},... | collective-permute-start | bytes 1179656 | tf_op jit(solution)/shard_map/ppermute | solution.py:46
  44.6 8.7 %collective-permute-start.5 = (bf16[272,384]{1,0:T(8,128)(2,1)S(1)}, bf16[272,384]{1,0:T(8,128)(2,1)S(1)}, u32[]{:S(2)}, u32[]{:S(2)}) collective-permute-start(bf16[272,384]{1,0:T(8,128)(2,1)S(1)} %get-tuple-element.59), channel_id=1, source_target_pairs={{0,8},{1,3},{2,10},{3,1},{4,12},{5,7},{6,14},{7,5},{8,0},{9,11},{1... | collective-permute-start | bytes 626696 | tf_op jit(solution)/shard_map/ppermute | solution.py:46
  53.4 8.8 %collective-permute-start.6 = (bf16[272,384]{1,0:T(8,128)(2,1)S(1)}, bf16[272,384]{1,0:T(8,128)(2,1)S(1)}, u32[]{:S(2)}, u32[]{:S(2)}) collective-permute-start(bf16[272,384]{1,0:T(8,128)(2,1)S(1)} %get-tuple-element.62.refs_1_), channel_id=1, source_target_pairs={{0,24},{1,25},{2,26},{3,27},{4,28},{5,29},{6,30},{7,31},{8,16},{9,... | collective-permute-start | bytes 626696 | tf_op jit(solution)/shard_map/ppermute | solution.py:46
  58.6 9.1 %collective-permute-start.9 = (bf16[256,384]{1,0:T(8,128)(2,1)S(1)}, bf16[256,384]{1,0:T(8,128)(2,1)S(1)}, u32[]{:S(2)}, u32[]{:S(2)}) collective-permute-start(bf16[256,384]{1,0:T(8,128)(2,1)S(1)} %get-tuple-element.72), channel_id=1, source_target_pairs={{0,2},{1,5},{2,0},{3,7},{4,6},{5,1},{6,4},{7,3},{8,10},{9,13},{10,... | collective-permute-start | bytes 589832 | tf_op jit(solution)/shard_map/ppermute | solution.py:46
  62.5 8.8 %collective-permute-start.7 = (bf16[256,384]{1,0:T(8,128)(2,1)S(1)}, bf16[256,384]{1,0:T(8,128)(2,1)S(1)}, u32[]{:S(2)}, u32[]{:S(2)}) collective-permute-start(bf16[256,384]{1,0:T(8,128)(2,1)S(1)} %get-tuple-element.65.refs_1_), channel_id=1, source_target_pairs={{0,8},{1,3},{2,10},{3,1},{4,12},{5,7},{6,14},{7,5},{8,0},{9,11},{1... | collective-permute-start | bytes 589832 | tf_op jit(solution)/shard_map/ppermute | solution.py:46
  68.5 7.5 %collective-permute-start.10 = (bf16[256,384]{1,0:T(8,128)(2,1)S(1)}, bf16[256,384]{1,0:T(8,128)(2,1)S(1)}, u32[]{:S(2)}, u32[]{:S(2)}) collective-permute-start(bf16[256,384]{1,0:T(8,128)(2,1)S(1)} %get-tuple-element.74.refs_1_), channel_id=1, source_target_pairs={{0,24},{1,25},{2,26},{3,27},{4,28},{5,29},{6,30},{7,31},{8,16},{9,... | collective-permute-start | bytes 589832 | tf_op jit(solution)/shard_map/ppermute | solution.py:46
  72.1 17.9 %collective-permute-start.13 = (bf16[512,384]{1,0:T(8,128)(2,1)}, bf16[512,384]{1,0:T(8,128)(2,1)}, u32[]{:S(2)}, u32[]{:S(2)}) collective-permute-start(bf16[512,384]{1,0:T(8,128)(2,1)} %get-tuple-element.83.refs_1_), channel_id=1, source_target_pairs={{0,4},{1,9},{2,6},{3,11},{4,0},{5,13},{6,2},{7,15},{8,12},{9,1},{1... | collective-permute-start | bytes 1179656 | tf_op jit(solution)/shard_map/ppermute | solution.py:46
  76.9 11.0 %copy-start.8 = (bf16[272,384]{1,0:T(8,128)(2,1)}, bf16[272,384]{1,0:T(8,128)(2,1)S(1)}, u32[]{:S(2)}) copy-start(bf16[272,384]{1,0:T(8,128)(2,1)S(1)} %get-tuple-element.79.refs_1_) | copy-start | bytes 626692
  76.9 11.0 %collective-permute-start.11 = (bf16[272,384]{1,0:T(8,128)(2,1)S(1)}, bf16[272,384]{1,0:T(8,128)(2,1)}, u32[]{:S(2)}, u32[]{:S(2)}) collective-permute-start(bf16[272,384]{1,0:T(8,128)(2,1)S(1)} %get-tuple-element.79.refs_1_), channel_id=1, source_target_pairs={{0,2},{1,5},{2,0},{3,7},{4,6},{5,1},{6,4},{7,3},{8,10},{9,13},{10,... | collective-permute-start | bytes 626696 | tf_op jit(solution)/shard_map/ppermute | solution.py:46
  81.0 1.1 copy-start.1
  82.1 1.5 %copy-start.5 = (bf16[1280,768]{1,0:T(8,128)(2,1)S(1)}, bf16[1280,768]{1,0:T(8,128)(2,1)}, u32[]{:S(2)}) copy-start(bf16[1280,768]{1,0:T(8,128)(2,1)} %refs_2_.1) | copy-start | bytes 5898244
  88.0 4.7 %copy-start.6 = (bf16[1280,16]{1,0:T(8,128)(2,1)}, bf16[1280,16]{1,0:T(8,128)(2,1)S(1)}, u32[]{:S(2)}) copy-start(bf16[1280,16]{1,0:T(8,128)(2,1)S(1)} %get-tuple-element.69.pick_ref) | copy-start | bytes 122884
  88.0 1.1 copy-start.9
  92.1 0.6 copy-start.12
  92.7 2.6 %collective-permute-start.14 = (bf16[1024,384]{1,0:T(8,128)(2,1)}, bf16[1024,384]{1,0:T(8,128)(2,1)}, u32[]{:S(2)}, u32[]{:S(2)}) collective-permute-start(bf16[1024,384]{1,0:T(8,128)(2,1)} %get-tuple-element.85.refs_1_), channel_id=1, source_target_pairs={{0,1},{1,0},{2,3},{3,2},{4,5},{5,4},{6,7},{7,6},{8,9},{9,8},{10,11... | collective-permute-start | bytes 2359304 | tf_op jit(solution)/shard_map/ppermute | solution.py:46
  92.7 15.6 %collective-permute-start.16 = (bf16[1024,384]{1,0:T(8,128)(2,1)}, bf16[1024,384]{1,0:T(8,128)(2,1)}, u32[]{:S(2)}, u32[]{:S(2)}) collective-permute-start(bf16[1024,384]{1,0:T(8,128)(2,1)} %get-tuple-element.85.refs_1_), channel_id=1, source_target_pairs={{0,2},{1,5},{2,0},{3,7},{4,6},{5,1},{6,4},{7,3},{8,10},{9,13},{10,... | collective-permute-start | bytes 2359304 | tf_op jit(solution)/shard_map/ppermute | solution.py:46
  92.7 11.5 %collective-permute-start.12 = (bf16[528,384]{1,0:T(8,128)(2,1)S(1)}, bf16[528,384]{1,0:T(8,128)(2,1)}, u32[]{:S(2)}, u32[]{:S(2)}) collective-permute-start(bf16[528,384]{1,0:T(8,128)(2,1)S(1)} %get-tuple-element.81.refs_1_), channel_id=1, source_target_pairs={{0,8},{1,9},{2,10},{3,11},{4,12},{5,13},{6,14},{7,15},{8,0},{9,1},... | collective-permute-start | bytes 1216520 | tf_op jit(solution)/shard_map/ppermute | solution.py:46
  95.3 0.7 copy-start.13
  106.2 13.3 %collective-permute-start.15 = (bf16[1040,384]{1,0:T(8,128)(2,1)}, bf16[1040,384]{1,0:T(8,128)(2,1)}, u32[]{:S(2)}, u32[]{:S(2)}) collective-permute-start(bf16[1040,384]{1,0:T(8,128)(2,1)} %get-tuple-element.88.rest_2_), channel_id=1, source_target_pairs={{0,4},{1,3},{2,6},{3,1},{4,0},{5,7},{6,2},{7,5},{8,12},{9,11},{10,... | collective-permute-start | bytes 2396168 | tf_op jit(solution)/shard_map/ppermute | solution.py:46
  108.3 3.6 %collective-permute-start.17 = (bf16[1024,384]{1,0:T(8,128)(2,1)}, bf16[1024,384]{1,0:T(8,128)(2,1)S(1)}, u32[]{:S(2)}, u32[]{:S(2)}) collective-permute-start(bf16[1024,384]{1,0:T(8,128)(2,1)} %collective-permute-done.16.refs_1_), channel_id=1, source_target_pairs={{0,1},{1,0},{2,3},{3,2},{4,5},{5,4},{6,7},{7,6},{8,9},{9,8},{10,11... | collective-permute-start | bytes 2359304 | tf_op jit(solution)/shard_map/ppermute | solution.py:46
  108.3 11.5 %collective-permute-start.19 = (bf16[1040,384]{1,0:T(8,128)(2,1)}, bf16[1040,384]{1,0:T(8,128)(2,1)}, u32[]{:S(2)}, u32[]{:S(2)}) collective-permute-start(bf16[1040,384]{1,0:T(8,128)(2,1)} %get-tuple-element.88.rest_2_), channel_id=1, source_target_pairs={{0,1},{1,0},{2,3},{3,2},{4,5},{5,4},{6,7},{7,6},{8,9},{9,8},{10,11... | collective-permute-start | bytes 2396168 | tf_op jit(solution)/shard_map/ppermute | solution.py:46
  111.9 10.3 %copy-start.7 = (bf16[1280,16]{1,0:T(8,128)(2,1)S(1)}, bf16[1280,16]{1,0:T(8,128)(2,1)}, u32[]{:S(2)}) copy-start(bf16[1280,16]{1,0:T(8,128)(2,1)} %copy-done.6) | copy-start | bytes 122884
  119.5 2.7 %collective-permute-start.18 = (bf16[1040,384]{1,0:T(8,128)(2,1)}, bf16[1040,384]{1,0:T(8,128)(2,1)}, u32[]{:S(2)}, u32[]{:S(2)}) collective-permute-start(bf16[1040,384]{1,0:T(8,128)(2,1)} %behind.1.rest_0_), channel_id=1, source_target_pairs={{0,1},{1,0},{2,3},{3,2},{4,5},{5,4},{6,7},{7,6},{8,9},{9,8},{10,11... | collective-permute-start | bytes 2396168 | tf_op jit(solution)/shard_map/ppermute | solution.py:46

commit v7 on v6

--- a/solution.py
+++ b/solution.py
@@ -30,10 +30,10 @@
     cut = len(inner) // 2
     other = inner[cut:] + inner[:cut]
     found = {}
-    found[0, 0] = inner + outer
+    found[0, 0] = inner[:cut] + outer[:1] + inner[cut:] + outer[1:]
     found[1, 0] = other[:cut] + outer[:1] + other[cut:] + outer[1:]
     found[0, 1] = found[1, 0]
-    found[1, 1] = inner[:cut] + outer[:1] + inner[cut:] + outer[1:]
+    found[1, 1] = found[0, 0]
     return found
 
 
@@ -127,15 +127,15 @@
     )(pos_row, own, other, *extra, token)
 
 
-def small_call(kernel, name, outs, token, *args, scalars=0, limit=4):
+def small_call(kernel, name, outs, token, *args):
     whole = pl.BlockSpec(memory_space=pltpu.VMEM)
     moved = sum(a.size * a.dtype.itemsize for a in (*args, *outs))
     return pl.pallas_call(
         hand_on(kernel, len(args)),
         out_shape=[*outs, token_shape()],
-        in_specs=[pl.BlockSpec(memory_space=pltpu.SMEM)] * scalars + [whole] * (len(args) + 1 - scalars),
-        out_specs=[whole if limit < 16 else pl.BlockSpec()] * len(outs) + [whole],
-        compiler_params=pltpu.CompilerParams(vmem_limit_bytes=limit << 20),
+        in_specs=[whole] * (len(args) + 1),
+        out_specs=[whole] * (len(outs) + 1),
+        compiler_params=pltpu.CompilerParams(vmem_limit_bytes=4 << 20),
         cost_estimate=pl.CostEstimate(flops=moved // 2, bytes_accessed=moved, transcendentals=0),
         name=name,
     )(*args, token)
@@ -254,46 +254,58 @@
     )(array, token)
 
 
-def mask_kernel(groups, columns, live_ref, label_ref, x_ref, *outs):
-    row = lax.broadcasted_iota(jnp.int32, label_ref.shape, 0)
-    gid = jnp.where(row < live_ref[0], label_ref[...], -1)
-    for (start, wide), out_ref in zip(columns, outs):
-        x = x_ref[:, start : start + wide]
-        for group in range(groups):
-            out_ref[:, group * wide : (group + 1) * wide] = jnp.where(gid == group, x, jnp.zeros_like(x))
-    pick_ref = outs[len(columns)]
-    lane = lax.broadcasted_iota(jnp.int32, pick_ref.shape, 1)
-    hit = (lane % groups == gid) & (lane < PARTS * groups)
-    pick_ref[...] = jnp.where(hit, -1.0, 0.0).astype(BF16)
+def row_loads(x_ref, gid_ref, x, gid, sem, start):
+    return (
+        pltpu.make_async_copy(x_ref.at[:, pl.ds(start, x.shape[1])], x, sem.at[0]),
+        pltpu.make_async_copy(gid_ref, gid, sem.at[1]),
+    )
+
+
+def mask_rows(groups, x, gid, out):
+    wide = x.shape[1]
+    for group in range(groups):
+        out[:, group * wide : (group + 1) * wide] = jnp.where(gid[...] == group, x[...], jnp.zeros_like(x))
+
+
+def row_scratch(rows, groups, wide):
+    return [
+        pltpu.VMEM((rows, groups * wide), BF16),
+        pltpu.VMEM((rows, wide), BF16),
+        pltpu.VMEM((rows, 1), jnp.int32),
+        pltpu.SemaphoreType.DMA((2,)),
+    ]
 
 
 def product(a, b):
     return lax.dot_general(a, b, (((1,), (1,)), ((), ())), preferred_element_type=F32)
 
 
-def part_kernel(groups, share, code_ref, masked_ref, own_ref, other_ref, *rest):
-    out_ref, cents, rows_of, sem = rest
-    load = pltpu.make_async_copy(masked_ref, rows_of, sem)
+def part_kernel(groups, share, start_at, code_ref, x_ref, gid_ref, own_ref, other_ref, *rest):
+    out_ref, cents, rows_of, x, gid, sem = rest
+    loads = row_loads(x_ref, gid_ref, x, gid, sem, start_at)
     wide = own_ref.shape[1]
     blocks = own_ref.shape[0] // share
 
     @pl.when(pl.program_id(0) == 0)
     def _():
-        load.start()
+        for load in loads:
+            load.start()
         for piece, ref in enumerate((own_ref, other_ref)):
             for block in range(blocks):
                 code = code_ref[piece * blocks + block]
                 slot = pl.multiple_of(code // groups * share, share)
                 cents[pl.ds(slot, share), pl.ds(pl.multiple_of(code % groups * wide, 128), wide)] = ref[block * share : (block + 1) * share, :]
-        load.wait()
+        for load in loads:
+            load.wait()
+        mask_rows(groups, x, gid, rows_of)
 
     step = out_ref.shape[1]
     start = pl.multiple_of(pl.program_id(0) * step, step)
-    out_ref[...] = product(rows_of[...], cents[pl.ds(start, step), :])
-
-
-def part_scores(token, masked, codes, pieces, before, groups, keys, share):
-    rows = masked.shape[0]
+    out_ref[...] = product(rows_of[...], cents[pl.ds(start, step), :]).astype(BF16)
+
+
+def part_scores(token, samples, gid, codes, pieces, before, groups, keys, share, start_at):
+    rows = samples.shape[0]
     wide = pieces[0].shape[1]
     half = pieces[0].shape[0] * len(pieces) // groups
     step = min(256, half)
@@ -304,8 +316,8 @@
     anywhere = pl.BlockSpec(memory_space=pl.ANY)
 
     def kernel(code_ref, *refs):
-        count = 3 + len(extra)
-        part_kernel(groups, share, code_ref, *refs[:3], refs[count + 1], *refs[-3:])
+        count = 4 + len(extra)
+        part_kernel(groups, share, start_at, code_ref, *refs[:4], refs[count + 1], *refs[-5:])
         refs[count + 2][...] = refs[count][...]
 
     return pl.pallas_call(
@@ -313,27 +325,26 @@
         grid_spec=pltpu.PrefetchScalarGridSpec(
             num_scalar_prefetch=1,
             grid=(steps,),
-            in_specs=[anywhere] + [whole] * 2 + [anywhere] * len(extra) + [whole],
+            in_specs=[anywhere] * 2 + [whole] * 2 + [anywhere] * len(extra) + [whole],
             out_specs=[pl.BlockSpec((rows, step), lambda i, w: (0, i + at)), whole],
             scratch_shapes=[
                 pltpu.VMEM((half, groups * wide), BF16),
-                pltpu.VMEM(masked.shape, BF16),
-                pltpu.SemaphoreType.DMA,
+                *row_scratch(rows, groups, wide),
             ],
         ),
-        out_shape=[jax.ShapeDtypeStruct((rows, keys), F32), token_shape()],
-        input_output_aliases={} if before is None else {4: 0},
+        out_shape=[jax.ShapeDtypeStruct((rows, keys), BF16), token_shape()],
+        input_output_aliases={} if before is None else {5: 0},
         compiler_params=pltpu.CompilerParams(vmem_limit_bytes=51 << 20),
         cost_estimate=pl.CostEstimate(flops=1, bytes_accessed=1, transcendentals=0),
         name="part_scores",
-    )(codes, masked, *pieces, *extra, token)
-
-
-def final_kernel(groups, share, code_ref, slot_ref, masked_ref, pick_ref, half_ref, *rest):
+    )(codes, samples, gid, *pieces, *extra, token)
+
+
+def final_kernel(groups, share, start_at, code_ref, slot_ref, x_ref, gid_ref, half_ref, *rest):
     pieces = 4
     piece_refs, total_refs = rest[:pieces], rest[pieces : pieces + 2]
-    out_ref, cents, half, rows_of, sem = rest[-5:]
-    load = pltpu.make_async_copy(masked_ref, rows_of, sem)
+    out_ref, cents, half, pick, rows_of, x, gid, sem = rest[-8:]
+    loads = row_loads(x_ref, gid_ref, x, gid, sem, start_at)
     keys = cents.shape[0]
     wide = cents.shape[1] // groups
     members = keys // share
@@ -342,7 +353,8 @@
 
     @pl.when(pl.program_id(0) == 0)
     def _():
-        load.start()
+        for load in loads:
+            load.start()
         half[...] = half_ref[...]
         for piece, ref in enumerate(piece_refs):
             for block in range(blocks):
@@ -362,31 +374,36 @@
                         row = tail[at : at + 1, term * share : (term + 1) * share]
                         filled = jnp.where(line == group + term * groups, row, filled)
                     half[:, lines] = filled
-        load.wait()
+        for load in loads:
+            load.wait()
+        mask_rows(groups, x, gid, rows_of)
+        lane = lax.broadcasted_iota(jnp.int32, pick.shape, 1)
+        hit = (lane % groups == gid[...]) & (lane < PARTS * groups)
+        pick[...] = jnp.where(hit, -1.0, 0.0).astype(BF16)
 
     step = out_ref.shape[1]
     start = pl.multiple_of(pl.program_id(0) * step, step)
     dots = product(rows_of[...], cents[pl.ds(start, step), :])
     offsets = half[:, pl.ds(start, step)].astype(BF16)
-    dots += jnp.dot(pick_ref[...], offsets, preferred_element_type=F32)
+    dots += jnp.dot(pick[...], offsets, preferred_element_type=F32)
     cut = step // 2
-    out_ref[:, :cut] = (dots[:, :cut] + total_refs[0][...]).astype(BF16)
-    out_ref[:, cut:] = (dots[:, cut:] + total_refs[1][...]).astype(BF16)
-
-
-def final_scores(masked, pick, codes, slots, pieces, total, half, groups, keys, share):
-    rows = masked.shape[0]
+    out_ref[:, :cut] = (dots[:, :cut] + total_refs[0][...].astype(F32)).astype(BF16)
+    out_ref[:, cut:] = (dots[:, cut:] + total_refs[1][...].astype(F32)).astype(BF16)
+
+
+def final_scores(samples, gid, codes, slots, pieces, total, half, groups, keys, share, start_at):
+    rows = samples.shape[0]
     wide = pieces[0].shape[1]
     step = min(256, keys)
     cut = step // 2
     whole = pl.BlockSpec(memory_space=pltpu.VMEM)
     return pl.pallas_call(
-        functools.partial(final_kernel, groups, share),
+        functools.partial(final_kernel, groups, share, start_at),
         grid_spec=pltpu.PrefetchScalarGridSpec(
             num_scalar_prefetch=2,
             grid=(keys // step,),
-            in_specs=[pl.BlockSpec(memory_space=pl.ANY)]
-            + [whole] * (2 + len(pieces))
+            in_specs=[pl.BlockSpec(memory_space=pl.ANY)] * 2
+            + [whole] * (1 + len(pieces))
             + [
                 pl.BlockSpec((rows, cut), lambda i, c, s: (0, s[2 * i])),
                 pl.BlockSpec((rows, cut), lambda i, c, s: (0, s[2 * i + 1])),
@@ -395,15 +412,15 @@
             scratch_shapes=[
                 pltpu.VMEM((keys, groups * wide), BF16),
                 pltpu.VMEM(half.shape, F32),
-                pltpu.VMEM(masked.shape, BF16),
-                pltpu.SemaphoreType.DMA,
+                pltpu.VMEM((rows, TILE), BF16),
+                *row_scratch(rows, groups, wide),
             ],
         ),
         out_shape=jax.ShapeDtypeStruct((rows, keys), BF16),
         compiler_params=pltpu.CompilerParams(vmem_limit_bytes=50 << 20),
         cost_estimate=pl.CostEstimate(flops=1, bytes_accessed=1, transcendentals=0),
         name="final_scores",
-    )(codes, slots, masked, pick, half, *pieces, total, total)
+    )(codes, slots, samples, gid, half, *pieces, total, total)
 
 
 def per_device(samples, coarse_label, fine_label, live_rows, old_centroids):
@@ -556,6 +573,7 @@
                 codes.append(jnp.where(core ^ flip == 0, *code))
         return jnp.stack(codes).astype(jnp.int32)
 
+    gid = jnp.where(live, coarse_label[:, 0], -1)[:, None]
     count = 2
     arrived = [None] * 2
     for stage in reversed(range(stages - 1)):
@@ -572,22 +590,9 @@
                 )
             else:
                 arrived[stream] = got
-            if (stage, stream) == (stages - 2, 0):
-                *masked, pick, tokens[0] = small_call(
-                    functools.partial(mask_kernel, groups, columns),
-                    "mask",
-                    [jax.ShapeDtypeStruct((rows, groups * wide), BF16) for _, wide in columns]
-                    + [jax.ShapeDtypeStruct((rows, TILE), BF16)],
-                    tokens[0],
-                    live_rows,
-                    coarse_label,
-                    samples,
-                    scalars=1,
-                    limit=48,
-                )
             if (stage, stream) == (1, 0):
                 total, tokens[0] = part_scores(
-                    tokens[0], masked[0], part_codes(1), [held[0], sibling(held[0])], None, groups, keys, share
+                    tokens[0], samples, gid, part_codes(1), [held[0], sibling(held[0])], None, groups, keys, share, 0
                 )
         count *= 2
 
@@ -602,7 +607,7 @@
         return jnp.stack(codes).astype(jnp.int32)
 
     total, token = part_scores(
-        tokens[1], masked[0], part_codes(0), [arrived[0], sibling(arrived[0])], total, groups, keys, share
+        tokens[1], samples, gid, part_codes(0), [arrived[0], sibling(arrived[0])], total, groups, keys, share, 0
     )
     last = behind(arrived[1], token)
     every = jnp.arange(members, dtype=jnp.int32)
@@ -629,9 +634,9 @@
         lane = jnp.arange(keys, dtype=jnp.int32)
         source = jnp.repeat(slots, share) * share + lane % share
         move = (lane[:, None] == source[None, :]).astype(F32)
-        total = jnp.dot(total, move, precision=lax.Precision.HIGHEST)
+        total = jnp.dot(total, move.astype(BF16))
         slots = jnp.arange(keys // 128, dtype=jnp.int32)
-    scores = final_scores(masked[1], pick, codes, slots, flat, total, half, groups, keys, share)
+    scores = final_scores(samples, gid, codes, slots, flat, total, half, groups, keys, share, columns[1][0])
     return scores, fresh[1][None]
 
 

time: 135 us -> 123 us (0.911)
  Pallas kernels: 61.2 us -> 51.5 us
  local copies, waits for them, and re-layouts: 11.5 us -> 8.91 us
  waiting for transfers between devices: 27.3 us -> 25.5 us
    pallas_call x13 -> x12, Pallas kernels: 16.2 us -> 7.87 us  [small_call(): pl.pallas_call(hand_on(kernel, len(args)), out_shape=[*outs, token_shape(...]
    unnamed x34 -> x26, local copies, waits for them, and re-layouts: 11.2 us -> 8.64 us
    ppermute x20, waiting for transfers between devices: 27.3 us -> 25.5 us  [exchange(): return lax.ppermute(array, AXES, pairs)]
  transfers between devices with their start and end apart: 20 -> 20, of which waited for: 11 -> 10; matrix products, arithmetic and copies ran while one was open for 2% -> 3% of each run, Pallas kernels for 32% -> 29%
where the time goes in v7:
time: 123 us; the launch traced here: 122 us
  Pallas kernels  51.5 us (42%)
  starting transfers between devices  30.4 us (25%)
  waiting for transfers between devices  25.5 us (21%)
  local copies, waits for them, and re-layouts  8.91 us (7%)
  other arithmetic  3.07 us (2%)
  between operations  1.83 us (1%)
    ppermute x20, starting transfers between devices, exchange(): return lax.ppermute(array, AXES, pairs)  30.4 us
    ppermute x20, waiting for transfers between devices, exchange(): return lax.ppermute(array, AXES, pairs)  25.5 us
    pallas_call x4, Pallas kernels, key_sums(): pl.pallas_call(hand_on(functools.partial(sums_kernel, base), 3 + len(extr...  18.2 us
    pallas_call x2, Pallas kernels, part_scores(): pl.pallas_call(kernel, grid_spec=pltpu.PrefetchScalarGridSpec(num_scalar_...  14.2 us
    pallas_call x1, Pallas kernels, final_scores(): pl.pallas_call(functools.partial(final_kernel, groups, share, start_at),...  11.2 us
    unnamed x26, local copies, waits for them, and re-layouts  8.64 us
    pallas_call x12, Pallas kernels, small_call(): pl.pallas_call(hand_on(kernel, len(args)), out_shape=[*outs, token_shape(...  7.87 us
  transfers between devices with their start and end apart: 20, of which 10 were waited for; matrix products, arithmetic and copies ran while one was open for 3% of the time, Pallas kernels for 29%

profile of v7, /device:TPU:0, one launch (start us, length us, event | category | flops | bytes accessed | tf_op | source)
XLA Modules:
  0.0 121.7 jit_solution(7387883300582248709)
XLA Ops:
  1.4 0.9 multiply_reduce_fusion
  2.3 0.7 add_select_fusion.9
  3.5 0.8 collective-permute-done
  5.2 2.6 %collective-permute-done.1.refs_2_ = bf16[1280,768]{1,0:T(8,128)(2,1)} collective-permute-done((bf16[1280,768]{1,0:T(8,128)(2,1)}, bf16[1280,768]{1,0:T(8,128)(2,1)}, u32[]{:S(2)}, u32[]{:S(2)}) %collective-permute-start.1) | collective-permute-done | bytes 1966112 | tf_op jit(solution)/shard_map/ppermute | solution.py:46
  7.8 1.5 %copy-done.1 = bf16[1280,768]{1,0:T(8,128)(2,1)S(1)} copy-done((bf16[1280,768]{1,0:T(8,128)(2,1)S(1)}, bf16[1280,768]{1,0:T(8,128)(2,1)}, u32[]{:S(2)}) %copy-start.1) | copy-done | bytes 1966104
  9.3 4.3 %key_sums.4 = (bf16[1040,384]{1,0:T(8,128)(2,1)S(1)}, f32[8,128]{1,0:T(8,128)S(1)}) custom-call(s32[1,2560]{1,0:T(1,128)S(1)} %get-tuple-element.86.refs_0_, bf16[1280,768]{1,0:T(8,128)(2,1)S(1)} %copy-done.1, bf16[1280,768]{1,0:T(8,128)(2,1)} %collective-permute-done.1.refs_2_, bf16[16,384]{1,0:T(8,128)(2,1)S(1)} %pad_maximum_fusion.refs_3_, ...), custom_call_target="tpu_custom_call" | custom-call | flops 2013265920 | bytes 2752512 | tf_op jit(solution)/shard_map/key_sums/pallas_call | solution.py:110
  13.6 2.7 %collective-permute-start.3 = (bf16[1040,384]{1,0:T(8,128)(2,1)S(1)}, bf16[1040,384]{1,0:T(8,128)(2,1)S(1)}, u32[]{:S(2)}, u32[]{:S(2)}) collective-permute-start(bf16[1040,384]{1,0:T(8,128)(2,1)S(1)} %get-tuple-element.49), channel_id=1, source_target_pairs={{0,2},{1,5},{2,0},{3,7},{4,6},{5,1},{6,4},{7,3},{8,10},{9,13},{10,... | collective-permute-start | bytes 2396168 | tf_op jit(solution)/shard_map/ppermute | solution.py:46
  16.4 5.0 %key_sums.5 = (bf16[1024,384]{1,0:T(8,128)(2,1)}, f32[8,128]{1,0:T(8,128)S(1)}) custom-call(s32[1,2560]{1,0:T(1,128)S(1)} %fusion.11.refs_0_, bf16[1280,768]{1,0:T(8,128)(2,1)S(1)} %copy-done.2, bf16[1280,768]{1,0:T(8,128)(2,1)} %collective-permute-done.1.refs_2_, f32[8,128]{1,0:T(8,128)S(1)} %get-tuple-element.44.refs_3_), custom_call_target="tpu_custom_call" | custom-call | flops 2013265920 | bytes 2752512 | tf_op jit(solution)/shard_map/key_sums/pallas_call | solution.py:110
  21.4 1.5 %collective-permute-start.2 = (bf16[1024,384]{1,0:T(8,128)(2,1)}, bf16[1024,384]{1,0:T(8,128)(2,1)}, u32[]{:S(2)}, u32[]{:S(2)}) collective-permute-start(bf16[1024,384]{1,0:T(8,128)(2,1)} %get-tuple-element.45), channel_id=1, source_target_pairs={{0,4},{1,3},{2,6},{3,1},{4,0},{5,7},{6,2},{7,5},{8,12},{9,11},{10,... | collective-permute-start | bytes 2359304 | tf_op jit(solution)/shard_map/ppermute | solution.py:46
  22.9 4.2 %key_sums.6 = (bf16[1040,384]{1,0:T(8,128)(2,1)S(1)}, f32[8,128]{1,0:T(8,128)S(1)}) custom-call(s32[1,2560]{1,0:T(1,128)S(1)} %get-tuple-element.86.refs_0_, bf16[1280,768]{1,0:T(8,128)(2,1)S(1)} %copy-done.2, bf16[1280,768]{1,0:T(8,128)(2,1)} %collective-permute-done.1.refs_2_, bf16[16,384]{1,0:T(8,128)(2,1)S(1)} %pad_maximum_fusion.refs_3_, ...), custom_call_target="tpu_custom_call" | custom-call | flops 2013265920 | bytes 2752512 | tf_op jit(solution)/shard_map/key_sums/pallas_call | solution.py:110
  27.1 1.3 %collective-permute-done.3.refs_0_ = bf16[1040,384]{1,0:T(8,128)(2,1)S(1)} collective-permute-done((bf16[1040,384]{1,0:T(8,128)(2,1)S(1)}, bf16[1040,384]{1,0:T(8,128)(2,1)S(1)}, u32[]{:S(2)}, u32[]{:S(2)}) %collective-permute-start.3) | collective-permute-done | bytes 798752 | tf_op jit(solution)/shard_map/ppermute | solution.py:46
  28.5 0.8 fold.4
  29.3 2.6 %collective-permute-start.5 = (bf16[528,384]{1,0:T(8,128)(2,1)}, bf16[528,384]{1,0:T(8,128)(2,1)}, u32[]{:S(2)}, u32[]{:S(2)}) collective-permute-start(bf16[528,384]{1,0:T(8,128)(2,1)} %get-tuple-element.54), channel_id=1, source_target_pairs={{0,8},{1,9},{2,10},{3,11},{4,12},{5,13},{6,14},{7,15},{8,0},{9,1},... | collective-permute-start | bytes 1216520 | tf_op jit(solution)/shard_map/ppermute | solution.py:46
  31.9 1.5 %copy-done.3 = bf16[1280,768]{1,0:T(8,128)(2,1)S(1)} copy-done((bf16[1280,768]{1,0:T(8,128)(2,1)S(1)}, bf16[1280,768]{1,0:T(8,128)(2,1)}, u32[]{:S(2)}) %copy-start.3) | copy-done | bytes 1966104
  33.5 0.7 copy-done.7
  34.2 0.7 copy-done.11
  34.8 4.7 %key_sums.7 = (bf16[1024,384]{1,0:T(8,128)(2,1)S(1)}, f32[8,128]{1,0:T(8,128)}) custom-call(s32[1,2560]{1,0:T(1,128)S(1)} %copy-done.7, bf16[1280,768]{1,0:T(8,128)(2,1)S(1)} %copy-done.3, bf16[1280,768]{1,0:T(8,128)(2,1)} %collective-permute-done.1.refs_2_, f32[8,128]{1,0:T(8,128)S(1)} %copy-done.11), custom_call_target="tpu_custom_call" | custom-call | flops 2013265920 | bytes 2752512 | tf_op jit(solution)/shard_map/key_sums/pallas_call | solution.py:110
  39.5 1.3 %fold.5 = (bf16[512,384]{1,0:T(8,128)(2,1)S(1)}, bf16[512,384]{1,0:T(8,128)(2,1)S(1)}, f32[8,128]{1,0:T(8,128)S(1)}) custom-call(bf16[1024,384]{1,0:T(8,128)(2,1)} %collective-permute-done.2.refs_0_, bf16[1024,384]{1,0:T(8,128)(2,1)S(1)} %get-tuple-element.48.refs_1_, f32[8,128]{1,0:T(8,128)S(1)} %get-tuple-element.51.refs_2_), custom_call_target="tpu_custom_call" | custom-call | flops 1179648 | bytes 2359296 | tf_op jit(solution)/shard_map/fold/pallas_call | solution.py:133
  40.9 1.1 fold.6
  42.0 3.2 %collective-permute-start.7 = (bf16[272,384]{1,0:T(8,128)(2,1)S(1)}, bf16[272,384]{1,0:T(8,128)(2,1)S(1)}, u32[]{:S(2)}, u32[]{:S(2)}) collective-permute-start(bf16[272,384]{1,0:T(8,128)(2,1)S(1)} %get-tuple-element.60), channel_id=1, source_target_pairs={{0,4},{1,3},{2,6},{3,1},{4,0},{5,7},{6,2},{7,5},{8,12},{9,11},{10,... | collective-permute-start | bytes 626696 | tf_op jit(solution)/shard_map/ppermute | solution.py:46
  45.3 3.8 %collective-permute-done.7.refs_0_ = bf16[272,384]{1,0:T(8,128)(2,1)S(1)} collective-permute-done((bf16[272,384]{1,0:T(8,128)(2,1)S(1)}, bf16[272,384]{1,0:T(8,128)(2,1)S(1)}, u32[]{:S(2)}, u32[]{:S(2)}) %collective-permute-start.7) | collective-permute-done | bytes 208928 | tf_op jit(solution)/shard_map/ppermute | solution.py:46
  49.1 3.5 %collective-permute-start.9 = (bf16[272,384]{1,0:T(8,128)(2,1)S(1)}, bf16[272,384]{1,0:T(8,128)(2,1)S(1)}, u32[]{:S(2)}, u32[]{:S(2)}) collective-permute-start(bf16[272,384]{1,0:T(8,128)(2,1)S(1)} %get-tuple-element.65.refs_1_), channel_id=1, source_target_pairs={{0,24},{1,25},{2,26},{3,27},{4,28},{5,29},{6,30},{7,31},{8,16},{9,... | collective-permute-start | bytes 626696 | tf_op jit(solution)/shard_map/ppermute | solution.py:46
  52.6 0.6 fold.7
  53.2 1.5 %collective-permute-start.6 = (bf16[256,384]{1,0:T(8,128)(2,1)S(1)}, bf16[256,384]{1,0:T(8,128)(2,1)S(1)}, u32[]{:S(2)}, u32[]{:S(2)}) collective-permute-start(bf16[256,384]{1,0:T(8,128)(2,1)S(1)} %get-tuple-element.58), channel_id=1, source_target_pairs={{0,2},{1,5},{2,0},{3,7},{4,6},{5,1},{6,4},{7,3},{8,10},{9,13},{10,... | collective-permute-start | bytes 589832 | tf_op jit(solution)/shard_map/ppermute | solution.py:46
  54.7 2.1 %collective-permute-done.9.refs_0_ = bf16[272,384]{1,0:T(8,128)(2,1)S(1)} collective-permute-done((bf16[272,384]{1,0:T(8,128)(2,1)S(1)}, bf16[272,384]{1,0:T(8,128)(2,1)S(1)}, u32[]{:S(2)}, u32[]{:S(2)}) %collective-permute-start.9) | collective-permute-done | bytes 208928 | tf_op jit(solution)/shard_map/ppermute | solution.py:46
  57.1 2.1 %collective-permute-start.11 = (bf16[256,384]{1,0:T(8,128)(2,1)S(1)}, bf16[256,384]{1,0:T(8,128)(2,1)S(1)}, u32[]{:S(2)}, u32[]{:S(2)}) collective-permute-start(bf16[256,384]{1,0:T(8,128)(2,1)S(1)} %get-tuple-element.72.refs_1_), channel_id=1, source_target_pairs={{0,4},{1,3},{2,6},{3,1},{4,0},{5,7},{6,2},{7,5},{8,12},{9,11},{10,... | collective-permute-start | bytes 589832 | tf_op jit(solution)/shard_map/ppermute | solution.py:46
  59.3 0.6 seed.3
  59.9 3.5 %collective-permute-start.8 = (bf16[256,384]{1,0:T(8,128)(2,1)S(1)}, bf16[256,384]{1,0:T(8,128)(2,1)S(1)}, u32[]{:S(2)}, u32[]{:S(2)}) collective-permute-start(bf16[256,384]{1,0:T(8,128)(2,1)S(1)} %get-tuple-element.63.refs_1_), channel_id=1, source_target_pairs={{0,24},{1,25},{2,26},{3,27},{4,28},{5,29},{6,30},{7,31},{8,16},{9,... | collective-permute-start | bytes 589832 | tf_op jit(solution)/shard_map/ppermute | solution.py:46
  63.4 1.8 %collective-permute-start.13 = (bf16[512,384]{1,0:T(8,128)(2,1)S(1)}, bf16[512,384]{1,0:T(8,128)(2,1)S(1)}, u32[]{:S(2)}, u32[]{:S(2)}) collective-permute-start(bf16[512,384]{1,0:T(8,128)(2,1)S(1)} %get-tuple-element.75.refs_1_), channel_id=1, source_target_pairs={{0,8},{1,9},{2,10},{3,11},{4,12},{5,13},{6,14},{7,15},{8,0},{9,1},... | collective-permute-start | bytes 1179656 | tf_op jit(solution)/shard_map/ppermute | solution.py:46
  65.2 4.2 %collective-permute-done.8.refs_0_ = bf16[256,384]{1,0:T(8,128)(2,1)S(1)} collective-permute-done((bf16[256,384]{1,0:T(8,128)(2,1)S(1)}, bf16[256,384]{1,0:T(8,128)(2,1)S(1)}, u32[]{:S(2)}, u32[]{:S(2)}) %collective-permute-start.8) | collective-permute-done | bytes 196640 | tf_op jit(solution)/shard_map/ppermute | solution.py:46
  69.5 1.0 last_centroids.1
  70.4 1.3 %collective-permute-start.10 = (bf16[272,384]{1,0:T(8,128)(2,1)S(1)}, bf16[272,384]{1,0:T(8,128)(2,1)S(1)}, u32[]{:S(2)}, u32[]{:S(2)}) collective-permute-start(bf16[272,384]{1,0:T(8,128)(2,1)S(1)} %get-tuple-element.71.refs_1_), channel_id=1, source_target_pairs={{0,2},{1,5},{2,0},{3,7},{4,6},{5,1},{6,4},{7,3},{8,10},{9,13},{10,... | collective-permute-start | bytes 626696 | tf_op jit(solution)/shard_map/ppermute | solution.py:46
  71.7 4.5 %collective-permute-done.10.refs_0_ = bf16[272,384]{1,0:T(8,128)(2,1)S(1)} collective-permute-done((bf16[272,384]{1,0:T(8,128)(2,1)S(1)}, bf16[272,384]{1,0:T(8,128)(2,1)S(1)}, u32[]{:S(2)}, u32[]{:S(2)}) %collective-permute-start.10) | collective-permute-done | bytes 208928 | tf_op jit(solution)/shard_map/ppermute | solution.py:46
  76.3 1.0 join.6
  77.8 1.3 %collective-permute-start.16 = (bf16[1024,384]{1,0:T(8,128)(2,1)}, bf16[1024,384]{1,0:T(8,128)(2,1)}, u32[]{:S(2)}, u32[]{:S(2)}) collective-permute-start(bf16[1024,384]{1,0:T(8,128)(2,1)} %get-tuple-element.77.refs_2_), channel_id=1, source_target_pairs={{0,2},{1,5},{2,0},{3,7},{4,6},{5,1},{6,4},{7,3},{8,10},{9,13},{10,... | collective-permute-start | bytes 2359304 | tf_op jit(solution)/shard_map/ppermute | solution.py:46
  79.1 1.8 %copy.10 = s32[1280,1]{1,0:T(8,128)} copy(s32[1280,1]{0,1:T(1,128)} %param.6) | data formatting | bytes 10240 | tf_op args[1]
  81.0 1.2 collective-permute-start.12
  82.2 1.2 fusion.3.refs_1_.gid_ref
  83.4 0.7 copy-done.9
  84.1 7.2 %part_scores.2 = (bf16[1280,1024]{1,0:T(8,128)(2,1)}, f32[8,128]{1,0:T(8,128)S(1)}) custom-call(s32[16]{0:T(128)S(1)} %stack.212.code_ref, bf16[1280,768]{1,0:T(8,128)(2,1)} %x_ref.1, s32[1280,1]{1,0:T(8,128)S(1)} %fusion.3.refs_1_.gid_ref, bf16[1024,384]{1,0:T(8,128)(2,1)} %get-tuple-element.77.refs_2_, bf16[1024,384]{1,0:T(8,128)(2,1)} %collective-permute-done.14.refs_3_, ...), custom_call_target="tpu_custom_call" | custom-call | flops 1 | bytes 1 | tf_op jit(solution)/shard_map/part_scores/pallas_call | solution.py:323
  91.3 0.7 collective-permute-done.12.refs_0_
  92.0 1.0 join.7
  93.0 2.9 %collective-permute-start.15 = (bf16[1040,384]{1,0:T(8,128)(2,1)}, bf16[1040,384]{1,0:T(8,128)(2,1)}, u32[]{:S(2)}, u32[]{:S(2)}) collective-permute-start(bf16[1040,384]{1,0:T(8,128)(2,1)} %get-tuple-element.80.rest_2_), channel_id=1, source_target_pairs={{0,4},{1,3},{2,6},{3,1},{4,0},{5,7},{6,2},{7,5},{8,12},{9,11},{10,... | collective-permute-start | bytes 2396168 | tf_op jit(solution)/shard_map/ppermute | solution.py:46
  96.4 3.1 %collective-permute-done.17.refs_3_ = bf16[1024,384]{1,0:T(8,128)(2,1)S(1)} collective-permute-done((bf16[1024,384]{1,0:T(8,128)(2,1)}, bf16[1024,384]{1,0:T(8,128)(2,1)S(1)}, u32[]{:S(2)}, u32[]{:S(2)}) %collective-permute-start.17) | collective-permute-done | bytes 786464 | tf_op jit(solution)/shard_map/ppermute | solution.py:46
  99.5 7.0 %part_scores.3 = (bf16[1280,1024]{1,0:T(8,128)(2,1)}, f32[8,128]{1,0:T(8,128)S(1)}) custom-call(s32[16]{0:T(128)S(1)} %stack.212.code_ref, bf16[1280,768]{1,0:T(8,128)(2,1)} %x_ref.1, s32[1280,1]{1,0:T(8,128)S(1)} %fusion.3.refs_1_.gid_ref, bf16[1024,384]{1,0:T(8,128)(2,1)} %collective-permute-done.16.refs_2_, ...), custom_call_target="tpu_custom_call", output_to_operand_aliasing={{0}: (5, {})} | custom-call | flops 1 | bytes 1 | tf_op jit(solution)/shard_map/part_scores/pallas_call | solution.py:323
  106.9 2.4 %collective-permute-done.18.rest_1_ = bf16[1040,384]{1,0:T(8,128)(2,1)} collective-permute-done((bf16[1040,384]{1,0:T(8,128)(2,1)}, bf16[1040,384]{1,0:T(8,128)(2,1)}, u32[]{:S(2)}, u32[]{:S(2)}) %collective-permute-start.18) | collective-permute-done | bytes 798752 | tf_op jit(solution)/shard_map/ppermute | solution.py:46
  109.2 1.1 copy-done.5
  110.3 11.2 %final_scores.1 = bf16[1280,1024]{1,0:T(8,128)(2,1)} custom-call(s32[32]{0:T(128)S(1)} %concatenate.104.code_ref, s32[8]{0:T(128)S(1)} %fusion.22.slot_ref, bf16[1280,768]{1,0:T(8,128)(2,1)} %x_ref.1, s32[1280,1]{1,0:T(8,128)S(1)} %copy-done.5, f32[16,1024]{1,0:T(8,128)S(1)} %broadcast_in_dim.28.half_ref, bf16[1040,384]{1,0:T(8,128)(2,1)} %behind.1.rest_0_, ...), custom_call_target="tpu_custom_call" | custom-call | flops 1 | bytes 1 | tf_op jit(solution)/shard_map/final_scores/pallas_call | solution.py:400
  (55 shorter events, 3.6 us)
Async XLA Ops:
  0.6 31.3 %copy-start = (f32[1,1024,768]{2,1,0:T(8,128)S(1)}, f32[1,1024,768]{2,1,0:T(8,128)}, u32[]{:S(2)}) copy-start(f32[1,1024,768]{2,1,0:T(8,128)} %param.9) | copy-start | bytes 9437188
  3.0 1.3 %collective-permute-start = (s32[1280]{0:T(1024)S(1)}, s32[1280]{0:T(1024)S(1)}, u32[]{:S(2)}, u32[]{:S(2)}) collective-permute-start(s32[1280]{0:T(1024)S(1)} %add_select_fusion.9), channel_id=1, source_target_pairs={{0,1},{1,0},{2,3},{3,2},{4,5},{5,4},{6,7},{7,6},{8,9},{9,8},{10,11... | collective-permute-start | bytes 15368 | tf_op jit(solution)/shard_map/ppermute | solution.py:46
  3.5 4.3 %collective-permute-start.1 = (bf16[1280,768]{1,0:T(8,128)(2,1)}, bf16[1280,768]{1,0:T(8,128)(2,1)}, u32[]{:S(2)}, u32[]{:S(2)}) collective-permute-start(bf16[1280,768]{1,0:T(8,128)(2,1)} %x_ref.1), channel_id=1, source_target_pairs={{0,1},{1,0},{2,3},{3,2},{4,5},{5,4},{6,7},{7,6},{8,9},{9,8},{10,11... | collective-permute-start | bytes 5898248 | tf_op jit(solution)/shard_map/ppermute | solution.py:46
  7.8 1.5 %copy-start.1 = (bf16[1280,768]{1,0:T(8,128)(2,1)S(1)}, bf16[1280,768]{1,0:T(8,128)(2,1)}, u32[]{:S(2)}) copy-start(bf16[1280,768]{1,0:T(8,128)(2,1)} %x_ref.1) | copy-start | bytes 5898244
  9.3 7.0 %copy-start.2 = (bf16[1280,768]{1,0:T(8,128)(2,1)S(1)}, bf16[1280,768]{1,0:T(8,128)(2,1)}, u32[]{:S(2)}) copy-start(bf16[1280,768]{1,0:T(8,128)(2,1)} %x_ref.1) | copy-start | bytes 5898244
  13.6 14.8 %collective-permute-start.3 = (bf16[1040,384]{1,0:T(8,128)(2,1)S(1)}, bf16[1040,384]{1,0:T(8,128)(2,1)S(1)}, u32[]{:S(2)}, u32[]{:S(2)}) collective-permute-start(bf16[1040,384]{1,0:T(8,128)(2,1)S(1)} %get-tuple-element.49), channel_id=1, source_target_pairs={{0,2},{1,5},{2,0},{3,7},{4,6},{5,1},{6,4},{7,3},{8,10},{9,13},{10,... | collective-permute-start | bytes 2396168 | tf_op jit(solution)/shard_map/ppermute | solution.py:46
  16.4 5.1 %copy-start.6 = (s32[1,2560]{1,0:T(1,128)}, s32[1,2560]{1,0:T(1,128)S(1)}, u32[]{:S(2)}) copy-start(s32[1,2560]{1,0:T(1,128)S(1)} %fusion.11.refs_0_) | copy-start | bytes 30724
  21.4 18.1 %collective-permute-start.2 = (bf16[1024,384]{1,0:T(8,128)(2,1)}, bf16[1024,384]{1,0:T(8,128)(2,1)}, u32[]{:S(2)}, u32[]{:S(2)}) collective-permute-start(bf16[1024,384]{1,0:T(8,128)(2,1)} %get-tuple-element.45), channel_id=1, source_target_pairs={{0,4},{1,3},{2,6},{3,1},{4,0},{5,7},{6,2},{7,5},{8,12},{9,11},{10,... | collective-permute-start | bytes 2359304 | tf_op jit(solution)/shard_map/ppermute | solution.py:46
  27.1 2.2 %copy-start.10 = (f32[8,128]{1,0:T(8,128)}, f32[8,128]{1,0:T(8,128)S(1)}, u32[]{:S(2)}) copy-start(f32[8,128]{1,0:T(8,128)S(1)} %get-tuple-element.47.refs_3_) | copy-start | bytes 12292
  29.3 11.6 %collective-permute-start.5 = (bf16[528,384]{1,0:T(8,128)(2,1)}, bf16[528,384]{1,0:T(8,128)(2,1)}, u32[]{:S(2)}, u32[]{:S(2)}) collective-permute-start(bf16[528,384]{1,0:T(8,128)(2,1)} %get-tuple-element.54), channel_id=1, source_target_pairs={{0,8},{1,9},{2,10},{3,11},{4,12},{5,13},{6,14},{7,15},{8,0},{9,1},... | collective-permute-start | bytes 1216520 | tf_op jit(solution)/shard_map/ppermute | solution.py:46
  31.9 1.5 %copy-start.3 = (bf16[1280,768]{1,0:T(8,128)(2,1)S(1)}, bf16[1280,768]{1,0:T(8,128)(2,1)}, u32[]{:S(2)}) copy-start(bf16[1280,768]{1,0:T(8,128)(2,1)} %x_ref.1) | copy-start | bytes 5898244
  33.5 0.7 copy-start.7
  34.2 0.7 copy-start.11
  40.8 11.8 %collective-permute-start.4 = (bf16[512,384]{1,0:T(8,128)(2,1)S(1)}, bf16[512,384]{1,0:T(8,128)(2,1)S(1)}, u32[]{:S(2)}, u32[]{:S(2)}) collective-permute-start(bf16[512,384]{1,0:T(8,128)(2,1)S(1)} %get-tuple-element.52), channel_id=1, source_target_pairs={{0,8},{1,9},{2,10},{3,11},{4,12},{5,13},{6,14},{7,15},{8,0},{9,1},... | collective-permute-start | bytes 1179656 | tf_op jit(solution)/shard_map/ppermute | solution.py:46
  42.0 7.0 %collective-permute-start.7 = (bf16[272,384]{1,0:T(8,128)(2,1)S(1)}, bf16[272,384]{1,0:T(8,128)(2,1)S(1)}, u32[]{:S(2)}, u32[]{:S(2)}) collective-permute-start(bf16[272,384]{1,0:T(8,128)(2,1)S(1)} %get-tuple-element.60), channel_id=1, source_target_pairs={{0,4},{1,3},{2,6},{3,1},{4,0},{5,7},{6,2},{7,5},{8,12},{9,11},{10,... | collective-permute-start | bytes 626696 | tf_op jit(solution)/shard_map/ppermute | solution.py:46
  49.1 7.7 %collective-permute-start.9 = (bf16[272,384]{1,0:T(8,128)(2,1)S(1)}, bf16[272,384]{1,0:T(8,128)(2,1)S(1)}, u32[]{:S(2)}, u32[]{:S(2)}) collective-permute-start(bf16[272,384]{1,0:T(8,128)(2,1)S(1)} %get-tuple-element.65.refs_1_), channel_id=1, source_target_pairs={{0,24},{1,25},{2,26},{3,27},{4,28},{5,29},{6,30},{7,31},{8,16},{9,... | collective-permute-start | bytes 626696 | tf_op jit(solution)/shard_map/ppermute | solution.py:46
  53.2 6.1 %collective-permute-start.6 = (bf16[256,384]{1,0:T(8,128)(2,1)S(1)}, bf16[256,384]{1,0:T(8,128)(2,1)S(1)}, u32[]{:S(2)}, u32[]{:S(2)}) collective-permute-start(bf16[256,384]{1,0:T(8,128)(2,1)S(1)} %get-tuple-element.58), channel_id=1, source_target_pairs={{0,2},{1,5},{2,0},{3,7},{4,6},{5,1},{6,4},{7,3},{8,10},{9,13},{10,... | collective-permute-start | bytes 589832 | tf_op jit(solution)/shard_map/ppermute | solution.py:46
  57.1 6.2 %collective-permute-start.11 = (bf16[256,384]{1,0:T(8,128)(2,1)S(1)}, bf16[256,384]{1,0:T(8,128)(2,1)S(1)}, u32[]{:S(2)}, u32[]{:S(2)}) collective-permute-start(bf16[256,384]{1,0:T(8,128)(2,1)S(1)} %get-tuple-element.72.refs_1_), channel_id=1, source_target_pairs={{0,4},{1,3},{2,6},{3,1},{4,0},{5,7},{6,2},{7,5},{8,12},{9,11},{10,... | collective-permute-start | bytes 589832 | tf_op jit(solution)/shard_map/ppermute | solution.py:46
  59.9 9.6 %collective-permute-start.8 = (bf16[256,384]{1,0:T(8,128)(2,1)S(1)}, bf16[256,384]{1,0:T(8,128)(2,1)S(1)}, u32[]{:S(2)}, u32[]{:S(2)}) collective-permute-start(bf16[256,384]{1,0:T(8,128)(2,1)S(1)} %get-tuple-element.63.refs_1_), channel_id=1, source_target_pairs={{0,24},{1,25},{2,26},{3,27},{4,28},{5,29},{6,30},{7,31},{8,16},{9,... | collective-permute-start | bytes 589832 | tf_op jit(solution)/shard_map/ppermute | solution.py:46
  63.4 12.9 %collective-permute-start.13 = (bf16[512,384]{1,0:T(8,128)(2,1)S(1)}, bf16[512,384]{1,0:T(8,128)(2,1)S(1)}, u32[]{:S(2)}, u32[]{:S(2)}) collective-permute-start(bf16[512,384]{1,0:T(8,128)(2,1)S(1)} %get-tuple-element.75.refs_1_), channel_id=1, source_target_pairs={{0,8},{1,9},{2,10},{3,11},{4,12},{5,13},{6,14},{7,15},{8,0},{9,1},... | collective-permute-start | bytes 1179656 | tf_op jit(solution)/shard_map/ppermute | solution.py:46
  70.4 5.8 %collective-permute-start.10 = (bf16[272,384]{1,0:T(8,128)(2,1)S(1)}, bf16[272,384]{1,0:T(8,128)(2,1)S(1)}, u32[]{:S(2)}, u32[]{:S(2)}) collective-permute-start(bf16[272,384]{1,0:T(8,128)(2,1)S(1)} %get-tuple-element.71.refs_1_), channel_id=1, source_target_pairs={{0,2},{1,5},{2,0},{3,7},{4,6},{5,1},{6,4},{7,3},{8,10},{9,13},{10,... | collective-permute-start | bytes 626696 | tf_op jit(solution)/shard_map/ppermute | solution.py:46
  77.2 0.6 copy-start.8
  77.8 5.6 %collective-permute-start.14 = (bf16[1024,384]{1,0:T(8,128)(2,1)}, bf16[1024,384]{1,0:T(8,128)(2,1)}, u32[]{:S(2)}, u32[]{:S(2)}) collective-permute-start(bf16[1024,384]{1,0:T(8,128)(2,1)} %get-tuple-element.77.refs_2_), channel_id=1, source_target_pairs={{0,1},{1,0},{2,3},{3,2},{4,5},{5,4},{6,7},{7,6},{8,9},{9,8},{10,11... | collective-permute-start | bytes 2359304 | tf_op jit(solution)/shard_map/ppermute | solution.py:46
  77.8 18.0 %collective-permute-start.16 = (bf16[1024,384]{1,0:T(8,128)(2,1)}, bf16[1024,384]{1,0:T(8,128)(2,1)}, u32[]{:S(2)}, u32[]{:S(2)}) collective-permute-start(bf16[1024,384]{1,0:T(8,128)(2,1)} %get-tuple-element.77.refs_2_), channel_id=1, source_target_pairs={{0,2},{1,5},{2,0},{3,7},{4,6},{5,1},{6,4},{7,3},{8,10},{9,13},{10,... | collective-permute-start | bytes 2359304 | tf_op jit(solution)/shard_map/ppermute | solution.py:46
  81.0 11.0 %collective-permute-start.12 = (bf16[528,384]{1,0:T(8,128)(2,1)S(1)}, bf16[528,384]{1,0:T(8,128)(2,1)S(1)}, u32[]{:S(2)}, u32[]{:S(2)}) collective-permute-start(bf16[528,384]{1,0:T(8,128)(2,1)S(1)} %get-tuple-element.74.refs_1_), channel_id=1, source_target_pairs={{0,8},{1,9},{2,10},{3,11},{4,12},{5,13},{6,14},{7,15},{8,0},{9,1},... | collective-permute-start | bytes 1216520 | tf_op jit(solution)/shard_map/ppermute | solution.py:46
  83.4 23.1 %copy-start.4 = (s32[1280,1]{1,0:T(8,128)}, s32[1280,1]{1,0:T(8,128)S(1)}, u32[]{:S(2)}) copy-start(s32[1280,1]{1,0:T(8,128)S(1)} %fusion.3.refs_1_.gid_ref) | copy-start | bytes 15364
  83.4 0.7 copy-start.9
  93.0 13.5 %collective-permute-start.15 = (bf16[1040,384]{1,0:T(8,128)(2,1)}, bf16[1040,384]{1,0:T(8,128)(2,1)}, u32[]{:S(2)}, u32[]{:S(2)}) collective-permute-start(bf16[1040,384]{1,0:T(8,128)(2,1)} %get-tuple-element.80.rest_2_), channel_id=1, source_target_pairs={{0,4},{1,3},{2,6},{3,1},{4,0},{5,7},{6,2},{7,5},{8,12},{9,11},{10,... | collective-permute-start | bytes 2396168 | tf_op jit(solution)/shard_map/ppermute | solution.py:46
  95.9 3.6 %collective-permute-start.17 = (bf16[1024,384]{1,0:T(8,128)(2,1)}, bf16[1024,384]{1,0:T(8,128)(2,1)S(1)}, u32[]{:S(2)}, u32[]{:S(2)}) collective-permute-start(bf16[1024,384]{1,0:T(8,128)(2,1)} %collective-permute-done.16.refs_2_), channel_id=1, source_target_pairs={{0,1},{1,0},{2,3},{3,2},{4,5},{5,4},{6,7},{7,6},{8,9},{9,8},{10,11... | collective-permute-start | bytes 2359304 | tf_op jit(solution)/shard_map/ppermute | solution.py:46
  95.9 11.0 %collective-permute-start.19 = (bf16[1040,384]{1,0:T(8,128)(2,1)}, bf16[1040,384]{1,0:T(8,128)(2,1)}, u32[]{:S(2)}, u32[]{:S(2)}) collective-permute-start(bf16[1040,384]{1,0:T(8,128)(2,1)} %get-tuple-element.80.rest_2_), channel_id=1, source_target_pairs={{0,1},{1,0},{2,3},{3,2},{4,5},{5,4},{6,7},{7,6},{8,9},{9,8},{10,11... | collective-permute-start | bytes 2396168 | tf_op jit(solution)/shard_map/ppermute | solution.py:46
  106.5 2.7 %collective-permute-start.18 = (bf16[1040,384]{1,0:T(8,128)(2,1)}, bf16[1040,384]{1,0:T(8,128)(2,1)}, u32[]{:S(2)}, u32[]{:S(2)}) collective-permute-start(bf16[1040,384]{1,0:T(8,128)(2,1)} %behind.1.rest_0_), channel_id=1, source_target_pairs={{0,1},{1,0},{2,3},{3,2},{4,5},{5,4},{6,7},{7,6},{8,9},{9,8},{10,11... | collective-permute-start | bytes 2396168 | tf_op jit(solution)/shard_map/ppermute | solution.py:46
  109.2 1.1 copy-start.5

commit v8 on v7

--- a/solution.py
+++ b/solution.py
@@ -102,8 +102,8 @@
         out_ref[keys:, :] = rest[0][...]
 
 
-def key_sums(token, pos_row, own, other, count_tile, base, keys, start, wide):
-    rows = own.shape[0]
+def key_sums(token, pos_row, own, other, count_tile, base, keys):
+    rows, wide = own.shape
     extra = [] if count_tile is None else [count_tile]
     out_rows = keys + sum(e.shape[0] for e in extra)
     whole = lambda shape: pl.BlockSpec(shape, lambda i: (0, 0))
@@ -113,8 +113,8 @@
         out_shape=[jax.ShapeDtypeStruct((out_rows, wide), BF16), token_shape()],
         in_specs=[
             whole((1, 2 * rows)),
-            pl.BlockSpec((rows, wide), lambda i: (0, start // wide)),
-            pl.BlockSpec((rows, wide), lambda i: (0, start // wide)),
+            whole((rows, wide)),
+            whole((rows, wide)),
         ]
         + [whole(e.shape) for e in extra]
         + [whole(token.shape)],
@@ -254,25 +254,26 @@
     )(array, token)
 
 
-def row_loads(x_ref, gid_ref, x, gid, sem, start):
-    return (
-        pltpu.make_async_copy(x_ref.at[:, pl.ds(start, x.shape[1])], x, sem.at[0]),
-        pltpu.make_async_copy(gid_ref, gid, sem.at[1]),
-    )
-
-
-def mask_rows(groups, x, gid, out):
+def row_load(x_ref, x, sem, start):
+    return pltpu.make_async_copy(x_ref.at[:, pl.ds(start, x.shape[1])], x, sem)
+
+
+def mask_rows(groups, x, gid_ref, out):
     wide = x.shape[1]
+    gid = jnp.transpose(jnp.broadcast_to(gid_ref[...], (128, gid_ref.shape[1])))
     for group in range(groups):
-        out[:, group * wide : (group + 1) * wide] = jnp.where(gid[...] == group, x[...], jnp.zeros_like(x))
+        keep = gid == group
+        for cut in range(0, wide, 128):
+            part = x[:, cut : cut + 128]
+            out[:, group * wide + cut : group * wide + cut + 128] = jnp.where(keep, part, jnp.zeros_like(part))
+    return gid
 
 
 def row_scratch(rows, groups, wide):
     return [
         pltpu.VMEM((rows, groups * wide), BF16),
         pltpu.VMEM((rows, wide), BF16),
-        pltpu.VMEM((rows, 1), jnp.int32),
-        pltpu.SemaphoreType.DMA((2,)),
+        pltpu.SemaphoreType.DMA,
     ]
 
 
@@ -281,23 +282,21 @@
 
 
 def part_kernel(groups, share, start_at, code_ref, x_ref, gid_ref, own_ref, other_ref, *rest):
-    out_ref, cents, rows_of, x, gid, sem = rest
-    loads = row_loads(x_ref, gid_ref, x, gid, sem, start_at)
+    out_ref, cents, rows_of, x, sem = rest
+    load = row_load(x_ref, x, sem, start_at)
     wide = own_ref.shape[1]
     blocks = own_ref.shape[0] // share
 
     @pl.when(pl.program_id(0) == 0)
     def _():
-        for load in loads:
-            load.start()
+        load.start()
         for piece, ref in enumerate((own_ref, other_ref)):
             for block in range(blocks):
                 code = code_ref[piece * blocks + block]
                 slot = pl.multiple_of(code // groups * share, share)
                 cents[pl.ds(slot, share), pl.ds(pl.multiple_of(code % groups * wide, 128), wide)] = ref[block * share : (block + 1) * share, :]
-        for load in loads:
-            load.wait()
-        mask_rows(groups, x, gid, rows_of)
+        load.wait()
+        mask_rows(groups, x, gid_ref, rows_of)
 
     step = out_ref.shape[1]
     start = pl.multiple_of(pl.program_id(0) * step, step)
@@ -317,7 +316,7 @@
 
     def kernel(code_ref, *refs):
         count = 4 + len(extra)
-        part_kernel(groups, share, start_at, code_ref, *refs[:4], refs[count + 1], *refs[-5:])
+        part_kernel(groups, share, start_at, code_ref, *refs[:4], refs[count + 1], *refs[-4:])
         refs[count + 2][...] = refs[count][...]
 
     return pl.pallas_call(
@@ -325,7 +324,7 @@
         grid_spec=pltpu.PrefetchScalarGridSpec(
             num_scalar_prefetch=1,
             grid=(steps,),
-            in_specs=[anywhere] * 2 + [whole] * 2 + [anywhere] * len(extra) + [whole],
+            in_specs=[anywhere] + [whole] * 3 + [anywhere] * len(extra) + [whole],
             out_specs=[pl.BlockSpec((rows, step), lambda i, w: (0, i + at)), whole],
             scratch_shapes=[
                 pltpu.VMEM((half, groups * wide), BF16),
@@ -343,8 +342,8 @@
 def final_kernel(groups, share, start_at, code_ref, slot_ref, x_ref, gid_ref, half_ref, *rest):
     pieces = 4
     piece_refs, total_refs = rest[:pieces], rest[pieces : pieces + 2]
-    out_ref, cents, half, pick, rows_of, x, gid, sem = rest[-8:]
-    loads = row_loads(x_ref, gid_ref, x, gid, sem, start_at)
+    out_ref, cents, half, pick, rows_of, x, sem = rest[-7:]
+    load = row_load(x_ref, x, sem, start_at)
     keys = cents.shape[0]
     wide = cents.shape[1] // groups
     members = keys // share
@@ -353,8 +352,7 @@
 
     @pl.when(pl.program_id(0) == 0)
     def _():
-        for load in loads:
-            load.start()
+        load.start()
         half[...] = half_ref[...]
         for piece, ref in enumerate(piece_refs):
             for block in range(blocks):
@@ -374,11 +372,10 @@
                         row = tail[at : at + 1, term * share : (term + 1) * share]
                         filled = jnp.where(line == group + term * groups, row, filled)
                     half[:, lines] = filled
-        for load in loads:
-            load.wait()
-        mask_rows(groups, x, gid, rows_of)
+        load.wait()
+        gid = mask_rows(groups, x, gid_ref, rows_of)[:, : pick.shape[1]]
         lane = lax.broadcasted_iota(jnp.int32, pick.shape, 1)
-        hit = (lane % groups == gid[...]) & (lane < PARTS * groups)
+        hit = (lane % groups == gid) & (lane < PARTS * groups)
         pick[...] = jnp.where(hit, -1.0, 0.0).astype(BF16)
 
     step = out_ref.shape[1]
@@ -402,8 +399,8 @@
         grid_spec=pltpu.PrefetchScalarGridSpec(
             num_scalar_prefetch=2,
             grid=(keys // step,),
-            in_specs=[pl.BlockSpec(memory_space=pl.ANY)] * 2
-            + [whole] * (1 + len(pieces))
+            in_specs=[pl.BlockSpec(memory_space=pl.ANY)]
+            + [whole] * (2 + len(pieces))
             + [
                 pl.BlockSpec((rows, cut), lambda i, c, s: (0, s[2 * i])),
                 pl.BlockSpec((rows, cut), lambda i, c, s: (0, s[2 * i + 1])),
@@ -447,7 +444,8 @@
     live = jnp.arange(rows, dtype=jnp.int32) < live_rows[0]
     label = jnp.where(live, coarse_label[:, 0] * keys + fine_label, -1)
     sibling = lambda a: exchange(a, lambda gz, m: (gz, m ^ 1), groups, members)
-    other_samples = sibling(samples)
+    cut_rows = [samples[:, start : start + wide] for start, wide in streams_of(width)]
+    other_rows = [sibling(part) for part in cut_rows]
     label_all = jnp.concatenate([label, sibling(label)])
 
     group_of = label_all // keys
@@ -490,7 +488,7 @@
     for part, found in enumerate((send, keep)):
         for stream, (start, wide) in enumerate(columns):
             found[stream], token = key_sums(
-                token, rows_of[stream], samples, other_samples, tiles[stream], part * half_keys, half_keys, start, wide
+                token, rows_of[stream], cut_rows[stream], other_rows[stream], tiles[stream], part * half_keys, half_keys
             )
 
     tokens = [start_token] * 2
@@ -573,7 +571,7 @@
                 codes.append(jnp.where(core ^ flip == 0, *code))
         return jnp.stack(codes).astype(jnp.int32)
 
-    gid = jnp.where(live, coarse_label[:, 0], -1)[:, None]
+    gid = jnp.where(live, coarse_label[:, 0], -1)[None, :]
     count = 2
     arrived = [None] * 2
     for stage in reversed(range(stages - 1)):

time: 123 us -> 121 us (0.984)
  local copies, waits for them, and re-layouts: 8.91 us -> 6.59 us
    unnamed x26 -> x19, local copies, waits for them, and re-layouts: 8.64 us -> 3.32 us
    slice x0 -> x1, local copies, waits for them, and re-layouts: none -> 3.01 us  [per_device(): samples[:, start:start + wide]]
    ppermute x20 -> x21, waiting for transfers between devices: 25.5 us -> 25.8 us  [exchange(): return lax.ppermute(array, AXES, pairs)]
    ppermute x20 -> x21, starting transfers between devices: 30.4 us -> 30.2 us  [exchange(): return lax.ppermute(array, AXES, pairs)]
  transfers between devices with their start and end apart: 20 -> 21, of which waited for: 10 -> 12; matrix products, arithmetic and copies ran while one was open for 3% -> 4% of each run, Pallas kernels for 29% -> 34%
where the time goes in v8:
time: 121 us; the launch traced here: 120 us
  Pallas kernels  52.3 us (43%)
  starting transfers between devices  30.2 us (25%)
  waiting for transfers between devices  25.8 us (21%)
  local copies, waits for them, and re-layouts  6.59 us (5%)
  other arithmetic  2.61 us (2%)
  between operations  1.8 us (1%)
    ppermute x21, starting transfers between devices, exchange(): return lax.ppermute(array, AXES, pairs)  30.2 us
    ppermute x21, waiting for transfers between devices, exchange(): return lax.ppermute(array, AXES, pairs)  25.8 us
    pallas_call x4, Pallas kernels, key_sums(): pl.pallas_call(hand_on(functools.partial(sums_kernel, base), 3 + len(extr...  18.8 us
    pallas_call x2, Pallas kernels, part_scores(): pl.pallas_call(kernel, grid_spec=pltpu.PrefetchScalarGridSpec(num_scalar_...  14.5 us
    pallas_call x1, Pallas kernels, final_scores(): pl.pallas_call(functools.partial(final_kernel, groups, share, start_at),...  11 us
    pallas_call x12, Pallas kernels, small_call(): pl.pallas_call(hand_on(kernel, len(args)), out_shape=[*outs, token_shape(...  7.89 us
    unnamed x19, local copies, waits for them, and re-layouts  3.32 us
    slice x1, local copies, waits for them, and re-layouts, per_device(): samples[:, start:start + wide]  3.01 us
  transfers between devices with their start and end apart: 21, of which 12 were waited for; matrix products, arithmetic and copies ran while one was open for 4% of the time, Pallas kernels for 34%

profile of v8, /device:TPU:0, one launch (start us, length us, event | category | flops | bytes accessed | tf_op | source)
XLA Modules:
  0.0 119.8 jit_solution(10501092094807724593)
XLA Ops:
  1.4 0.9 multiply_reduce_fusion
  2.3 0.7 add_select_fusion.9
  3.5 3.0 %fusion.22 = (bf16[1280,384]{1,0:T(8,128)(2,1)}, bf16[1280,384]{1,0:T(8,128)(2,1)}) fusion(bf16[1280,768]{1,0:T(8,128)(2,1)} %x_ref.1), kind=kLoop, calls=%fused_computation.77 | loop fusion | bytes 3932160 | tf_op jit(solution)/shard_map/slice | solution.py:447
  7.3 0.6 fusion.15
  7.9 1.5 %collective-permute-done.2.refs_2_ = bf16[1280,384]{1,0:T(8,128)(2,1)} collective-permute-done((bf16[1280,384]{1,0:T(8,128)(2,1)}, bf16[1280,384]{1,0:T(8,128)(2,1)}, u32[]{:S(2)}, u32[]{:S(2)}) %collective-permute-start.2) | collective-permute-done | bytes 983072 | tf_op jit(solution)/shard_map/ppermute | solution.py:46
  9.4 4.4 %key_sums.4 = (bf16[1040,384]{1,0:T(8,128)(2,1)S(1)}, f32[8,128]{1,0:T(8,128)S(1)}) custom-call(s32[1,2560]{1,0:T(1,128)S(1)} %get-tuple-element.86.refs_0_, bf16[1280,384]{1,0:T(8,128)(2,1)} %get-tuple-element.93.refs_1_, bf16[1280,384]{1,0:T(8,128)(2,1)} %collective-permute-done.2.refs_2_, bf16[16,384]{1,0:T(8,128)(2,1)S(1)} %pad_maximum_fusion.refs_3_, ...), custom_call_target="tpu_custom_call" | custom-call | flops 2013265920 | bytes 2752512 | tf_op jit(solution)/shard_map/key_sums/pallas_call | solution.py:110
  13.7 2.7 %collective-permute-start.4 = (bf16[1040,384]{1,0:T(8,128)(2,1)S(1)}, bf16[1040,384]{1,0:T(8,128)(2,1)S(1)}, u32[]{:S(2)}, u32[]{:S(2)}) collective-permute-start(bf16[1040,384]{1,0:T(8,128)(2,1)S(1)} %get-tuple-element.49), channel_id=1, source_target_pairs={{0,2},{1,5},{2,0},{3,7},{4,6},{5,1},{6,4},{7,3},{8,10},{9,13},{10,... | collective-permute-start | bytes 2396168 | tf_op jit(solution)/shard_map/ppermute | solution.py:46
  16.5 5.2 %key_sums.5 = (bf16[1024,384]{1,0:T(8,128)(2,1)}, f32[8,128]{1,0:T(8,128)S(1)}) custom-call(s32[1,2560]{1,0:T(1,128)S(1)} %fusion.10.refs_0_, bf16[1280,384]{1,0:T(8,128)(2,1)} %get-tuple-element.94.refs_1_, bf16[1280,384]{1,0:T(8,128)(2,1)} %collective-permute-done.1.refs_2_, f32[8,128]{1,0:T(8,128)S(1)} %get-tuple-element.44.refs_3_), custom_call_target="tpu_custom_call" | custom-call | flops 2013265920 | bytes 2752512 | tf_op jit(solution)/shard_map/key_sums/pallas_call | solution.py:110
  21.8 1.5 %collective-permute-start.3 = (bf16[1024,384]{1,0:T(8,128)(2,1)}, bf16[1024,384]{1,0:T(8,128)(2,1)}, u32[]{:S(2)}, u32[]{:S(2)}) collective-permute-start(bf16[1024,384]{1,0:T(8,128)(2,1)} %get-tuple-element.45), channel_id=1, source_target_pairs={{0,4},{1,3},{2,6},{3,1},{4,0},{5,7},{6,2},{7,5},{8,12},{9,11},{10,... | collective-permute-start | bytes 2359304 | tf_op jit(solution)/shard_map/ppermute | solution.py:46
  23.3 4.4 %key_sums.6 = (bf16[1040,384]{1,0:T(8,128)(2,1)S(1)}, f32[8,128]{1,0:T(8,128)S(1)}) custom-call(s32[1,2560]{1,0:T(1,128)S(1)} %get-tuple-element.86.refs_0_, bf16[1280,384]{1,0:T(8,128)(2,1)} %get-tuple-element.93.refs_1_, bf16[1280,384]{1,0:T(8,128)(2,1)} %collective-permute-done.2.refs_2_, bf16[16,384]{1,0:T(8,128)(2,1)S(1)} %pad_maximum_fusion.refs_3_, ...), custom_call_target="tpu_custom_call" | custom-call | flops 2013265920 | bytes 2752512 | tf_op jit(solution)/shard_map/key_sums/pallas_call | solution.py:110
  27.7 0.7 collective-permute-done.4.refs_0_
  28.4 0.9 fold.4
  29.2 2.6 %collective-permute-start.6 = (bf16[528,384]{1,0:T(8,128)(2,1)}, bf16[528,384]{1,0:T(8,128)(2,1)}, u32[]{:S(2)}, u32[]{:S(2)}) collective-permute-start(bf16[528,384]{1,0:T(8,128)(2,1)} %get-tuple-element.54), channel_id=1, source_target_pairs={{0,8},{1,9},{2,10},{3,11},{4,12},{5,13},{6,14},{7,15},{8,0},{9,1},... | collective-permute-start | bytes 1216520 | tf_op jit(solution)/shard_map/ppermute | solution.py:46
  31.9 0.7 copy-done.4
  32.6 0.7 copy-done.8
  33.2 4.9 %key_sums.7 = (bf16[1024,384]{1,0:T(8,128)(2,1)S(1)}, f32[8,128]{1,0:T(8,128)}) custom-call(s32[1,2560]{1,0:T(1,128)S(1)} %copy-done.4, bf16[1280,384]{1,0:T(8,128)(2,1)} %get-tuple-element.94.refs_1_, bf16[1280,384]{1,0:T(8,128)(2,1)} %collective-permute-done.1.refs_2_, f32[8,128]{1,0:T(8,128)S(1)} %copy-done.8), custom_call_target="tpu_custom_call" | custom-call | flops 2013265920 | bytes 2752512 | tf_op jit(solution)/shard_map/key_sums/pallas_call | solution.py:110
  38.1 1.3 %fold.5 = (bf16[512,384]{1,0:T(8,128)(2,1)S(1)}, bf16[512,384]{1,0:T(8,128)(2,1)S(1)}, f32[8,128]{1,0:T(8,128)S(1)}) custom-call(bf16[1024,384]{1,0:T(8,128)(2,1)} %collective-permute-done.3.refs_0_, bf16[1024,384]{1,0:T(8,128)(2,1)S(1)} %get-tuple-element.48.refs_1_, f32[8,128]{1,0:T(8,128)S(1)} %get-tuple-element.51.refs_2_), custom_call_target="tpu_custom_call" | custom-call | flops 1179648 | bytes 2359296 | tf_op jit(solution)/shard_map/fold/pallas_call | solution.py:133
  39.9 1.1 fold.6
  41.0 2.8 %collective-permute-start.8 = (bf16[272,384]{1,0:T(8,128)(2,1)S(1)}, bf16[272,384]{1,0:T(8,128)(2,1)S(1)}, u32[]{:S(2)}, u32[]{:S(2)}) collective-permute-start(bf16[272,384]{1,0:T(8,128)(2,1)S(1)} %get-tuple-element.60), channel_id=1, source_target_pairs={{0,4},{1,3},{2,6},{3,1},{4,0},{5,7},{6,2},{7,5},{8,12},{9,11},{10,... | collective-permute-start | bytes 626696 | tf_op jit(solution)/shard_map/ppermute | solution.py:46
  43.9 3.8 %collective-permute-done.8.refs_0_ = bf16[272,384]{1,0:T(8,128)(2,1)S(1)} collective-permute-done((bf16[272,384]{1,0:T(8,128)(2,1)S(1)}, bf16[272,384]{1,0:T(8,128)(2,1)S(1)}, u32[]{:S(2)}, u32[]{:S(2)}) %collective-permute-start.8) | collective-permute-done | bytes 208928 | tf_op jit(solution)/shard_map/ppermute | solution.py:46
  47.7 3.5 %collective-permute-start.10 = (bf16[272,384]{1,0:T(8,128)(2,1)S(1)}, bf16[272,384]{1,0:T(8,128)(2,1)S(1)}, u32[]{:S(2)}, u32[]{:S(2)}) collective-permute-start(bf16[272,384]{1,0:T(8,128)(2,1)S(1)} %get-tuple-element.65.refs_1_), channel_id=1, source_target_pairs={{0,24},{1,25},{2,26},{3,27},{4,28},{5,29},{6,30},{7,31},{8,16},{9,... | collective-permute-start | bytes 626696 | tf_op jit(solution)/shard_map/ppermute | solution.py:46
  51.2 0.6 fold.7
  51.8 3.0 %collective-permute-start.7 = (bf16[256,384]{1,0:T(8,128)(2,1)S(1)}, bf16[256,384]{1,0:T(8,128)(2,1)S(1)}, u32[]{:S(2)}, u32[]{:S(2)}) collective-permute-start(bf16[256,384]{1,0:T(8,128)(2,1)S(1)} %get-tuple-element.58), channel_id=1, source_target_pairs={{0,2},{1,5},{2,0},{3,7},{4,6},{5,1},{6,4},{7,3},{8,10},{9,13},{10,... | collective-permute-start | bytes 589832 | tf_op jit(solution)/shard_map/ppermute | solution.py:46
  54.8 0.6 collective-permute-done.10.refs_0_
  55.7 2.1 %collective-permute-start.12 = (bf16[256,384]{1,0:T(8,128)(2,1)S(1)}, bf16[256,384]{1,0:T(8,128)(2,1)S(1)}, u32[]{:S(2)}, u32[]{:S(2)}) collective-permute-start(bf16[256,384]{1,0:T(8,128)(2,1)S(1)} %get-tuple-element.72.refs_1_), channel_id=1, source_target_pairs={{0,4},{1,3},{2,6},{3,1},{4,0},{5,7},{6,2},{7,5},{8,12},{9,11},{10,... | collective-permute-start | bytes 589832 | tf_op jit(solution)/shard_map/ppermute | solution.py:46
  57.8 2.5 %collective-permute-done.7.refs_0_ = bf16[256,384]{1,0:T(8,128)(2,1)S(1)} collective-permute-done((bf16[256,384]{1,0:T(8,128)(2,1)S(1)}, bf16[256,384]{1,0:T(8,128)(2,1)S(1)}, u32[]{:S(2)}, u32[]{:S(2)}) %collective-permute-start.7) | collective-permute-done | bytes 196640 | tf_op jit(solution)/shard_map/ppermute | solution.py:46
  60.4 0.6 seed.3
  61.0 0.9 collective-permute-start.9
  61.9 2.7 %collective-permute-start.14 = (bf16[512,384]{1,0:T(8,128)(2,1)S(1)}, bf16[512,384]{1,0:T(8,128)(2,1)S(1)}, u32[]{:S(2)}, u32[]{:S(2)}) collective-permute-start(bf16[512,384]{1,0:T(8,128)(2,1)S(1)} %get-tuple-element.75.refs_1_), channel_id=1, source_target_pairs={{0,8},{1,9},{2,10},{3,11},{4,12},{5,13},{6,14},{7,15},{8,0},{9,1},... | collective-permute-start | bytes 1179656 | tf_op jit(solution)/shard_map/ppermute | solution.py:46
  64.6 4.3 %collective-permute-done.9.refs_0_ = bf16[256,384]{1,0:T(8,128)(2,1)S(1)} collective-permute-done((bf16[256,384]{1,0:T(8,128)(2,1)S(1)}, bf16[256,384]{1,0:T(8,128)(2,1)S(1)}, u32[]{:S(2)}, u32[]{:S(2)}) %collective-permute-start.9) | collective-permute-done | bytes 196640 | tf_op jit(solution)/shard_map/ppermute | solution.py:46
  68.9 1.0 last_centroids.1
  69.9 2.1 %collective-permute-start.11 = (bf16[272,384]{1,0:T(8,128)(2,1)S(1)}, bf16[272,384]{1,0:T(8,128)(2,1)S(1)}, u32[]{:S(2)}, u32[]{:S(2)}) collective-permute-start(bf16[272,384]{1,0:T(8,128)(2,1)S(1)} %get-tuple-element.71.refs_1_), channel_id=1, source_target_pairs={{0,2},{1,5},{2,0},{3,7},{4,6},{5,1},{6,4},{7,3},{8,10},{9,13},{10,... | collective-permute-start | bytes 626696 | tf_op jit(solution)/shard_map/ppermute | solution.py:46
  72.0 3.8 %collective-permute-done.11.refs_0_ = bf16[272,384]{1,0:T(8,128)(2,1)S(1)} collective-permute-done((bf16[272,384]{1,0:T(8,128)(2,1)S(1)}, bf16[272,384]{1,0:T(8,128)(2,1)S(1)}, u32[]{:S(2)}, u32[]{:S(2)}) %collective-permute-start.11) | collective-permute-done | bytes 208928 | tf_op jit(solution)/shard_map/ppermute | solution.py:46
  75.8 1.0 join.6
  76.8 0.6 copy-done.5
  77.4 2.0 %collective-permute-start.17 = (bf16[1024,384]{1,0:T(8,128)(2,1)}, bf16[1024,384]{1,0:T(8,128)(2,1)}, u32[]{:S(2)}, u32[]{:S(2)}) collective-permute-start(bf16[1024,384]{1,0:T(8,128)(2,1)} %get-tuple-element.77.refs_2_), channel_id=1, source_target_pairs={{0,2},{1,5},{2,0},{3,7},{4,6},{5,1},{6,4},{7,3},{8,10},{9,13},{10,... | collective-permute-start | bytes 2359304 | tf_op jit(solution)/shard_map/ppermute | solution.py:46
  79.5 2.4 %collective-permute-start.13 = (bf16[528,384]{1,0:T(8,128)(2,1)S(1)}, bf16[528,384]{1,0:T(8,128)(2,1)S(1)}, u32[]{:S(2)}, u32[]{:S(2)}) collective-permute-start(bf16[528,384]{1,0:T(8,128)(2,1)S(1)} %get-tuple-element.74.refs_1_), channel_id=1, source_target_pairs={{0,8},{1,9},{2,10},{3,11},{4,12},{5,13},{6,14},{7,15},{8,0},{9,1},... | collective-permute-start | bytes 1216520 | tf_op jit(solution)/shard_map/ppermute | solution.py:46
  81.9 0.7 compare_select_fusion.6.refs_1_.gid_ref
  82.6 0.7 copy-done.6
  83.3 7.4 %part_scores.2 = (bf16[1280,1024]{1,0:T(8,128)(2,1)}, f32[8,128]{1,0:T(8,128)S(1)}) custom-call(s32[16]{0:T(128)S(1)} %stack.212.code_ref, bf16[1280,768]{1,0:T(8,128)(2,1)} %x_ref.1, s32[1,1280]{1,0:T(1,128)S(1)} %compare_select_fusion.6.refs_1_.gid_ref, bf16[1024,384]{1,0:T(8,128)(2,1)} %get-tuple-element.77.refs_2_, ...), custom_call_target="tpu_custom_call" | custom-call | flops 1 | bytes 1 | tf_op jit(solution)/shard_map/part_scores/pallas_call | solution.py:322
  90.7 1.2 collective-permute-done.13.refs_0_
  91.8 1.0 join.7
  93.6 3.1 %collective-permute-done.18.refs_3_ = bf16[1024,384]{1,0:T(8,128)(2,1)S(1)} collective-permute-done((bf16[1024,384]{1,0:T(8,128)(2,1)}, bf16[1024,384]{1,0:T(8,128)(2,1)S(1)}, u32[]{:S(2)}, u32[]{:S(2)}) %collective-permute-start.18) | collective-permute-done | bytes 786464 | tf_op jit(solution)/shard_map/ppermute | solution.py:46
  96.7 7.2 %part_scores.3 = (bf16[1280,1024]{1,0:T(8,128)(2,1)}, f32[8,128]{1,0:T(8,128)S(1)}) custom-call(s32[16]{0:T(128)S(1)} %stack.212.code_ref, bf16[1280,768]{1,0:T(8,128)(2,1)} %x_ref.1, s32[1,1280]{1,0:T(1,128)S(1)} %compare_select_fusion.6.refs_1_.gid_ref, bf16[1024,384]{1,0:T(8,128)(2,1)} %collective-permute-done.17.refs_2_, ...), custom_call_target="tpu_custom_call", output_to_operand_aliasing={{0}: (5, {})} | custom-call | flops 1 | bytes 1 | tf_op jit(solution)/shard_map/part_scores/pallas_call | solution.py:322
  103.9 1.4 %collective-permute-done.16.in_ref = bf16[1040,384]{1,0:T(8,128)(2,1)} collective-permute-done((bf16[1040,384]{1,0:T(8,128)(2,1)}, bf16[1040,384]{1,0:T(8,128)(2,1)}, u32[]{:S(2)}, u32[]{:S(2)}) %collective-permute-start.16) | collective-permute-done | bytes 798752 | tf_op jit(solution)/shard_map/ppermute | solution.py:46
  105.4 2.5 %collective-permute-done.19.rest_1_ = bf16[1040,384]{1,0:T(8,128)(2,1)} collective-permute-done((bf16[1040,384]{1,0:T(8,128)(2,1)}, bf16[1040,384]{1,0:T(8,128)(2,1)}, u32[]{:S(2)}, u32[]{:S(2)}) %collective-permute-start.19) | collective-permute-done | bytes 798752 | tf_op jit(solution)/shard_map/ppermute | solution.py:46
  107.9 0.7 copy-done.2
  108.6 11.0 %final_scores.1 = bf16[1280,1024]{1,0:T(8,128)(2,1)} custom-call(s32[32]{0:T(128)S(1)} %concatenate.104.code_ref, s32[8]{0:T(128)S(1)} %fusion.21.slot_ref, bf16[1280,768]{1,0:T(8,128)(2,1)} %x_ref.1, s32[1,1280]{1,0:T(1,128)S(1)} %copy-done.2, f32[16,1024]{1,0:T(8,128)S(1)} %broadcast_in_dim.28.half_ref, bf16[1040,384]{1,0:T(8,128)(2,1)} %behind.1.rest_0_, ...), custom_call_target="tpu_custom_call" | custom-call | flops 1 | bytes 1 | tf_op jit(solution)/shard_map/final_scores/pallas_call | solution.py:397
  (51 shorter events, 3.4 us)
Async XLA Ops:
  0.6 31.2 %copy-start = (f32[1,1024,768]{2,1,0:T(8,128)S(1)}, f32[1,1024,768]{2,1,0:T(8,128)}, u32[]{:S(2)}) copy-start(f32[1,1024,768]{2,1,0:T(8,128)} %param.9) | copy-start | bytes 9437188
  3.0 4.0 %collective-permute-start = (s32[1280]{0:T(1024)S(1)}, s32[1280]{0:T(1024)S(1)}, u32[]{:S(2)}, u32[]{:S(2)}) collective-permute-start(s32[1280]{0:T(1024)S(1)} %add_select_fusion.9), channel_id=1, source_target_pairs={{0,1},{1,0},{2,3},{3,2},{4,5},{5,4},{6,7},{7,6},{8,9},{9,8},{10,11... | collective-permute-start | bytes 15368 | tf_op jit(solution)/shard_map/ppermute | solution.py:46
  6.5 2.9 %collective-permute-start.2 = (bf16[1280,384]{1,0:T(8,128)(2,1)}, bf16[1280,384]{1,0:T(8,128)(2,1)}, u32[]{:S(2)}, u32[]{:S(2)}) collective-permute-start(bf16[1280,384]{1,0:T(8,128)(2,1)} %get-tuple-element.93.refs_1_), channel_id=1, source_target_pairs={{0,1},{1,0},{2,3},{3,2},{4,5},{5,4},{6,7},{7,6},{8,9},{9,8},{10,11... | collective-permute-start | bytes 2949128 | tf_op jit(solution)/shard_map/ppermute | solution.py:46
  6.5 10.0 %collective-permute-start.1 = (bf16[1280,384]{1,0:T(8,128)(2,1)}, bf16[1280,384]{1,0:T(8,128)(2,1)}, u32[]{:S(2)}, u32[]{:S(2)}) collective-permute-start(bf16[1280,384]{1,0:T(8,128)(2,1)} %get-tuple-element.94.refs_1_), channel_id=1, source_target_pairs={{0,1},{1,0},{2,3},{3,2},{4,5},{5,4},{6,7},{7,6},{8,9},{9,8},{10,11... | collective-permute-start | bytes 2949128 | tf_op jit(solution)/shard_map/ppermute | solution.py:46
  13.7 14.6 %collective-permute-start.4 = (bf16[1040,384]{1,0:T(8,128)(2,1)S(1)}, bf16[1040,384]{1,0:T(8,128)(2,1)S(1)}, u32[]{:S(2)}, u32[]{:S(2)}) collective-permute-start(bf16[1040,384]{1,0:T(8,128)(2,1)S(1)} %get-tuple-element.49), channel_id=1, source_target_pairs={{0,2},{1,5},{2,0},{3,7},{4,6},{5,1},{6,4},{7,3},{8,10},{9,13},{10,... | collective-permute-start | bytes 2396168 | tf_op jit(solution)/shard_map/ppermute | solution.py:46
  16.5 5.3 %copy-start.3 = (s32[1,2560]{1,0:T(1,128)}, s32[1,2560]{1,0:T(1,128)S(1)}, u32[]{:S(2)}) copy-start(s32[1,2560]{1,0:T(1,128)S(1)} %fusion.10.refs_0_) | copy-start | bytes 30724
  21.8 16.3 %collective-permute-start.3 = (bf16[1024,384]{1,0:T(8,128)(2,1)}, bf16[1024,384]{1,0:T(8,128)(2,1)}, u32[]{:S(2)}, u32[]{:S(2)}) collective-permute-start(bf16[1024,384]{1,0:T(8,128)(2,1)} %get-tuple-element.45), channel_id=1, source_target_pairs={{0,4},{1,3},{2,6},{3,1},{4,0},{5,7},{6,2},{7,5},{8,12},{9,11},{10,... | collective-permute-start | bytes 2359304 | tf_op jit(solution)/shard_map/ppermute | solution.py:46
  27.6 1.6 %copy-start.7 = (f32[8,128]{1,0:T(8,128)}, f32[8,128]{1,0:T(8,128)S(1)}, u32[]{:S(2)}) copy-start(f32[8,128]{1,0:T(8,128)S(1)} %get-tuple-element.47.refs_3_) | copy-start | bytes 12292
  29.2 10.7 %collective-permute-start.6 = (bf16[528,384]{1,0:T(8,128)(2,1)}, bf16[528,384]{1,0:T(8,128)(2,1)}, u32[]{:S(2)}, u32[]{:S(2)}) collective-permute-start(bf16[528,384]{1,0:T(8,128)(2,1)} %get-tuple-element.54), channel_id=1, source_target_pairs={{0,8},{1,9},{2,10},{3,11},{4,12},{5,13},{6,14},{7,15},{8,0},{9,1},... | collective-permute-start | bytes 1216520 | tf_op jit(solution)/shard_map/ppermute | solution.py:46
  31.8 0.7 copy-start.4
  32.6 0.7 copy-start.8
  39.4 11.8 %collective-permute-start.5 = (bf16[512,384]{1,0:T(8,128)(2,1)S(1)}, bf16[512,384]{1,0:T(8,128)(2,1)S(1)}, u32[]{:S(2)}, u32[]{:S(2)}) collective-permute-start(bf16[512,384]{1,0:T(8,128)(2,1)S(1)} %get-tuple-element.52), channel_id=1, source_target_pairs={{0,8},{1,9},{2,10},{3,11},{4,12},{5,13},{6,14},{7,15},{8,0},{9,1},... | collective-permute-start | bytes 1179656 | tf_op jit(solution)/shard_map/ppermute | solution.py:46
  41.0 6.6 %collective-permute-start.8 = (bf16[272,384]{1,0:T(8,128)(2,1)S(1)}, bf16[272,384]{1,0:T(8,128)(2,1)S(1)}, u32[]{:S(2)}, u32[]{:S(2)}) collective-permute-start(bf16[272,384]{1,0:T(8,128)(2,1)S(1)} %get-tuple-element.60), channel_id=1, source_target_pairs={{0,4},{1,3},{2,6},{3,1},{4,0},{5,7},{6,2},{7,5},{8,12},{9,11},{10,... | collective-permute-start | bytes 626696 | tf_op jit(solution)/shard_map/ppermute | solution.py:46
  47.7 7.7 %collective-permute-start.10 = (bf16[272,384]{1,0:T(8,128)(2,1)S(1)}, bf16[272,384]{1,0:T(8,128)(2,1)S(1)}, u32[]{:S(2)}, u32[]{:S(2)}) collective-permute-start(bf16[272,384]{1,0:T(8,128)(2,1)S(1)} %get-tuple-element.65.refs_1_), channel_id=1, source_target_pairs={{0,24},{1,25},{2,26},{3,27},{4,28},{5,29},{6,30},{7,31},{8,16},{9,... | collective-permute-start | bytes 626696 | tf_op jit(solution)/shard_map/ppermute | solution.py:46
  51.8 8.6 %collective-permute-start.7 = (bf16[256,384]{1,0:T(8,128)(2,1)S(1)}, bf16[256,384]{1,0:T(8,128)(2,1)S(1)}, u32[]{:S(2)}, u32[]{:S(2)}) collective-permute-start(bf16[256,384]{1,0:T(8,128)(2,1)S(1)} %get-tuple-element.58), channel_id=1, source_target_pairs={{0,2},{1,5},{2,0},{3,7},{4,6},{5,1},{6,4},{7,3},{8,10},{9,13},{10,... | collective-permute-start | bytes 589832 | tf_op jit(solution)/shard_map/ppermute | solution.py:46
  55.7 6.1 %collective-permute-start.12 = (bf16[256,384]{1,0:T(8,128)(2,1)S(1)}, bf16[256,384]{1,0:T(8,128)(2,1)S(1)}, u32[]{:S(2)}, u32[]{:S(2)}) collective-permute-start(bf16[256,384]{1,0:T(8,128)(2,1)S(1)} %get-tuple-element.72.refs_1_), channel_id=1, source_target_pairs={{0,4},{1,3},{2,6},{3,1},{4,0},{5,7},{6,2},{7,5},{8,12},{9,11},{10,... | collective-permute-start | bytes 589832 | tf_op jit(solution)/shard_map/ppermute | solution.py:46
  61.0 7.9 %collective-permute-start.9 = (bf16[256,384]{1,0:T(8,128)(2,1)S(1)}, bf16[256,384]{1,0:T(8,128)(2,1)S(1)}, u32[]{:S(2)}, u32[]{:S(2)}) collective-permute-start(bf16[256,384]{1,0:T(8,128)(2,1)S(1)} %get-tuple-element.63.refs_1_), channel_id=1, source_target_pairs={{0,24},{1,25},{2,26},{3,27},{4,28},{5,29},{6,30},{7,31},{8,16},{9,... | collective-permute-start | bytes 589832 | tf_op jit(solution)/shard_map/ppermute | solution.py:46
  61.9 13.9 %collective-permute-start.14 = (bf16[512,384]{1,0:T(8,128)(2,1)S(1)}, bf16[512,384]{1,0:T(8,128)(2,1)S(1)}, u32[]{:S(2)}, u32[]{:S(2)}) collective-permute-start(bf16[512,384]{1,0:T(8,128)(2,1)S(1)} %get-tuple-element.75.refs_1_), channel_id=1, source_target_pairs={{0,8},{1,9},{2,10},{3,11},{4,12},{5,13},{6,14},{7,15},{8,0},{9,1},... | collective-permute-start | bytes 1179656 | tf_op jit(solution)/shard_map/ppermute | solution.py:46
  69.9 5.9 %collective-permute-start.11 = (bf16[272,384]{1,0:T(8,128)(2,1)S(1)}, bf16[272,384]{1,0:T(8,128)(2,1)S(1)}, u32[]{:S(2)}, u32[]{:S(2)}) collective-permute-start(bf16[272,384]{1,0:T(8,128)(2,1)S(1)} %get-tuple-element.71.refs_1_), channel_id=1, source_target_pairs={{0,2},{1,5},{2,0},{3,7},{4,6},{5,1},{6,4},{7,3},{8,10},{9,13},{10,... | collective-permute-start | bytes 626696 | tf_op jit(solution)/shard_map/ppermute | solution.py:46
  76.8 0.6 copy-start.5
  77.4 5.2 %collective-permute-start.15 = (bf16[1024,384]{1,0:T(8,128)(2,1)}, bf16[1024,384]{1,0:T(8,128)(2,1)}, u32[]{:S(2)}, u32[]{:S(2)}) collective-permute-start(bf16[1024,384]{1,0:T(8,128)(2,1)} %get-tuple-element.77.refs_2_), channel_id=1, source_target_pairs={{0,1},{1,0},{2,3},{3,2},{4,5},{5,4},{6,7},{7,6},{8,9},{9,8},{10,11... | collective-permute-start | bytes 2359304 | tf_op jit(solution)/shard_map/ppermute | solution.py:46
  77.4 15.7 %collective-permute-start.17 = (bf16[1024,384]{1,0:T(8,128)(2,1)}, bf16[1024,384]{1,0:T(8,128)(2,1)}, u32[]{:S(2)}, u32[]{:S(2)}) collective-permute-start(bf16[1024,384]{1,0:T(8,128)(2,1)} %get-tuple-element.77.refs_2_), channel_id=1, source_target_pairs={{0,2},{1,5},{2,0},{3,7},{4,6},{5,1},{6,4},{7,3},{8,10},{9,13},{10,... | collective-permute-start | bytes 2359304 | tf_op jit(solution)/shard_map/ppermute | solution.py:46
  79.5 12.4 %collective-permute-start.13 = (bf16[528,384]{1,0:T(8,128)(2,1)S(1)}, bf16[528,384]{1,0:T(8,128)(2,1)S(1)}, u32[]{:S(2)}, u32[]{:S(2)}) collective-permute-start(bf16[528,384]{1,0:T(8,128)(2,1)S(1)} %get-tuple-element.74.refs_1_), channel_id=1, source_target_pairs={{0,8},{1,9},{2,10},{3,11},{4,12},{5,13},{6,14},{7,15},{8,0},{9,1},... | collective-permute-start | bytes 1216520 | tf_op jit(solution)/shard_map/ppermute | solution.py:46
  82.6 21.3 %copy-start.1 = (s32[1,1280]{1,0:T(1,128)}, s32[1,1280]{1,0:T(1,128)S(1)}, u32[]{:S(2)}) copy-start(s32[1,1280]{1,0:T(1,128)S(1)} %compare_select_fusion.6.refs_1_.gid_ref) | copy-start | bytes 15364
  82.6 0.7 copy-start.6
  92.8 12.4 %collective-permute-start.16 = (bf16[1040,384]{1,0:T(8,128)(2,1)}, bf16[1040,384]{1,0:T(8,128)(2,1)}, u32[]{:S(2)}, u32[]{:S(2)}) collective-permute-start(bf16[1040,384]{1,0:T(8,128)(2,1)} %get-tuple-element.80.rest_2_), channel_id=1, source_target_pairs={{0,4},{1,3},{2,6},{3,1},{4,0},{5,7},{6,2},{7,5},{8,12},{9,11},{10,... | collective-permute-start | bytes 2396168 | tf_op jit(solution)/shard_map/ppermute | solution.py:46
  93.1 3.6 %collective-permute-start.18 = (bf16[1024,384]{1,0:T(8,128)(2,1)}, bf16[1024,384]{1,0:T(8,128)(2,1)S(1)}, u32[]{:S(2)}, u32[]{:S(2)}) collective-permute-start(bf16[1024,384]{1,0:T(8,128)(2,1)} %collective-permute-done.17.refs_2_), channel_id=1, source_target_pairs={{0,1},{1,0},{2,3},{3,2},{4,5},{5,4},{6,7},{7,6},{8,9},{9,8},{10,11... | collective-permute-start | bytes 2359304 | tf_op jit(solution)/shard_map/ppermute | solution.py:46
  93.1 12.3 %collective-permute-start.20 = (bf16[1040,384]{1,0:T(8,128)(2,1)}, bf16[1040,384]{1,0:T(8,128)(2,1)}, u32[]{:S(2)}, u32[]{:S(2)}) collective-permute-start(bf16[1040,384]{1,0:T(8,128)(2,1)} %get-tuple-element.80.rest_2_), channel_id=1, source_target_pairs={{0,1},{1,0},{2,3},{3,2},{4,5},{5,4},{6,7},{7,6},{8,9},{9,8},{10,11... | collective-permute-start | bytes 2396168 | tf_op jit(solution)/shard_map/ppermute | solution.py:46
  105.3 2.6 %collective-permute-start.19 = (bf16[1040,384]{1,0:T(8,128)(2,1)}, bf16[1040,384]{1,0:T(8,128)(2,1)}, u32[]{:S(2)}, u32[]{:S(2)}) collective-permute-start(bf16[1040,384]{1,0:T(8,128)(2,1)} %behind.1.rest_0_), channel_id=1, source_target_pairs={{0,1},{1,0},{2,3},{3,2},{4,5},{5,4},{6,7},{7,6},{8,9},{9,8},{10,11... | collective-permute-start | bytes 2396168 | tf_op jit(solution)/shard_map/ppermute | solution.py:46
  107.9 0.7 copy-start.2

commit v9 on v7

--- a/solution.py
+++ b/solution.py
@@ -102,8 +102,8 @@
         out_ref[keys:, :] = rest[0][...]
 
 
-def key_sums(token, pos_row, own, other, count_tile, base, keys, start, wide):
-    rows = own.shape[0]
+def key_sums(token, pos_row, own, other, count_tile, base, keys):
+    rows, wide = own.shape
     extra = [] if count_tile is None else [count_tile]
     out_rows = keys + sum(e.shape[0] for e in extra)
     whole = lambda shape: pl.BlockSpec(shape, lambda i: (0, 0))
@@ -113,8 +113,8 @@
         out_shape=[jax.ShapeDtypeStruct((out_rows, wide), BF16), token_shape()],
         in_specs=[
             whole((1, 2 * rows)),
-            pl.BlockSpec((rows, wide), lambda i: (0, start // wide)),
-            pl.BlockSpec((rows, wide), lambda i: (0, start // wide)),
+            whole((rows, wide)),
+            whole((rows, wide)),
         ]
         + [whole(e.shape) for e in extra]
         + [whole(token.shape)],
@@ -261,17 +261,22 @@
     )
 
 
-def mask_rows(groups, x, gid, out):
+def mask_rows(groups, x, gid_ref, out):
     wide = x.shape[1]
+    gid = jnp.transpose(jnp.broadcast_to(gid_ref[...], (128, gid_ref.shape[1])))
     for group in range(groups):
-        out[:, group * wide : (group + 1) * wide] = jnp.where(gid[...] == group, x[...], jnp.zeros_like(x))
+        keep = gid == group
+        for cut in range(0, wide, 128):
+            part = x[:, cut : cut + 128]
+            out[:, group * wide + cut : group * wide + cut + 128] = jnp.where(keep, part, jnp.zeros_like(part))
+    return gid
 
 
 def row_scratch(rows, groups, wide):
     return [
         pltpu.VMEM((rows, groups * wide), BF16),
         pltpu.VMEM((rows, wide), BF16),
-        pltpu.VMEM((rows, 1), jnp.int32),
+        pltpu.VMEM((1, rows), jnp.int32),
         pltpu.SemaphoreType.DMA((2,)),
     ]
 
@@ -281,8 +286,8 @@
 
 
 def part_kernel(groups, share, start_at, code_ref, x_ref, gid_ref, own_ref, other_ref, *rest):
-    out_ref, cents, rows_of, x, gid, sem = rest
-    loads = row_loads(x_ref, gid_ref, x, gid, sem, start_at)
+    out_ref, cents, rows_of, x, gid_row, sem = rest
+    loads = row_loads(x_ref, gid_ref, x, gid_row, sem, start_at)
     wide = own_ref.shape[1]
     blocks = own_ref.shape[0] // share
 
@@ -297,7 +302,7 @@
                 cents[pl.ds(slot, share), pl.ds(pl.multiple_of(code % groups * wide, 128), wide)] = ref[block * share : (block + 1) * share, :]
         for load in loads:
             load.wait()
-        mask_rows(groups, x, gid, rows_of)
+        mask_rows(groups, x, gid_row, rows_of)
 
     step = out_ref.shape[1]
     start = pl.multiple_of(pl.program_id(0) * step, step)
@@ -343,8 +348,8 @@
 def final_kernel(groups, share, start_at, code_ref, slot_ref, x_ref, gid_ref, half_ref, *rest):
     pieces = 4
     piece_refs, total_refs = rest[:pieces], rest[pieces : pieces + 2]
-    out_ref, cents, half, pick, rows_of, x, gid, sem = rest[-8:]
-    loads = row_loads(x_ref, gid_ref, x, gid, sem, start_at)
+    out_ref, cents, half, pick, rows_of, x, gid_row, sem = rest[-8:]
+    loads = row_loads(x_ref, gid_ref, x, gid_row, sem, start_at)
     keys = cents.shape[0]
     wide = cents.shape[1] // groups
     members = keys // share
@@ -376,9 +381,9 @@
                     half[:, lines] = filled
         for load in loads:
             load.wait()
-        mask_rows(groups, x, gid, rows_of)
+        gid = mask_rows(groups, x, gid_row, rows_of)[:, : pick.shape[1]]
         lane = lax.broadcasted_iota(jnp.int32, pick.shape, 1)
-        hit = (lane % groups == gid[...]) & (lane < PARTS * groups)
+        hit = (lane % groups == gid) & (lane < PARTS * groups)
         pick[...] = jnp.where(hit, -1.0, 0.0).astype(BF16)
 
     step = out_ref.shape[1]
@@ -447,7 +452,8 @@
     live = jnp.arange(rows, dtype=jnp.int32) < live_rows[0]
     label = jnp.where(live, coarse_label[:, 0] * keys + fine_label, -1)
     sibling = lambda a: exchange(a, lambda gz, m: (gz, m ^ 1), groups, members)
-    other_samples = sibling(samples)
+    cut_rows = [samples[:, start : start + wide] for start, wide in streams_of(width)]
+    other_rows = [sibling(part) for part in cut_rows]
     label_all = jnp.concatenate([label, sibling(label)])
 
     group_of = label_all // keys
@@ -490,7 +496,7 @@
     for part, found in enumerate((send, keep)):
         for stream, (start, wide) in enumerate(columns):
             found[stream], token = key_sums(
-                token, rows_of[stream], samples, other_samples, tiles[stream], part * half_keys, half_keys, start, wide
+                token, rows_of[stream], cut_rows[stream], other_rows[stream], tiles[stream], part * half_keys, half_keys
             )
 
     tokens = [start_token] * 2
@@ -573,7 +579,7 @@
                 codes.append(jnp.where(core ^ flip == 0, *code))
         return jnp.stack(codes).astype(jnp.int32)
 
-    gid = jnp.where(live, coarse_label[:, 0], -1)[:, None]
+    gid = jnp.where(live, coarse_label[:, 0], -1)[None, :]
     count = 2
     arrived = [None] * 2
     for stage in reversed(range(stages - 1)):

time: 123 us -> 121 us (0.984)
  local copies, waits for them, and re-layouts: 8.91 us -> 6.59 us
    unnamed x26 -> x19, local copies, waits for them, and re-layouts: 8.64 us -> 3.32 us
    slice x0 -> x1, local copies, waits for them, and re-layouts: none -> 3.01 us  [per_device(): samples[:, start:start + wide]]
    ppermute x20 -> x21, waiting for transfers between devices: 25.5 us -> 26.1 us  [exchange(): return lax.ppermute(array, AXES, pairs)]
    ppermute x20 -> x21, starting transfers between devices: 30.4 us -> 30.2 us  [exchange(): return lax.ppermute(array, AXES, pairs)]
  transfers between devices with their start and end apart: 20 -> 21, of which waited for: 10 -> 12; matrix products, arithmetic and copies ran while one was open for 3% -> 4% of each run, Pallas kernels for 29% -> 33%
where the time goes in v9:
time: 121 us; the launch traced here: 120 us
  Pallas kernels  52 us (43%)
  starting transfers between devices  30.2 us (25%)
  waiting for transfers between devices  26.1 us (22%)
  local copies, waits for them, and re-layouts  6.59 us (5%)
  other arithmetic  2.61 us (2%)
  between operations  1.8 us (1%)
    ppermute x21, starting transfers between devices, exchange(): return lax.ppermute(array, AXES, pairs)  30.2 us
    ppermute x21, waiting for transfers between devices, exchange(): return lax.ppermute(array, AXES, pairs)  26.1 us
    pallas_call x4, Pallas kernels, key_sums(): pl.pallas_call(hand_on(functools.partial(sums_kernel, base), 3 + len(extr...  18.8 us
    pallas_call x2, Pallas kernels, part_scores(): pl.pallas_call(kernel, grid_spec=pltpu.PrefetchScalarGridSpec(num_scalar_...  14.3 us
    pallas_call x1, Pallas kernels, final_scores(): pl.pallas_call(functools.partial(final_kernel, groups, share, start_at),...  11 us
    pallas_call x12, Pallas kernels, small_call(): pl.pallas_call(hand_on(kernel, len(args)), out_shape=[*outs, token_shape(...  7.89 us
    unnamed x19, local copies, waits for them, and re-layouts  3.32 us
    slice x1, local copies, waits for them, and re-layouts, per_device(): samples[:, start:start + wide]  3.01 us
  transfers between devices with their start and end apart: 21, of which 12 were waited for; matrix products, arithmetic and copies ran while one was open for 4% of the time, Pallas kernels for 33%

profile of v9, /device:TPU:0, one launch (start us, length us, event | category | flops | bytes accessed | tf_op | source)
XLA Modules:
  0.0 119.8 jit_solution(3720176544475259244)
XLA Ops:
  1.4 0.9 multiply_reduce_fusion
  2.3 0.7 add_select_fusion.9
  3.5 3.0 %fusion.22 = (bf16[1280,384]{1,0:T(8,128)(2,1)}, bf16[1280,384]{1,0:T(8,128)(2,1)}) fusion(bf16[1280,768]{1,0:T(8,128)(2,1)} %x_ref.1), kind=kLoop, calls=%fused_computation.77 | loop fusion | bytes 3932160 | tf_op jit(solution)/shard_map/slice | solution.py:455
  7.3 0.6 fusion.15
  7.9 1.5 %collective-permute-done.2.refs_2_ = bf16[1280,384]{1,0:T(8,128)(2,1)} collective-permute-done((bf16[1280,384]{1,0:T(8,128)(2,1)}, bf16[1280,384]{1,0:T(8,128)(2,1)}, u32[]{:S(2)}, u32[]{:S(2)}) %collective-permute-start.2) | collective-permute-done | bytes 983072 | tf_op jit(solution)/shard_map/ppermute | solution.py:46
  9.4 4.4 %key_sums.4 = (bf16[1040,384]{1,0:T(8,128)(2,1)S(1)}, f32[8,128]{1,0:T(8,128)S(1)}) custom-call(s32[1,2560]{1,0:T(1,128)S(1)} %get-tuple-element.86.refs_0_, bf16[1280,384]{1,0:T(8,128)(2,1)} %get-tuple-element.93.refs_1_, bf16[1280,384]{1,0:T(8,128)(2,1)} %collective-permute-done.2.refs_2_, bf16[16,384]{1,0:T(8,128)(2,1)S(1)} %pad_maximum_fusion.refs_3_, ...), custom_call_target="tpu_custom_call" | custom-call | flops 2013265920 | bytes 2752512 | tf_op jit(solution)/shard_map/key_sums/pallas_call | solution.py:110
  13.7 2.7 %collective-permute-start.4 = (bf16[1040,384]{1,0:T(8,128)(2,1)S(1)}, bf16[1040,384]{1,0:T(8,128)(2,1)S(1)}, u32[]{:S(2)}, u32[]{:S(2)}) collective-permute-start(bf16[1040,384]{1,0:T(8,128)(2,1)S(1)} %get-tuple-element.49), channel_id=1, source_target_pairs={{0,2},{1,5},{2,0},{3,7},{4,6},{5,1},{6,4},{7,3},{8,10},{9,13},{10,... | collective-permute-start | bytes 2396168 | tf_op jit(solution)/shard_map/ppermute | solution.py:46
  16.5 5.2 %key_sums.5 = (bf16[1024,384]{1,0:T(8,128)(2,1)}, f32[8,128]{1,0:T(8,128)S(1)}) custom-call(s32[1,2560]{1,0:T(1,128)S(1)} %fusion.10.refs_0_, bf16[1280,384]{1,0:T(8,128)(2,1)} %get-tuple-element.94.refs_1_, bf16[1280,384]{1,0:T(8,128)(2,1)} %collective-permute-done.1.refs_2_, f32[8,128]{1,0:T(8,128)S(1)} %get-tuple-element.44.refs_3_), custom_call_target="tpu_custom_call" | custom-call | flops 2013265920 | bytes 2752512 | tf_op jit(solution)/shard_map/key_sums/pallas_call | solution.py:110
  21.8 1.5 %collective-permute-start.3 = (bf16[1024,384]{1,0:T(8,128)(2,1)}, bf16[1024,384]{1,0:T(8,128)(2,1)}, u32[]{:S(2)}, u32[]{:S(2)}) collective-permute-start(bf16[1024,384]{1,0:T(8,128)(2,1)} %get-tuple-element.45), channel_id=1, source_target_pairs={{0,4},{1,3},{2,6},{3,1},{4,0},{5,7},{6,2},{7,5},{8,12},{9,11},{10,... | collective-permute-start | bytes 2359304 | tf_op jit(solution)/shard_map/ppermute | solution.py:46
  23.3 4.4 %key_sums.6 = (bf16[1040,384]{1,0:T(8,128)(2,1)S(1)}, f32[8,128]{1,0:T(8,128)S(1)}) custom-call(s32[1,2560]{1,0:T(1,128)S(1)} %get-tuple-element.86.refs_0_, bf16[1280,384]{1,0:T(8,128)(2,1)} %get-tuple-element.93.refs_1_, bf16[1280,384]{1,0:T(8,128)(2,1)} %collective-permute-done.2.refs_2_, bf16[16,384]{1,0:T(8,128)(2,1)S(1)} %pad_maximum_fusion.refs_3_, ...), custom_call_target="tpu_custom_call" | custom-call | flops 2013265920 | bytes 2752512 | tf_op jit(solution)/shard_map/key_sums/pallas_call | solution.py:110
  27.7 0.7 collective-permute-done.4.refs_0_
  28.4 0.9 fold.4
  29.2 2.6 %collective-permute-start.6 = (bf16[528,384]{1,0:T(8,128)(2,1)}, bf16[528,384]{1,0:T(8,128)(2,1)}, u32[]{:S(2)}, u32[]{:S(2)}) collective-permute-start(bf16[528,384]{1,0:T(8,128)(2,1)} %get-tuple-element.54), channel_id=1, source_target_pairs={{0,8},{1,9},{2,10},{3,11},{4,12},{5,13},{6,14},{7,15},{8,0},{9,1},... | collective-permute-start | bytes 1216520 | tf_op jit(solution)/shard_map/ppermute | solution.py:46
  31.9 0.7 copy-done.4
  32.6 0.7 copy-done.8
  33.2 4.9 %key_sums.7 = (bf16[1024,384]{1,0:T(8,128)(2,1)S(1)}, f32[8,128]{1,0:T(8,128)}) custom-call(s32[1,2560]{1,0:T(1,128)S(1)} %copy-done.4, bf16[1280,384]{1,0:T(8,128)(2,1)} %get-tuple-element.94.refs_1_, bf16[1280,384]{1,0:T(8,128)(2,1)} %collective-permute-done.1.refs_2_, f32[8,128]{1,0:T(8,128)S(1)} %copy-done.8), custom_call_target="tpu_custom_call" | custom-call | flops 2013265920 | bytes 2752512 | tf_op jit(solution)/shard_map/key_sums/pallas_call | solution.py:110
  38.1 1.3 %fold.5 = (bf16[512,384]{1,0:T(8,128)(2,1)S(1)}, bf16[512,384]{1,0:T(8,128)(2,1)S(1)}, f32[8,128]{1,0:T(8,128)S(1)}) custom-call(bf16[1024,384]{1,0:T(8,128)(2,1)} %collective-permute-done.3.refs_0_, bf16[1024,384]{1,0:T(8,128)(2,1)S(1)} %get-tuple-element.48.refs_1_, f32[8,128]{1,0:T(8,128)S(1)} %get-tuple-element.51.refs_2_), custom_call_target="tpu_custom_call" | custom-call | flops 1179648 | bytes 2359296 | tf_op jit(solution)/shard_map/fold/pallas_call | solution.py:133
  39.9 1.1 fold.6
  41.0 2.8 %collective-permute-start.8 = (bf16[272,384]{1,0:T(8,128)(2,1)S(1)}, bf16[272,384]{1,0:T(8,128)(2,1)S(1)}, u32[]{:S(2)}, u32[]{:S(2)}) collective-permute-start(bf16[272,384]{1,0:T(8,128)(2,1)S(1)} %get-tuple-element.60), channel_id=1, source_target_pairs={{0,4},{1,3},{2,6},{3,1},{4,0},{5,7},{6,2},{7,5},{8,12},{9,11},{10,... | collective-permute-start | bytes 626696 | tf_op jit(solution)/shard_map/ppermute | solution.py:46
  43.9 3.8 %collective-permute-done.8.refs_0_ = bf16[272,384]{1,0:T(8,128)(2,1)S(1)} collective-permute-done((bf16[272,384]{1,0:T(8,128)(2,1)S(1)}, bf16[272,384]{1,0:T(8,128)(2,1)S(1)}, u32[]{:S(2)}, u32[]{:S(2)}) %collective-permute-start.8) | collective-permute-done | bytes 208928 | tf_op jit(solution)/shard_map/ppermute | solution.py:46
  47.7 3.5 %collective-permute-start.10 = (bf16[272,384]{1,0:T(8,128)(2,1)S(1)}, bf16[272,384]{1,0:T(8,128)(2,1)S(1)}, u32[]{:S(2)}, u32[]{:S(2)}) collective-permute-start(bf16[272,384]{1,0:T(8,128)(2,1)S(1)} %get-tuple-element.65.refs_1_), channel_id=1, source_target_pairs={{0,24},{1,25},{2,26},{3,27},{4,28},{5,29},{6,30},{7,31},{8,16},{9,... | collective-permute-start | bytes 626696 | tf_op jit(solution)/shard_map/ppermute | solution.py:46
  51.2 0.6 fold.7
  51.8 3.0 %collective-permute-start.7 = (bf16[256,384]{1,0:T(8,128)(2,1)S(1)}, bf16[256,384]{1,0:T(8,128)(2,1)S(1)}, u32[]{:S(2)}, u32[]{:S(2)}) collective-permute-start(bf16[256,384]{1,0:T(8,128)(2,1)S(1)} %get-tuple-element.58), channel_id=1, source_target_pairs={{0,2},{1,5},{2,0},{3,7},{4,6},{5,1},{6,4},{7,3},{8,10},{9,13},{10,... | collective-permute-start | bytes 589832 | tf_op jit(solution)/shard_map/ppermute | solution.py:46
  54.8 0.6 collective-permute-done.10.refs_0_
  55.7 2.1 %collective-permute-start.12 = (bf16[256,384]{1,0:T(8,128)(2,1)S(1)}, bf16[256,384]{1,0:T(8,128)(2,1)S(1)}, u32[]{:S(2)}, u32[]{:S(2)}) collective-permute-start(bf16[256,384]{1,0:T(8,128)(2,1)S(1)} %get-tuple-element.72.refs_1_), channel_id=1, source_target_pairs={{0,4},{1,3},{2,6},{3,1},{4,0},{5,7},{6,2},{7,5},{8,12},{9,11},{10,... | collective-permute-start | bytes 589832 | tf_op jit(solution)/shard_map/ppermute | solution.py:46
  57.8 2.5 %collective-permute-done.7.refs_0_ = bf16[256,384]{1,0:T(8,128)(2,1)S(1)} collective-permute-done((bf16[256,384]{1,0:T(8,128)(2,1)S(1)}, bf16[256,384]{1,0:T(8,128)(2,1)S(1)}, u32[]{:S(2)}, u32[]{:S(2)}) %collective-permute-start.7) | collective-permute-done | bytes 196640 | tf_op jit(solution)/shard_map/ppermute | solution.py:46
  60.4 0.6 seed.3
  61.0 0.9 collective-permute-start.9
  61.9 2.7 %collective-permute-start.14 = (bf16[512,384]{1,0:T(8,128)(2,1)S(1)}, bf16[512,384]{1,0:T(8,128)(2,1)S(1)}, u32[]{:S(2)}, u32[]{:S(2)}) collective-permute-start(bf16[512,384]{1,0:T(8,128)(2,1)S(1)} %get-tuple-element.75.refs_1_), channel_id=1, source_target_pairs={{0,8},{1,9},{2,10},{3,11},{4,12},{5,13},{6,14},{7,15},{8,0},{9,1},... | collective-permute-start | bytes 1179656 | tf_op jit(solution)/shard_map/ppermute | solution.py:46
  64.6 4.3 %collective-permute-done.9.refs_0_ = bf16[256,384]{1,0:T(8,128)(2,1)S(1)} collective-permute-done((bf16[256,384]{1,0:T(8,128)(2,1)S(1)}, bf16[256,384]{1,0:T(8,128)(2,1)S(1)}, u32[]{:S(2)}, u32[]{:S(2)}) %collective-permute-start.9) | collective-permute-done | bytes 196640 | tf_op jit(solution)/shard_map/ppermute | solution.py:46
  68.9 1.0 last_centroids.1
  69.9 2.1 %collective-permute-start.11 = (bf16[272,384]{1,0:T(8,128)(2,1)S(1)}, bf16[272,384]{1,0:T(8,128)(2,1)S(1)}, u32[]{:S(2)}, u32[]{:S(2)}) collective-permute-start(bf16[272,384]{1,0:T(8,128)(2,1)S(1)} %get-tuple-element.71.refs_1_), channel_id=1, source_target_pairs={{0,2},{1,5},{2,0},{3,7},{4,6},{5,1},{6,4},{7,3},{8,10},{9,13},{10,... | collective-permute-start | bytes 626696 | tf_op jit(solution)/shard_map/ppermute | solution.py:46
  72.0 3.8 %collective-permute-done.11.refs_0_ = bf16[272,384]{1,0:T(8,128)(2,1)S(1)} collective-permute-done((bf16[272,384]{1,0:T(8,128)(2,1)S(1)}, bf16[272,384]{1,0:T(8,128)(2,1)S(1)}, u32[]{:S(2)}, u32[]{:S(2)}) %collective-permute-start.11) | collective-permute-done | bytes 208928 | tf_op jit(solution)/shard_map/ppermute | solution.py:46
  75.8 1.0 join.6
  76.8 0.6 copy-done.5
  77.4 2.0 %collective-permute-start.17 = (bf16[1024,384]{1,0:T(8,128)(2,1)}, bf16[1024,384]{1,0:T(8,128)(2,1)}, u32[]{:S(2)}, u32[]{:S(2)}) collective-permute-start(bf16[1024,384]{1,0:T(8,128)(2,1)} %get-tuple-element.77.refs_2_), channel_id=1, source_target_pairs={{0,2},{1,5},{2,0},{3,7},{4,6},{5,1},{6,4},{7,3},{8,10},{9,13},{10,... | collective-permute-start | bytes 2359304 | tf_op jit(solution)/shard_map/ppermute | solution.py:46
  79.5 2.4 %collective-permute-start.13 = (bf16[528,384]{1,0:T(8,128)(2,1)S(1)}, bf16[528,384]{1,0:T(8,128)(2,1)S(1)}, u32[]{:S(2)}, u32[]{:S(2)}) collective-permute-start(bf16[528,384]{1,0:T(8,128)(2,1)S(1)} %get-tuple-element.74.refs_1_), channel_id=1, source_target_pairs={{0,8},{1,9},{2,10},{3,11},{4,12},{5,13},{6,14},{7,15},{8,0},{9,1},... | collective-permute-start | bytes 1216520 | tf_op jit(solution)/shard_map/ppermute | solution.py:46
  81.9 0.7 compare_select_fusion.6.refs_1_.gid_ref
  82.6 0.7 copy-done.6
  83.3 7.2 %part_scores.2 = (bf16[1280,1024]{1,0:T(8,128)(2,1)}, f32[8,128]{1,0:T(8,128)S(1)}) custom-call(s32[16]{0:T(128)S(1)} %stack.212.code_ref, bf16[1280,768]{1,0:T(8,128)(2,1)} %x_ref.1, s32[1,1280]{1,0:T(1,128)S(1)} %compare_select_fusion.6.refs_1_.gid_ref, bf16[1024,384]{1,0:T(8,128)(2,1)} %get-tuple-element.77.refs_2_, ...), custom_call_target="tpu_custom_call" | custom-call | flops 1 | bytes 1 | tf_op jit(solution)/shard_map/part_scores/pallas_call | solution.py:328
  90.5 1.3 %collective-permute-done.13.refs_0_ = bf16[528,384]{1,0:T(8,128)(2,1)S(1)} collective-permute-done((bf16[528,384]{1,0:T(8,128)(2,1)S(1)}, bf16[528,384]{1,0:T(8,128)(2,1)S(1)}, u32[]{:S(2)}, u32[]{:S(2)}) %collective-permute-start.13) | collective-permute-done | bytes 405536 | tf_op jit(solution)/shard_map/ppermute | solution.py:46
  91.8 1.0 join.7
  93.6 3.1 %collective-permute-done.18.refs_3_ = bf16[1024,384]{1,0:T(8,128)(2,1)S(1)} collective-permute-done((bf16[1024,384]{1,0:T(8,128)(2,1)}, bf16[1024,384]{1,0:T(8,128)(2,1)S(1)}, u32[]{:S(2)}, u32[]{:S(2)}) %collective-permute-start.18) | collective-permute-done | bytes 786464 | tf_op jit(solution)/shard_map/ppermute | solution.py:46
  96.7 7.0 %part_scores.3 = (bf16[1280,1024]{1,0:T(8,128)(2,1)}, f32[8,128]{1,0:T(8,128)S(1)}) custom-call(s32[16]{0:T(128)S(1)} %stack.212.code_ref, bf16[1280,768]{1,0:T(8,128)(2,1)} %x_ref.1, s32[1,1280]{1,0:T(1,128)S(1)} %compare_select_fusion.6.refs_1_.gid_ref, bf16[1024,384]{1,0:T(8,128)(2,1)} %collective-permute-done.17.refs_2_, ...), custom_call_target="tpu_custom_call", output_to_operand_aliasing={{0}: (5, {})} | custom-call | flops 1 | bytes 1 | tf_op jit(solution)/shard_map/part_scores/pallas_call | solution.py:328
  103.7 1.5 %collective-permute-done.16.in_ref = bf16[1040,384]{1,0:T(8,128)(2,1)} collective-permute-done((bf16[1040,384]{1,0:T(8,128)(2,1)}, bf16[1040,384]{1,0:T(8,128)(2,1)}, u32[]{:S(2)}, u32[]{:S(2)}) %collective-permute-start.16) | collective-permute-done | bytes 798752 | tf_op jit(solution)/shard_map/ppermute | solution.py:46
  105.4 2.5 %collective-permute-done.19.rest_1_ = bf16[1040,384]{1,0:T(8,128)(2,1)} collective-permute-done((bf16[1040,384]{1,0:T(8,128)(2,1)}, bf16[1040,384]{1,0:T(8,128)(2,1)}, u32[]{:S(2)}, u32[]{:S(2)}) %collective-permute-start.19) | collective-permute-done | bytes 798752 | tf_op jit(solution)/shard_map/ppermute | solution.py:46
  107.9 0.7 copy-done.2
  108.6 11.0 %final_scores.1 = bf16[1280,1024]{1,0:T(8,128)(2,1)} custom-call(s32[32]{0:T(128)S(1)} %concatenate.104.code_ref, s32[8]{0:T(128)S(1)} %fusion.21.slot_ref, bf16[1280,768]{1,0:T(8,128)(2,1)} %x_ref.1, s32[1,1280]{1,0:T(1,128)S(1)} %copy-done.2, f32[16,1024]{1,0:T(8,128)S(1)} %broadcast_in_dim.28.half_ref, bf16[1040,384]{1,0:T(8,128)(2,1)} %behind.1.rest_0_, ...), custom_call_target="tpu_custom_call" | custom-call | flops 1 | bytes 1 | tf_op jit(solution)/shard_map/final_scores/pallas_call | solution.py:405
  (51 shorter events, 3.4 us)
Async XLA Ops:
  0.6 31.2 %copy-start = (f32[1,1024,768]{2,1,0:T(8,128)S(1)}, f32[1,1024,768]{2,1,0:T(8,128)}, u32[]{:S(2)}) copy-start(f32[1,1024,768]{2,1,0:T(8,128)} %param.9) | copy-start | bytes 9437188
  3.0 4.0 %collective-permute-start = (s32[1280]{0:T(1024)S(1)}, s32[1280]{0:T(1024)S(1)}, u32[]{:S(2)}, u32[]{:S(2)}) collective-permute-start(s32[1280]{0:T(1024)S(1)} %add_select_fusion.9), channel_id=1, source_target_pairs={{0,1},{1,0},{2,3},{3,2},{4,5},{5,4},{6,7},{7,6},{8,9},{9,8},{10,11... | collective-permute-start | bytes 15368 | tf_op jit(solution)/shard_map/ppermute | solution.py:46
  6.5 2.9 %collective-permute-start.2 = (bf16[1280,384]{1,0:T(8,128)(2,1)}, bf16[1280,384]{1,0:T(8,128)(2,1)}, u32[]{:S(2)}, u32[]{:S(2)}) collective-permute-start(bf16[1280,384]{1,0:T(8,128)(2,1)} %get-tuple-element.93.refs_1_), channel_id=1, source_target_pairs={{0,1},{1,0},{2,3},{3,2},{4,5},{5,4},{6,7},{7,6},{8,9},{9,8},{10,11... | collective-permute-start | bytes 2949128 | tf_op jit(solution)/shard_map/ppermute | solution.py:46
  6.5 10.0 %collective-permute-start.1 = (bf16[1280,384]{1,0:T(8,128)(2,1)}, bf16[1280,384]{1,0:T(8,128)(2,1)}, u32[]{:S(2)}, u32[]{:S(2)}) collective-permute-start(bf16[1280,384]{1,0:T(8,128)(2,1)} %get-tuple-element.94.refs_1_), channel_id=1, source_target_pairs={{0,1},{1,0},{2,3},{3,2},{4,5},{5,4},{6,7},{7,6},{8,9},{9,8},{10,11... | collective-permute-start | bytes 2949128 | tf_op jit(solution)/shard_map/ppermute | solution.py:46
  13.7 14.6 %collective-permute-start.4 = (bf16[1040,384]{1,0:T(8,128)(2,1)S(1)}, bf16[1040,384]{1,0:T(8,128)(2,1)S(1)}, u32[]{:S(2)}, u32[]{:S(2)}) collective-permute-start(bf16[1040,384]{1,0:T(8,128)(2,1)S(1)} %get-tuple-element.49), channel_id=1, source_target_pairs={{0,2},{1,5},{2,0},{3,7},{4,6},{5,1},{6,4},{7,3},{8,10},{9,13},{10,... | collective-permute-start | bytes 2396168 | tf_op jit(solution)/shard_map/ppermute | solution.py:46
  16.5 5.3 %copy-start.3 = (s32[1,2560]{1,0:T(1,128)}, s32[1,2560]{1,0:T(1,128)S(1)}, u32[]{:S(2)}) copy-start(s32[1,2560]{1,0:T(1,128)S(1)} %fusion.10.refs_0_) | copy-start | bytes 30724
  21.8 16.3 %collective-permute-start.3 = (bf16[1024,384]{1,0:T(8,128)(2,1)}, bf16[1024,384]{1,0:T(8,128)(2,1)}, u32[]{:S(2)}, u32[]{:S(2)}) collective-permute-start(bf16[1024,384]{1,0:T(8,128)(2,1)} %get-tuple-element.45), channel_id=1, source_target_pairs={{0,4},{1,3},{2,6},{3,1},{4,0},{5,7},{6,2},{7,5},{8,12},{9,11},{10,... | collective-permute-start | bytes 2359304 | tf_op jit(solution)/shard_map/ppermute | solution.py:46
  27.6 1.6 %copy-start.7 = (f32[8,128]{1,0:T(8,128)}, f32[8,128]{1,0:T(8,128)S(1)}, u32[]{:S(2)}) copy-start(f32[8,128]{1,0:T(8,128)S(1)} %get-tuple-element.47.refs_3_) | copy-start | bytes 12292
  29.2 10.7 %collective-permute-start.6 = (bf16[528,384]{1,0:T(8,128)(2,1)}, bf16[528,384]{1,0:T(8,128)(2,1)}, u32[]{:S(2)}, u32[]{:S(2)}) collective-permute-start(bf16[528,384]{1,0:T(8,128)(2,1)} %get-tuple-element.54), channel_id=1, source_target_pairs={{0,8},{1,9},{2,10},{3,11},{4,12},{5,13},{6,14},{7,15},{8,0},{9,1},... | collective-permute-start | bytes 1216520 | tf_op jit(solution)/shard_map/ppermute | solution.py:46
  31.8 0.7 copy-start.4
  32.6 0.7 copy-start.8
  39.4 11.8 %collective-permute-start.5 = (bf16[512,384]{1,0:T(8,128)(2,1)S(1)}, bf16[512,384]{1,0:T(8,128)(2,1)S(1)}, u32[]{:S(2)}, u32[]{:S(2)}) collective-permute-start(bf16[512,384]{1,0:T(8,128)(2,1)S(1)} %get-tuple-element.52), channel_id=1, source_target_pairs={{0,8},{1,9},{2,10},{3,11},{4,12},{5,13},{6,14},{7,15},{8,0},{9,1},... | collective-permute-start | bytes 1179656 | tf_op jit(solution)/shard_map/ppermute | solution.py:46
  41.0 6.6 %collective-permute-start.8 = (bf16[272,384]{1,0:T(8,128)(2,1)S(1)}, bf16[272,384]{1,0:T(8,128)(2,1)S(1)}, u32[]{:S(2)}, u32[]{:S(2)}) collective-permute-start(bf16[272,384]{1,0:T(8,128)(2,1)S(1)} %get-tuple-element.60), channel_id=1, source_target_pairs={{0,4},{1,3},{2,6},{3,1},{4,0},{5,7},{6,2},{7,5},{8,12},{9,11},{10,... | collective-permute-start | bytes 626696 | tf_op jit(solution)/shard_map/ppermute | solution.py:46
  47.7 7.7 %collective-permute-start.10 = (bf16[272,384]{1,0:T(8,128)(2,1)S(1)}, bf16[272,384]{1,0:T(8,128)(2,1)S(1)}, u32[]{:S(2)}, u32[]{:S(2)}) collective-permute-start(bf16[272,384]{1,0:T(8,128)(2,1)S(1)} %get-tuple-element.65.refs_1_), channel_id=1, source_target_pairs={{0,24},{1,25},{2,26},{3,27},{4,28},{5,29},{6,30},{7,31},{8,16},{9,... | collective-permute-start | bytes 626696 | tf_op jit(solution)/shard_map/ppermute | solution.py:46
  51.8 8.6 %collective-permute-start.7 = (bf16[256,384]{1,0:T(8,128)(2,1)S(1)}, bf16[256,384]{1,0:T(8,128)(2,1)S(1)}, u32[]{:S(2)}, u32[]{:S(2)}) collective-permute-start(bf16[256,384]{1,0:T(8,128)(2,1)S(1)} %get-tuple-element.58), channel_id=1, source_target_pairs={{0,2},{1,5},{2,0},{3,7},{4,6},{5,1},{6,4},{7,3},{8,10},{9,13},{10,... | collective-permute-start | bytes 589832 | tf_op jit(solution)/shard_map/ppermute | solution.py:46
  55.7 6.1 %collective-permute-start.12 = (bf16[256,384]{1,0:T(8,128)(2,1)S(1)}, bf16[256,384]{1,0:T(8,128)(2,1)S(1)}, u32[]{:S(2)}, u32[]{:S(2)}) collective-permute-start(bf16[256,384]{1,0:T(8,128)(2,1)S(1)} %get-tuple-element.72.refs_1_), channel_id=1, source_target_pairs={{0,4},{1,3},{2,6},{3,1},{4,0},{5,7},{6,2},{7,5},{8,12},{9,11},{10,... | collective-permute-start | bytes 589832 | tf_op jit(solution)/shard_map/ppermute | solution.py:46
  61.0 7.9 %collective-permute-start.9 = (bf16[256,384]{1,0:T(8,128)(2,1)S(1)}, bf16[256,384]{1,0:T(8,128)(2,1)S(1)}, u32[]{:S(2)}, u32[]{:S(2)}) collective-permute-start(bf16[256,384]{1,0:T(8,128)(2,1)S(1)} %get-tuple-element.63.refs_1_), channel_id=1, source_target_pairs={{0,24},{1,25},{2,26},{3,27},{4,28},{5,29},{6,30},{7,31},{8,16},{9,... | collective-permute-start | bytes 589832 | tf_op jit(solution)/shard_map/ppermute | solution.py:46
  61.9 13.9 %collective-permute-start.14 = (bf16[512,384]{1,0:T(8,128)(2,1)S(1)}, bf16[512,384]{1,0:T(8,128)(2,1)S(1)}, u32[]{:S(2)}, u32[]{:S(2)}) collective-permute-start(bf16[512,384]{1,0:T(8,128)(2,1)S(1)} %get-tuple-element.75.refs_1_), channel_id=1, source_target_pairs={{0,8},{1,9},{2,10},{3,11},{4,12},{5,13},{6,14},{7,15},{8,0},{9,1},... | collective-permute-start | bytes 1179656 | tf_op jit(solution)/shard_map/ppermute | solution.py:46
  69.9 5.9 %collective-permute-start.11 = (bf16[272,384]{1,0:T(8,128)(2,1)S(1)}, bf16[272,384]{1,0:T(8,128)(2,1)S(1)}, u32[]{:S(2)}, u32[]{:S(2)}) collective-permute-start(bf16[272,384]{1,0:T(8,128)(2,1)S(1)} %get-tuple-element.71.refs_1_), channel_id=1, source_target_pairs={{0,2},{1,5},{2,0},{3,7},{4,6},{5,1},{6,4},{7,3},{8,10},{9,13},{10,... | collective-permute-start | bytes 626696 | tf_op jit(solution)/shard_map/ppermute | solution.py:46
  76.8 0.6 copy-start.5
  77.4 5.2 %collective-permute-start.15 = (bf16[1024,384]{1,0:T(8,128)(2,1)}, bf16[1024,384]{1,0:T(8,128)(2,1)}, u32[]{:S(2)}, u32[]{:S(2)}) collective-permute-start(bf16[1024,384]{1,0:T(8,128)(2,1)} %get-tuple-element.77.refs_2_), channel_id=1, source_target_pairs={{0,1},{1,0},{2,3},{3,2},{4,5},{5,4},{6,7},{7,6},{8,9},{9,8},{10,11... | collective-permute-start | bytes 2359304 | tf_op jit(solution)/shard_map/ppermute | solution.py:46
  77.4 15.7 %collective-permute-start.17 = (bf16[1024,384]{1,0:T(8,128)(2,1)}, bf16[1024,384]{1,0:T(8,128)(2,1)}, u32[]{:S(2)}, u32[]{:S(2)}) collective-permute-start(bf16[1024,384]{1,0:T(8,128)(2,1)} %get-tuple-element.77.refs_2_), channel_id=1, source_target_pairs={{0,2},{1,5},{2,0},{3,7},{4,6},{5,1},{6,4},{7,3},{8,10},{9,13},{10,... | collective-permute-start | bytes 2359304 | tf_op jit(solution)/shard_map/ppermute | solution.py:46
  79.5 12.4 %collective-permute-start.13 = (bf16[528,384]{1,0:T(8,128)(2,1)S(1)}, bf16[528,384]{1,0:T(8,128)(2,1)S(1)}, u32[]{:S(2)}, u32[]{:S(2)}) collective-permute-start(bf16[528,384]{1,0:T(8,128)(2,1)S(1)} %get-tuple-element.74.refs_1_), channel_id=1, source_target_pairs={{0,8},{1,9},{2,10},{3,11},{4,12},{5,13},{6,14},{7,15},{8,0},{9,1},... | collective-permute-start | bytes 1216520 | tf_op jit(solution)/shard_map/ppermute | solution.py:46
  82.6 21.1 %copy-start.1 = (s32[1,1280]{1,0:T(1,128)}, s32[1,1280]{1,0:T(1,128)S(1)}, u32[]{:S(2)}) copy-start(s32[1,1280]{1,0:T(1,128)S(1)} %compare_select_fusion.6.refs_1_.gid_ref) | copy-start | bytes 15364
  82.6 0.7 copy-start.6
  92.8 12.4 %collective-permute-start.16 = (bf16[1040,384]{1,0:T(8,128)(2,1)}, bf16[1040,384]{1,0:T(8,128)(2,1)}, u32[]{:S(2)}, u32[]{:S(2)}) collective-permute-start(bf16[1040,384]{1,0:T(8,128)(2,1)} %get-tuple-element.80.rest_2_), channel_id=1, source_target_pairs={{0,4},{1,3},{2,6},{3,1},{4,0},{5,7},{6,2},{7,5},{8,12},{9,11},{10,... | collective-permute-start | bytes 2396168 | tf_op jit(solution)/shard_map/ppermute | solution.py:46
  93.1 3.6 %collective-permute-start.18 = (bf16[1024,384]{1,0:T(8,128)(2,1)}, bf16[1024,384]{1,0:T(8,128)(2,1)S(1)}, u32[]{:S(2)}, u32[]{:S(2)}) collective-permute-start(bf16[1024,384]{1,0:T(8,128)(2,1)} %collective-permute-done.17.refs_2_), channel_id=1, source_target_pairs={{0,1},{1,0},{2,3},{3,2},{4,5},{5,4},{6,7},{7,6},{8,9},{9,8},{10,11... | collective-permute-start | bytes 2359304 | tf_op jit(solution)/shard_map/ppermute | solution.py:46
  93.1 12.3 %collective-permute-start.20 = (bf16[1040,384]{1,0:T(8,128)(2,1)}, bf16[1040,384]{1,0:T(8,128)(2,1)}, u32[]{:S(2)}, u32[]{:S(2)}) collective-permute-start(bf16[1040,384]{1,0:T(8,128)(2,1)} %get-tuple-element.80.rest_2_), channel_id=1, source_target_pairs={{0,1},{1,0},{2,3},{3,2},{4,5},{5,4},{6,7},{7,6},{8,9},{9,8},{10,11... | collective-permute-start | bytes 2396168 | tf_op jit(solution)/shard_map/ppermute | solution.py:46
  105.3 2.6 %collective-permute-start.19 = (bf16[1040,384]{1,0:T(8,128)(2,1)}, bf16[1040,384]{1,0:T(8,128)(2,1)}, u32[]{:S(2)}, u32[]{:S(2)}) collective-permute-start(bf16[1040,384]{1,0:T(8,128)(2,1)} %behind.1.rest_0_), channel_id=1, source_target_pairs={{0,1},{1,0},{2,3},{3,2},{4,5},{5,4},{6,7},{7,6},{8,9},{9,8},{10,11... | collective-permute-start | bytes 2396168 | tf_op jit(solution)/shard_map/ppermute | solution.py:46
  107.9 0.7 copy-start.2

commit v10 on v9

--- a/solution.py
+++ b/solution.py
@@ -102,8 +102,8 @@
         out_ref[keys:, :] = rest[0][...]
 
 
-def key_sums(token, pos_row, own, other, count_tile, base, keys):
-    rows, wide = own.shape
+def key_sums(token, pos_row, own, other, count_tile, base, keys, start, wide):
+    rows = own.shape[0]
     extra = [] if count_tile is None else [count_tile]
     out_rows = keys + sum(e.shape[0] for e in extra)
     whole = lambda shape: pl.BlockSpec(shape, lambda i: (0, 0))
@@ -113,13 +113,13 @@
         out_shape=[jax.ShapeDtypeStruct((out_rows, wide), BF16), token_shape()],
         in_specs=[
             whole((1, 2 * rows)),
-            whole((rows, wide)),
-            whole((rows, wide)),
+            pl.BlockSpec((rows, wide), lambda i: (0, start // wide)),
+            pl.BlockSpec((rows, wide), lambda i: (0, start // wide)),
         ]
         + [whole(e.shape) for e in extra]
         + [whole(token.shape)],
         out_specs=[whole((out_rows, wide)), whole(token.shape)],
-        compiler_params=pltpu.CompilerParams(vmem_limit_bytes=16 << 20),
+        compiler_params=pltpu.CompilerParams(vmem_limit_bytes=56 << 20),
         cost_estimate=pl.CostEstimate(
             flops=2 * keys * 2 * rows * wide, bytes_accessed=(4 * rows + 2 * keys) * wide, transcendentals=0
         ),
@@ -452,8 +452,7 @@
     live = jnp.arange(rows, dtype=jnp.int32) < live_rows[0]
     label = jnp.where(live, coarse_label[:, 0] * keys + fine_label, -1)
     sibling = lambda a: exchange(a, lambda gz, m: (gz, m ^ 1), groups, members)
-    cut_rows = [samples[:, start : start + wide] for start, wide in streams_of(width)]
-    other_rows = [sibling(part) for part in cut_rows]
+    other_samples = sibling(samples)
     label_all = jnp.concatenate([label, sibling(label)])
 
     group_of = label_all // keys
@@ -496,7 +495,7 @@
     for part, found in enumerate((send, keep)):
         for stream, (start, wide) in enumerate(columns):
             found[stream], token = key_sums(
-                token, rows_of[stream], cut_rows[stream], other_rows[stream], tiles[stream], part * half_keys, half_keys
+                token, rows_of[stream], samples, other_samples, tiles[stream], part * half_keys, half_keys, start, wide
             )
 
     tokens = [start_token] * 2

time: 121 us -> 121 us (level)
  starting transfers between devices: 30.2 us -> 22.1 us
  waiting for transfers between devices: 26.1 us -> 32.1 us
  Pallas kernels: 52 us -> 54.5 us
  other arithmetic: 2.61 us -> 4.41 us
  local copies, waits for them, and re-layouts: 6.59 us -> 5.08 us
    ppermute x21 -> x20, starting transfers between devices: 30.2 us -> 22.1 us  [exchange(): return lax.ppermute(array, AXES, pairs)]
    ppermute x21 -> x20, waiting for transfers between devices: 26.1 us -> 32.1 us  [exchange(): return lax.ppermute(array, AXES, pairs)]
    slice x1 -> x0, local copies, waits for them, and re-layouts: 3.01 us -> none  [per_device(): samples[:, start:start + wide]]
    pallas_call x4, Pallas kernels: 18.8 us -> 21.1 us  [key_sums(): pl.pallas_call(hand_on(functools.partial(sums_kernel, base), 3 + len(extr...]
    unnamed x19 -> x17, local copies, waits for them, and re-layouts: 3.32 us -> 4.23 us
  transfers between devices with their start and end apart: 21 -> 20, of which waited for: 12 -> 13; matrix products, arithmetic and copies ran while one was open for 4% -> 3% of each run, Pallas kernels for 33% -> 31%
where the time goes in v10:
time: 121 us
  Pallas kernels  54.5 us (45%)
  waiting for transfers between devices  32.1 us (27%)
  starting transfers between devices  22.1 us (18%)
  local copies, waits for them, and re-layouts  5.08 us (4%)
  other arithmetic  4.41 us (4%)
  between operations  1.75 us (1%)
    ppermute x20, waiting for transfers between devices, exchange(): return lax.ppermute(array, AXES, pairs)  32.1 us
    ppermute x20, starting transfers between devices, exchange(): return lax.ppermute(array, AXES, pairs)  22.1 us
    pallas_call x4, Pallas kernels, key_sums(): pl.pallas_call(hand_on(functools.partial(sums_kernel, base), 3 + len(extr...  21.1 us
    pallas_call x2, Pallas kernels, part_scores(): pl.pallas_call(kernel, grid_spec=pltpu.PrefetchScalarGridSpec(num_scalar_...  14.4 us
    pallas_call x1, Pallas kernels, final_scores(): pl.pallas_call(functools.partial(final_kernel, groups, share, start_at),...  11 us
    pallas_call x12, Pallas kernels, small_call(): pl.pallas_call(hand_on(kernel, len(args)), out_shape=[*outs, token_shape(...  7.92 us
    unnamed x17, local copies, waits for them, and re-layouts  4.23 us
  transfers between devices with their start and end apart: 20, of which 13 were waited for; matrix products, arithmetic and copies ran while one was open for 3% of the time, Pallas kernels for 31%

profile of v10, /device:TPU:0, one launch (start us, length us, event | category | flops | bytes accessed | tf_op | source)
XLA Modules:
  0.0 120.5 jit_solution(10292070997459443228)
XLA Ops:
  1.4 0.9 multiply_reduce_fusion
  2.3 0.7 add_select_fusion.9
  3.5 0.8 collective-permute-done
  5.6 0.8 fusion.13
  6.4 1.4 %collective-permute-done.1.refs_2_ = bf16[1280,768]{1,0:T(8,128)(2,1)} collective-permute-done((bf16[1280,768]{1,0:T(8,128)(2,1)}, bf16[1280,768]{1,0:T(8,128)(2,1)}, u32[]{:S(2)}, u32[]{:S(2)}) %collective-permute-start.1) | collective-permute-done | bytes 1966112 | tf_op jit(solution)/shard_map/ppermute | solution.py:46
  8.4 5.3 %key_sums.4 = (bf16[1040,384]{1,0:T(8,128)(2,1)}, f32[8,128]{1,0:T(8,128)}) custom-call(s32[1,2560]{1,0:T(1,128)} %get-tuple-element.86.refs_0_, bf16[1280,768]{1,0:T(8,128)(2,1)} %x_ref.1, bf16[1280,768]{1,0:T(8,128)(2,1)} %collective-permute-done.1.refs_2_, bf16[16,384]{1,0:T(8,128)(2,1)} %pad_maximum_fusion.refs_3_, f32[8,128]{1,0:T(8,128)} %broadcast_in_dim.30.refs_4_.refs_2_), custom_call_target="tpu_custom_call" | custom-call | flops 2013265920 | bytes 2752512 | tf_op jit(solution)/shard_map/key_sums/pallas_call | solution.py:110
  13.6 2.6 %collective-permute-start.3 = (bf16[1040,384]{1,0:T(8,128)(2,1)}, bf16[1040,384]{1,0:T(8,128)(2,1)S(1)}, u32[]{:S(2)}, u32[]{:S(2)}) collective-permute-start(bf16[1040,384]{1,0:T(8,128)(2,1)} %get-tuple-element.49), channel_id=1, source_target_pairs={{0,2},{1,5},{2,0},{3,7},{4,6},{5,1},{6,4},{7,3},{8,10},{9,13},{10,... | collective-permute-start | bytes 2396168 | tf_op jit(solution)/shard_map/ppermute | solution.py:46
  16.3 0.6 fusion.10.refs_0_
  16.9 5.3 %key_sums.5 = (bf16[1024,384]{1,0:T(8,128)(2,1)}, f32[8,128]{1,0:T(8,128)}) custom-call(s32[1,2560]{1,0:T(1,128)} %fusion.10.refs_0_, bf16[1280,768]{1,0:T(8,128)(2,1)} %x_ref.1, bf16[1280,768]{1,0:T(8,128)(2,1)} %collective-permute-done.1.refs_2_, f32[8,128]{1,0:T(8,128)} %get-tuple-element.44.refs_3_), custom_call_target="tpu_custom_call" | custom-call | flops 2013265920 | bytes 2752512 | tf_op jit(solution)/shard_map/key_sums/pallas_call | solution.py:110
  22.2 1.5 %collective-permute-start.2 = (bf16[1024,384]{1,0:T(8,128)(2,1)}, bf16[1024,384]{1,0:T(8,128)(2,1)}, u32[]{:S(2)}, u32[]{:S(2)}) collective-permute-start(bf16[1024,384]{1,0:T(8,128)(2,1)} %get-tuple-element.45), channel_id=1, source_target_pairs={{0,4},{1,3},{2,6},{3,1},{4,0},{5,7},{6,2},{7,5},{8,12},{9,11},{10,... | collective-permute-start | bytes 2359304 | tf_op jit(solution)/shard_map/ppermute | solution.py:46
  23.7 5.3 %key_sums.6 = (bf16[1040,384]{1,0:T(8,128)(2,1)}, f32[8,128]{1,0:T(8,128)}) custom-call(s32[1,2560]{1,0:T(1,128)} %get-tuple-element.86.refs_0_, bf16[1280,768]{1,0:T(8,128)(2,1)} %x_ref.1, bf16[1280,768]{1,0:T(8,128)(2,1)} %collective-permute-done.1.refs_2_, bf16[16,384]{1,0:T(8,128)(2,1)} %pad_maximum_fusion.refs_3_, f32[8,128]{1,0:T(8,128)} %get-tuple-element.46.refs_4_), custom_call_target="tpu_custom_call" | custom-call | flops 2013265920 | bytes 2752512 | tf_op jit(solution)/shard_map/key_sums/pallas_call | solution.py:110
  29.0 1.1 copy-done.1
  30.2 0.9 fold.4
  31.0 1.6 %collective-permute-start.5 = (bf16[528,384]{1,0:T(8,128)(2,1)}, bf16[528,384]{1,0:T(8,128)(2,1)}, u32[]{:S(2)}, u32[]{:S(2)}) collective-permute-start(bf16[528,384]{1,0:T(8,128)(2,1)} %get-tuple-element.54), channel_id=1, source_target_pairs={{0,8},{1,9},{2,10},{3,11},{4,12},{5,13},{6,14},{7,15},{8,0},{9,1},... | collective-permute-start | bytes 1216520 | tf_op jit(solution)/shard_map/ppermute | solution.py:46
  32.7 5.3 %key_sums.7 = (bf16[1024,384]{1,0:T(8,128)(2,1)}, f32[8,128]{1,0:T(8,128)}) custom-call(s32[1,2560]{1,0:T(1,128)} %fusion.10.refs_0_, bf16[1280,768]{1,0:T(8,128)(2,1)} %x_ref.1, bf16[1280,768]{1,0:T(8,128)(2,1)} %collective-permute-done.1.refs_2_, f32[8,128]{1,0:T(8,128)} %get-tuple-element.47.refs_3_), custom_call_target="tpu_custom_call" | custom-call | flops 2013265920 | bytes 2752512 | tf_op jit(solution)/shard_map/key_sums/pallas_call | solution.py:110
  37.9 1.1 copy-done.2
  39.1 1.3 %fold.5 = (bf16[512,384]{1,0:T(8,128)(2,1)S(1)}, bf16[512,384]{1,0:T(8,128)(2,1)S(1)}, f32[8,128]{1,0:T(8,128)S(1)}) custom-call(bf16[1024,384]{1,0:T(8,128)(2,1)} %collective-permute-done.2.refs_0_, bf16[1024,384]{1,0:T(8,128)(2,1)S(1)} %copy-done.2, f32[8,128]{1,0:T(8,128)S(1)} %get-tuple-element.51.refs_2_), custom_call_target="tpu_custom_call" | custom-call | flops 1179648 | bytes 2359296 | tf_op jit(solution)/shard_map/fold/pallas_call | solution.py:133
  40.9 1.5 %collective-permute-done.5.refs_0_ = bf16[528,384]{1,0:T(8,128)(2,1)} collective-permute-done((bf16[528,384]{1,0:T(8,128)(2,1)}, bf16[528,384]{1,0:T(8,128)(2,1)}, u32[]{:S(2)}, u32[]{:S(2)}) %collective-permute-start.5) | collective-permute-done | bytes 405536 | tf_op jit(solution)/shard_map/ppermute | solution.py:46
  42.4 1.1 fold.6
  43.5 1.3 %collective-permute-start.7 = (bf16[272,384]{1,0:T(8,128)(2,1)S(1)}, bf16[272,384]{1,0:T(8,128)(2,1)S(1)}, u32[]{:S(2)}, u32[]{:S(2)}) collective-permute-start(bf16[272,384]{1,0:T(8,128)(2,1)S(1)} %get-tuple-element.60), channel_id=1, source_target_pairs={{0,4},{1,3},{2,6},{3,1},{4,0},{5,7},{6,2},{7,5},{8,12},{9,11},{10,... | collective-permute-start | bytes 626696 | tf_op jit(solution)/shard_map/ppermute | solution.py:46
  44.9 4.5 %collective-permute-done.7.refs_0_ = bf16[272,384]{1,0:T(8,128)(2,1)S(1)} collective-permute-done((bf16[272,384]{1,0:T(8,128)(2,1)S(1)}, bf16[272,384]{1,0:T(8,128)(2,1)S(1)}, u32[]{:S(2)}, u32[]{:S(2)}) %collective-permute-start.7) | collective-permute-done | bytes 208928 | tf_op jit(solution)/shard_map/ppermute | solution.py:46
  49.5 4.5 %collective-permute-start.9 = (bf16[272,384]{1,0:T(8,128)(2,1)S(1)}, bf16[272,384]{1,0:T(8,128)(2,1)S(1)}, u32[]{:S(2)}, u32[]{:S(2)}) collective-permute-start(bf16[272,384]{1,0:T(8,128)(2,1)S(1)} %get-tuple-element.65.refs_1_), channel_id=1, source_target_pairs={{0,24},{1,25},{2,26},{3,27},{4,28},{5,29},{6,30},{7,31},{8,16},{9,... | collective-permute-start | bytes 626696 | tf_op jit(solution)/shard_map/ppermute | solution.py:46
  54.0 0.6 fold.7
  54.6 0.8 collective-permute-start.6
  55.3 2.5 %collective-permute-done.9.refs_0_ = bf16[272,384]{1,0:T(8,128)(2,1)S(1)} collective-permute-done((bf16[272,384]{1,0:T(8,128)(2,1)S(1)}, bf16[272,384]{1,0:T(8,128)(2,1)S(1)}, u32[]{:S(2)}, u32[]{:S(2)}) %collective-permute-start.9) | collective-permute-done | bytes 208928 | tf_op jit(solution)/shard_map/ppermute | solution.py:46
  58.1 0.7 collective-permute-start.11
  58.8 3.5 %collective-permute-done.6.refs_0_ = bf16[256,384]{1,0:T(8,128)(2,1)S(1)} collective-permute-done((bf16[256,384]{1,0:T(8,128)(2,1)S(1)}, bf16[256,384]{1,0:T(8,128)(2,1)S(1)}, u32[]{:S(2)}, u32[]{:S(2)}) %collective-permute-start.6) | collective-permute-done | bytes 196640 | tf_op jit(solution)/shard_map/ppermute | solution.py:46
  63.0 0.8 collective-permute-done.11.refs_0_
  63.9 3.0 %collective-permute-start.13 = (bf16[512,384]{1,0:T(8,128)(2,1)S(1)}, bf16[512,384]{1,0:T(8,128)(2,1)S(1)}, u32[]{:S(2)}, u32[]{:S(2)}) collective-permute-start(bf16[512,384]{1,0:T(8,128)(2,1)S(1)} %get-tuple-element.75.refs_1_), channel_id=1, source_target_pairs={{0,8},{1,9},{2,10},{3,11},{4,12},{5,13},{6,14},{7,15},{8,0},{9,1},... | collective-permute-start | bytes 1179656 | tf_op jit(solution)/shard_map/ppermute | solution.py:46
  66.8 4.5 %collective-permute-done.8.refs_0_ = bf16[256,384]{1,0:T(8,128)(2,1)S(1)} collective-permute-done((bf16[256,384]{1,0:T(8,128)(2,1)S(1)}, bf16[256,384]{1,0:T(8,128)(2,1)S(1)}, u32[]{:S(2)}, u32[]{:S(2)}) %collective-permute-start.8) | collective-permute-done | bytes 196640 | tf_op jit(solution)/shard_map/ppermute | solution.py:46
  71.3 1.0 last_centroids.1
  72.3 0.6 collective-permute-start.10
  72.9 5.2 %collective-permute-done.10.refs_0_ = bf16[272,384]{1,0:T(8,128)(2,1)S(1)} collective-permute-done((bf16[272,384]{1,0:T(8,128)(2,1)S(1)}, bf16[272,384]{1,0:T(8,128)(2,1)S(1)}, u32[]{:S(2)}, u32[]{:S(2)}) %collective-permute-start.10) | collective-permute-done | bytes 208928 | tf_op jit(solution)/shard_map/ppermute | solution.py:46
  78.1 1.0 join.6
  79.7 0.6 collective-permute-start.16
  80.4 2.5 %collective-permute-start.12 = (bf16[528,384]{1,0:T(8,128)(2,1)S(1)}, bf16[528,384]{1,0:T(8,128)(2,1)S(1)}, u32[]{:S(2)}, u32[]{:S(2)}) collective-permute-start(bf16[528,384]{1,0:T(8,128)(2,1)S(1)} %get-tuple-element.74.refs_1_), channel_id=1, source_target_pairs={{0,8},{1,9},{2,10},{3,11},{4,12},{5,13},{6,14},{7,15},{8,0},{9,1},... | collective-permute-start | bytes 1216520 | tf_op jit(solution)/shard_map/ppermute | solution.py:46
  82.9 0.7 compare_select_fusion.6.refs_1_.gid_ref
  83.6 0.7 copy-done.7
  84.3 7.4 %part_scores.2 = (bf16[1280,1024]{1,0:T(8,128)(2,1)}, f32[8,128]{1,0:T(8,128)S(1)}) custom-call(s32[16]{0:T(128)S(1)} %stack.212.code_ref, bf16[1280,768]{1,0:T(8,128)(2,1)} %x_ref.1, s32[1,1280]{1,0:T(1,128)S(1)} %compare_select_fusion.6.refs_1_.gid_ref, bf16[1024,384]{1,0:T(8,128)(2,1)} %get-tuple-element.77.refs_2_, ...), custom_call_target="tpu_custom_call" | custom-call | flops 1 | bytes 1 | tf_op jit(solution)/shard_map/part_scores/pallas_call | solution.py:328
  91.7 0.8 collective-permute-done.12.refs_0_
  92.6 1.0 join.7
  93.6 0.8 collective-permute-start.15
  94.9 2.0 %collective-permute-done.17.refs_3_ = bf16[1024,384]{1,0:T(8,128)(2,1)S(1)} collective-permute-done((bf16[1024,384]{1,0:T(8,128)(2,1)}, bf16[1024,384]{1,0:T(8,128)(2,1)S(1)}, u32[]{:S(2)}, u32[]{:S(2)}) %collective-permute-start.17) | collective-permute-done | bytes 786464 | tf_op jit(solution)/shard_map/ppermute | solution.py:46
  96.9 7.0 %part_scores.3 = (bf16[1280,1024]{1,0:T(8,128)(2,1)}, f32[8,128]{1,0:T(8,128)S(1)}) custom-call(s32[16]{0:T(128)S(1)} %stack.212.code_ref, bf16[1280,768]{1,0:T(8,128)(2,1)} %x_ref.1, s32[1,1280]{1,0:T(1,128)S(1)} %compare_select_fusion.6.refs_1_.gid_ref, bf16[1024,384]{1,0:T(8,128)(2,1)} %collective-permute-done.16.refs_2_, ...), custom_call_target="tpu_custom_call", output_to_operand_aliasing={{0}: (5, {})} | custom-call | flops 1 | bytes 1 | tf_op jit(solution)/shard_map/part_scores/pallas_call | solution.py:328
  103.9 2.1 %collective-permute-done.15.in_ref = bf16[1040,384]{1,0:T(8,128)(2,1)} collective-permute-done((bf16[1040,384]{1,0:T(8,128)(2,1)}, bf16[1040,384]{1,0:T(8,128)(2,1)}, u32[]{:S(2)}, u32[]{:S(2)}) %collective-permute-start.15) | collective-permute-done | bytes 798752 | tf_op jit(solution)/shard_map/ppermute | solution.py:46
  106.1 2.5 %collective-permute-done.18.rest_1_ = bf16[1040,384]{1,0:T(8,128)(2,1)} collective-permute-done((bf16[1040,384]{1,0:T(8,128)(2,1)}, bf16[1040,384]{1,0:T(8,128)(2,1)}, u32[]{:S(2)}, u32[]{:S(2)}) %collective-permute-start.18) | collective-permute-done | bytes 798752 | tf_op jit(solution)/shard_map/ppermute | solution.py:46
  108.6 0.7 copy-done.4
  109.3 11.0 %final_scores.1 = bf16[1280,1024]{1,0:T(8,128)(2,1)} custom-call(s32[32]{0:T(128)S(1)} %concatenate.104.code_ref, s32[8]{0:T(128)S(1)} %fusion.21.slot_ref, bf16[1280,768]{1,0:T(8,128)(2,1)} %x_ref.1, s32[1,1280]{1,0:T(1,128)S(1)} %copy-done.4, f32[16,1024]{1,0:T(8,128)S(1)} %broadcast_in_dim.28.half_ref, bf16[1040,384]{1,0:T(8,128)(2,1)} %behind.1.rest_0_, ...), custom_call_target="tpu_custom_call" | custom-call | flops 1 | bytes 1 | tf_op jit(solution)/shard_map/final_scores/pallas_call | solution.py:405
  (46 shorter events, 5.3 us)
Async XLA Ops:
  0.6 32.0 %copy-start = (f32[1,1024,768]{2,1,0:T(8,128)S(1)}, f32[1,1024,768]{2,1,0:T(8,128)}, u32[]{:S(2)}) copy-start(f32[1,1024,768]{2,1,0:T(8,128)} %param.9) | copy-start | bytes 9437188
  3.0 1.3 %collective-permute-start = (s32[1280]{0:T(1024)S(1)}, s32[1280]{0:T(1024)S(1)}, u32[]{:S(2)}, u32[]{:S(2)}) collective-permute-start(s32[1280]{0:T(1024)S(1)} %add_select_fusion.9), channel_id=1, source_target_pairs={{0,1},{1,0},{2,3},{3,2},{4,5},{5,4},{6,7},{7,6},{8,9},{9,8},{10,11... | collective-permute-start | bytes 15368 | tf_op jit(solution)/shard_map/ppermute | solution.py:46
  3.5 4.3 %collective-permute-start.1 = (bf16[1280,768]{1,0:T(8,128)(2,1)}, bf16[1280,768]{1,0:T(8,128)(2,1)}, u32[]{:S(2)}, u32[]{:S(2)}) collective-permute-start(bf16[1280,768]{1,0:T(8,128)(2,1)} %x_ref.1), channel_id=1, source_target_pairs={{0,1},{1,0},{2,3},{3,2},{4,5},{5,4},{6,7},{7,6},{8,9},{9,8},{10,11... | collective-permute-start | bytes 5898248 | tf_op jit(solution)/shard_map/ppermute | solution.py:46
  13.6 15.4 %collective-permute-start.3 = (bf16[1040,384]{1,0:T(8,128)(2,1)}, bf16[1040,384]{1,0:T(8,128)(2,1)S(1)}, u32[]{:S(2)}, u32[]{:S(2)}) collective-permute-start(bf16[1040,384]{1,0:T(8,128)(2,1)} %get-tuple-element.49), channel_id=1, source_target_pairs={{0,2},{1,5},{2,0},{3,7},{4,6},{5,1},{6,4},{7,3},{8,10},{9,13},{10,... | collective-permute-start | bytes 2396168 | tf_op jit(solution)/shard_map/ppermute | solution.py:46
  22.2 15.8 %collective-permute-start.2 = (bf16[1024,384]{1,0:T(8,128)(2,1)}, bf16[1024,384]{1,0:T(8,128)(2,1)}, u32[]{:S(2)}, u32[]{:S(2)}) collective-permute-start(bf16[1024,384]{1,0:T(8,128)(2,1)} %get-tuple-element.45), channel_id=1, source_target_pairs={{0,4},{1,3},{2,6},{3,1},{4,0},{5,7},{6,2},{7,5},{8,12},{9,11},{10,... | collective-permute-start | bytes 2359304 | tf_op jit(solution)/shard_map/ppermute | solution.py:46
  23.7 5.3 %copy-start.5 = (f32[8,128]{1,0:T(8,128)S(1)}, f32[8,128]{1,0:T(8,128)}, u32[]{:S(2)}) copy-start(f32[8,128]{1,0:T(8,128)} %broadcast_in_dim.30.refs_4_.refs_2_) | copy-start | bytes 12292
  29.0 1.1 copy-start.1
  31.0 11.4 %collective-permute-start.5 = (bf16[528,384]{1,0:T(8,128)(2,1)}, bf16[528,384]{1,0:T(8,128)(2,1)}, u32[]{:S(2)}, u32[]{:S(2)}) collective-permute-start(bf16[528,384]{1,0:T(8,128)(2,1)} %get-tuple-element.54), channel_id=1, source_target_pairs={{0,8},{1,9},{2,10},{3,11},{4,12},{5,13},{6,14},{7,15},{8,0},{9,1},... | collective-permute-start | bytes 1216520 | tf_op jit(solution)/shard_map/ppermute | solution.py:46
  37.9 1.1 copy-start.2
  40.4 13.5 %collective-permute-start.4 = (bf16[512,384]{1,0:T(8,128)(2,1)S(1)}, bf16[512,384]{1,0:T(8,128)(2,1)S(1)}, u32[]{:S(2)}, u32[]{:S(2)}) collective-permute-start(bf16[512,384]{1,0:T(8,128)(2,1)S(1)} %get-tuple-element.52), channel_id=1, source_target_pairs={{0,8},{1,9},{2,10},{3,11},{4,12},{5,13},{6,14},{7,15},{8,0},{9,1},... | collective-permute-start | bytes 1179656 | tf_op jit(solution)/shard_map/ppermute | solution.py:46
  43.5 5.9 %collective-permute-start.7 = (bf16[272,384]{1,0:T(8,128)(2,1)S(1)}, bf16[272,384]{1,0:T(8,128)(2,1)S(1)}, u32[]{:S(2)}, u32[]{:S(2)}) collective-permute-start(bf16[272,384]{1,0:T(8,128)(2,1)S(1)} %get-tuple-element.60), channel_id=1, source_target_pairs={{0,4},{1,3},{2,6},{3,1},{4,0},{5,7},{6,2},{7,5},{8,12},{9,11},{10,... | collective-permute-start | bytes 626696 | tf_op jit(solution)/shard_map/ppermute | solution.py:46
  49.5 8.3 %collective-permute-start.9 = (bf16[272,384]{1,0:T(8,128)(2,1)S(1)}, bf16[272,384]{1,0:T(8,128)(2,1)S(1)}, u32[]{:S(2)}, u32[]{:S(2)}) collective-permute-start(bf16[272,384]{1,0:T(8,128)(2,1)S(1)} %get-tuple-element.65.refs_1_), channel_id=1, source_target_pairs={{0,24},{1,25},{2,26},{3,27},{4,28},{5,29},{6,30},{7,31},{8,16},{9,... | collective-permute-start | bytes 626696 | tf_op jit(solution)/shard_map/ppermute | solution.py:46
  54.6 7.8 %collective-permute-start.6 = (bf16[256,384]{1,0:T(8,128)(2,1)S(1)}, bf16[256,384]{1,0:T(8,128)(2,1)S(1)}, u32[]{:S(2)}, u32[]{:S(2)}) collective-permute-start(bf16[256,384]{1,0:T(8,128)(2,1)S(1)} %get-tuple-element.58), channel_id=1, source_target_pairs={{0,2},{1,5},{2,0},{3,7},{4,6},{5,1},{6,4},{7,3},{8,10},{9,13},{10,... | collective-permute-start | bytes 589832 | tf_op jit(solution)/shard_map/ppermute | solution.py:46
  58.1 5.7 %collective-permute-start.11 = (bf16[256,384]{1,0:T(8,128)(2,1)S(1)}, bf16[256,384]{1,0:T(8,128)(2,1)S(1)}, u32[]{:S(2)}, u32[]{:S(2)}) collective-permute-start(bf16[256,384]{1,0:T(8,128)(2,1)S(1)} %get-tuple-element.72.refs_1_), channel_id=1, source_target_pairs={{0,4},{1,3},{2,6},{3,1},{4,0},{5,7},{6,2},{7,5},{8,12},{9,11},{10,... | collective-permute-start | bytes 589832 | tf_op jit(solution)/shard_map/ppermute | solution.py:46
  63.0 8.3 %collective-permute-start.8 = (bf16[256,384]{1,0:T(8,128)(2,1)S(1)}, bf16[256,384]{1,0:T(8,128)(2,1)S(1)}, u32[]{:S(2)}, u32[]{:S(2)}) collective-permute-start(bf16[256,384]{1,0:T(8,128)(2,1)S(1)} %get-tuple-element.63.refs_1_), channel_id=1, source_target_pairs={{0,24},{1,25},{2,26},{3,27},{4,28},{5,29},{6,30},{7,31},{8,16},{9,... | collective-permute-start | bytes 589832 | tf_op jit(solution)/shard_map/ppermute | solution.py:46
  63.9 14.3 %collective-permute-start.13 = (bf16[512,384]{1,0:T(8,128)(2,1)S(1)}, bf16[512,384]{1,0:T(8,128)(2,1)S(1)}, u32[]{:S(2)}, u32[]{:S(2)}) collective-permute-start(bf16[512,384]{1,0:T(8,128)(2,1)S(1)} %get-tuple-element.75.refs_1_), channel_id=1, source_target_pairs={{0,8},{1,9},{2,10},{3,11},{4,12},{5,13},{6,14},{7,15},{8,0},{9,1},... | collective-permute-start | bytes 1179656 | tf_op jit(solution)/shard_map/ppermute | solution.py:46
  72.3 5.8 %collective-permute-start.10 = (bf16[272,384]{1,0:T(8,128)(2,1)S(1)}, bf16[272,384]{1,0:T(8,128)(2,1)S(1)}, u32[]{:S(2)}, u32[]{:S(2)}) collective-permute-start(bf16[272,384]{1,0:T(8,128)(2,1)S(1)} %get-tuple-element.71.refs_1_), channel_id=1, source_target_pairs={{0,2},{1,5},{2,0},{3,7},{4,6},{5,1},{6,4},{7,3},{8,10},{9,13},{10,... | collective-permute-start | bytes 626696 | tf_op jit(solution)/shard_map/ppermute | solution.py:46
  79.1 0.6 copy-start.6
  79.7 3.9 %collective-permute-start.14 = (bf16[1024,384]{1,0:T(8,128)(2,1)}, bf16[1024,384]{1,0:T(8,128)(2,1)}, u32[]{:S(2)}, u32[]{:S(2)}) collective-permute-start(bf16[1024,384]{1,0:T(8,128)(2,1)} %get-tuple-element.77.refs_2_), channel_id=1, source_target_pairs={{0,1},{1,0},{2,3},{3,2},{4,5},{5,4},{6,7},{7,6},{8,9},{9,8},{10,11... | collective-permute-start | bytes 2359304 | tf_op jit(solution)/shard_map/ppermute | solution.py:46
  79.7 14.7 %collective-permute-start.16 = (bf16[1024,384]{1,0:T(8,128)(2,1)}, bf16[1024,384]{1,0:T(8,128)(2,1)}, u32[]{:S(2)}, u32[]{:S(2)}) collective-permute-start(bf16[1024,384]{1,0:T(8,128)(2,1)} %get-tuple-element.77.refs_2_), channel_id=1, source_target_pairs={{0,2},{1,5},{2,0},{3,7},{4,6},{5,1},{6,4},{7,3},{8,10},{9,13},{10,... | collective-permute-start | bytes 2359304 | tf_op jit(solution)/shard_map/ppermute | solution.py:46
  80.4 12.2 %collective-permute-start.12 = (bf16[528,384]{1,0:T(8,128)(2,1)S(1)}, bf16[528,384]{1,0:T(8,128)(2,1)S(1)}, u32[]{:S(2)}, u32[]{:S(2)}) collective-permute-start(bf16[528,384]{1,0:T(8,128)(2,1)S(1)} %get-tuple-element.74.refs_1_), channel_id=1, source_target_pairs={{0,8},{1,9},{2,10},{3,11},{4,12},{5,13},{6,14},{7,15},{8,0},{9,1},... | collective-permute-start | bytes 1216520 | tf_op jit(solution)/shard_map/ppermute | solution.py:46
  83.6 20.3 %copy-start.3 = (s32[1,1280]{1,0:T(1,128)}, s32[1,1280]{1,0:T(1,128)S(1)}, u32[]{:S(2)}) copy-start(s32[1,1280]{1,0:T(1,128)S(1)} %compare_select_fusion.6.refs_1_.gid_ref) | copy-start | bytes 15364
  83.6 0.7 copy-start.7
  93.6 12.4 %collective-permute-start.15 = (bf16[1040,384]{1,0:T(8,128)(2,1)}, bf16[1040,384]{1,0:T(8,128)(2,1)}, u32[]{:S(2)}, u32[]{:S(2)}) collective-permute-start(bf16[1040,384]{1,0:T(8,128)(2,1)} %get-tuple-element.80.rest_2_), channel_id=1, source_target_pairs={{0,4},{1,3},{2,6},{3,1},{4,0},{5,7},{6,2},{7,5},{8,12},{9,11},{10,... | collective-permute-start | bytes 2396168 | tf_op jit(solution)/shard_map/ppermute | solution.py:46
  94.4 2.5 %collective-permute-start.17 = (bf16[1024,384]{1,0:T(8,128)(2,1)}, bf16[1024,384]{1,0:T(8,128)(2,1)S(1)}, u32[]{:S(2)}, u32[]{:S(2)}) collective-permute-start(bf16[1024,384]{1,0:T(8,128)(2,1)} %collective-permute-done.16.refs_2_), channel_id=1, source_target_pairs={{0,1},{1,0},{2,3},{3,2},{4,5},{5,4},{6,7},{7,6},{8,9},{9,8},{10,11... | collective-permute-start | bytes 2359304 | tf_op jit(solution)/shard_map/ppermute | solution.py:46
  94.7 11.4 %collective-permute-start.19 = (bf16[1040,384]{1,0:T(8,128)(2,1)}, bf16[1040,384]{1,0:T(8,128)(2,1)}, u32[]{:S(2)}, u32[]{:S(2)}) collective-permute-start(bf16[1040,384]{1,0:T(8,128)(2,1)} %get-tuple-element.80.rest_2_), channel_id=1, source_target_pairs={{0,1},{1,0},{2,3},{3,2},{4,5},{5,4},{6,7},{7,6},{8,9},{9,8},{10,11... | collective-permute-start | bytes 2396168 | tf_op jit(solution)/shard_map/ppermute | solution.py:46
  106.0 2.6 %collective-permute-start.18 = (bf16[1040,384]{1,0:T(8,128)(2,1)}, bf16[1040,384]{1,0:T(8,128)(2,1)}, u32[]{:S(2)}, u32[]{:S(2)}) collective-permute-start(bf16[1040,384]{1,0:T(8,128)(2,1)} %behind.1.rest_0_), channel_id=1, source_target_pairs={{0,1},{1,0},{2,3},{3,2},{4,5},{5,4},{6,7},{7,6},{8,9},{9,8},{10,11... | collective-permute-start | bytes 2396168 | tf_op jit(solution)/shard_map/ppermute | solution.py:46
  108.6 0.7 copy-start.4

commit v11 on v9

--- a/solution.py
+++ b/solution.py
@@ -596,9 +596,9 @@
                 )
             else:
                 arrived[stream] = got
-            if (stage, stream) == (1, 0):
-                total, tokens[0] = part_scores(
-                    tokens[0], samples, gid, part_codes(1), [held[0], sibling(held[0])], None, groups, keys, share, 0
+            if (stage, stream) == (1, 1):
+                total, tokens[1] = part_scores(
+                    tokens[1], samples, gid, part_codes(1), [held[0], sibling(held[0])], None, groups, keys, share, 0
                 )
         count *= 2
 
@@ -615,7 +615,7 @@
     total, token = part_scores(
         tokens[1], samples, gid, part_codes(0), [arrived[0], sibling(arrived[0])], total, groups, keys, share, 0
     )
-    last = behind(arrived[1], token)
+    last = behind(arrived[1], tokens[1])
     every = jnp.arange(members, dtype=jnp.int32)
     flip_of = (every ^ me) & 1
     spot = jnp.where(

time: 121 us -> 143 us (1.18)
  waiting for transfers between devices: 26.1 us -> 47.6 us
  starting transfers between devices: 30.2 us -> 33.1 us
  local copies, waits for them, and re-layouts: 6.59 us -> 5.04 us
    ppermute x21, waiting for transfers between devices: 26.1 us -> 47.6 us  [exchange(): return lax.ppermute(array, AXES, pairs)]
    ppermute x21, starting transfers between devices: 30.2 us -> 33.1 us  [exchange(): return lax.ppermute(array, AXES, pairs)]
    unnamed x19 -> x9, local copies, waits for them, and re-layouts: 3.32 us -> 1.78 us
  transfers between devices with their start and end apart: 21 -> 21, of which waited for: 12 -> 12; matrix products, arithmetic and copies ran while one was open for 4% -> 3% of each run, Pallas kernels for 33% -> 27%
where the time goes in v11:
time: 143 us; the launch traced here: 142 us
  Pallas kernels  52 us (36%)
  waiting for transfers between devices  47.6 us (33%)
  starting transfers between devices  33.1 us (23%)
  local copies, waits for them, and re-layouts  5.04 us (4%)
  other arithmetic  1.93 us (1%)
  between operations  1.81 us (1%)
    ppermute x21, waiting for transfers between devices, exchange(): return lax.ppermute(array, AXES, pairs)  47.6 us
    ppermute x21, starting transfers between devices, exchange(): return lax.ppermute(array, AXES, pairs)  33.1 us
    pallas_call x4, Pallas kernels, key_sums(): pl.pallas_call(hand_on(functools.partial(sums_kernel, base), 3 + len(extr...  17.9 us
    pallas_call x2, Pallas kernels, part_scores(): pl.pallas_call(kernel, grid_spec=pltpu.PrefetchScalarGridSpec(num_scalar_...  14.5 us
    pallas_call x1, Pallas kernels, final_scores(): pl.pallas_call(functools.partial(final_kernel, groups, share, start_at),...  11.1 us
    pallas_call x12, Pallas kernels, small_call(): pl.pallas_call(hand_on(kernel, len(args)), out_shape=[*outs, token_shape(...  8.55 us
    slice x1, local copies, waits for them, and re-layouts, per_device(): samples[:, start:start + wide]  2.99 us
  transfers between devices with their start and end apart: 21, of which 12 were waited for; matrix products, arithmetic and copies ran while one was open for 3% of the time, Pallas kernels for 27%

profile of v11, /device:TPU:0, one launch (start us, length us, event | category | flops | bytes accessed | tf_op | source)
XLA Modules:
  0.0 142.1 jit_solution(15658786908682176092)
XLA Ops:
  1.4 0.9 multiply_reduce_fusion
  2.3 0.7 add_select_fusion.9
  3.0 0.5 collective-permute-start
  3.5 3.0 %fusion.22 = (bf16[1280,384]{1,0:T(8,128)(2,1)}, bf16[1280,384]{1,0:T(8,128)(2,1)}) fusion(bf16[1280,768]{1,0:T(8,128)(2,1)} %x_ref.1), kind=kLoop, calls=%fused_computation.77 | loop fusion | bytes 3932160 | tf_op jit(solution)/shard_map/slice | solution.py:455
  6.5 0.5 collective-permute-start.1
  7.3 0.6 fusion.15
  7.9 1.5 %collective-permute-done.2.refs_2_ = bf16[1280,384]{1,0:T(8,128)(2,1)} collective-permute-done((bf16[1280,384]{1,0:T(8,128)(2,1)}, bf16[1280,384]{1,0:T(8,128)(2,1)}, u32[]{:S(2)}, u32[]{:S(2)}) %collective-permute-start.2) | collective-permute-done | bytes 983072 | tf_op jit(solution)/shard_map/ppermute | solution.py:46
  9.4 4.4 %key_sums.4 = (bf16[1040,384]{1,0:T(8,128)(2,1)S(1)}, f32[8,128]{1,0:T(8,128)S(1)}) custom-call(s32[1,2560]{1,0:T(1,128)S(1)} %get-tuple-element.84.refs_0_, bf16[1280,384]{1,0:T(8,128)(2,1)} %get-tuple-element.91.refs_1_, bf16[1280,384]{1,0:T(8,128)(2,1)} %collective-permute-done.2.refs_2_, bf16[16,384]{1,0:T(8,128)(2,1)S(1)} %pad_maximum_fusion.refs_3_, ...), custom_call_target="tpu_custom_call" | custom-call | flops 2013265920 | bytes 2752512 | tf_op jit(solution)/shard_map/key_sums/pallas_call | solution.py:110
  13.7 2.7 %collective-permute-start.4 = (bf16[1040,384]{1,0:T(8,128)(2,1)S(1)}, bf16[1040,384]{1,0:T(8,128)(2,1)S(1)}, u32[]{:S(2)}, u32[]{:S(2)}) collective-permute-start(bf16[1040,384]{1,0:T(8,128)(2,1)S(1)} %get-tuple-element.48), channel_id=1, source_target_pairs={{0,2},{1,5},{2,0},{3,7},{4,6},{5,1},{6,4},{7,3},{8,10},{9,13},{10,... | collective-permute-start | bytes 2396168 | tf_op jit(solution)/shard_map/ppermute | solution.py:46
  16.5 4.4 %key_sums.5 = (bf16[1024,384]{1,0:T(8,128)(2,1)S(1)}, f32[8,128]{1,0:T(8,128)S(1)}) custom-call(s32[1,2560]{1,0:T(1,128)S(1)} %fusion.10.refs_0_, bf16[1280,384]{1,0:T(8,128)(2,1)} %get-tuple-element.92.refs_1_, bf16[1280,384]{1,0:T(8,128)(2,1)} %collective-permute-done.1.refs_2_, f32[8,128]{1,0:T(8,128)S(1)} %get-tuple-element.43.refs_3_), custom_call_target="tpu_custom_call" | custom-call | flops 2013265920 | bytes 2752512 | tf_op jit(solution)/shard_map/key_sums/pallas_call | solution.py:110
  20.8 1.6 %collective-permute-start.3 = (bf16[1024,384]{1,0:T(8,128)(2,1)S(1)}, bf16[1024,384]{1,0:T(8,128)(2,1)S(1)}, u32[]{:S(2)}, u32[]{:S(2)}) collective-permute-start(bf16[1024,384]{1,0:T(8,128)(2,1)S(1)} %get-tuple-element.44), channel_id=1, source_target_pairs={{0,4},{1,3},{2,6},{3,1},{4,0},{5,7},{6,2},{7,5},{8,12},{9,11},{10,... | collective-permute-start | bytes 2359304 | tf_op jit(solution)/shard_map/ppermute | solution.py:46
  22.4 4.4 %key_sums.6 = (bf16[1040,384]{1,0:T(8,128)(2,1)S(1)}, f32[8,128]{1,0:T(8,128)S(1)}) custom-call(s32[1,2560]{1,0:T(1,128)S(1)} %get-tuple-element.84.refs_0_, bf16[1280,384]{1,0:T(8,128)(2,1)} %get-tuple-element.91.refs_1_, bf16[1280,384]{1,0:T(8,128)(2,1)} %collective-permute-done.2.refs_2_, bf16[16,384]{1,0:T(8,128)(2,1)S(1)} %pad_maximum_fusion.refs_3_, ...), custom_call_target="tpu_custom_call" | custom-call | flops 2013265920 | bytes 2752512 | tf_op jit(solution)/shard_map/key_sums/pallas_call | solution.py:110
  26.8 2.6 %collective-permute-done.4.refs_0_ = bf16[1040,384]{1,0:T(8,128)(2,1)S(1)} collective-permute-done((bf16[1040,384]{1,0:T(8,128)(2,1)S(1)}, bf16[1040,384]{1,0:T(8,128)(2,1)S(1)}, u32[]{:S(2)}, u32[]{:S(2)}) %collective-permute-start.4) | collective-permute-done | bytes 798752 | tf_op jit(solution)/shard_map/ppermute | solution.py:46
  29.4 0.8 fold.4
  30.3 2.6 %collective-permute-start.6 = (bf16[528,384]{1,0:T(8,128)(2,1)}, bf16[528,384]{1,0:T(8,128)(2,1)}, u32[]{:S(2)}, u32[]{:S(2)}) collective-permute-start(bf16[528,384]{1,0:T(8,128)(2,1)} %get-tuple-element.53), channel_id=1, source_target_pairs={{0,8},{1,9},{2,10},{3,11},{4,12},{5,13},{6,14},{7,15},{8,0},{9,1},... | collective-permute-start | bytes 1216520 | tf_op jit(solution)/shard_map/ppermute | solution.py:46
  32.8 4.9 %key_sums.7 = (bf16[1024,384]{1,0:T(8,128)(2,1)S(1)}, f32[8,128]{1,0:T(8,128)}) custom-call(s32[1,2560]{1,0:T(1,128)S(1)} %fusion.10.refs_0_, bf16[1280,384]{1,0:T(8,128)(2,1)} %get-tuple-element.92.refs_1_, bf16[1280,384]{1,0:T(8,128)(2,1)} %collective-permute-done.1.refs_2_, f32[8,128]{1,0:T(8,128)S(1)} %get-tuple-element.46.refs_3_), custom_call_target="tpu_custom_call" | custom-call | flops 2013265920 | bytes 2752512 | tf_op jit(solution)/shard_map/key_sums/pallas_call | solution.py:110
  37.7 0.8 fold.5
  38.6 0.8 copy-done.1
  39.4 2.1 %collective-permute-done.6.refs_0_ = bf16[528,384]{1,0:T(8,128)(2,1)} collective-permute-done((bf16[528,384]{1,0:T(8,128)(2,1)}, bf16[528,384]{1,0:T(8,128)(2,1)}, u32[]{:S(2)}, u32[]{:S(2)}) %collective-permute-start.6) | collective-permute-done | bytes 405536 | tf_op jit(solution)/shard_map/ppermute | solution.py:46
  41.4 1.1 fold.6
  42.5 1.9 %collective-permute-start.8 = (bf16[272,384]{1,0:T(8,128)(2,1)S(1)}, bf16[272,384]{1,0:T(8,128)(2,1)S(1)}, u32[]{:S(2)}, u32[]{:S(2)}) collective-permute-start(bf16[272,384]{1,0:T(8,128)(2,1)S(1)} %get-tuple-element.59), channel_id=1, source_target_pairs={{0,4},{1,3},{2,6},{3,1},{4,0},{5,7},{6,2},{7,5},{8,12},{9,11},{10,... | collective-permute-start | bytes 626696 | tf_op jit(solution)/shard_map/ppermute | solution.py:46
  44.5 4.7 %collective-permute-done.5.refs_0_ = bf16[512,384]{1,0:T(8,128)(2,1)} collective-permute-done((bf16[512,384]{1,0:T(8,128)(2,1)}, bf16[512,384]{1,0:T(8,128)(2,1)}, u32[]{:S(2)}, u32[]{:S(2)}) %collective-permute-start.5) | collective-permute-done | bytes 393248 | tf_op jit(solution)/shard_map/ppermute | solution.py:46
  49.2 1.0 copy-done.2
  50.2 1.6 %fold.7 = (bf16[256,384]{1,0:T(8,128)(2,1)S(1)}, bf16[256,384]{1,0:T(8,128)(2,1)S(1)}, f32[8,128]{1,0:T(8,128)}) custom-call(bf16[512,384]{1,0:T(8,128)(2,1)} %collective-permute-done.5.refs_0_, bf16[512,384]{1,0:T(8,128)(2,1)S(1)} %copy-done.2, f32[8,128]{1,0:T(8,128)S(1)} %get-tuple-element.56.refs_2_.refs_3_), custom_call_target="tpu_custom_call" | custom-call | flops 589824 | bytes 1179648 | tf_op jit(solution)/shard_map/fold/pallas_call | solution.py:133
  51.8 3.1 %collective-permute-start.7 = (bf16[256,384]{1,0:T(8,128)(2,1)S(1)}, bf16[256,384]{1,0:T(8,128)(2,1)S(1)}, u32[]{:S(2)}, u32[]{:S(2)}) collective-permute-start(bf16[256,384]{1,0:T(8,128)(2,1)S(1)} %get-tuple-element.57), channel_id=1, source_target_pairs={{0,2},{1,5},{2,0},{3,7},{4,6},{5,1},{6,4},{7,3},{8,10},{9,13},{10,... | collective-permute-start | bytes 589832 | tf_op jit(solution)/shard_map/ppermute | solution.py:46
  55.0 3.2 %collective-permute-start.10 = (bf16[272,384]{1,0:T(8,128)(2,1)S(1)}, bf16[272,384]{1,0:T(8,128)(2,1)S(1)}, u32[]{:S(2)}, u32[]{:S(2)}) collective-permute-start(bf16[272,384]{1,0:T(8,128)(2,1)S(1)} %get-tuple-element.64.refs_1_), channel_id=1, source_target_pairs={{0,24},{1,25},{2,26},{3,27},{4,28},{5,29},{6,30},{7,31},{8,16},{9,... | collective-permute-start | bytes 626696 | tf_op jit(solution)/shard_map/ppermute | solution.py:46
  58.2 0.4 collective-permute-done.7.refs_0_
  58.5 0.6 seed.3
  59.2 3.1 %collective-permute-start.9 = (bf16[256,384]{1,0:T(8,128)(2,1)S(1)}, bf16[256,384]{1,0:T(8,128)(2,1)S(1)}, u32[]{:S(2)}, u32[]{:S(2)}) collective-permute-start(bf16[256,384]{1,0:T(8,128)(2,1)S(1)} %get-tuple-element.62.refs_1_), channel_id=1, source_target_pairs={{0,24},{1,25},{2,26},{3,27},{4,28},{5,29},{6,30},{7,31},{8,16},{9,... | collective-permute-start | bytes 589832 | tf_op jit(solution)/shard_map/ppermute | solution.py:46
  62.3 2.6 %collective-permute-done.10.refs_0_ = bf16[272,384]{1,0:T(8,128)(2,1)S(1)} collective-permute-done((bf16[272,384]{1,0:T(8,128)(2,1)S(1)}, bf16[272,384]{1,0:T(8,128)(2,1)S(1)}, u32[]{:S(2)}, u32[]{:S(2)}) %collective-permute-start.10) | collective-permute-done | bytes 208928 | tf_op jit(solution)/shard_map/ppermute | solution.py:46
  65.2 1.8 %collective-permute-done.9.refs_0_ = bf16[256,384]{1,0:T(8,128)(2,1)S(1)} collective-permute-done((bf16[256,384]{1,0:T(8,128)(2,1)S(1)}, bf16[256,384]{1,0:T(8,128)(2,1)S(1)}, u32[]{:S(2)}, u32[]{:S(2)}) %collective-permute-start.9) | collective-permute-done | bytes 196640 | tf_op jit(solution)/shard_map/ppermute | solution.py:46
  67.0 1.2 last_centroids.1
  68.2 1.8 %collective-permute-start.11 = (bf16[272,384]{1,0:T(8,128)(2,1)S(1)}, bf16[272,384]{1,0:T(8,128)(2,1)S(1)}, u32[]{:S(2)}, u32[]{:S(2)}) collective-permute-start(bf16[272,384]{1,0:T(8,128)(2,1)S(1)} %get-tuple-element.70.refs_1_), channel_id=1, source_target_pairs={{0,2},{1,5},{2,0},{3,7},{4,6},{5,1},{6,4},{7,3},{8,10},{9,13},{10,... | collective-permute-start | bytes 626696 | tf_op jit(solution)/shard_map/ppermute | solution.py:46
  69.9 1.0 collective-permute-start.12
  70.9 4.7 %collective-permute-done.12.refs_0_ = bf16[256,384]{1,0:T(8,128)(2,1)S(1)} collective-permute-done((bf16[256,384]{1,0:T(8,128)(2,1)S(1)}, bf16[256,384]{1,0:T(8,128)(2,1)S(1)}, u32[]{:S(2)}, u32[]{:S(2)}) %collective-permute-start.12) | collective-permute-done | bytes 196640 | tf_op jit(solution)/shard_map/ppermute | solution.py:46
  75.7 6.8 %collective-permute-start.13 = (bf16[528,384]{1,0:T(8,128)(2,1)S(1)}, bf16[528,384]{1,0:T(8,128)(2,1)S(1)}, u32[]{:S(2)}, u32[]{:S(2)}) collective-permute-start(bf16[528,384]{1,0:T(8,128)(2,1)S(1)} %get-tuple-element.73.refs_1_), channel_id=1, source_target_pairs={{0,8},{1,9},{2,10},{3,11},{4,12},{5,13},{6,14},{7,15},{8,0},{9,1},... | collective-permute-start | bytes 1216520 | tf_op jit(solution)/shard_map/ppermute | solution.py:46
  82.6 15.2 %collective-permute-done.14.refs_0_ = bf16[512,384]{1,0:T(8,128)(2,1)S(1)} collective-permute-done((bf16[512,384]{1,0:T(8,128)(2,1)S(1)}, bf16[512,384]{1,0:T(8,128)(2,1)S(1)}, u32[]{:S(2)}, u32[]{:S(2)}) %collective-permute-start.14) | collective-permute-done | bytes 393248 | tf_op jit(solution)/shard_map/ppermute | solution.py:46
  97.8 0.9 join.6
  98.7 1.0 join.7
  99.7 1.9 %collective-permute-start.15 = (bf16[1040,384]{1,0:T(8,128)(2,1)}, bf16[1040,384]{1,0:T(8,128)(2,1)}, u32[]{:S(2)}, u32[]{:S(2)}) collective-permute-start(bf16[1040,384]{1,0:T(8,128)(2,1)} %get-tuple-element.77.rest_2_), channel_id=1, source_target_pairs={{0,4},{1,3},{2,6},{3,1},{4,0},{5,7},{6,2},{7,5},{8,12},{9,11},{10,... | collective-permute-start | bytes 2396168 | tf_op jit(solution)/shard_map/ppermute | solution.py:46
  101.6 1.8 %collective-permute-start.19 = (bf16[1024,384]{1,0:T(8,128)(2,1)}, bf16[1024,384]{1,0:T(8,128)(2,1)}, u32[]{:S(2)}, u32[]{:S(2)}) collective-permute-start(bf16[1024,384]{1,0:T(8,128)(2,1)} %get-tuple-element.78.refs_2_), channel_id=1, source_target_pairs={{0,2},{1,5},{2,0},{3,7},{4,6},{5,1},{6,4},{7,3},{8,10},{9,13},{10,... | collective-permute-start | bytes 2359304 | tf_op jit(solution)/shard_map/ppermute | solution.py:46
  103.6 0.6 collective-permute-done.16.refs_3_
  104.2 7.2 %part_scores.2 = (bf16[1280,1024]{1,0:T(8,128)(2,1)}, f32[8,128]{1,0:T(8,128)S(1)}) custom-call(s32[16]{0:T(128)S(1)} %stack.212.code_ref, bf16[1280,768]{1,0:T(8,128)(2,1)} %x_ref.1, s32[1,1280]{1,0:T(1,128)S(1)} %compare_select_fusion.6.refs_1_.gid_ref, bf16[1024,384]{1,0:T(8,128)(2,1)} %get-tuple-element.78.refs_2_, ...), custom_call_target="tpu_custom_call" | custom-call | flops 1 | bytes 1 | tf_op jit(solution)/shard_map/part_scores/pallas_call | solution.py:328
  111.4 8.4 %collective-permute-done.15.in_ref = bf16[1040,384]{1,0:T(8,128)(2,1)} collective-permute-done((bf16[1040,384]{1,0:T(8,128)(2,1)}, bf16[1040,384]{1,0:T(8,128)(2,1)}, u32[]{:S(2)}, u32[]{:S(2)}) %collective-permute-start.15) | collective-permute-done | bytes 798752 | tf_op jit(solution)/shard_map/ppermute | solution.py:46
  119.8 0.6 collective-permute-start.20
  120.5 3.0 %collective-permute-done.20.refs_3_ = bf16[1024,384]{1,0:T(8,128)(2,1)} collective-permute-done((bf16[1024,384]{1,0:T(8,128)(2,1)}, bf16[1024,384]{1,0:T(8,128)(2,1)}, u32[]{:S(2)}, u32[]{:S(2)}) %collective-permute-start.20) | collective-permute-done | bytes 786464 | tf_op jit(solution)/shard_map/ppermute | solution.py:46
  123.6 7.3 %part_scores.3 = (bf16[1280,1024]{1,0:T(8,128)(2,1)}, f32[8,128]{1,0:T(8,128)}) custom-call(s32[16]{0:T(128)S(1)} %stack.212.code_ref, bf16[1280,768]{1,0:T(8,128)(2,1)} %x_ref.1, s32[1,1280]{1,0:T(1,128)S(1)} %compare_select_fusion.6.refs_1_.gid_ref, bf16[1024,384]{1,0:T(8,128)(2,1)} %collective-permute-done.19.refs_2_, ...), custom_call_target="tpu_custom_call", output_to_operand_aliasing={{0}: (5, {})} | custom-call | flops 1 | bytes 1 | tf_op jit(solution)/shard_map/part_scores/pallas_call | solution.py:328
  130.9 11.1 %final_scores.1 = bf16[1280,1024]{1,0:T(8,128)(2,1)} custom-call(s32[32]{0:T(128)S(1)} %concatenate.104.code_ref, s32[8]{0:T(128)S(1)} %fusion.21.slot_ref, bf16[1280,768]{1,0:T(8,128)(2,1)} %x_ref.1, s32[1,1280]{1,0:T(1,128)S(1)} %compare_select_fusion.6.refs_1_.gid_ref, f32[16,1024]{1,0:T(8,128)S(1)} %broadcast_in_dim.28.half_ref, ...), custom_call_target="tpu_custom_call" | custom-call | flops 1 | bytes 1 | tf_op jit(solution)/shard_map/final_scores/pallas_call | solution.py:405
  (41 shorter events, 1.3 us)
Async XLA Ops:
  0.6 38.7 %copy-start = (f32[1,1024,768]{2,1,0:T(8,128)S(1)}, f32[1,1024,768]{2,1,0:T(8,128)}, u32[]{:S(2)}) copy-start(f32[1,1024,768]{2,1,0:T(8,128)} %param.9) | copy-start | bytes 9437188
  3.0 4.0 %collective-permute-start = (s32[1280]{0:T(1024)S(1)}, s32[1280]{0:T(1024)S(1)}, u32[]{:S(2)}, u32[]{:S(2)}) collective-permute-start(s32[1280]{0:T(1024)S(1)} %add_select_fusion.9), channel_id=1, source_target_pairs={{0,1},{1,0},{2,3},{3,2},{4,5},{5,4},{6,7},{7,6},{8,9},{9,8},{10,11... | collective-permute-start | bytes 15368 | tf_op jit(solution)/shard_map/ppermute | solution.py:46
  6.5 2.9 %collective-permute-start.2 = (bf16[1280,384]{1,0:T(8,128)(2,1)}, bf16[1280,384]{1,0:T(8,128)(2,1)}, u32[]{:S(2)}, u32[]{:S(2)}) collective-permute-start(bf16[1280,384]{1,0:T(8,128)(2,1)} %get-tuple-element.91.refs_1_), channel_id=1, source_target_pairs={{0,1},{1,0},{2,3},{3,2},{4,5},{5,4},{6,7},{7,6},{8,9},{9,8},{10,11... | collective-permute-start | bytes 2949128 | tf_op jit(solution)/shard_map/ppermute | solution.py:46
  6.5 10.0 %collective-permute-start.1 = (bf16[1280,384]{1,0:T(8,128)(2,1)}, bf16[1280,384]{1,0:T(8,128)(2,1)}, u32[]{:S(2)}, u32[]{:S(2)}) collective-permute-start(bf16[1280,384]{1,0:T(8,128)(2,1)} %get-tuple-element.92.refs_1_), channel_id=1, source_target_pairs={{0,1},{1,0},{2,3},{3,2},{4,5},{5,4},{6,7},{7,6},{8,9},{9,8},{10,11... | collective-permute-start | bytes 2949128 | tf_op jit(solution)/shard_map/ppermute | solution.py:46
  13.7 15.7 %collective-permute-start.4 = (bf16[1040,384]{1,0:T(8,128)(2,1)S(1)}, bf16[1040,384]{1,0:T(8,128)(2,1)S(1)}, u32[]{:S(2)}, u32[]{:S(2)}) collective-permute-start(bf16[1040,384]{1,0:T(8,128)(2,1)S(1)} %get-tuple-element.48), channel_id=1, source_target_pairs={{0,2},{1,5},{2,0},{3,7},{4,6},{5,1},{6,4},{7,3},{8,10},{9,13},{10,... | collective-permute-start | bytes 2396168 | tf_op jit(solution)/shard_map/ppermute | solution.py:46
  20.8 16.9 %collective-permute-start.3 = (bf16[1024,384]{1,0:T(8,128)(2,1)S(1)}, bf16[1024,384]{1,0:T(8,128)(2,1)S(1)}, u32[]{:S(2)}, u32[]{:S(2)}) collective-permute-start(bf16[1024,384]{1,0:T(8,128)(2,1)S(1)} %get-tuple-element.44), channel_id=1, source_target_pairs={{0,4},{1,3},{2,6},{3,1},{4,0},{5,7},{6,2},{7,5},{8,12},{9,11},{10,... | collective-permute-start | bytes 2359304 | tf_op jit(solution)/shard_map/ppermute | solution.py:46
  30.3 11.1 %collective-permute-start.6 = (bf16[528,384]{1,0:T(8,128)(2,1)}, bf16[528,384]{1,0:T(8,128)(2,1)}, u32[]{:S(2)}, u32[]{:S(2)}) collective-permute-start(bf16[528,384]{1,0:T(8,128)(2,1)} %get-tuple-element.53), channel_id=1, source_target_pairs={{0,8},{1,9},{2,10},{3,11},{4,12},{5,13},{6,14},{7,15},{8,0},{9,1},... | collective-permute-start | bytes 1216520 | tf_op jit(solution)/shard_map/ppermute | solution.py:46
  38.6 0.8 copy-start.1
  39.3 9.9 %collective-permute-start.5 = (bf16[512,384]{1,0:T(8,128)(2,1)}, bf16[512,384]{1,0:T(8,128)(2,1)}, u32[]{:S(2)}, u32[]{:S(2)}) collective-permute-start(bf16[512,384]{1,0:T(8,128)(2,1)} %get-tuple-element.51), channel_id=1, source_target_pairs={{0,8},{1,9},{2,10},{3,11},{4,12},{5,13},{6,14},{7,15},{8,0},{9,1},... | collective-permute-start | bytes 1179656 | tf_op jit(solution)/shard_map/ppermute | solution.py:46
  42.5 12.4 %collective-permute-start.8 = (bf16[272,384]{1,0:T(8,128)(2,1)S(1)}, bf16[272,384]{1,0:T(8,128)(2,1)S(1)}, u32[]{:S(2)}, u32[]{:S(2)}) collective-permute-start(bf16[272,384]{1,0:T(8,128)(2,1)S(1)} %get-tuple-element.59), channel_id=1, source_target_pairs={{0,4},{1,3},{2,6},{3,1},{4,0},{5,7},{6,2},{7,5},{8,12},{9,11},{10,... | collective-permute-start | bytes 626696 | tf_op jit(solution)/shard_map/ppermute | solution.py:46
  49.2 1.0 copy-start.2
  51.8 6.8 %collective-permute-start.7 = (bf16[256,384]{1,0:T(8,128)(2,1)S(1)}, bf16[256,384]{1,0:T(8,128)(2,1)S(1)}, u32[]{:S(2)}, u32[]{:S(2)}) collective-permute-start(bf16[256,384]{1,0:T(8,128)(2,1)S(1)} %get-tuple-element.57), channel_id=1, source_target_pairs={{0,2},{1,5},{2,0},{3,7},{4,6},{5,1},{6,4},{7,3},{8,10},{9,13},{10,... | collective-permute-start | bytes 589832 | tf_op jit(solution)/shard_map/ppermute | solution.py:46
  54.9 48.5 %copy-start.3 = (s32[1280,1]{0,1:T(1,128)S(1)}, s32[1280,1]{0,1:T(1,128)}, u32[]{:S(2)}) copy-start(s32[1280,1]{0,1:T(1,128)} %param.6) | copy-start | bytes 15364
  55.0 9.9 %collective-permute-start.10 = (bf16[272,384]{1,0:T(8,128)(2,1)S(1)}, bf16[272,384]{1,0:T(8,128)(2,1)S(1)}, u32[]{:S(2)}, u32[]{:S(2)}) collective-permute-start(bf16[272,384]{1,0:T(8,128)(2,1)S(1)} %get-tuple-element.64.refs_1_), channel_id=1, source_target_pairs={{0,24},{1,25},{2,26},{3,27},{4,28},{5,29},{6,30},{7,31},{8,16},{9,... | collective-permute-start | bytes 626696 | tf_op jit(solution)/shard_map/ppermute | solution.py:46
  59.2 7.8 %collective-permute-start.9 = (bf16[256,384]{1,0:T(8,128)(2,1)S(1)}, bf16[256,384]{1,0:T(8,128)(2,1)S(1)}, u32[]{:S(2)}, u32[]{:S(2)}) collective-permute-start(bf16[256,384]{1,0:T(8,128)(2,1)S(1)} %get-tuple-element.62.refs_1_), channel_id=1, source_target_pairs={{0,24},{1,25},{2,26},{3,27},{4,28},{5,29},{6,30},{7,31},{8,16},{9,... | collective-permute-start | bytes 589832 | tf_op jit(solution)/shard_map/ppermute | solution.py:46
  68.2 7.5 %collective-permute-start.11 = (bf16[272,384]{1,0:T(8,128)(2,1)S(1)}, bf16[272,384]{1,0:T(8,128)(2,1)S(1)}, u32[]{:S(2)}, u32[]{:S(2)}) collective-permute-start(bf16[272,384]{1,0:T(8,128)(2,1)S(1)} %get-tuple-element.70.refs_1_), channel_id=1, source_target_pairs={{0,2},{1,5},{2,0},{3,7},{4,6},{5,1},{6,4},{7,3},{8,10},{9,13},{10,... | collective-permute-start | bytes 626696 | tf_op jit(solution)/shard_map/ppermute | solution.py:46
  69.9 5.7 %collective-permute-start.12 = (bf16[256,384]{1,0:T(8,128)(2,1)S(1)}, bf16[256,384]{1,0:T(8,128)(2,1)S(1)}, u32[]{:S(2)}, u32[]{:S(2)}) collective-permute-start(bf16[256,384]{1,0:T(8,128)(2,1)S(1)} %get-tuple-element.71.refs_1_), channel_id=1, source_target_pairs={{0,4},{1,3},{2,6},{3,1},{4,0},{5,7},{6,2},{7,5},{8,12},{9,11},{10,... | collective-permute-start | bytes 589832 | tf_op jit(solution)/shard_map/ppermute | solution.py:46
  75.7 23.0 %collective-permute-start.13 = (bf16[528,384]{1,0:T(8,128)(2,1)S(1)}, bf16[528,384]{1,0:T(8,128)(2,1)S(1)}, u32[]{:S(2)}, u32[]{:S(2)}) collective-permute-start(bf16[528,384]{1,0:T(8,128)(2,1)S(1)} %get-tuple-element.73.refs_1_), channel_id=1, source_target_pairs={{0,8},{1,9},{2,10},{3,11},{4,12},{5,13},{6,14},{7,15},{8,0},{9,1},... | collective-permute-start | bytes 1216520 | tf_op jit(solution)/shard_map/ppermute | solution.py:46
  82.5 15.3 %collective-permute-start.14 = (bf16[512,384]{1,0:T(8,128)(2,1)S(1)}, bf16[512,384]{1,0:T(8,128)(2,1)S(1)}, u32[]{:S(2)}, u32[]{:S(2)}) collective-permute-start(bf16[512,384]{1,0:T(8,128)(2,1)S(1)} %get-tuple-element.74.refs_1_), channel_id=1, source_target_pairs={{0,8},{1,9},{2,10},{3,11},{4,12},{5,13},{6,14},{7,15},{8,0},{9,1},... | collective-permute-start | bytes 1179656 | tf_op jit(solution)/shard_map/ppermute | solution.py:46
  99.7 20.1 %collective-permute-start.15 = (bf16[1040,384]{1,0:T(8,128)(2,1)}, bf16[1040,384]{1,0:T(8,128)(2,1)}, u32[]{:S(2)}, u32[]{:S(2)}) collective-permute-start(bf16[1040,384]{1,0:T(8,128)(2,1)} %get-tuple-element.77.rest_2_), channel_id=1, source_target_pairs={{0,4},{1,3},{2,6},{3,1},{4,0},{5,7},{6,2},{7,5},{8,12},{9,11},{10,... | collective-permute-start | bytes 2396168 | tf_op jit(solution)/shard_map/ppermute | solution.py:46
  101.6 2.6 %collective-permute-start.16 = (bf16[1024,384]{1,0:T(8,128)(2,1)}, bf16[1024,384]{1,0:T(8,128)(2,1)}, u32[]{:S(2)}, u32[]{:S(2)}) collective-permute-start(bf16[1024,384]{1,0:T(8,128)(2,1)} %get-tuple-element.78.refs_2_), channel_id=1, source_target_pairs={{0,1},{1,0},{2,3},{3,2},{4,5},{5,4},{6,7},{7,6},{8,9},{9,8},{10,11... | collective-permute-start | bytes 2359304 | tf_op jit(solution)/shard_map/ppermute | solution.py:46
  101.6 18.2 %collective-permute-start.19 = (bf16[1024,384]{1,0:T(8,128)(2,1)}, bf16[1024,384]{1,0:T(8,128)(2,1)}, u32[]{:S(2)}, u32[]{:S(2)}) collective-permute-start(bf16[1024,384]{1,0:T(8,128)(2,1)} %get-tuple-element.78.refs_2_), channel_id=1, source_target_pairs={{0,2},{1,5},{2,0},{3,7},{4,6},{5,1},{6,4},{7,3},{8,10},{9,13},{10,... | collective-permute-start | bytes 2359304 | tf_op jit(solution)/shard_map/ppermute | solution.py:46
  103.5 27.4 %collective-permute-start.18 = (bf16[1040,384]{1,0:T(8,128)(2,1)}, bf16[1040,384]{1,0:T(8,128)(2,1)}, u32[]{:S(2)}, u32[]{:S(2)}) collective-permute-start(bf16[1040,384]{1,0:T(8,128)(2,1)} %get-tuple-element.77.rest_2_), channel_id=1, source_target_pairs={{0,1},{1,0},{2,3},{3,2},{4,5},{5,4},{6,7},{7,6},{8,9},{9,8},{10,11... | collective-permute-start | bytes 2396168 | tf_op jit(solution)/shard_map/ppermute | solution.py:46
  119.8 11.1 %collective-permute-start.17 = (bf16[1040,384]{1,0:T(8,128)(2,1)}, bf16[1040,384]{1,0:T(8,128)(2,1)}, u32[]{:S(2)}, u32[]{:S(2)}) collective-permute-start(bf16[1040,384]{1,0:T(8,128)(2,1)} %behind.1.rest_0_), channel_id=1, source_target_pairs={{0,1},{1,0},{2,3},{3,2},{4,5},{5,4},{6,7},{7,6},{8,9},{9,8},{10,11... | collective-permute-start | bytes 2396168 | tf_op jit(solution)/shard_map/ppermute | solution.py:46
  119.8 3.8 %collective-permute-start.20 = (bf16[1024,384]{1,0:T(8,128)(2,1)}, bf16[1024,384]{1,0:T(8,128)(2,1)}, u32[]{:S(2)}, u32[]{:S(2)}) collective-permute-start(bf16[1024,384]{1,0:T(8,128)(2,1)} %collective-permute-done.19.refs_2_), channel_id=1, source_target_pairs={{0,1},{1,0},{2,3},{3,2},{4,5},{5,4},{6,7},{7,6},{8,9},{9,8},{10,11... | collective-permute-start | bytes 2359304 | tf_op jit(solution)/shard_map/ppermute | solution.py:46

commit v12 on v9

--- a/solution.py
+++ b/solution.py
@@ -31,9 +31,9 @@
     other = inner[cut:] + inner[:cut]
     found = {}
     found[0, 0] = inner[:cut] + outer[:1] + inner[cut:] + outer[1:]
-    found[1, 0] = other[:cut] + outer[:1] + other[cut:] + outer[1:]
-    found[0, 1] = found[1, 0]
-    found[1, 1] = found[0, 0]
+    found[1, 0] = other + outer
+    found[0, 1] = other[:cut] + outer[:1] + other[cut:] + outer[1:]
+    found[1, 1] = inner + outer
     return found
 
 

time: 121 us -> 124 us (1.025)
  the two profiles are of different devices: /device:TPU:0 before, /device:TPU:9 now
where the time goes in v12:
time: 124 us; the launch traced here: 123 us
  Pallas kernels  52.1 us (42%)
  waiting for transfers between devices  33.7 us (27%)
  starting transfers between devices  25.9 us (21%)
  local copies, waits for them, and re-layouts  6.64 us (5%)
  other arithmetic  2.68 us (2%)
  between operations  1.84 us (1%)
    ppermute x21, waiting for transfers between devices, exchange(): return lax.ppermute(array, AXES, pairs)  33.7 us
    ppermute x21, starting transfers between devices, exchange(): return lax.ppermute(array, AXES, pairs)  25.9 us
    pallas_call x4, Pallas kernels, key_sums(): pl.pallas_call(hand_on(functools.partial(sums_kernel, base), 3 + len(extr...  18.8 us
    pallas_call x2, Pallas kernels, part_scores(): pl.pallas_call(kernel, grid_spec=pltpu.PrefetchScalarGridSpec(num_scalar_...  14.3 us
    pallas_call x1, Pallas kernels, final_scores(): pl.pallas_call(functools.partial(final_kernel, groups, share, start_at),...  11.1 us
    pallas_call x12, Pallas kernels, small_call(): pl.pallas_call(hand_on(kernel, len(args)), out_shape=[*outs, token_shape(...  7.9 us
    unnamed x19, local copies, waits for them, and re-layouts  3.36 us
    slice x1, local copies, waits for them, and re-layouts, per_device(): samples[:, start:start + wide]  3.01 us
  transfers between devices with their start and end apart: 21, of which 9 were waited for; matrix products, arithmetic and copies ran while one was open for 4% of the time, Pallas kernels for 32%

profile of v12, /device:TPU:9, one launch (start us, length us, event | category | flops | bytes accessed | tf_op | source)
XLA Modules:
  0.0 123.5 jit_solution(2556392128254392867)
XLA Ops:
  1.4 0.9 multiply_reduce_fusion
  2.3 0.7 add_select_fusion.9
  3.0 0.7 collective-permute-start
  3.7 3.0 %fusion.23 = (bf16[1280,384]{1,0:T(8,128)(2,1)}, bf16[1280,384]{1,0:T(8,128)(2,1)}) fusion(bf16[1280,768]{1,0:T(8,128)(2,1)} %x_ref.1), kind=kLoop, calls=%fused_computation.75 | loop fusion | bytes 3932160 | tf_op jit(solution)/shard_map/slice | solution.py:455
  7.5 0.6 fusion.15
  8.1 1.5 %collective-permute-done.2.refs_2_ = bf16[1280,384]{1,0:T(8,128)(2,1)} collective-permute-done((bf16[1280,384]{1,0:T(8,128)(2,1)}, bf16[1280,384]{1,0:T(8,128)(2,1)}, u32[]{:S(2)}, u32[]{:S(2)}) %collective-permute-start.2) | collective-permute-done | bytes 983072 | tf_op jit(solution)/shard_map/ppermute | solution.py:46
  9.6 4.4 %key_sums.4 = (bf16[1040,384]{1,0:T(8,128)(2,1)S(1)}, f32[8,128]{1,0:T(8,128)S(1)}) custom-call(s32[1,2560]{1,0:T(1,128)S(1)} %get-tuple-element.86.refs_0_, bf16[1280,384]{1,0:T(8,128)(2,1)} %get-tuple-element.90.refs_1_, bf16[1280,384]{1,0:T(8,128)(2,1)} %collective-permute-done.2.refs_2_, bf16[16,384]{1,0:T(8,128)(2,1)S(1)} %pad_maximum_fusion.refs_3_, ...), custom_call_target="tpu_custom_call" | custom-call | flops 2013265920 | bytes 2752512 | tf_op jit(solution)/shard_map/key_sums/pallas_call | solution.py:110
  14.0 1.3 %collective-permute-start.4 = (bf16[1040,384]{1,0:T(8,128)(2,1)S(1)}, bf16[1040,384]{1,0:T(8,128)(2,1)S(1)}, u32[]{:S(2)}, u32[]{:S(2)}) collective-permute-start(bf16[1040,384]{1,0:T(8,128)(2,1)S(1)} %get-tuple-element.49), channel_id=1, source_target_pairs={{0,2},{1,5},{2,0},{3,7},{4,6},{5,1},{6,4},{7,3},{8,10},{9,13},{10,... | collective-permute-start | bytes 2396168 | tf_op jit(solution)/shard_map/ppermute | solution.py:46
  15.4 5.3 %key_sums.5 = (bf16[1024,384]{1,0:T(8,128)(2,1)}, f32[8,128]{1,0:T(8,128)S(1)}) custom-call(s32[1,2560]{1,0:T(1,128)S(1)} %fusion.10.refs_0_, bf16[1280,384]{1,0:T(8,128)(2,1)} %get-tuple-element.91.refs_1_, bf16[1280,384]{1,0:T(8,128)(2,1)} %collective-permute-done.1.refs_2_, f32[8,128]{1,0:T(8,128)S(1)} %get-tuple-element.44.refs_3_), custom_call_target="tpu_custom_call" | custom-call | flops 2013265920 | bytes 2752512 | tf_op jit(solution)/shard_map/key_sums/pallas_call | solution.py:110
  20.7 1.2 collective-permute-start.3
  21.9 4.4 %key_sums.6 = (bf16[1040,384]{1,0:T(8,128)(2,1)S(1)}, f32[8,128]{1,0:T(8,128)S(1)}) custom-call(s32[1,2560]{1,0:T(1,128)S(1)} %get-tuple-element.86.refs_0_, bf16[1280,384]{1,0:T(8,128)(2,1)} %get-tuple-element.90.refs_1_, bf16[1280,384]{1,0:T(8,128)(2,1)} %collective-permute-done.2.refs_2_, bf16[16,384]{1,0:T(8,128)(2,1)S(1)} %pad_maximum_fusion.refs_3_, ...), custom_call_target="tpu_custom_call" | custom-call | flops 2013265920 | bytes 2752512 | tf_op jit(solution)/shard_map/key_sums/pallas_call | solution.py:110
  26.3 0.9 fold.4
  27.1 2.1 %collective-permute-start.6 = (bf16[528,384]{1,0:T(8,128)(2,1)}, bf16[528,384]{1,0:T(8,128)(2,1)}, u32[]{:S(2)}, u32[]{:S(2)}) collective-permute-start(bf16[528,384]{1,0:T(8,128)(2,1)} %get-tuple-element.54), channel_id=1, source_target_pairs={{0,8},{1,3},{2,10},{3,1},{4,12},{5,7},{6,14},{7,5},{8,0},{9,11},{1... | collective-permute-start | bytes 1216520 | tf_op jit(solution)/shard_map/ppermute | solution.py:46
  29.3 0.7 copy-done.4
  30.0 0.7 copy-done.8
  30.7 4.9 %key_sums.7 = (bf16[1024,384]{1,0:T(8,128)(2,1)S(1)}, f32[8,128]{1,0:T(8,128)}) custom-call(s32[1,2560]{1,0:T(1,128)S(1)} %copy-done.4, bf16[1280,384]{1,0:T(8,128)(2,1)} %get-tuple-element.91.refs_1_, bf16[1280,384]{1,0:T(8,128)(2,1)} %collective-permute-done.1.refs_2_, f32[8,128]{1,0:T(8,128)S(1)} %copy-done.8), custom_call_target="tpu_custom_call" | custom-call | flops 2013265920 | bytes 2752512 | tf_op jit(solution)/shard_map/key_sums/pallas_call | solution.py:110
  35.5 1.3 %fold.5 = (bf16[512,384]{1,0:T(8,128)(2,1)S(1)}, bf16[512,384]{1,0:T(8,128)(2,1)S(1)}, f32[8,128]{1,0:T(8,128)S(1)}) custom-call(bf16[1024,384]{1,0:T(8,128)(2,1)} %collective-permute-done.3.refs_0_, bf16[1024,384]{1,0:T(8,128)(2,1)S(1)} %get-tuple-element.48.refs_1_, f32[8,128]{1,0:T(8,128)S(1)} %get-tuple-element.51.refs_2_), custom_call_target="tpu_custom_call" | custom-call | flops 1179648 | bytes 2359296 | tf_op jit(solution)/shard_map/fold/pallas_call | solution.py:133
  36.9 1.3 %collective-permute-start.5 = (bf16[512,384]{1,0:T(8,128)(2,1)S(1)}, bf16[512,384]{1,0:T(8,128)(2,1)S(1)}, u32[]{:S(2)}, u32[]{:S(2)}) collective-permute-start(bf16[512,384]{1,0:T(8,128)(2,1)S(1)} %get-tuple-element.52), channel_id=1, source_target_pairs={{0,8},{1,5},{2,10},{3,7},{4,12},{5,1},{6,14},{7,3},{8,0},{9,13},{1... | collective-permute-start | bytes 1179656 | tf_op jit(solution)/shard_map/ppermute | solution.py:46
  38.5 1.1 fold.6
  39.7 6.8 %collective-permute-done.8.refs_0_ = bf16[272,384]{1,0:T(8,128)(2,1)S(1)} collective-permute-done((bf16[272,384]{1,0:T(8,128)(2,1)S(1)}, bf16[272,384]{1,0:T(8,128)(2,1)S(1)}, u32[]{:S(2)}, u32[]{:S(2)}) %collective-permute-start.8) | collective-permute-done | bytes 208928 | tf_op jit(solution)/shard_map/ppermute | solution.py:46
  46.6 1.6 %collective-permute-start.10 = (bf16[272,384]{1,0:T(8,128)(2,1)S(1)}, bf16[272,384]{1,0:T(8,128)(2,1)S(1)}, u32[]{:S(2)}, u32[]{:S(2)}) collective-permute-start(bf16[272,384]{1,0:T(8,128)(2,1)S(1)} %get-tuple-element.65.refs_1_), channel_id=1, source_target_pairs={{0,24},{1,25},{2,26},{3,27},{4,28},{5,29},{6,30},{7,31},{8,16},{9,... | collective-permute-start | bytes 626696 | tf_op jit(solution)/shard_map/ppermute | solution.py:46
  48.2 0.6 fold.7
  48.9 2.3 %collective-permute-start.7 = (bf16[256,384]{1,0:T(8,128)(2,1)S(1)}, bf16[256,384]{1,0:T(8,128)(2,1)S(1)}, u32[]{:S(2)}, u32[]{:S(2)}) collective-permute-start(bf16[256,384]{1,0:T(8,128)(2,1)S(1)} %get-tuple-element.58), channel_id=1, source_target_pairs={{0,2},{1,9},{2,0},{3,11},{4,6},{5,13},{6,4},{7,15},{8,10},{9,1},{1... | collective-permute-start | bytes 589832 | tf_op jit(solution)/shard_map/ppermute | solution.py:46
  51.2 6.9 %collective-permute-done.10.refs_0_ = bf16[272,384]{1,0:T(8,128)(2,1)S(1)} collective-permute-done((bf16[272,384]{1,0:T(8,128)(2,1)S(1)}, bf16[272,384]{1,0:T(8,128)(2,1)S(1)}, u32[]{:S(2)}, u32[]{:S(2)}) %collective-permute-start.10) | collective-permute-done | bytes 208928 | tf_op jit(solution)/shard_map/ppermute | solution.py:46
  58.4 0.6 seed.3
  59.1 1.5 %collective-permute-start.9 = (bf16[256,384]{1,0:T(8,128)(2,1)S(1)}, bf16[256,384]{1,0:T(8,128)(2,1)S(1)}, u32[]{:S(2)}, u32[]{:S(2)}) collective-permute-start(bf16[256,384]{1,0:T(8,128)(2,1)S(1)} %get-tuple-element.63.refs_1_), channel_id=1, source_target_pairs={{0,24},{1,25},{2,26},{3,27},{4,28},{5,29},{6,30},{7,31},{8,16},{9,... | collective-permute-start | bytes 589832 | tf_op jit(solution)/shard_map/ppermute | solution.py:46
  60.6 2.6 %collective-permute-done.12.refs_0_ = bf16[256,384]{1,0:T(8,128)(2,1)S(1)} collective-permute-done((bf16[256,384]{1,0:T(8,128)(2,1)S(1)}, bf16[256,384]{1,0:T(8,128)(2,1)S(1)}, u32[]{:S(2)}, u32[]{:S(2)}) %collective-permute-start.12) | collective-permute-done | bytes 196640 | tf_op jit(solution)/shard_map/ppermute | solution.py:46
  63.3 1.8 %collective-permute-start.14 = (bf16[512,384]{1,0:T(8,128)(2,1)S(1)}, bf16[512,384]{1,0:T(8,128)(2,1)S(1)}, u32[]{:S(2)}, u32[]{:S(2)}) collective-permute-start(bf16[512,384]{1,0:T(8,128)(2,1)S(1)} %get-tuple-element.75.refs_1_), channel_id=1, source_target_pairs={{0,8},{1,3},{2,10},{3,1},{4,12},{5,7},{6,14},{7,5},{8,0},{9,11},{1... | collective-permute-start | bytes 1179656 | tf_op jit(solution)/shard_map/ppermute | solution.py:46
  65.1 1.0 last_centroids.1
  66.0 4.7 %collective-permute-start.11 = (bf16[272,384]{1,0:T(8,128)(2,1)S(1)}, bf16[272,384]{1,0:T(8,128)(2,1)S(1)}, u32[]{:S(2)}, u32[]{:S(2)}) collective-permute-start(bf16[272,384]{1,0:T(8,128)(2,1)S(1)} %get-tuple-element.71.refs_1_), channel_id=1, source_target_pairs={{0,2},{1,9},{2,0},{3,11},{4,6},{5,13},{6,4},{7,15},{8,10},{9,1},{1... | collective-permute-start | bytes 626696 | tf_op jit(solution)/shard_map/ppermute | solution.py:46
  70.8 3.8 %collective-permute-done.11.refs_0_ = bf16[272,384]{1,0:T(8,128)(2,1)S(1)} collective-permute-done((bf16[272,384]{1,0:T(8,128)(2,1)S(1)}, bf16[272,384]{1,0:T(8,128)(2,1)S(1)}, u32[]{:S(2)}, u32[]{:S(2)}) %collective-permute-start.11) | collective-permute-done | bytes 208928 | tf_op jit(solution)/shard_map/ppermute | solution.py:46
  74.7 1.0 join.6
  75.6 0.6 copy-done.5
  76.2 3.1 %collective-permute-start.15 = (bf16[1024,384]{1,0:T(8,128)(2,1)}, bf16[1024,384]{1,0:T(8,128)(2,1)}, u32[]{:S(2)}, u32[]{:S(2)}) collective-permute-start(bf16[1024,384]{1,0:T(8,128)(2,1)} %get-tuple-element.77.refs_2_), channel_id=1, source_target_pairs={{0,1},{1,0},{2,3},{3,2},{4,5},{5,4},{6,7},{7,6},{8,9},{9,8},{10,11... | collective-permute-start | bytes 2359304 | tf_op jit(solution)/shard_map/ppermute | solution.py:46
  79.3 0.8 collective-permute-start.17
  80.2 0.8 collective-permute-start.13
  80.9 0.7 compare_select_fusion.6.refs_1_.gid_ref
  81.7 0.7 copy-done.6
  82.3 7.2 %part_scores.2 = (bf16[1280,1024]{1,0:T(8,128)(2,1)}, f32[8,128]{1,0:T(8,128)S(1)}) custom-call(s32[16]{0:T(128)S(1)} %stack.212.code_ref, bf16[1280,768]{1,0:T(8,128)(2,1)} %x_ref.1, s32[1,1280]{1,0:T(1,128)S(1)} %compare_select_fusion.6.refs_1_.gid_ref, bf16[1024,384]{1,0:T(8,128)(2,1)} %get-tuple-element.77.refs_2_, ...), custom_call_target="tpu_custom_call" | custom-call | flops 1 | bytes 1 | tf_op jit(solution)/shard_map/part_scores/pallas_call | solution.py:328
  89.6 6.2 %collective-permute-done.13.refs_0_ = bf16[528,384]{1,0:T(8,128)(2,1)S(1)} collective-permute-done((bf16[528,384]{1,0:T(8,128)(2,1)S(1)}, bf16[528,384]{1,0:T(8,128)(2,1)S(1)}, u32[]{:S(2)}, u32[]{:S(2)}) %collective-permute-start.13) | collective-permute-done | bytes 405536 | tf_op jit(solution)/shard_map/ppermute | solution.py:46
  95.8 1.0 join.7
  96.8 1.4 %collective-permute-start.16 = (bf16[1040,384]{1,0:T(8,128)(2,1)}, bf16[1040,384]{1,0:T(8,128)(2,1)}, u32[]{:S(2)}, u32[]{:S(2)}) collective-permute-start(bf16[1040,384]{1,0:T(8,128)(2,1)} %get-tuple-element.80.rest_2_), channel_id=1, source_target_pairs={{0,4},{1,3},{2,6},{3,1},{4,0},{5,7},{6,2},{7,5},{8,12},{9,11},{10,... | collective-permute-start | bytes 2396168 | tf_op jit(solution)/shard_map/ppermute | solution.py:46
  98.2 0.5 collective-permute-start.20
  98.7 3.1 %collective-permute-done.18.refs_3_ = bf16[1024,384]{1,0:T(8,128)(2,1)S(1)} collective-permute-done((bf16[1024,384]{1,0:T(8,128)(2,1)}, bf16[1024,384]{1,0:T(8,128)(2,1)S(1)}, u32[]{:S(2)}, u32[]{:S(2)}) %collective-permute-start.18) | collective-permute-done | bytes 786464 | tf_op jit(solution)/shard_map/ppermute | solution.py:46
  101.8 7.0 %part_scores.3 = (bf16[1280,1024]{1,0:T(8,128)(2,1)}, f32[8,128]{1,0:T(8,128)S(1)}) custom-call(s32[16]{0:T(128)S(1)} %stack.212.code_ref, bf16[1280,768]{1,0:T(8,128)(2,1)} %x_ref.1, s32[1,1280]{1,0:T(1,128)S(1)} %compare_select_fusion.6.refs_1_.gid_ref, bf16[1024,384]{1,0:T(8,128)(2,1)} %collective-permute-done.17.refs_2_, ...), custom_call_target="tpu_custom_call", output_to_operand_aliasing={{0}: (5, {})} | custom-call | flops 1 | bytes 1 | tf_op jit(solution)/shard_map/part_scores/pallas_call | solution.py:328
  109.2 2.4 %collective-permute-done.19.rest_1_ = bf16[1040,384]{1,0:T(8,128)(2,1)} collective-permute-done((bf16[1040,384]{1,0:T(8,128)(2,1)}, bf16[1040,384]{1,0:T(8,128)(2,1)}, u32[]{:S(2)}, u32[]{:S(2)}) %collective-permute-start.19) | collective-permute-done | bytes 798752 | tf_op jit(solution)/shard_map/ppermute | solution.py:46
  111.6 0.7 copy-done.2
  112.2 11.1 %final_scores.1 = bf16[1280,1024]{1,0:T(8,128)(2,1)} custom-call(s32[32]{0:T(128)S(1)} %concatenate.104.code_ref, s32[8]{0:T(128)S(1)} %fusion.21.slot_ref, bf16[1280,768]{1,0:T(8,128)(2,1)} %x_ref.1, s32[1,1280]{1,0:T(1,128)S(1)} %copy-done.2, f32[16,1024]{1,0:T(8,128)S(1)} %broadcast_in_dim.28.half_ref, bf16[1040,384]{1,0:T(8,128)(2,1)} %behind.1.rest_0_, ...), custom_call_target="tpu_custom_call" | custom-call | flops 1 | bytes 1 | tf_op jit(solution)/shard_map/final_scores/pallas_call | solution.py:405
  (50 shorter events, 2.4 us)
Async XLA Ops:
  0.6 28.6 %copy-start = (f32[1,1024,768]{2,1,0:T(8,128)S(1)}, f32[1,1024,768]{2,1,0:T(8,128)}, u32[]{:S(2)}) copy-start(f32[1,1024,768]{2,1,0:T(8,128)} %param.9) | copy-start | bytes 9437188
  3.0 4.2 %collective-permute-start = (s32[1280]{0:T(1024)S(1)}, s32[1280]{0:T(1024)S(1)}, u32[]{:S(2)}, u32[]{:S(2)}) collective-permute-start(s32[1280]{0:T(1024)S(1)} %add_select_fusion.9), channel_id=1, source_target_pairs={{0,1},{1,0},{2,3},{3,2},{4,5},{5,4},{6,7},{7,6},{8,9},{9,8},{10,11... | collective-permute-start | bytes 15368 | tf_op jit(solution)/shard_map/ppermute | solution.py:46
  6.7 2.9 %collective-permute-start.2 = (bf16[1280,384]{1,0:T(8,128)(2,1)}, bf16[1280,384]{1,0:T(8,128)(2,1)}, u32[]{:S(2)}, u32[]{:S(2)}) collective-permute-start(bf16[1280,384]{1,0:T(8,128)(2,1)} %get-tuple-element.90.refs_1_), channel_id=1, source_target_pairs={{0,1},{1,0},{2,3},{3,2},{4,5},{5,4},{6,7},{7,6},{8,9},{9,8},{10,11... | collective-permute-start | bytes 2949128 | tf_op jit(solution)/shard_map/ppermute | solution.py:46
  6.7 8.7 %collective-permute-start.1 = (bf16[1280,384]{1,0:T(8,128)(2,1)}, bf16[1280,384]{1,0:T(8,128)(2,1)}, u32[]{:S(2)}, u32[]{:S(2)}) collective-permute-start(bf16[1280,384]{1,0:T(8,128)(2,1)} %get-tuple-element.91.refs_1_), channel_id=1, source_target_pairs={{0,1},{1,0},{2,3},{3,2},{4,5},{5,4},{6,7},{7,6},{8,9},{9,8},{10,11... | collective-permute-start | bytes 2949128 | tf_op jit(solution)/shard_map/ppermute | solution.py:46
  14.0 12.3 %collective-permute-start.4 = (bf16[1040,384]{1,0:T(8,128)(2,1)S(1)}, bf16[1040,384]{1,0:T(8,128)(2,1)S(1)}, u32[]{:S(2)}, u32[]{:S(2)}) collective-permute-start(bf16[1040,384]{1,0:T(8,128)(2,1)S(1)} %get-tuple-element.49), channel_id=1, source_target_pairs={{0,2},{1,5},{2,0},{3,7},{4,6},{5,1},{6,4},{7,3},{8,10},{9,13},{10,... | collective-permute-start | bytes 2396168 | tf_op jit(solution)/shard_map/ppermute | solution.py:46
  15.4 5.3 %copy-start.3 = (s32[1,2560]{1,0:T(1,128)}, s32[1,2560]{1,0:T(1,128)S(1)}, u32[]{:S(2)}) copy-start(s32[1,2560]{1,0:T(1,128)S(1)} %fusion.10.refs_0_) | copy-start | bytes 30724
  20.7 14.9 %collective-permute-start.3 = (bf16[1024,384]{1,0:T(8,128)(2,1)}, bf16[1024,384]{1,0:T(8,128)(2,1)}, u32[]{:S(2)}, u32[]{:S(2)}) collective-permute-start(bf16[1024,384]{1,0:T(8,128)(2,1)} %get-tuple-element.45), channel_id=1, source_target_pairs={{0,4},{1,3},{2,6},{3,1},{4,0},{5,7},{6,2},{7,5},{8,12},{9,11},{10,... | collective-permute-start | bytes 2359304 | tf_op jit(solution)/shard_map/ppermute | solution.py:46
  26.2 0.9 copy-start.7
  27.1 11.4 %collective-permute-start.6 = (bf16[528,384]{1,0:T(8,128)(2,1)}, bf16[528,384]{1,0:T(8,128)(2,1)}, u32[]{:S(2)}, u32[]{:S(2)}) collective-permute-start(bf16[528,384]{1,0:T(8,128)(2,1)} %get-tuple-element.54), channel_id=1, source_target_pairs={{0,8},{1,3},{2,10},{3,1},{4,12},{5,7},{6,14},{7,5},{8,0},{9,11},{1... | collective-permute-start | bytes 1216520 | tf_op jit(solution)/shard_map/ppermute | solution.py:46
  29.3 0.7 copy-start.4
  30.0 0.7 copy-start.8
  36.9 11.4 %collective-permute-start.5 = (bf16[512,384]{1,0:T(8,128)(2,1)S(1)}, bf16[512,384]{1,0:T(8,128)(2,1)S(1)}, u32[]{:S(2)}, u32[]{:S(2)}) collective-permute-start(bf16[512,384]{1,0:T(8,128)(2,1)S(1)} %get-tuple-element.52), channel_id=1, source_target_pairs={{0,8},{1,5},{2,10},{3,7},{4,12},{5,1},{6,14},{7,3},{8,0},{9,13},{1... | collective-permute-start | bytes 1179656 | tf_op jit(solution)/shard_map/ppermute | solution.py:46
  39.6 6.9 %collective-permute-start.8 = (bf16[272,384]{1,0:T(8,128)(2,1)S(1)}, bf16[272,384]{1,0:T(8,128)(2,1)S(1)}, u32[]{:S(2)}, u32[]{:S(2)}) collective-permute-start(bf16[272,384]{1,0:T(8,128)(2,1)S(1)} %get-tuple-element.60), channel_id=1, source_target_pairs={{0,4},{1,9},{2,6},{3,11},{4,0},{5,13},{6,2},{7,15},{8,12},{9,1},{1... | collective-permute-start | bytes 626696 | tf_op jit(solution)/shard_map/ppermute | solution.py:46
  46.6 11.4 %collective-permute-start.10 = (bf16[272,384]{1,0:T(8,128)(2,1)S(1)}, bf16[272,384]{1,0:T(8,128)(2,1)S(1)}, u32[]{:S(2)}, u32[]{:S(2)}) collective-permute-start(bf16[272,384]{1,0:T(8,128)(2,1)S(1)} %get-tuple-element.65.refs_1_), channel_id=1, source_target_pairs={{0,24},{1,25},{2,26},{3,27},{4,28},{5,29},{6,30},{7,31},{8,16},{9,... | collective-permute-start | bytes 626696 | tf_op jit(solution)/shard_map/ppermute | solution.py:46
  48.9 9.6 %collective-permute-start.7 = (bf16[256,384]{1,0:T(8,128)(2,1)S(1)}, bf16[256,384]{1,0:T(8,128)(2,1)S(1)}, u32[]{:S(2)}, u32[]{:S(2)}) collective-permute-start(bf16[256,384]{1,0:T(8,128)(2,1)S(1)} %get-tuple-element.58), channel_id=1, source_target_pairs={{0,2},{1,9},{2,0},{3,11},{4,6},{5,13},{6,4},{7,15},{8,10},{9,1},{1... | collective-permute-start | bytes 589832 | tf_op jit(solution)/shard_map/ppermute | solution.py:46
  58.4 4.9 %collective-permute-start.12 = (bf16[256,384]{1,0:T(8,128)(2,1)S(1)}, bf16[256,384]{1,0:T(8,128)(2,1)S(1)}, u32[]{:S(2)}, u32[]{:S(2)}) collective-permute-start(bf16[256,384]{1,0:T(8,128)(2,1)S(1)} %get-tuple-element.72.refs_1_), channel_id=1, source_target_pairs={{0,4},{1,9},{2,6},{3,11},{4,0},{5,13},{6,2},{7,15},{8,12},{9,1},{1... | collective-permute-start | bytes 589832 | tf_op jit(solution)/shard_map/ppermute | solution.py:46
  59.1 6.0 %collective-permute-start.9 = (bf16[256,384]{1,0:T(8,128)(2,1)S(1)}, bf16[256,384]{1,0:T(8,128)(2,1)S(1)}, u32[]{:S(2)}, u32[]{:S(2)}) collective-permute-start(bf16[256,384]{1,0:T(8,128)(2,1)S(1)} %get-tuple-element.63.refs_1_), channel_id=1, source_target_pairs={{0,24},{1,25},{2,26},{3,27},{4,28},{5,29},{6,30},{7,31},{8,16},{9,... | collective-permute-start | bytes 589832 | tf_op jit(solution)/shard_map/ppermute | solution.py:46
  63.3 11.4 %collective-permute-start.14 = (bf16[512,384]{1,0:T(8,128)(2,1)S(1)}, bf16[512,384]{1,0:T(8,128)(2,1)S(1)}, u32[]{:S(2)}, u32[]{:S(2)}) collective-permute-start(bf16[512,384]{1,0:T(8,128)(2,1)S(1)} %get-tuple-element.75.refs_1_), channel_id=1, source_target_pairs={{0,8},{1,3},{2,10},{3,1},{4,12},{5,7},{6,14},{7,5},{8,0},{9,11},{1... | collective-permute-start | bytes 1179656 | tf_op jit(solution)/shard_map/ppermute | solution.py:46
  66.0 8.6 %collective-permute-start.11 = (bf16[272,384]{1,0:T(8,128)(2,1)S(1)}, bf16[272,384]{1,0:T(8,128)(2,1)S(1)}, u32[]{:S(2)}, u32[]{:S(2)}) collective-permute-start(bf16[272,384]{1,0:T(8,128)(2,1)S(1)} %get-tuple-element.71.refs_1_), channel_id=1, source_target_pairs={{0,2},{1,9},{2,0},{3,11},{4,6},{5,13},{6,4},{7,15},{8,10},{9,1},{1... | collective-permute-start | bytes 626696 | tf_op jit(solution)/shard_map/ppermute | solution.py:46
  75.6 0.6 copy-start.5
  76.2 5.5 %collective-permute-start.15 = (bf16[1024,384]{1,0:T(8,128)(2,1)}, bf16[1024,384]{1,0:T(8,128)(2,1)}, u32[]{:S(2)}, u32[]{:S(2)}) collective-permute-start(bf16[1024,384]{1,0:T(8,128)(2,1)} %get-tuple-element.77.refs_2_), channel_id=1, source_target_pairs={{0,1},{1,0},{2,3},{3,2},{4,5},{5,4},{6,7},{7,6},{8,9},{9,8},{10,11... | collective-permute-start | bytes 2359304 | tf_op jit(solution)/shard_map/ppermute | solution.py:46
  79.3 18.9 %collective-permute-start.17 = (bf16[1024,384]{1,0:T(8,128)(2,1)}, bf16[1024,384]{1,0:T(8,128)(2,1)}, u32[]{:S(2)}, u32[]{:S(2)}) collective-permute-start(bf16[1024,384]{1,0:T(8,128)(2,1)} %get-tuple-element.77.refs_2_), channel_id=1, source_target_pairs={{0,2},{1,5},{2,0},{3,7},{4,6},{5,1},{6,4},{7,3},{8,10},{9,13},{10,... | collective-permute-start | bytes 2359304 | tf_op jit(solution)/shard_map/ppermute | solution.py:46
  80.2 15.7 %collective-permute-start.13 = (bf16[528,384]{1,0:T(8,128)(2,1)S(1)}, bf16[528,384]{1,0:T(8,128)(2,1)S(1)}, u32[]{:S(2)}, u32[]{:S(2)}) collective-permute-start(bf16[528,384]{1,0:T(8,128)(2,1)S(1)} %get-tuple-element.74.refs_1_), channel_id=1, source_target_pairs={{0,8},{1,5},{2,10},{3,7},{4,12},{5,1},{6,14},{7,3},{8,0},{9,13},{1... | collective-permute-start | bytes 1216520 | tf_op jit(solution)/shard_map/ppermute | solution.py:46
  81.6 27.2 %copy-start.1 = (s32[1,1280]{1,0:T(1,128)}, s32[1,1280]{1,0:T(1,128)S(1)}, u32[]{:S(2)}) copy-start(s32[1,1280]{1,0:T(1,128)S(1)} %compare_select_fusion.6.refs_1_.gid_ref) | copy-start | bytes 15364
  81.7 0.7 copy-start.6
  96.8 12.0 %collective-permute-start.16 = (bf16[1040,384]{1,0:T(8,128)(2,1)}, bf16[1040,384]{1,0:T(8,128)(2,1)}, u32[]{:S(2)}, u32[]{:S(2)}) collective-permute-start(bf16[1040,384]{1,0:T(8,128)(2,1)} %get-tuple-element.80.rest_2_), channel_id=1, source_target_pairs={{0,4},{1,3},{2,6},{3,1},{4,0},{5,7},{6,2},{7,5},{8,12},{9,11},{10,... | collective-permute-start | bytes 2396168 | tf_op jit(solution)/shard_map/ppermute | solution.py:46
  98.2 3.6 %collective-permute-start.18 = (bf16[1024,384]{1,0:T(8,128)(2,1)}, bf16[1024,384]{1,0:T(8,128)(2,1)S(1)}, u32[]{:S(2)}, u32[]{:S(2)}) collective-permute-start(bf16[1024,384]{1,0:T(8,128)(2,1)} %collective-permute-done.17.refs_2_), channel_id=1, source_target_pairs={{0,1},{1,0},{2,3},{3,2},{4,5},{5,4},{6,7},{7,6},{8,9},{9,8},{10,11... | collective-permute-start | bytes 2359304 | tf_op jit(solution)/shard_map/ppermute | solution.py:46
  98.2 11.0 %collective-permute-start.20 = (bf16[1040,384]{1,0:T(8,128)(2,1)}, bf16[1040,384]{1,0:T(8,128)(2,1)}, u32[]{:S(2)}, u32[]{:S(2)}) collective-permute-start(bf16[1040,384]{1,0:T(8,128)(2,1)} %get-tuple-element.80.rest_2_), channel_id=1, source_target_pairs={{0,1},{1,0},{2,3},{3,2},{4,5},{5,4},{6,7},{7,6},{8,9},{9,8},{10,11... | collective-permute-start | bytes 2396168 | tf_op jit(solution)/shard_map/ppermute | solution.py:46
  108.8 2.7 %collective-permute-start.19 = (bf16[1040,384]{1,0:T(8,128)(2,1)}, bf16[1040,384]{1,0:T(8,128)(2,1)}, u32[]{:S(2)}, u32[]{:S(2)}) collective-permute-start(bf16[1040,384]{1,0:T(8,128)(2,1)} %behind.1.rest_0_), channel_id=1, source_target_pairs={{0,1},{1,0},{2,3},{3,2},{4,5},{5,4},{6,7},{7,6},{8,9},{9,8},{10,11... | collective-permute-start | bytes 2396168 | tf_op jit(solution)/shard_map/ppermute | solution.py:46
  111.5 0.7 copy-start.2

commit v13 on v10

--- a/solution.py
+++ b/solution.py
@@ -119,7 +119,7 @@
         + [whole(e.shape) for e in extra]
         + [whole(token.shape)],
         out_specs=[whole((out_rows, wide)), whole(token.shape)],
-        compiler_params=pltpu.CompilerParams(vmem_limit_bytes=56 << 20),
+        compiler_params=pltpu.CompilerParams(vmem_limit_bytes=16 << 20),
         cost_estimate=pl.CostEstimate(
             flops=2 * keys * 2 * rows * wide, bytes_accessed=(4 * rows + 2 * keys) * wide, transcendentals=0
         ),

time: 121 us -> 120 us (level)
  starting transfers between devices: 22.1 us -> 30.4 us
  waiting for transfers between devices: 32.1 us -> 26 us
  Pallas kernels: 54.5 us -> 51.3 us
  other arithmetic: 4.41 us -> 2.61 us
  local copies, waits for them, and re-layouts: 5.08 us -> 6.7 us
    ppermute x20, starting transfers between devices: 22.1 us -> 30.4 us  [exchange(): return lax.ppermute(array, AXES, pairs)]
    ppermute x20, waiting for transfers between devices: 32.1 us -> 26 us  [exchange(): return lax.ppermute(array, AXES, pairs)]
    pallas_call x4, Pallas kernels: 21.1 us -> 18.2 us  [key_sums(): pl.pallas_call(hand_on(functools.partial(sums_kernel, base), 3 + len(extr...]
    unnamed x17 -> x25, local copies, waits for them, and re-layouts: 4.23 us -> 6.44 us
  transfers between devices with their start and end apart: 20 -> 20, of which waited for: 13 -> 10; matrix products, arithmetic and copies ran while one was open for 3% -> 2% of each run, Pallas kernels for 31% -> 29%
where the time goes in v13:
time: 120 us; the launch traced here: 119 us
  Pallas kernels  51.3 us (43%)
  starting transfers between devices  30.4 us (25%)
  waiting for transfers between devices  26 us (22%)
  local copies, waits for them, and re-layouts  6.7 us (6%)
  other arithmetic  2.61 us (2%)
  between operations  1.82 us (2%)
    ppermute x20, starting transfers between devices, exchange(): return lax.ppermute(array, AXES, pairs)  30.4 us
    ppermute x20, waiting for transfers between devices, exchange(): return lax.ppermute(array, AXES, pairs)  26 us
    pallas_call x4, Pallas kernels, key_sums(): pl.pallas_call(hand_on(functools.partial(sums_kernel, base), 3 + len(extr...  18.2 us
    pallas_call x2, Pallas kernels, part_scores(): pl.pallas_call(kernel, grid_spec=pltpu.PrefetchScalarGridSpec(num_scalar_...  14.2 us
    pallas_call x1, Pallas kernels, final_scores(): pl.pallas_call(functools.partial(final_kernel, groups, share, start_at),...  11 us
    pallas_call x12, Pallas kernels, small_call(): pl.pallas_call(hand_on(kernel, len(args)), out_shape=[*outs, token_shape(...  7.87 us
    unnamed x25, local copies, waits for them, and re-layouts  6.44 us
  transfers between devices with their start and end apart: 20, of which 10 were waited for; matrix products, arithmetic and copies ran while one was open for 2% of the time, Pallas kernels for 29%

profile of v13, /device:TPU:0, one launch (start us, length us, event | category | flops | bytes accessed | tf_op | source)
XLA Modules:
  0.0 119.3 jit_solution(2364553934086419590)
XLA Ops:
  1.4 0.9 multiply_reduce_fusion
  2.3 0.7 add_select_fusion.9
  3.5 0.8 collective-permute-done
  5.2 2.6 %collective-permute-done.1.refs_2_ = bf16[1280,768]{1,0:T(8,128)(2,1)} collective-permute-done((bf16[1280,768]{1,0:T(8,128)(2,1)}, bf16[1280,768]{1,0:T(8,128)(2,1)}, u32[]{:S(2)}, u32[]{:S(2)}) %collective-permute-start.1) | collective-permute-done | bytes 1966112 | tf_op jit(solution)/shard_map/ppermute | solution.py:46
  7.8 1.5 %copy-done.1 = bf16[1280,768]{1,0:T(8,128)(2,1)S(1)} copy-done((bf16[1280,768]{1,0:T(8,128)(2,1)S(1)}, bf16[1280,768]{1,0:T(8,128)(2,1)}, u32[]{:S(2)}) %copy-start.1) | copy-done | bytes 1966104
  9.3 4.3 %key_sums.4 = (bf16[1040,384]{1,0:T(8,128)(2,1)S(1)}, f32[8,128]{1,0:T(8,128)S(1)}) custom-call(s32[1,2560]{1,0:T(1,128)S(1)} %get-tuple-element.86.refs_0_, bf16[1280,768]{1,0:T(8,128)(2,1)S(1)} %copy-done.1, bf16[1280,768]{1,0:T(8,128)(2,1)} %collective-permute-done.1.refs_2_, bf16[16,384]{1,0:T(8,128)(2,1)S(1)} %pad_maximum_fusion.refs_3_, ...), custom_call_target="tpu_custom_call" | custom-call | flops 2013265920 | bytes 2752512 | tf_op jit(solution)/shard_map/key_sums/pallas_call | solution.py:110
  13.6 2.7 %collective-permute-start.3 = (bf16[1040,384]{1,0:T(8,128)(2,1)S(1)}, bf16[1040,384]{1,0:T(8,128)(2,1)S(1)}, u32[]{:S(2)}, u32[]{:S(2)}) collective-permute-start(bf16[1040,384]{1,0:T(8,128)(2,1)S(1)} %get-tuple-element.49), channel_id=1, source_target_pairs={{0,2},{1,5},{2,0},{3,7},{4,6},{5,1},{6,4},{7,3},{8,10},{9,13},{10,... | collective-permute-start | bytes 2396168 | tf_op jit(solution)/shard_map/ppermute | solution.py:46
  16.4 5.0 %key_sums.5 = (bf16[1024,384]{1,0:T(8,128)(2,1)}, f32[8,128]{1,0:T(8,128)S(1)}) custom-call(s32[1,2560]{1,0:T(1,128)S(1)} %fusion.10.refs_0_, bf16[1280,768]{1,0:T(8,128)(2,1)S(1)} %copy-done.2, bf16[1280,768]{1,0:T(8,128)(2,1)} %collective-permute-done.1.refs_2_, f32[8,128]{1,0:T(8,128)S(1)} %get-tuple-element.44.refs_3_), custom_call_target="tpu_custom_call" | custom-call | flops 2013265920 | bytes 2752512 | tf_op jit(solution)/shard_map/key_sums/pallas_call | solution.py:110
  21.4 1.5 %collective-permute-start.2 = (bf16[1024,384]{1,0:T(8,128)(2,1)}, bf16[1024,384]{1,0:T(8,128)(2,1)}, u32[]{:S(2)}, u32[]{:S(2)}) collective-permute-start(bf16[1024,384]{1,0:T(8,128)(2,1)} %get-tuple-element.45), channel_id=1, source_target_pairs={{0,4},{1,3},{2,6},{3,1},{4,0},{5,7},{6,2},{7,5},{8,12},{9,11},{10,... | collective-permute-start | bytes 2359304 | tf_op jit(solution)/shard_map/ppermute | solution.py:46
  22.9 4.2 %key_sums.6 = (bf16[1040,384]{1,0:T(8,128)(2,1)S(1)}, f32[8,128]{1,0:T(8,128)S(1)}) custom-call(s32[1,2560]{1,0:T(1,128)S(1)} %get-tuple-element.86.refs_0_, bf16[1280,768]{1,0:T(8,128)(2,1)S(1)} %copy-done.2, bf16[1280,768]{1,0:T(8,128)(2,1)} %collective-permute-done.1.refs_2_, bf16[16,384]{1,0:T(8,128)(2,1)S(1)} %pad_maximum_fusion.refs_3_, ...), custom_call_target="tpu_custom_call" | custom-call | flops 2013265920 | bytes 2752512 | tf_op jit(solution)/shard_map/key_sums/pallas_call | solution.py:110
  27.1 1.3 %collective-permute-done.3.refs_0_ = bf16[1040,384]{1,0:T(8,128)(2,1)S(1)} collective-permute-done((bf16[1040,384]{1,0:T(8,128)(2,1)S(1)}, bf16[1040,384]{1,0:T(8,128)(2,1)S(1)}, u32[]{:S(2)}, u32[]{:S(2)}) %collective-permute-start.3) | collective-permute-done | bytes 798752 | tf_op jit(solution)/shard_map/ppermute | solution.py:46
  28.5 0.8 fold.4
  29.3 2.6 %collective-permute-start.5 = (bf16[528,384]{1,0:T(8,128)(2,1)}, bf16[528,384]{1,0:T(8,128)(2,1)}, u32[]{:S(2)}, u32[]{:S(2)}) collective-permute-start(bf16[528,384]{1,0:T(8,128)(2,1)} %get-tuple-element.54), channel_id=1, source_target_pairs={{0,8},{1,9},{2,10},{3,11},{4,12},{5,13},{6,14},{7,15},{8,0},{9,1},... | collective-permute-start | bytes 1216520 | tf_op jit(solution)/shard_map/ppermute | solution.py:46
  31.9 1.5 %copy-done.3 = bf16[1280,768]{1,0:T(8,128)(2,1)S(1)} copy-done((bf16[1280,768]{1,0:T(8,128)(2,1)S(1)}, bf16[1280,768]{1,0:T(8,128)(2,1)}, u32[]{:S(2)}) %copy-start.3) | copy-done | bytes 1966104
  33.5 0.7 copy-done.7
  34.2 0.7 copy-done.11
  34.8 4.7 %key_sums.7 = (bf16[1024,384]{1,0:T(8,128)(2,1)S(1)}, f32[8,128]{1,0:T(8,128)}) custom-call(s32[1,2560]{1,0:T(1,128)S(1)} %copy-done.7, bf16[1280,768]{1,0:T(8,128)(2,1)S(1)} %copy-done.3, bf16[1280,768]{1,0:T(8,128)(2,1)} %collective-permute-done.1.refs_2_, f32[8,128]{1,0:T(8,128)S(1)} %copy-done.11), custom_call_target="tpu_custom_call" | custom-call | flops 2013265920 | bytes 2752512 | tf_op jit(solution)/shard_map/key_sums/pallas_call | solution.py:110
  39.5 1.3 %fold.5 = (bf16[512,384]{1,0:T(8,128)(2,1)S(1)}, bf16[512,384]{1,0:T(8,128)(2,1)S(1)}, f32[8,128]{1,0:T(8,128)S(1)}) custom-call(bf16[1024,384]{1,0:T(8,128)(2,1)} %collective-permute-done.2.refs_0_, bf16[1024,384]{1,0:T(8,128)(2,1)S(1)} %get-tuple-element.48.refs_1_, f32[8,128]{1,0:T(8,128)S(1)} %get-tuple-element.51.refs_2_), custom_call_target="tpu_custom_call" | custom-call | flops 1179648 | bytes 2359296 | tf_op jit(solution)/shard_map/fold/pallas_call | solution.py:133
  40.9 1.1 fold.6
  42.0 3.2 %collective-permute-start.7 = (bf16[272,384]{1,0:T(8,128)(2,1)S(1)}, bf16[272,384]{1,0:T(8,128)(2,1)S(1)}, u32[]{:S(2)}, u32[]{:S(2)}) collective-permute-start(bf16[272,384]{1,0:T(8,128)(2,1)S(1)} %get-tuple-element.60), channel_id=1, source_target_pairs={{0,4},{1,3},{2,6},{3,1},{4,0},{5,7},{6,2},{7,5},{8,12},{9,11},{10,... | collective-permute-start | bytes 626696 | tf_op jit(solution)/shard_map/ppermute | solution.py:46
  45.3 3.8 %collective-permute-done.7.refs_0_ = bf16[272,384]{1,0:T(8,128)(2,1)S(1)} collective-permute-done((bf16[272,384]{1,0:T(8,128)(2,1)S(1)}, bf16[272,384]{1,0:T(8,128)(2,1)S(1)}, u32[]{:S(2)}, u32[]{:S(2)}) %collective-permute-start.7) | collective-permute-done | bytes 208928 | tf_op jit(solution)/shard_map/ppermute | solution.py:46
  49.1 3.5 %collective-permute-start.9 = (bf16[272,384]{1,0:T(8,128)(2,1)S(1)}, bf16[272,384]{1,0:T(8,128)(2,1)S(1)}, u32[]{:S(2)}, u32[]{:S(2)}) collective-permute-start(bf16[272,384]{1,0:T(8,128)(2,1)S(1)} %get-tuple-element.65.refs_1_), channel_id=1, source_target_pairs={{0,24},{1,25},{2,26},{3,27},{4,28},{5,29},{6,30},{7,31},{8,16},{9,... | collective-permute-start | bytes 626696 | tf_op jit(solution)/shard_map/ppermute | solution.py:46
  52.6 0.6 fold.7
  53.2 1.5 %collective-permute-start.6 = (bf16[256,384]{1,0:T(8,128)(2,1)S(1)}, bf16[256,384]{1,0:T(8,128)(2,1)S(1)}, u32[]{:S(2)}, u32[]{:S(2)}) collective-permute-start(bf16[256,384]{1,0:T(8,128)(2,1)S(1)} %get-tuple-element.58), channel_id=1, source_target_pairs={{0,2},{1,5},{2,0},{3,7},{4,6},{5,1},{6,4},{7,3},{8,10},{9,13},{10,... | collective-permute-start | bytes 589832 | tf_op jit(solution)/shard_map/ppermute | solution.py:46
  54.7 2.1 %collective-permute-done.9.refs_0_ = bf16[272,384]{1,0:T(8,128)(2,1)S(1)} collective-permute-done((bf16[272,384]{1,0:T(8,128)(2,1)S(1)}, bf16[272,384]{1,0:T(8,128)(2,1)S(1)}, u32[]{:S(2)}, u32[]{:S(2)}) %collective-permute-start.9) | collective-permute-done | bytes 208928 | tf_op jit(solution)/shard_map/ppermute | solution.py:46
  57.1 2.1 %collective-permute-start.11 = (bf16[256,384]{1,0:T(8,128)(2,1)S(1)}, bf16[256,384]{1,0:T(8,128)(2,1)S(1)}, u32[]{:S(2)}, u32[]{:S(2)}) collective-permute-start(bf16[256,384]{1,0:T(8,128)(2,1)S(1)} %get-tuple-element.72.refs_1_), channel_id=1, source_target_pairs={{0,4},{1,3},{2,6},{3,1},{4,0},{5,7},{6,2},{7,5},{8,12},{9,11},{10,... | collective-permute-start | bytes 589832 | tf_op jit(solution)/shard_map/ppermute | solution.py:46
  59.3 0.6 seed.3
  59.9 3.5 %collective-permute-start.8 = (bf16[256,384]{1,0:T(8,128)(2,1)S(1)}, bf16[256,384]{1,0:T(8,128)(2,1)S(1)}, u32[]{:S(2)}, u32[]{:S(2)}) collective-permute-start(bf16[256,384]{1,0:T(8,128)(2,1)S(1)} %get-tuple-element.63.refs_1_), channel_id=1, source_target_pairs={{0,24},{1,25},{2,26},{3,27},{4,28},{5,29},{6,30},{7,31},{8,16},{9,... | collective-permute-start | bytes 589832 | tf_op jit(solution)/shard_map/ppermute | solution.py:46
  63.4 1.8 %collective-permute-start.13 = (bf16[512,384]{1,0:T(8,128)(2,1)S(1)}, bf16[512,384]{1,0:T(8,128)(2,1)S(1)}, u32[]{:S(2)}, u32[]{:S(2)}) collective-permute-start(bf16[512,384]{1,0:T(8,128)(2,1)S(1)} %get-tuple-element.75.refs_1_), channel_id=1, source_target_pairs={{0,8},{1,9},{2,10},{3,11},{4,12},{5,13},{6,14},{7,15},{8,0},{9,1},... | collective-permute-start | bytes 1179656 | tf_op jit(solution)/shard_map/ppermute | solution.py:46
  65.2 4.2 %collective-permute-done.8.refs_0_ = bf16[256,384]{1,0:T(8,128)(2,1)S(1)} collective-permute-done((bf16[256,384]{1,0:T(8,128)(2,1)S(1)}, bf16[256,384]{1,0:T(8,128)(2,1)S(1)}, u32[]{:S(2)}, u32[]{:S(2)}) %collective-permute-start.8) | collective-permute-done | bytes 196640 | tf_op jit(solution)/shard_map/ppermute | solution.py:46
  69.5 1.0 last_centroids.1
  70.4 1.3 %collective-permute-start.10 = (bf16[272,384]{1,0:T(8,128)(2,1)S(1)}, bf16[272,384]{1,0:T(8,128)(2,1)S(1)}, u32[]{:S(2)}, u32[]{:S(2)}) collective-permute-start(bf16[272,384]{1,0:T(8,128)(2,1)S(1)} %get-tuple-element.71.refs_1_), channel_id=1, source_target_pairs={{0,2},{1,5},{2,0},{3,7},{4,6},{5,1},{6,4},{7,3},{8,10},{9,13},{10,... | collective-permute-start | bytes 626696 | tf_op jit(solution)/shard_map/ppermute | solution.py:46
  71.7 4.5 %collective-permute-done.10.refs_0_ = bf16[272,384]{1,0:T(8,128)(2,1)S(1)} collective-permute-done((bf16[272,384]{1,0:T(8,128)(2,1)S(1)}, bf16[272,384]{1,0:T(8,128)(2,1)S(1)}, u32[]{:S(2)}, u32[]{:S(2)}) %collective-permute-start.10) | collective-permute-done | bytes 208928 | tf_op jit(solution)/shard_map/ppermute | solution.py:46
  76.3 1.0 join.6
  77.2 0.6 copy-done.8
  77.8 1.3 %collective-permute-start.16 = (bf16[1024,384]{1,0:T(8,128)(2,1)}, bf16[1024,384]{1,0:T(8,128)(2,1)}, u32[]{:S(2)}, u32[]{:S(2)}) collective-permute-start(bf16[1024,384]{1,0:T(8,128)(2,1)} %get-tuple-element.77.refs_2_), channel_id=1, source_target_pairs={{0,2},{1,5},{2,0},{3,7},{4,6},{5,1},{6,4},{7,3},{8,10},{9,13},{10,... | collective-permute-start | bytes 2359304 | tf_op jit(solution)/shard_map/ppermute | solution.py:46
  79.2 1.2 %collective-permute-start.12 = (bf16[528,384]{1,0:T(8,128)(2,1)S(1)}, bf16[528,384]{1,0:T(8,128)(2,1)S(1)}, u32[]{:S(2)}, u32[]{:S(2)}) collective-permute-start(bf16[528,384]{1,0:T(8,128)(2,1)S(1)} %get-tuple-element.74.refs_1_), channel_id=1, source_target_pairs={{0,8},{1,9},{2,10},{3,11},{4,12},{5,13},{6,14},{7,15},{8,0},{9,1},... | collective-permute-start | bytes 1216520 | tf_op jit(solution)/shard_map/ppermute | solution.py:46
  80.4 0.7 compare_select_fusion.6.refs_1_.gid_ref
  81.2 0.7 copy-done.9
  81.8 7.2 %part_scores.2 = (bf16[1280,1024]{1,0:T(8,128)(2,1)}, f32[8,128]{1,0:T(8,128)S(1)}) custom-call(s32[16]{0:T(128)S(1)} %stack.212.code_ref, bf16[1280,768]{1,0:T(8,128)(2,1)} %x_ref.1, s32[1,1280]{1,0:T(1,128)S(1)} %compare_select_fusion.6.refs_1_.gid_ref, bf16[1024,384]{1,0:T(8,128)(2,1)} %get-tuple-element.77.refs_2_, ...), custom_call_target="tpu_custom_call" | custom-call | flops 1 | bytes 1 | tf_op jit(solution)/shard_map/part_scores/pallas_call | solution.py:328
  89.1 1.2 collective-permute-done.12.refs_0_
  90.2 1.0 join.7
  91.2 2.9 %collective-permute-start.15 = (bf16[1040,384]{1,0:T(8,128)(2,1)}, bf16[1040,384]{1,0:T(8,128)(2,1)}, u32[]{:S(2)}, u32[]{:S(2)}) collective-permute-start(bf16[1040,384]{1,0:T(8,128)(2,1)} %get-tuple-element.80.rest_2_), channel_id=1, source_target_pairs={{0,4},{1,3},{2,6},{3,1},{4,0},{5,7},{6,2},{7,5},{8,12},{9,11},{10,... | collective-permute-start | bytes 2396168 | tf_op jit(solution)/shard_map/ppermute | solution.py:46
  94.6 3.1 %collective-permute-done.17.refs_3_ = bf16[1024,384]{1,0:T(8,128)(2,1)S(1)} collective-permute-done((bf16[1024,384]{1,0:T(8,128)(2,1)}, bf16[1024,384]{1,0:T(8,128)(2,1)S(1)}, u32[]{:S(2)}, u32[]{:S(2)}) %collective-permute-start.17) | collective-permute-done | bytes 786464 | tf_op jit(solution)/shard_map/ppermute | solution.py:46
  97.7 7.0 %part_scores.3 = (bf16[1280,1024]{1,0:T(8,128)(2,1)}, f32[8,128]{1,0:T(8,128)S(1)}) custom-call(s32[16]{0:T(128)S(1)} %stack.212.code_ref, bf16[1280,768]{1,0:T(8,128)(2,1)} %x_ref.1, s32[1,1280]{1,0:T(1,128)S(1)} %compare_select_fusion.6.refs_1_.gid_ref, bf16[1024,384]{1,0:T(8,128)(2,1)} %collective-permute-done.16.refs_2_, ...), custom_call_target="tpu_custom_call", output_to_operand_aliasing={{0}: (5, {})} | custom-call | flops 1 | bytes 1 | tf_op jit(solution)/shard_map/part_scores/pallas_call | solution.py:328
  105.1 2.4 %collective-permute-done.18.rest_1_ = bf16[1040,384]{1,0:T(8,128)(2,1)} collective-permute-done((bf16[1040,384]{1,0:T(8,128)(2,1)}, bf16[1040,384]{1,0:T(8,128)(2,1)}, u32[]{:S(2)}, u32[]{:S(2)}) %collective-permute-start.18) | collective-permute-done | bytes 798752 | tf_op jit(solution)/shard_map/ppermute | solution.py:46
  107.5 0.7 copy-done.5
  108.1 11.0 %final_scores.1 = bf16[1280,1024]{1,0:T(8,128)(2,1)} custom-call(s32[32]{0:T(128)S(1)} %concatenate.104.code_ref, s32[8]{0:T(128)S(1)} %fusion.21.slot_ref, bf16[1280,768]{1,0:T(8,128)(2,1)} %x_ref.1, s32[1,1280]{1,0:T(1,128)S(1)} %copy-done.5, f32[16,1024]{1,0:T(8,128)S(1)} %broadcast_in_dim.28.half_ref, bf16[1040,384]{1,0:T(8,128)(2,1)} %behind.1.rest_0_, ...), custom_call_target="tpu_custom_call" | custom-call | flops 1 | bytes 1 | tf_op jit(solution)/shard_map/final_scores/pallas_call | solution.py:405
  (54 shorter events, 3.0 us)
Async XLA Ops:
  0.6 31.3 %copy-start = (f32[1,1024,768]{2,1,0:T(8,128)S(1)}, f32[1,1024,768]{2,1,0:T(8,128)}, u32[]{:S(2)}) copy-start(f32[1,1024,768]{2,1,0:T(8,128)} %param.9) | copy-start | bytes 9437188
  3.0 1.3 %collective-permute-start = (s32[1280]{0:T(1024)S(1)}, s32[1280]{0:T(1024)S(1)}, u32[]{:S(2)}, u32[]{:S(2)}) collective-permute-start(s32[1280]{0:T(1024)S(1)} %add_select_fusion.9), channel_id=1, source_target_pairs={{0,1},{1,0},{2,3},{3,2},{4,5},{5,4},{6,7},{7,6},{8,9},{9,8},{10,11... | collective-permute-start | bytes 15368 | tf_op jit(solution)/shard_map/ppermute | solution.py:46
  3.5 4.3 %collective-permute-start.1 = (bf16[1280,768]{1,0:T(8,128)(2,1)}, bf16[1280,768]{1,0:T(8,128)(2,1)}, u32[]{:S(2)}, u32[]{:S(2)}) collective-permute-start(bf16[1280,768]{1,0:T(8,128)(2,1)} %x_ref.1), channel_id=1, source_target_pairs={{0,1},{1,0},{2,3},{3,2},{4,5},{5,4},{6,7},{7,6},{8,9},{9,8},{10,11... | collective-permute-start | bytes 5898248 | tf_op jit(solution)/shard_map/ppermute | solution.py:46
  7.8 1.5 %copy-start.1 = (bf16[1280,768]{1,0:T(8,128)(2,1)S(1)}, bf16[1280,768]{1,0:T(8,128)(2,1)}, u32[]{:S(2)}) copy-start(bf16[1280,768]{1,0:T(8,128)(2,1)} %x_ref.1) | copy-start | bytes 5898244
  9.3 7.0 %copy-start.2 = (bf16[1280,768]{1,0:T(8,128)(2,1)S(1)}, bf16[1280,768]{1,0:T(8,128)(2,1)}, u32[]{:S(2)}) copy-start(bf16[1280,768]{1,0:T(8,128)(2,1)} %x_ref.1) | copy-start | bytes 5898244
  13.6 14.8 %collective-permute-start.3 = (bf16[1040,384]{1,0:T(8,128)(2,1)S(1)}, bf16[1040,384]{1,0:T(8,128)(2,1)S(1)}, u32[]{:S(2)}, u32[]{:S(2)}) collective-permute-start(bf16[1040,384]{1,0:T(8,128)(2,1)S(1)} %get-tuple-element.49), channel_id=1, source_target_pairs={{0,2},{1,5},{2,0},{3,7},{4,6},{5,1},{6,4},{7,3},{8,10},{9,13},{10,... | collective-permute-start | bytes 2396168 | tf_op jit(solution)/shard_map/ppermute | solution.py:46
  16.4 5.1 %copy-start.6 = (s32[1,2560]{1,0:T(1,128)}, s32[1,2560]{1,0:T(1,128)S(1)}, u32[]{:S(2)}) copy-start(s32[1,2560]{1,0:T(1,128)S(1)} %fusion.10.refs_0_) | copy-start | bytes 30724
  21.4 18.1 %collective-permute-start.2 = (bf16[1024,384]{1,0:T(8,128)(2,1)}, bf16[1024,384]{1,0:T(8,128)(2,1)}, u32[]{:S(2)}, u32[]{:S(2)}) collective-permute-start(bf16[1024,384]{1,0:T(8,128)(2,1)} %get-tuple-element.45), channel_id=1, source_target_pairs={{0,4},{1,3},{2,6},{3,1},{4,0},{5,7},{6,2},{7,5},{8,12},{9,11},{10,... | collective-permute-start | bytes 2359304 | tf_op jit(solution)/shard_map/ppermute | solution.py:46
  27.1 2.2 %copy-start.10 = (f32[8,128]{1,0:T(8,128)}, f32[8,128]{1,0:T(8,128)S(1)}, u32[]{:S(2)}) copy-start(f32[8,128]{1,0:T(8,128)S(1)} %get-tuple-element.47.refs_3_) | copy-start | bytes 12292
  29.3 11.6 %collective-permute-start.5 = (bf16[528,384]{1,0:T(8,128)(2,1)}, bf16[528,384]{1,0:T(8,128)(2,1)}, u32[]{:S(2)}, u32[]{:S(2)}) collective-permute-start(bf16[528,384]{1,0:T(8,128)(2,1)} %get-tuple-element.54), channel_id=1, source_target_pairs={{0,8},{1,9},{2,10},{3,11},{4,12},{5,13},{6,14},{7,15},{8,0},{9,1},... | collective-permute-start | bytes 1216520 | tf_op jit(solution)/shard_map/ppermute | solution.py:46
  31.9 1.5 %copy-start.3 = (bf16[1280,768]{1,0:T(8,128)(2,1)S(1)}, bf16[1280,768]{1,0:T(8,128)(2,1)}, u32[]{:S(2)}) copy-start(bf16[1280,768]{1,0:T(8,128)(2,1)} %x_ref.1) | copy-start | bytes 5898244
  33.5 0.7 copy-start.7
  34.2 0.7 copy-start.11
  40.8 11.8 %collective-permute-start.4 = (bf16[512,384]{1,0:T(8,128)(2,1)S(1)}, bf16[512,384]{1,0:T(8,128)(2,1)S(1)}, u32[]{:S(2)}, u32[]{:S(2)}) collective-permute-start(bf16[512,384]{1,0:T(8,128)(2,1)S(1)} %get-tuple-element.52), channel_id=1, source_target_pairs={{0,8},{1,9},{2,10},{3,11},{4,12},{5,13},{6,14},{7,15},{8,0},{9,1},... | collective-permute-start | bytes 1179656 | tf_op jit(solution)/shard_map/ppermute | solution.py:46
  42.0 7.0 %collective-permute-start.7 = (bf16[272,384]{1,0:T(8,128)(2,1)S(1)}, bf16[272,384]{1,0:T(8,128)(2,1)S(1)}, u32[]{:S(2)}, u32[]{:S(2)}) collective-permute-start(bf16[272,384]{1,0:T(8,128)(2,1)S(1)} %get-tuple-element.60), channel_id=1, source_target_pairs={{0,4},{1,3},{2,6},{3,1},{4,0},{5,7},{6,2},{7,5},{8,12},{9,11},{10,... | collective-permute-start | bytes 626696 | tf_op jit(solution)/shard_map/ppermute | solution.py:46
  49.1 7.7 %collective-permute-start.9 = (bf16[272,384]{1,0:T(8,128)(2,1)S(1)}, bf16[272,384]{1,0:T(8,128)(2,1)S(1)}, u32[]{:S(2)}, u32[]{:S(2)}) collective-permute-start(bf16[272,384]{1,0:T(8,128)(2,1)S(1)} %get-tuple-element.65.refs_1_), channel_id=1, source_target_pairs={{0,24},{1,25},{2,26},{3,27},{4,28},{5,29},{6,30},{7,31},{8,16},{9,... | collective-permute-start | bytes 626696 | tf_op jit(solution)/shard_map/ppermute | solution.py:46
  53.2 6.1 %collective-permute-start.6 = (bf16[256,384]{1,0:T(8,128)(2,1)S(1)}, bf16[256,384]{1,0:T(8,128)(2,1)S(1)}, u32[]{:S(2)}, u32[]{:S(2)}) collective-permute-start(bf16[256,384]{1,0:T(8,128)(2,1)S(1)} %get-tuple-element.58), channel_id=1, source_target_pairs={{0,2},{1,5},{2,0},{3,7},{4,6},{5,1},{6,4},{7,3},{8,10},{9,13},{10,... | collective-permute-start | bytes 589832 | tf_op jit(solution)/shard_map/ppermute | solution.py:46
  57.1 6.2 %collective-permute-start.11 = (bf16[256,384]{1,0:T(8,128)(2,1)S(1)}, bf16[256,384]{1,0:T(8,128)(2,1)S(1)}, u32[]{:S(2)}, u32[]{:S(2)}) collective-permute-start(bf16[256,384]{1,0:T(8,128)(2,1)S(1)} %get-tuple-element.72.refs_1_), channel_id=1, source_target_pairs={{0,4},{1,3},{2,6},{3,1},{4,0},{5,7},{6,2},{7,5},{8,12},{9,11},{10,... | collective-permute-start | bytes 589832 | tf_op jit(solution)/shard_map/ppermute | solution.py:46
  59.9 9.6 %collective-permute-start.8 = (bf16[256,384]{1,0:T(8,128)(2,1)S(1)}, bf16[256,384]{1,0:T(8,128)(2,1)S(1)}, u32[]{:S(2)}, u32[]{:S(2)}) collective-permute-start(bf16[256,384]{1,0:T(8,128)(2,1)S(1)} %get-tuple-element.63.refs_1_), channel_id=1, source_target_pairs={{0,24},{1,25},{2,26},{3,27},{4,28},{5,29},{6,30},{7,31},{8,16},{9,... | collective-permute-start | bytes 589832 | tf_op jit(solution)/shard_map/ppermute | solution.py:46
  63.4 12.9 %collective-permute-start.13 = (bf16[512,384]{1,0:T(8,128)(2,1)S(1)}, bf16[512,384]{1,0:T(8,128)(2,1)S(1)}, u32[]{:S(2)}, u32[]{:S(2)}) collective-permute-start(bf16[512,384]{1,0:T(8,128)(2,1)S(1)} %get-tuple-element.75.refs_1_), channel_id=1, source_target_pairs={{0,8},{1,9},{2,10},{3,11},{4,12},{5,13},{6,14},{7,15},{8,0},{9,1},... | collective-permute-start | bytes 1179656 | tf_op jit(solution)/shard_map/ppermute | solution.py:46
  70.4 5.8 %collective-permute-start.10 = (bf16[272,384]{1,0:T(8,128)(2,1)S(1)}, bf16[272,384]{1,0:T(8,128)(2,1)S(1)}, u32[]{:S(2)}, u32[]{:S(2)}) collective-permute-start(bf16[272,384]{1,0:T(8,128)(2,1)S(1)} %get-tuple-element.71.refs_1_), channel_id=1, source_target_pairs={{0,2},{1,5},{2,0},{3,7},{4,6},{5,1},{6,4},{7,3},{8,10},{9,13},{10,... | collective-permute-start | bytes 626696 | tf_op jit(solution)/shard_map/ppermute | solution.py:46
  77.2 0.6 copy-start.8
  77.8 3.3 %collective-permute-start.14 = (bf16[1024,384]{1,0:T(8,128)(2,1)}, bf16[1024,384]{1,0:T(8,128)(2,1)}, u32[]{:S(2)}, u32[]{:S(2)}) collective-permute-start(bf16[1024,384]{1,0:T(8,128)(2,1)} %get-tuple-element.77.refs_2_), channel_id=1, source_target_pairs={{0,1},{1,0},{2,3},{3,2},{4,5},{5,4},{6,7},{7,6},{8,9},{9,8},{10,11... | collective-permute-start | bytes 2359304 | tf_op jit(solution)/shard_map/ppermute | solution.py:46
  77.8 16.2 %collective-permute-start.16 = (bf16[1024,384]{1,0:T(8,128)(2,1)}, bf16[1024,384]{1,0:T(8,128)(2,1)}, u32[]{:S(2)}, u32[]{:S(2)}) collective-permute-start(bf16[1024,384]{1,0:T(8,128)(2,1)} %get-tuple-element.77.refs_2_), channel_id=1, source_target_pairs={{0,2},{1,5},{2,0},{3,7},{4,6},{5,1},{6,4},{7,3},{8,10},{9,13},{10,... | collective-permute-start | bytes 2359304 | tf_op jit(solution)/shard_map/ppermute | solution.py:46
  79.2 11.0 %collective-permute-start.12 = (bf16[528,384]{1,0:T(8,128)(2,1)S(1)}, bf16[528,384]{1,0:T(8,128)(2,1)S(1)}, u32[]{:S(2)}, u32[]{:S(2)}) collective-permute-start(bf16[528,384]{1,0:T(8,128)(2,1)S(1)} %get-tuple-element.74.refs_1_), channel_id=1, source_target_pairs={{0,8},{1,9},{2,10},{3,11},{4,12},{5,13},{6,14},{7,15},{8,0},{9,1},... | collective-permute-start | bytes 1216520 | tf_op jit(solution)/shard_map/ppermute | solution.py:46
  81.1 23.6 %copy-start.4 = (s32[1,1280]{1,0:T(1,128)}, s32[1,1280]{1,0:T(1,128)S(1)}, u32[]{:S(2)}) copy-start(s32[1,1280]{1,0:T(1,128)S(1)} %compare_select_fusion.6.refs_1_.gid_ref) | copy-start | bytes 15364
  81.2 0.7 copy-start.9
  91.2 13.5 %collective-permute-start.15 = (bf16[1040,384]{1,0:T(8,128)(2,1)}, bf16[1040,384]{1,0:T(8,128)(2,1)}, u32[]{:S(2)}, u32[]{:S(2)}) collective-permute-start(bf16[1040,384]{1,0:T(8,128)(2,1)} %get-tuple-element.80.rest_2_), channel_id=1, source_target_pairs={{0,4},{1,3},{2,6},{3,1},{4,0},{5,7},{6,2},{7,5},{8,12},{9,11},{10,... | collective-permute-start | bytes 2396168 | tf_op jit(solution)/shard_map/ppermute | solution.py:46
  94.1 3.6 %collective-permute-start.17 = (bf16[1024,384]{1,0:T(8,128)(2,1)}, bf16[1024,384]{1,0:T(8,128)(2,1)S(1)}, u32[]{:S(2)}, u32[]{:S(2)}) collective-permute-start(bf16[1024,384]{1,0:T(8,128)(2,1)} %collective-permute-done.16.refs_2_), channel_id=1, source_target_pairs={{0,1},{1,0},{2,3},{3,2},{4,5},{5,4},{6,7},{7,6},{8,9},{9,8},{10,11... | collective-permute-start | bytes 2359304 | tf_op jit(solution)/shard_map/ppermute | solution.py:46
  94.1 11.0 %collective-permute-start.19 = (bf16[1040,384]{1,0:T(8,128)(2,1)}, bf16[1040,384]{1,0:T(8,128)(2,1)}, u32[]{:S(2)}, u32[]{:S(2)}) collective-permute-start(bf16[1040,384]{1,0:T(8,128)(2,1)} %get-tuple-element.80.rest_2_), channel_id=1, source_target_pairs={{0,1},{1,0},{2,3},{3,2},{4,5},{5,4},{6,7},{7,6},{8,9},{9,8},{10,11... | collective-permute-start | bytes 2396168 | tf_op jit(solution)/shard_map/ppermute | solution.py:46
  104.7 2.7 %collective-permute-start.18 = (bf16[1040,384]{1,0:T(8,128)(2,1)}, bf16[1040,384]{1,0:T(8,128)(2,1)}, u32[]{:S(2)}, u32[]{:S(2)}) collective-permute-start(bf16[1040,384]{1,0:T(8,128)(2,1)} %behind.1.rest_0_), channel_id=1, source_target_pairs={{0,1},{1,0},{2,3},{3,2},{4,5},{5,4},{6,7},{7,6},{8,9},{9,8},{10,11... | collective-permute-start | bytes 2396168 | tf_op jit(solution)/shard_map/ppermute | solution.py:46
  107.4 0.7 copy-start.5
